TPU v7x, 32 devices: a whole 2x2x4 slice. The times are simulated.
32 devices in a mesh: group: 2 (over y), dp: 4 (over z), tensor: 4 (over x, core).
Axes of the slice: x: 2, y: 2, z: 4, core: 2. Of those that a mesh axis runs over, the one named last changes fastest.
Arguments:
- acts: bfloat16 [3072, 6144], P(('group', 'dp'), 'tensor'), parts along dimension 0, may hold values from -6 to 6
- grads: bfloat16 [3072, 2, 16384], P(('group', 'dp'), None, 'tensor'), parts along dimension 0, may hold values from -6 to 6
- routes: int32 [3072, 2], P(('group', 'dp')), parts along dimension 0, may hold values from 0 to 7, as said below
- example_ids: int32 [3072], P(('group', 'dp')), parts along dimension 0, may hold values from 0 to 3, as said below
- expert_counts: int32 [4], P('group'), parts along dimension 0, may hold values from 384 to 1535
- basis_in: bfloat16 [2, 6144, 512], P(None, 'tensor'), may hold values from -0.078125 to 0.078125
- basis_out: bfloat16 [2, 16384, 512], P(None, 'tensor'), may hold values from -0.046875 to 0.046875
Outputs:
- eigen_corrected: float32 [4, 512, 512], P('group', 'tensor', 'dp'), parts along dimension 0
There are 2 independent parts, one for each index of `group`. A program takes and returns all parts, laid end to end along the dimension named above; an argument that names none is the same for every part. Nothing has to cross between parts.
Inputs may be any that keep to these rules, and one draw needn't show every extreme that they name: `routes`: each token names two different experts; in the rows of one device each of experts 0 and 1 is named at most 192 times, and one of them exactly 192 times. `example_ids`: the rows of one device form four nonempty contiguous runs belonging to four different examples; every example holds between 192 and 576 tokens.
All inputs are finite; a program needn't handle non-finite values.
Results may differ from a plain program's by a relative error of at most 0.0036.
Values may be sent and summed in bfloat16 or wider, within the bound.
No kernel may reach another device: no remote copies, remote signals or barrier semaphores. Data moves between devices by JAX's collectives and lax.ppermute only.
A program may use at most 64 MiB of HBM per device.

v0:
```python
import jax
import jax.numpy as jnp
from jax import lax
from jax.sharding import PartitionSpec as P

EX_DEV = 1


def compact(routes, expert, capacity):
    tok_count = routes.shape[0]
    second_hit = routes[:, 1] == expert
    routed = (routes[:, 0] == expert) | second_hit
    order = jnp.cumsum(routed.astype(jnp.int32)) - 1
    slots = jnp.arange(capacity, dtype=jnp.int32)
    match = routed[None, :] & (order[None, :] == slots[:, None])
    token_index = jnp.arange(tok_count, dtype=jnp.int32)
    positions = jnp.sum(jnp.where(match, token_index[None, :], 0), axis=1)
    filled = jnp.any(match, axis=1)
    return (positions, filled, second_hit[positions])


def shards(acts, grads, routes, example_ids, expert_counts, basis_in, basis_out):
    capacity = acts.shape[0] // 2
    experts = basis_in.shape[0]
    parts_in, parts_out, label_rows = ([], [], [])
    for expert in range(experts):
        positions, filled, second = compact(routes, expert, capacity)
        chosen = grads[positions]
        grad_rows = jnp.where(second[:, None], chosen[:, 1, :], chosen[:, 0, :])
        parts_in.append(
            jnp.dot(acts[positions], basis_in[expert], preferred_element_type=jnp.float32)
        )
        parts_out.append(jnp.dot(grad_rows, basis_out[expert], preferred_element_type=jnp.float32))
        label_rows.append(jnp.where(filled, example_ids[positions], -1))
    part_in = jnp.stack(parts_in)
    part_out = jnp.stack(parts_out)
    labels = jnp.stack(label_rows)
    slice_width = basis_out.shape[2] // lax.axis_size("tensor")
    summed_in, summed_out = lax.psum((part_in, part_out), "tensor")
    rot_in = summed_in.astype(jnp.bfloat16)
    rot_out = lax.dynamic_slice_in_dim(
        summed_out.astype(jnp.bfloat16), lax.axis_index("tensor") * slice_width, slice_width, 2
    )
    owned_count = EX_DEV
    wanted = jnp.arange(lax.axis_size("dp") * owned_count, dtype=jnp.int32)
    onehot = (labels[:, :, None] == wanted[None, None, :]).astype(jnp.bfloat16)
    spread = onehot[:, :, :, None] * rot_out[:, :, None, :]
    owned_sums = lax.psum_scatter(
        jnp.einsum("ecnw,eca->newa", spread, rot_in, preferred_element_type=jnp.float32),
        "dp",
        scatter_dimension=0,
        tiled=True,
    )
    squared = jnp.sum(owned_sums * owned_sums, axis=0)
    totals = lax.psum_scatter(squared, "dp", scatter_dimension=2, tiled=True)
    return totals / expert_counts.astype(jnp.float32)[:, None, None]


def solution(mesh):
    placed = (
        P(("group", "dp"), "tensor"),
        P(("group", "dp"), None, "tensor"),
        P(("group", "dp"), None),
        P(("group", "dp")),
        P("group"),
        P(None, "tensor", None),
        P(None, "tensor", None),
    )
    return jax.shard_map(
        shards, mesh=mesh, in_specs=placed, out_specs=P("group", "tensor", "dp"), check_vma=False
    )
```

profile of v0, /device:TPU:0, one launch (start us, length us, event | category | flops | bytes accessed | tf_op | source)
XLA Modules:
  0.0 223.6 jit_solution(7591835700973723009)
XLA Ops:
  6.5 0.0 all-reduce.5.cloned.1.call-start
  6.5 0.8 compare_reduce_fusion.2
  7.4 0.8 fusion.43
  8.1 0.3 reduce-window.16
  8.5 0.1 slice.48
  8.6 0.1 slice_reduce_fusion.1
  8.7 0.1 add_bitcast_fusion.1
  8.8 0.1 select_reduce_fusion.1
  8.9 1.6 gather_fusion.4
  10.5 13.9 %gather_fusion.5 = bf16[192,2,4096]{2,1,0:T(2,128)(2,1)} fusion(bf16[384,2,4096]{2,1,0:T(2,128)(2,1)} %param.8, s32[1024]{0:T(1024)S(1)} %pad_clamp_fusion.1), kind=kCustom, calls=%fused_computation.5 | custom fusion | bytes 6292224 | tf_op jit(solution)/shard_map/gather | solution.py:28
  24.4 0.3 reduce-window.24
  24.7 0.1 slice.51
  24.8 0.1 slice_reduce_fusion
  24.9 0.1 add_bitcast_fusion
  25.0 0.1 select_reduce_fusion
  25.2 1.6 gather_fusion.6
  26.7 13.7 %gather_fusion.7 = bf16[192,2,4096]{2,1,0:T(2,128)(2,1)} fusion(bf16[384,2,4096]{2,1,0:T(2,128)(2,1)} %param.8, s32[1024]{0:T(1024)S(1)} %pad_clamp_fusion), kind=kCustom, calls=%fused_computation.7 | custom fusion | bytes 6292224 | tf_op jit(solution)/shard_map/gather | solution.py:28
  40.4 1.1 gather_fusion
  41.5 0.0 copy-start.1
  41.5 1.1 gather_fusion.1
  42.6 0.1 fusion.37
  42.7 1.6 gather_fusion.2
  44.3 1.6 gather_fusion.3
  46.0 0.1 fusion.39
  46.1 0.0 slice-start
  46.1 8.2 %broadcast_select_fusion.1 = bf16[192,1,4096]{2,1,0:T(2,128)(2,1)S(1)} fusion(pred[192]{0:T(512)(128)(4,1)S(1)} %gather_fusion.4, bf16[192,2,4096]{2,1,0:T(2,128)(2,1)} %gather_fusion.5), kind=kLoop, calls=%fused_computation.9 | loop fusion | flops 786432 | bytes 4718784 | tf_op jit(solution)/shard_map/jit(_where)/select_n | solution.py:29
  54.3 0.0 slice-start.1
  54.3 4.4 %fusion.22 = f32[1,192,512]{2,1,0:T(8,128)S(1)} fusion(bf16[2,4096,512]{2,1,0:T(8,128)(2,1)} %param.13, bf16[192,1,4096]{2,1,0:T(2,128)(2,1)S(1)} %broadcast_select_fusion.1), kind=kOutput, calls=%fused_computation.29 | convolution fusion | flops 805306368 | bytes 6160384 | tf_op jit(solution)/shard_map/dot_general | solution.py:33
  58.7 6.0 %broadcast_select_fusion = bf16[192,1,4096]{2,1,0:T(2,128)(2,1)S(1)} fusion(pred[192]{0:T(512)(128)(4,1)S(1)} %gather_fusion.6, bf16[192,2,4096]{2,1,0:T(2,128)(2,1)S(1)} %copy-done.2), kind=kLoop, calls=%fused_computation.8 | loop fusion | flops 786432 | bytes 4718784 | tf_op jit(solution)/shard_map/jit(_where)/select_n | solution.py:29
  64.7 0.0 slice-done
  64.8 0.0 copy-start.3
  64.8 2.0 fusion.27
  66.8 0.5 fusion.16
  67.2 0.5 fusion.19
  67.7 0.1 pad_maximum_fusion
  67.9 0.0 copy-start.5
  67.9 34.3 %all-reduce.6 = (bf16[2,192,512]{2,1,0:T(8,128)(2,1)S(1)}, bf16[2,192,512]{2,1,0:T(8,128)(2,1)S(1)}) all-reduce(f32[2,192,512]{2,1,0:T(8,128)S(1)} %get-tuple-element.13, f32[2,192,512]{2,1,0:T(8,128)S(1)} %get-tuple-element.14), channel_id=1, replica_groups=mesh['group'=2,'dp'=4,'tensor'=4] {'tensor'}, use_global_device_ids=true, to_apply=%region_6.7 | all-reduce | flops 393216 | bytes 2359296 | tf_op jit(solution)/shard_map/psum | solution.py:39
  102.3 0.0 copy-start.4
  102.3 2.0 convolution_bitcast_fusion
  104.3 0.0 all-reduce.5.cloned.1.call-update
  104.3 0.0 reduce-scatter.5.cloned.1.call-start
  104.4 0.6 dynamic-slice
  105.0 86.7 %all-reduce.5.cloned.1.call-done = f32[4,2,128,512]{2,3,0,1:T(8,128)} async-done(((f32[4,2,128,512]{2,3,0,1:T(8,128)}), f32[4,2,128,512]{2,3,0,1:T(8,128)}) %all-reduce.5.cloned.1.call-update) | async-done | bytes 2097168
  191.7 2.5 %fusion.32 = f32[2,128,512]{1,2,0:T(8,128)} fusion(f32[4,2,128,512]{2,3,0,1:T(8,128)} %all-reduce.5.cloned.1.call-done, u32[]{:T(128)} %bitcast.29), kind=kLoop, calls=%fused_computation.34 | loop fusion | flops 131072 | bytes 1048580 | tf_op jit(solution)/shard_map/reduce_sum | solution.py:54
  194.2 0.0 reduce-scatter.5.cloned.1.call-update
  194.3 20.8 %reduce-scatter.5.cloned.1.call-done = f32[2,128,128]{1,2,0:T(8,128)} async-done(((f32[2,128,512]{1,2,0:T(8,128)}), f32[2,128,128]{1,2,0:T(8,128)}) %reduce-scatter.5.cloned.1.call-update) | async-done | bytes 131088 | tf_op jit(solution)/shard_map/reduce_scatter | solution.py:55
  215.0 1.0 broadcast_divide_fusion
  216.0 0.8 copy.12
  (24 shorter events, 0.2 us)
Async XLA Ops:
  6.5 33.9 %copy-start = (bf16[384,1536]{1,0:T(8,128)(2,1)S(1)}, bf16[384,1536]{1,0:T(8,128)(2,1)}, u32[]{:S(2)}) copy-start(bf16[384,1536]{1,0:T(8,128)(2,1)} %param.7) | copy-start | bytes 3538948
  6.5 185.2 %all-reduce.5.cloned.1.call-start = ((), (), s32[]{:S(2)}) async-start(), calls=%async_computation.2 | async-start | bytes 4194304
  41.5 1.2 copy-start.1
  46.1 18.6 %slice-start = ((s8[8388608]{0:T(1024)(128)(4,1)}), s8[4194304]{0:T(1024)(128)(4,1)S(1)}, s32[]{:S(2)}) async-start(s8[8388608]{0:T(1024)(128)(4,1)} %bitcast.78), calls=%async_computation.3 | async-start | bytes 8388608
  54.3 4.4 %copy-start.2 = (bf16[192,2,4096]{2,1,0:T(2,128)(2,1)S(1)}, bf16[192,2,4096]{2,1,0:T(2,128)(2,1)}, u32[]{:S(2)}) copy-start(bf16[192,2,4096]{2,1,0:T(2,128)(2,1)} %gather_fusion.7) | copy-start | bytes 9437188
  54.3 10.4 %slice-start.1 = ((s8[8388608]{0:T(1024)(128)(4,1)}), s8[4194304]{0:T(1024)(128)(4,1)S(1)}, s32[]{:S(2)}) async-start(s8[8388608]{0:T(1024)(128)(4,1)} %bitcast.78), calls=%async_computation.4 | async-start | bytes 8388608
  64.8 2.0 copy-start.3
  67.9 36.5 %copy-start.5 = (u32[32]{0:T(128)S(1)}, u32[32]{0:T(128)}, u32[]{:S(2)}) copy-start(u32[32]{0:T(128)} %constant.29) | copy-start | bytes 388
  102.3 91.9 %copy-start.4 = (s32[2]{0:T(128)S(1)}, s32[2]{0:T(128)}, u32[]{:S(2)}) copy-start(s32[2]{0:T(128)} %param.11) | copy-start | bytes 28
  104.3 110.7 %reduce-scatter.5.cloned.1.call-start = ((), (), s32[]{:S(2)}) async-start(), calls=%async_computation.1 | async-start | bytes 655360 | tf_op jit(solution)/shard_map/reduce_scatter | solution.py:55
Sparse Core Ops, SparseCore 0:
  104.5 87.1 all-reduce.4
  194.4 20.6 reduce-scatter.4
where the time goes:
time: 224 us
  waiting for transfers between devices  108 us (48%)
  local copies, waits for them, and re-layouts  37.8 us (17%)
  blocking collectives  34.3 us (15%)
  other arithmetic  20.9 us (9%)
  between operations  13.7 us (6%)
  matrix products  9.33 us (4%)
    unnamed x3, waiting for transfers between devices  86.7 us
    psum x1, blocking collectives, shards(): summed_in, summed_out = lax.psum((part_in, part_out), 'tensor')  34.3 us
    gather x2, local copies, waits for them, and re-layouts, shards(): chosen = grads[positions]  27.6 us
    reduce_scatter x1, waiting for transfers between devices, shards(): totals = lax.psum_scatter(squared, 'dp', scatter_dimension=2, tiled=True)  20.8 us
    select_n x2, other arithmetic, shards(): grad_rows = jnp.where(second[:, None], chosen[:, 1, :], chosen[:, 0, :])  14.2 us
    dot_general x2, matrix products, shards(): jnp.dot(grad_rows, basis_out[expert], preferred_element_type=jnp.float32)  6.4 us
  transfers between devices with their start and end apart: 2, of which 2 were waited for; matrix products, arithmetic and copies ran while one was open for 0% of the time, Pallas kernels for 0%

commit v1 on v0

--- a/solution.py
+++ b/solution.py
@@ -1,7 +1,262 @@
+import functools
+
 import jax
 import jax.numpy as jnp
 from jax import lax
+from jax.experimental import pallas as pl
+from jax.experimental.pallas import tpu as pltpu
 from jax.sharding import PartitionSpec as P
+
+F32 = jnp.float32
+BF16 = jnp.bfloat16
+CHUNK = 512
+VMEM = 40 * 2**20
+LABEL_ROWS = 16
+
+
+def iota(shape, dim):
+    return lax.broadcasted_iota(jnp.int32, shape, dim)
+
+
+def dot(a, b):
+    return jnp.dot(a, b, preferred_element_type=F32)
+
+
+def rotate_kernel(
+    acts, grads, routes, ids, basis_in, basis_out,
+    keep, send, label,
+    acts_v, grads_v, routes_v, ids_v, bin_v, bout_v, acc_in, acc_out, pick, sems,
+):
+    tokens, _, hidden = grads.shape
+    experts, features, width = basis_in.shape
+    cap = tokens // 2
+    steps = hidden // CHUNK
+    copies = []
+
+    def fetch(src, dst):
+        copy = pltpu.make_async_copy(src, dst, sems.at[len(copies)])
+        copy.start()
+        copies.append(copy)
+        return copy
+
+    first = [fetch(routes, routes_v), fetch(ids, ids_v)]
+    acts_in = fetch(acts, acts_v)
+    bases_in = [fetch(basis_in.at[e], bin_v.at[e]) for e in range(experts)]
+    outs = []
+    for s in range(steps):
+        cols = pl.ds(s * CHUNK, CHUNK)
+        outs.append(
+            (fetch(grads.at[:, :, cols], grads_v.at[s]), fetch(basis_out.at[:, cols, :], bout_v.at[s]))
+        )
+
+    for copy in first:
+        copy.wait()
+    routes_f = routes_v[...].astype(F32)
+    hits = [
+        jnp.max((routes_v[...] == e).astype(F32), axis=0, keepdims=True) for e in range(experts)
+    ]
+    rows = jnp.concatenate(hits + [jnp.zeros((8 - experts, tokens), F32)], axis=0).astype(BF16)
+    upto = (iota((tokens, tokens), 0) <= iota((tokens, tokens), 1)).astype(BF16)
+    order = dot(rows, upto)
+    slots = iota((cap, tokens), 0).astype(F32) + 1.0
+    pick_in = jnp.concatenate(
+        [((order[e : e + 1] == slots) & (hits[e] > 0.5)).astype(BF16) for e in range(experts)],
+        axis=0,
+    )
+    repeat = (iota((tokens, 2 * tokens), 0) == iota((tokens, 2 * tokens), 1) // 2).astype(BF16)
+    wide = dot(
+        jnp.concatenate([order[:experts], routes_f, jnp.zeros((8 - experts - 2, tokens), F32)], axis=0).astype(BF16),
+        repeat,
+    )
+    odd = iota((1, 2 * tokens), 1) % 2 == 1
+    routed_to = jnp.where(odd, wide[experts + 1 : experts + 2], wide[experts : experts + 1])
+    slots = iota((cap, 2 * tokens), 0).astype(F32) + 1.0
+    for e in range(experts):
+        pick[e * cap : (e + 1) * cap, :] = (
+            (wide[e : e + 1] == slots) & (routed_to == float(e))
+        ).astype(BF16)
+    numbers = jnp.broadcast_to(ids_v[...].astype(F32) + 1.0, (8, tokens)).astype(BF16)
+    named = lax.dot_general(numbers, pick_in, (((1,), (1,)), ((), ())), preferred_element_type=F32)
+    block = jnp.zeros((LABEL_ROWS, 128), F32)
+    row = iota((LABEL_ROWS, 128), 0)
+    for e in range(experts):
+        mine = named[0:1, e * cap : (e + 1) * cap]
+        mine = jnp.concatenate([mine, jnp.zeros((1, 256 - cap), F32)], axis=1)
+        for half in range(2):
+            block = jnp.where(row == 2 * e + half, mine[:, half * 128 : (half + 1) * 128], block)
+    label[...] = block.astype(BF16)
+
+    acts_in.wait()
+    chosen = dot(pick_in, acts_v[...]).astype(BF16)
+    for e in range(experts):
+        bases_in[e].wait()
+        acc_in[e] = dot(chosen[e * cap : (e + 1) * cap], bin_v[e])
+    for s in range(steps):
+        for copy in outs[s]:
+            copy.wait()
+        chosen = dot(pick[...], grads_v[s].reshape(2 * tokens, CHUNK)).astype(BF16)
+        for e in range(experts):
+            part = dot(chosen[e * cap : (e + 1) * cap], bout_v[s, e])
+            if s == 0:
+                acc_out[e] = part
+            else:
+                acc_out[e] += part
+
+    core = lax.rem(lax.axis_index("tensor"), 2)
+    half = cap // 2
+    at = 0
+    for q in range(width // 128):
+        for e in range(experts):
+            for ref, which in ((keep, core), (send, 1 - core)):
+                ref[at : at + half, :] = acc_in[
+                    e, pl.ds(pl.multiple_of(which * half, 8), half), q * 128 : (q + 1) * 128
+                ]
+            at += half
+    for x in range(width // 256):
+        for e in range(experts):
+            for ref, which in ((keep, core), (send, 1 - core)):
+                ref[at : at + cap, :] = acc_out[
+                    e, :, pl.ds(pl.multiple_of((2 * x + which) * 128, 128), 128)
+                ]
+            at += cap
+
+
+def pair_kernel(kept, got, keep, send):
+    inner = kept.shape[0] // 2
+    outer = inner // 2
+    x = lax.div(lax.axis_index("tensor"), 2)
+    total = kept[:inner, :] + got[:inner, :]
+    keep[:inner, :] = total
+    send[:inner, :] = total.astype(BF16)
+    mine = pl.ds(pl.multiple_of(inner + x * outer, 8), outer)
+    keep[inner:, :] = kept[mine, :] + got[mine, :]
+    other = pl.ds(pl.multiple_of(inner + (1 - x) * outer, 8), outer)
+    send[inner:, :] = (kept[other, :] + got[other, :]).astype(BF16)
+
+
+def payload_kernel(kept, got, label, *pays):
+    dp = len(pays)
+    outer = kept.shape[0] // 3
+    slab = 2 * outer // dp
+    d = lax.axis_index("dp")
+    out = (kept[2 * outer :, :] + got[2 * outer :, :].astype(F32)).astype(BF16)
+    for k, pay in enumerate(pays):
+        rows = pl.ds(pl.multiple_of((d ^ k) * slab, 16), slab)
+        pay[:slab, :] = (kept[rows, :] + got[rows, :].astype(F32)).astype(BF16)
+        pay[slab : slab + outer, :] = out
+        pay[slab + outer :, :] = label[...]
+
+
+def block_kernel(dp, counts, *refs):
+    own, sibling, result = refs[:dp], refs[dp : 2 * dp], refs[2 * dp]
+    experts = result.shape[0]
+    outer = (own[0].shape[0] - LABEL_ROWS) * 2 // 3
+    slab = outer // 2
+    cap = outer // experts
+    half = cap // 2
+    first = lax.rem(lax.axis_index("tensor"), 2) == 0
+    for e in range(experts):
+        total = None
+        for k in range(dp):
+            labels = own[k][slab + outer :, :].astype(F32)
+            labels = jnp.concatenate(
+                [labels[2 * e : 2 * e + 1], labels[2 * e + 1 : 2 * e + 2, : cap - 128]], axis=1
+            )
+            rows_out = own[k][slab + e * cap : slab + (e + 1) * cap, :].T
+            mine = own[k][e * half : (e + 1) * half, :]
+            theirs = sibling[k][e * half : (e + 1) * half, :]
+            rows_in = jnp.concatenate(
+                [jnp.where(first, mine, theirs), jnp.where(first, theirs, mine)], axis=0
+            )
+            masked = jnp.concatenate(
+                [
+                    jnp.where(labels == float(n + 1), rows_out, jnp.zeros_like(rows_out))
+                    for n in range(dp)
+                ],
+                axis=0,
+            )
+            part = dot(masked, rows_in)
+            total = part if total is None else total + part
+        side = total.shape[0] // dp
+        squares = total * total
+        summed = squares[:side]
+        for n in range(1, dp):
+            summed = summed + squares[n * side : (n + 1) * side]
+        result[e] = summed / counts[e].astype(F32)
+
+
+def any_spec():
+    return pl.BlockSpec(memory_space=pl.ANY)
+
+
+def params():
+    return pltpu.CompilerParams(vmem_limit_bytes=VMEM)
+
+
+def fast(acts, grads, routes, example_ids, expert_counts, basis_in, basis_out):
+    tokens, _, hidden = grads.shape
+    experts, features, width = basis_in.shape
+    cap = tokens // 2
+    dp = lax.axis_size("dp")
+    steps = hidden // CHUNK
+    rows = 2 * experts * cap * width // 256
+    f32_rows = jax.ShapeDtypeStruct((rows, 128), F32)
+    copies = 2 + 1 + experts + 2 * steps
+    keep, send, label = pl.pallas_call(
+        rotate_kernel,
+        out_shape=(f32_rows, f32_rows, jax.ShapeDtypeStruct((LABEL_ROWS, 128), BF16)),
+        in_specs=[any_spec()] * 6,
+        scratch_shapes=[
+            pltpu.VMEM(acts.shape, BF16),
+            pltpu.VMEM((steps, tokens, 2, CHUNK), BF16),
+            pltpu.VMEM((2, tokens), jnp.int32),
+            pltpu.VMEM((1, tokens), jnp.int32),
+            pltpu.VMEM(basis_in.shape, BF16),
+            pltpu.VMEM((steps, experts, CHUNK, width), BF16),
+            pltpu.VMEM((experts, cap, width), F32),
+            pltpu.VMEM((experts, cap, width), F32),
+            pltpu.VMEM((experts * cap, 2 * tokens), BF16),
+            pltpu.SemaphoreType.DMA((copies,)),
+        ],
+        compiler_params=params(),
+        name="rotate",
+    )(acts, grads, routes.T, example_ids.reshape(1, tokens), basis_in, basis_out)
+
+    core = [(t, t ^ 1) for t in range(4)]
+    across = [(t, t ^ 2) for t in range(4)]
+    got = lax.ppermute(send, "tensor", core)
+    shorter = rows * 3 // 4
+    keep, send = pl.pallas_call(
+        pair_kernel,
+        out_shape=(
+            jax.ShapeDtypeStruct((shorter, 128), F32),
+            jax.ShapeDtypeStruct((shorter, 128), BF16),
+        ),
+        compiler_params=params(),
+        name="pair",
+    )(keep, got)
+    got = lax.ppermute(send, "tensor", across)
+    outer = shorter // 3
+    pay_rows = 2 * outer // dp + outer + LABEL_ROWS
+    pays = pl.pallas_call(
+        payload_kernel,
+        out_shape=[jax.ShapeDtypeStruct((pay_rows, 128), BF16)] * dp,
+        compiler_params=params(),
+        name="payload",
+    )(keep, got, label)
+    own = [pays[0]]
+    for k in range(1, dp):
+        own.append(lax.ppermute(pays[k], "dp", [(d, d ^ k) for d in range(dp)]))
+    sibling = [lax.ppermute(pay, "tensor", core) for pay in own]
+    return pl.pallas_call(
+        functools.partial(block_kernel, dp),
+        out_shape=jax.ShapeDtypeStruct((experts, 128, 128), F32),
+        in_specs=[pl.BlockSpec(memory_space=pltpu.SMEM)]
+        + [pl.BlockSpec(memory_space=pltpu.VMEM)] * (2 * dp),
+        compiler_params=params(),
+        name="blocks",
+    )(expert_counts, *own, *sibling)
+
 
 EX_DEV = 1
 
@@ -19,7 +274,7 @@
     return (positions, filled, second_hit[positions])
 
 
-def shards(acts, grads, routes, example_ids, expert_counts, basis_in, basis_out):
+def general(acts, grads, routes, example_ids, expert_counts, basis_in, basis_out):
     capacity = acts.shape[0] // 2
     experts = basis_in.shape[0]
     parts_in, parts_out, label_rows = ([], [], [])
@@ -56,6 +311,12 @@
     return totals / expert_counts.astype(jnp.float32)[:, None, None]
 
 
+def shards(*args):
+    width = args[5].shape[2]
+    fits = lax.axis_size("tensor") == 4 and lax.axis_size("dp") == 4 and width == 512
+    return (fast if fits else general)(*args)
+
+
 def solution(mesh):
     placed = (
         P(("group", "dp"), "tensor"),

time: 224 us -> 49.6 us (0.22)
  waiting for transfers between devices: 108 us -> 21.6 us
  blocking collectives: 34.3 us -> 0 us
  local copies, waits for them, and re-layouts: 37.8 us -> 7.31 us
  other arithmetic: 20.9 us -> 0 us
  between operations: 13.7 us -> 0.03 us
  Pallas kernels: 0 us -> 11.9 us
  matrix products: 9.33 us -> 0 us
  starting transfers between devices: 0.04 us -> 8.44 us
    unnamed x3 -> x0, waiting for transfers between devices: 86.7 us -> none
    gather x8 -> x0, local copies, waits for them, and re-layouts: 36 us -> none  [the longest x2 27.6 us: shards(): chosen = grads[positions]]
    psum x1 -> x0, blocking collectives: 34.3 us -> none  [shards(): summed_in, summed_out = lax.psum((part_in, part_out), 'tensor')]
    ppermute x0 -> x9, waiting for transfers between devices: none -> 21.6 us  [the longest x3 11.3 us: fast(): own.append(lax.ppermute(pays[k], 'dp', [(d, d ^ k) for d in range(dp)]))]
    reduce_scatter x1 -> x0, waiting for transfers between devices: 20.8 us -> none  [shards(): totals = lax.psum_scatter(squared, 'dp', scatter_dimension=2, tiled=True)]
    select_n x6 -> x0, other arithmetic: 14.2 us -> none  [the longest x2 14.2 us: shards(): grad_rows = jnp.where(second[:, None], chosen[:, 1, :], chosen[:, 0, :])]
    pallas_call x0 -> x4, Pallas kernels: none -> 11.9 us  [the longest x1 9.79 us: fast(): pl.pallas_call(rotate_kernel, out_shape=(f32_rows, f32_rows, jax.ShapeDty...]
    dot_general x5 -> x0, matrix products: 9.33 us -> none  [the longest x2 6.4 us: shards(): jnp.dot(grad_rows, basis_out[expert], preferred_element_type=jnp.float32)]
  transfers between devices with their start and end apart: 2 -> 9, of which waited for: 2 -> 6; matrix products, arithmetic and copies ran while one was open for 0% -> 0% of each run, Pallas kernels for 0% -> 0%
where the time goes in v1:
time: 49.6 us; the launch traced here: 49.3 us
  waiting for transfers between devices  21.6 us (44%)
  Pallas kernels  11.9 us (24%)
  starting transfers between devices  8.44 us (17%)
  local copies, waits for them, and re-layouts  7.31 us (15%)
    ppermute x3, waiting for transfers between devices, fast(): own.append(lax.ppermute(pays[k], 'dp', [(d, d ^ k) for d in range(dp)]))  11.3 us
    pallas_call x1, Pallas kernels, fast(): pl.pallas_call(rotate_kernel, out_shape=(f32_rows, f32_rows, jax.ShapeDty...  9.79 us
    ppermute x1, waiting for transfers between devices, fast(): got = lax.ppermute(send, 'tensor', across)  7.31 us
    unnamed x10, local copies, waits for them, and re-layouts  6.63 us
    ppermute x3, starting transfers between devices, fast(): own.append(lax.ppermute(pays[k], 'dp', [(d, d ^ k) for d in range(dp)]))  4.48 us
    ppermute x1, starting transfers between devices, fast(): got = lax.ppermute(send, 'tensor', across)  2.92 us
    pallas_call x1, Pallas kernels, fast(): pl.pallas_call(functools.partial(block_kernel, dp), out_shape=jax.ShapeDt...  1.95 us
    ppermute x1, waiting for transfers between devices, fast(): got = lax.ppermute(send, 'tensor', core)  1.91 us
  transfers between devices with their start and end apart: 9, of which 6 were waited for; matrix products, arithmetic and copies ran while one was open for 0% of the time, Pallas kernels for 0%

profile of v1, /device:TPU:0, one launch (start us, length us, event | category | flops | bytes accessed | tf_op | source)
XLA Modules:
  0.0 49.3 jit_solution(15096697538163021916)
XLA Ops:
  0.0 0.7 %reshape.3.ids = s32[1,384]{1,0:T(1,128)S(1)} reshape(s32[384]{0:T(512)} %param.10) | data formatting | bytes 3072 | tf_op jit(solution)/shard_map/reshape | solution.py:223
  0.7 0.0 copy-start
  0.7 2.8 %copy-done = bf16[384,2,4096]{2,1,0:T(2,128)(2,1)S(1)} copy-done((bf16[384,2,4096]{2,1,0:T(2,128)(2,1)S(1)}, bf16[384,2,4096]{2,1,0:T(2,128)(2,1)}, u32[]{:S(2)}) %copy-start) | copy-done | bytes 6291480
  3.5 0.0 copy-start.1
  3.5 1.9 %copy-done.1 = bf16[2,1536,512]{2,1,0:T(8,128)(2,1)S(1)} copy-done((bf16[2,1536,512]{2,1,0:T(8,128)(2,1)S(1)}, bf16[2,1536,512]{2,1,0:T(8,128)(2,1)}, u32[]{:S(2)}) %copy-start.1) | copy-done | bytes 3145752
  5.4 0.0 copy-start.2
  5.4 1.3 %copy-done.2 = bf16[384,1536]{1,0:T(8,128)(2,1)S(1)} copy-done((bf16[384,1536]{1,0:T(8,128)(2,1)S(1)}, bf16[384,1536]{1,0:T(8,128)(2,1)}, u32[]{:S(2)}) %copy-start.2) | copy-done | bytes 1179672
  6.6 0.0 copy-start.3
  6.6 0.7 %copy-done.3 = s32[384,2]{0,1:T(2,128)S(1)} copy-done((s32[384,2]{0,1:T(2,128)S(1)}, s32[384,2]{0,1:T(2,128)}, u32[]{:S(2)}) %copy-start.3) | copy-done | bytes 3096
  7.3 0.0 copy-start.4
  7.3 9.8 %rotate.1 = (f32[1536,128]{1,0:T(8,128)S(1)}, f32[1536,128]{1,0:T(8,128)S(1)}, bf16[16,128]{1,0:T(8,128)(2,1)S(1)}) custom-call(bf16[384,1536]{1,0:T(8,128)(2,1)S(1)} %copy-done.2, bf16[384,2,4096]{2,1,0:T(2,128)(2,1)S(1)} %copy-done, s32[2,384]{1,0:T(2,128)S(1)} %bitcast.1, s32[1,384]{1,0:T(1,128)S(1)} %reshape.3.ids, bf16[2,1536,512]{2,1,0:T(8,128)(2,1)S(1)} %copy-done.1, ...), custom_call_target="tpu_custom_call" | custom-call | tf_op jit(solution)/shard_map/rotate/pallas_call | solution.py:205
  17.1 0.5 %collective-permute-start = (f32[1536,128]{1,0:T(8,128)S(1)}, f32[1536,128]{1,0:T(8,128)S(1)}, u32[]{:S(2)}, u32[]{:S(2)}) collective-permute-start(f32[1536,128]{1,0:T(8,128)S(1)} %get-tuple-element.15), channel_id=1, source_target_pairs={{0,1},{1,0},{2,3},{3,2},{4,5},{5,4},{6,7},{7,6},{8,9},{9,8},{10,11... | collective-permute-start | bytes 2359304 | tf_op jit(solution)/shard_map/ppermute | solution.py:227
  17.6 1.9 %collective-permute-done.got = f32[1536,128]{1,0:T(8,128)S(1)} collective-permute-done((f32[1536,128]{1,0:T(8,128)S(1)}, f32[1536,128]{1,0:T(8,128)S(1)}, u32[]{:S(2)}, u32[]{:S(2)}) %collective-permute-start) | collective-permute-done | bytes 786464 | tf_op jit(solution)/shard_map/ppermute | solution.py:227
  19.6 0.1 pair.1
  19.7 2.9 %collective-permute-start.1 = (bf16[1152,128]{1,0:T(8,128)(2,1)S(1)}, bf16[1152,128]{1,0:T(8,128)(2,1)S(1)}, u32[]{:S(2)}, u32[]{:S(2)}) collective-permute-start(bf16[1152,128]{1,0:T(8,128)(2,1)S(1)} %get-tuple-element.17), channel_id=1, source_target_pairs={{0,2},{1,3},{2,0},{3,1},{4,6},{5,7},{6,4},{7,5},{8,10},{9,11},{10,... | collective-permute-start | bytes 884744 | tf_op jit(solution)/shard_map/ppermute | solution.py:238
  22.6 7.3 %collective-permute-done.1.got = bf16[1152,128]{1,0:T(8,128)(2,1)S(1)} collective-permute-done((bf16[1152,128]{1,0:T(8,128)(2,1)S(1)}, bf16[1152,128]{1,0:T(8,128)(2,1)S(1)}, u32[]{:S(2)}, u32[]{:S(2)}) %collective-permute-start.1) | collective-permute-done | bytes 294944 | tf_op jit(solution)/shard_map/ppermute | solution.py:238
  29.9 0.1 payload.1
  30.0 1.9 %collective-permute-start.2 = (bf16[592,128]{1,0:T(8,128)(2,1)S(1)}, bf16[592,128]{1,0:T(8,128)(2,1)S(1)}, u32[]{:S(2)}, u32[]{:S(2)}) collective-permute-start(bf16[592,128]{1,0:T(8,128)(2,1)S(1)} %get-tuple-element.20), channel_id=1, source_target_pairs={{0,4},{4,0},{8,12},{12,8},{1,5},{5,1},{9,13},{13,9},{2,6},{6,2},{1... | collective-permute-start | bytes 454664 | tf_op jit(solution)/shard_map/ppermute | solution.py:249
  31.9 2.6 %collective-permute-start.3 = (bf16[592,128]{1,0:T(8,128)(2,1)S(1)}, bf16[592,128]{1,0:T(8,128)(2,1)S(1)}, u32[]{:S(2)}, u32[]{:S(2)}) collective-permute-start(bf16[592,128]{1,0:T(8,128)(2,1)S(1)} %get-tuple-element.21), channel_id=1, source_target_pairs={{0,8},{4,12},{8,0},{12,4},{1,9},{5,13},{9,1},{13,5},{2,10},{6,14},... | collective-permute-start | bytes 454664 | tf_op jit(solution)/shard_map/ppermute | solution.py:249
  34.4 0.0 collective-permute-start.4
  34.4 0.0 collective-permute-start.5
  34.4 2.9 %collective-permute-done.2.refs_1_ = bf16[592,128]{1,0:T(8,128)(2,1)S(1)} collective-permute-done((bf16[592,128]{1,0:T(8,128)(2,1)S(1)}, bf16[592,128]{1,0:T(8,128)(2,1)S(1)}, u32[]{:S(2)}, u32[]{:S(2)}) %collective-permute-start.2) | collective-permute-done | bytes 151584 | tf_op jit(solution)/shard_map/ppermute | solution.py:249
  37.3 0.0 collective-permute-start.6
  37.3 8.4 %collective-permute-done.3.refs_2_ = bf16[592,128]{1,0:T(8,128)(2,1)S(1)} collective-permute-done((bf16[592,128]{1,0:T(8,128)(2,1)S(1)}, bf16[592,128]{1,0:T(8,128)(2,1)S(1)}, u32[]{:S(2)}, u32[]{:S(2)}) %collective-permute-start.3) | collective-permute-done | bytes 151584 | tf_op jit(solution)/shard_map/ppermute | solution.py:249
  45.8 0.0 collective-permute-start.7
  45.8 0.0 collective-permute-done.4.refs_3_
  45.8 0.5 %collective-permute-start.8 = (bf16[592,128]{1,0:T(8,128)(2,1)S(1)}, bf16[592,128]{1,0:T(8,128)(2,1)S(1)}, u32[]{:S(2)}, u32[]{:S(2)}) collective-permute-start(bf16[592,128]{1,0:T(8,128)(2,1)S(1)} %collective-permute-done.4.refs_3_), channel_id=1, source_target_pairs={{0,1},{1,0},{2,3},{3,2},{4,5},{5,4},{6,7},{7,6},{8,9},{9,8},{10,11... | collective-permute-start | bytes 454664 | tf_op jit(solution)/shard_map/ppermute | solution.py:250
  46.3 0.0 collective-permute-done.5.refs_4_
  46.3 0.0 collective-permute-done.6.refs_5_
  46.3 0.9 %collective-permute-done.7.refs_6_ = bf16[592,128]{1,0:T(8,128)(2,1)S(1)} collective-permute-done((bf16[592,128]{1,0:T(8,128)(2,1)S(1)}, bf16[592,128]{1,0:T(8,128)(2,1)S(1)}, u32[]{:S(2)}, u32[]{:S(2)}) %collective-permute-start.7) | collective-permute-done | bytes 151584 | tf_op jit(solution)/shard_map/ppermute | solution.py:250
  47.2 0.2 collective-permute-done.8.refs_7_
  47.4 0.0 copy-done.4
  47.4 2.0 %blocks.1 = f32[2,128,128]{2,1,0:T(8,128)} custom-call(s32[2]{0:T(128)S(1)} %copy-done.4, bf16[592,128]{1,0:T(8,128)(2,1)S(1)} %get-tuple-element.19.refs_0_, bf16[592,128]{1,0:T(8,128)(2,1)S(1)} %collective-permute-done.2.refs_1_, bf16[592,128]{1,0:T(8,128)(2,1)S(1)} %collective-permute-done.3.refs_2_, bf16[592,128]{1,0:T(8,128)(2,1)S(1)} %collective-permute-done.4.refs_3_, ...), custom_call_target="tpu_custom_call" | custom-call | tf_op jit(solution)/shard_map/blocks/pallas_call | solution.py:251
Async XLA Ops:
  0.7 2.8 %copy-start = (bf16[384,2,4096]{2,1,0:T(2,128)(2,1)S(1)}, bf16[384,2,4096]{2,1,0:T(2,128)(2,1)}, u32[]{:S(2)}) copy-start(bf16[384,2,4096]{2,1,0:T(2,128)(2,1)} %grads.1) | copy-start | bytes 18874372
  3.5 1.9 %copy-start.1 = (bf16[2,1536,512]{2,1,0:T(8,128)(2,1)S(1)}, bf16[2,1536,512]{2,1,0:T(8,128)(2,1)}, u32[]{:S(2)}) copy-start(bf16[2,1536,512]{2,1,0:T(8,128)(2,1)} %basis_in.1) | copy-start | bytes 9437188
  5.4 1.3 %copy-start.2 = (bf16[384,1536]{1,0:T(8,128)(2,1)S(1)}, bf16[384,1536]{1,0:T(8,128)(2,1)}, u32[]{:S(2)}) copy-start(bf16[384,1536]{1,0:T(8,128)(2,1)} %acts.1) | copy-start | bytes 3538948
  6.6 0.7 %copy-start.3 = (s32[384,2]{0,1:T(2,128)S(1)}, s32[384,2]{0,1:T(2,128)}, u32[]{:S(2)}) copy-start(s32[384,2]{0,1:T(2,128)} %param.9) | copy-start | bytes 9220
  7.3 40.1 %copy-start.4 = (s32[2]{0:T(128)S(1)}, s32[2]{0:T(128)}, u32[]{:S(2)}) copy-start(s32[2]{0:T(128)} %counts.1) | copy-start | bytes 28
  17.1 2.4 %collective-permute-start = (f32[1536,128]{1,0:T(8,128)S(1)}, f32[1536,128]{1,0:T(8,128)S(1)}, u32[]{:S(2)}, u32[]{:S(2)}) collective-permute-start(f32[1536,128]{1,0:T(8,128)S(1)} %get-tuple-element.15), channel_id=1, source_target_pairs={{0,1},{1,0},{2,3},{3,2},{4,5},{5,4},{6,7},{7,6},{8,9},{9,8},{10,11... | collective-permute-start | bytes 2359304 | tf_op jit(solution)/shard_map/ppermute | solution.py:227
  19.7 10.2 %collective-permute-start.1 = (bf16[1152,128]{1,0:T(8,128)(2,1)S(1)}, bf16[1152,128]{1,0:T(8,128)(2,1)S(1)}, u32[]{:S(2)}, u32[]{:S(2)}) collective-permute-start(bf16[1152,128]{1,0:T(8,128)(2,1)S(1)} %get-tuple-element.17), channel_id=1, source_target_pairs={{0,2},{1,3},{2,0},{3,1},{4,6},{5,7},{6,4},{7,5},{8,10},{9,11},{10,... | collective-permute-start | bytes 884744 | tf_op jit(solution)/shard_map/ppermute | solution.py:238
  30.0 7.4 %collective-permute-start.2 = (bf16[592,128]{1,0:T(8,128)(2,1)S(1)}, bf16[592,128]{1,0:T(8,128)(2,1)S(1)}, u32[]{:S(2)}, u32[]{:S(2)}) collective-permute-start(bf16[592,128]{1,0:T(8,128)(2,1)S(1)} %get-tuple-element.20), channel_id=1, source_target_pairs={{0,4},{4,0},{8,12},{12,8},{1,5},{5,1},{9,13},{13,9},{2,6},{6,2},{1... | collective-permute-start | bytes 454664 | tf_op jit(solution)/shard_map/ppermute | solution.py:249
  31.9 13.9 %collective-permute-start.3 = (bf16[592,128]{1,0:T(8,128)(2,1)S(1)}, bf16[592,128]{1,0:T(8,128)(2,1)S(1)}, u32[]{:S(2)}, u32[]{:S(2)}) collective-permute-start(bf16[592,128]{1,0:T(8,128)(2,1)S(1)} %get-tuple-element.21), channel_id=1, source_target_pairs={{0,8},{4,12},{8,0},{12,4},{1,9},{5,13},{9,1},{13,5},{2,10},{6,14},... | collective-permute-start | bytes 454664 | tf_op jit(solution)/shard_map/ppermute | solution.py:249
  34.4 11.4 %collective-permute-start.4 = (bf16[592,128]{1,0:T(8,128)(2,1)S(1)}, bf16[592,128]{1,0:T(8,128)(2,1)S(1)}, u32[]{:S(2)}, u32[]{:S(2)}) collective-permute-start(bf16[592,128]{1,0:T(8,128)(2,1)S(1)} %get-tuple-element.22), channel_id=1, source_target_pairs={{0,12},{4,8},{8,4},{12,0},{1,13},{5,9},{9,5},{13,1},{2,14},{6,10},... | collective-permute-start | bytes 454664 | tf_op jit(solution)/shard_map/ppermute | solution.py:249
  34.4 11.9 %collective-permute-start.5 = (bf16[592,128]{1,0:T(8,128)(2,1)S(1)}, bf16[592,128]{1,0:T(8,128)(2,1)S(1)}, u32[]{:S(2)}, u32[]{:S(2)}) collective-permute-start(bf16[592,128]{1,0:T(8,128)(2,1)S(1)} %get-tuple-element.19.refs_0_), channel_id=1, source_target_pairs={{0,1},{1,0},{2,3},{3,2},{4,5},{5,4},{6,7},{7,6},{8,9},{9,8},{10,11... | collective-permute-start | bytes 454664 | tf_op jit(solution)/shard_map/ppermute | solution.py:250
  37.3 9.0 %collective-permute-start.6 = (bf16[592,128]{1,0:T(8,128)(2,1)S(1)}, bf16[592,128]{1,0:T(8,128)(2,1)S(1)}, u32[]{:S(2)}, u32[]{:S(2)}) collective-permute-start(bf16[592,128]{1,0:T(8,128)(2,1)S(1)} %collective-permute-done.2.refs_1_), channel_id=1, source_target_pairs={{0,1},{1,0},{2,3},{3,2},{4,5},{5,4},{6,7},{7,6},{8,9},{9,8},{10,11... | collective-permute-start | bytes 454664 | tf_op jit(solution)/shard_map/ppermute | solution.py:250
  45.8 1.4 %collective-permute-start.7 = (bf16[592,128]{1,0:T(8,128)(2,1)S(1)}, bf16[592,128]{1,0:T(8,128)(2,1)S(1)}, u32[]{:S(2)}, u32[]{:S(2)}) collective-permute-start(bf16[592,128]{1,0:T(8,128)(2,1)S(1)} %collective-permute-done.3.refs_2_), channel_id=1, source_target_pairs={{0,1},{1,0},{2,3},{3,2},{4,5},{5,4},{6,7},{7,6},{8,9},{9,8},{10,11... | collective-permute-start | bytes 454664 | tf_op jit(solution)/shard_map/ppermute | solution.py:250
  45.8 1.6 %collective-permute-start.8 = (bf16[592,128]{1,0:T(8,128)(2,1)S(1)}, bf16[592,128]{1,0:T(8,128)(2,1)S(1)}, u32[]{:S(2)}, u32[]{:S(2)}) collective-permute-start(bf16[592,128]{1,0:T(8,128)(2,1)S(1)} %collective-permute-done.4.refs_3_), channel_id=1, source_target_pairs={{0,1},{1,0},{2,3},{3,2},{4,5},{5,4},{6,7},{7,6},{8,9},{9,8},{10,11... | collective-permute-start | bytes 454664 | tf_op jit(solution)/shard_map/ppermute | solution.py:250

commit v2 on v0

--- a/solution.py
+++ b/solution.py
@@ -1,7 +1,301 @@
+import functools
+
 import jax
 import jax.numpy as jnp
 from jax import lax
+from jax.experimental import pallas as pl
+from jax.experimental.pallas import tpu as pltpu
 from jax.sharding import PartitionSpec as P
+
+F32 = jnp.float32
+BF16 = jnp.bfloat16
+CHUNK = 512
+VMEM = 40 * 2**20
+LABEL_ROWS = 16
+
+
+def iota(shape, dim):
+    return lax.broadcasted_iota(jnp.int32, shape, dim)
+
+
+def dot(a, b):
+    return jnp.dot(a, b, preferred_element_type=F32)
+
+
+def fetcher(sems):
+    count = iter(range(sems.shape[0]))
+
+    def fetch(src, dst):
+        copy = pltpu.make_async_copy(src, dst, sems.at[next(count)])
+        copy.start()
+        return copy
+
+    return fetch
+
+
+def rotate_in_kernel(
+    acts, routes, ids, basis_in,
+    keep, send, label, pick,
+    acts_v, routes_v, ids_v, basis_v, acc, sems,
+):
+    tokens = acts.shape[0]
+    experts, _, width = basis_in.shape
+    cap = tokens // 2
+    fetch = fetcher(sems)
+    first = [fetch(routes, routes_v), fetch(ids, ids_v)]
+    acts_in = fetch(acts, acts_v)
+    bases = [fetch(basis_in.at[e], basis_v.at[e]) for e in range(experts)]
+    for copy in first:
+        copy.wait()
+    hits = [
+        jnp.max((routes_v[...] == e).astype(F32), axis=0, keepdims=True) for e in range(experts)
+    ]
+    rows = jnp.concatenate(hits + [jnp.zeros((8 - experts, tokens), F32)], axis=0).astype(BF16)
+    upto = (iota((tokens, tokens), 0) <= iota((tokens, tokens), 1)).astype(BF16)
+    order = dot(rows, upto)
+    slots = iota((cap, tokens), 0).astype(F32) + 1.0
+    pick_in = jnp.concatenate(
+        [((order[e : e + 1] == slots) & (hits[e] > 0.5)).astype(BF16) for e in range(experts)],
+        axis=0,
+    )
+    repeat = (iota((tokens, 2 * tokens), 0) == iota((tokens, 2 * tokens), 1) // 2).astype(BF16)
+    wide = dot(
+        jnp.concatenate(
+            [order[:experts], routes_v[...].astype(F32), jnp.zeros((6 - experts, tokens), F32)],
+            axis=0,
+        ).astype(BF16),
+        repeat,
+    )
+    odd = iota((1, 2 * tokens), 1) % 2 == 1
+    routed_to = jnp.where(odd, wide[experts + 1 : experts + 2], wide[experts : experts + 1])
+    slots = iota((cap, 2 * tokens), 0).astype(F32) + 1.0
+    for e in range(experts):
+        pick[e * cap : (e + 1) * cap, :] = (
+            (wide[e : e + 1] == slots) & (routed_to == float(e))
+        ).astype(BF16)
+    numbers = jnp.broadcast_to(ids_v[...].astype(F32) + 1.0, (8, tokens)).astype(BF16)
+    named = lax.dot_general(numbers, pick_in, (((1,), (1,)), ((), ())), preferred_element_type=F32)
+    block = jnp.zeros((LABEL_ROWS, 128), F32)
+    row = iota((LABEL_ROWS, 128), 0)
+    half = cap // 2
+    for at in range(2 * experts):
+        mine = named[0:1, at * half : (at + 1) * half]
+        mine = jnp.concatenate([mine, jnp.zeros((1, 128 - half), F32)], axis=1)
+        block = jnp.where(row == at, mine, block)
+    label[...] = block.astype(BF16)
+
+    acts_in.wait()
+    chosen = dot(pick_in, acts_v[...]).astype(BF16)
+    for e in range(experts):
+        bases[e].wait()
+        acc[e] = dot(chosen[e * cap : (e + 1) * cap], basis_v[e])
+    core = lax.rem(lax.axis_index("tensor"), 2)
+    at = 0
+    for q in range(width // 128):
+        for e in range(experts):
+            for ref, which in ((keep, core), (send, 1 - core)):
+                ref[at : at + half, :] = acc[
+                    e, pl.ds(pl.multiple_of(which * half, 8), half), q * 128 : (q + 1) * 128
+                ]
+            at += half
+
+
+def rotate_out_kernel(grads, pick, basis_out, _, acc, grads_v, basis_v, sems):
+    tokens, _, hidden = grads.shape
+    experts, _, width = basis_out.shape
+    cap = tokens // 2
+    fetch = fetcher(sems)
+    steps = hidden // CHUNK
+    copies = []
+    for s in range(steps):
+        cols = pl.ds(s * CHUNK, CHUNK)
+        copies.append(
+            (fetch(grads.at[:, :, cols], grads_v.at[s]), fetch(basis_out.at[:, cols, :], basis_v.at[s]))
+        )
+    for s in range(steps):
+        for copy in copies[s]:
+            copy.wait()
+        chosen = dot(pick[...], grads_v[s].reshape(2 * tokens, CHUNK)).astype(BF16)
+        for e in range(experts):
+            part = dot(chosen[e * cap : (e + 1) * cap], basis_v[s, e])
+            if s == 0:
+                acc[e] = part
+            else:
+                acc[e] += part
+
+
+def split_out_kernel(acc, _, keep, send):
+    experts, cap, width = acc.shape
+    core = lax.rem(lax.axis_index("tensor"), 2)
+    at = 0
+    for x in range(width // 256):
+        for e in range(experts):
+            for ref, which in ((keep, core), (send, 1 - core)):
+                ref[at : at + cap, :] = acc[
+                    e, :, pl.ds(pl.multiple_of((2 * x + which) * 128, 128), 128)
+                ]
+            at += cap
+
+
+def pair_in_kernel(kept, got, label, *pays):
+    slab = kept.shape[0] // len(pays)
+    d = lax.axis_index("dp")
+    for k, pay in enumerate(pays):
+        rows = pl.ds(pl.multiple_of((d ^ k) * slab, 16), slab)
+        pay[:slab, :] = (kept[rows, :] + got[rows, :]).astype(BF16)
+        pay[slab:, :] = label[...]
+
+
+def pair_out_kernel(kept, got, keep, send):
+    outer = keep.shape[0]
+    x = lax.div(lax.axis_index("tensor"), 2)
+    mine = pl.ds(pl.multiple_of(x * outer, 16), outer)
+    keep[...] = kept[mine, :] + got[mine, :]
+    other = pl.ds(pl.multiple_of((1 - x) * outer, 16), outer)
+    send[...] = (kept[other, :] + got[other, :]).astype(BF16)
+
+
+def round_kernel(kept, got, out):
+    out[...] = (kept[...] + got[...].astype(F32)).astype(BF16)
+
+
+def stack_kernel(*refs):
+    *pieces, out = refs
+    slab = pieces[0].shape[0] - LABEL_ROWS
+    for k, piece in enumerate(pieces):
+        out[k * slab : (k + 1) * slab, :] = piece[:slab, :]
+
+
+def half_blocks(dp, e, which, rows, far, outs, pieces):
+    half = rows.shape[0] // (2 * dp)
+    slab = pieces[0].shape[0] - LABEL_ROWS
+    rows_in, rows_out, labels = [], [], []
+    for k in range(dp):
+        at = pl.ds((2 * k + e) * half, half)
+        rows_in.append((rows[at, :].astype(F32) + far[at, :].astype(F32)).astype(BF16))
+        at = pl.ds(pl.multiple_of((2 * e + which) * half, 16), half)
+        rows_out.append(outs[k][at, :])
+        label = pieces[k][slab:, :].astype(F32)[2 * e : 2 * e + 2, :half]
+        labels.append(jnp.where(which == 0, label[0:1], label[1:2]))
+    rows_in = jnp.concatenate(rows_in, axis=0)
+    rows_out = jnp.concatenate(rows_out, axis=0).T
+    labels = jnp.concatenate(labels, axis=1)
+    masked = [
+        jnp.where(labels == float(n + 1), rows_out, jnp.zeros_like(rows_out)) for n in range(dp)
+    ]
+    return dot(jnp.concatenate(masked, axis=0), rows_in)
+
+
+def first_blocks_kernel(dp, rows, far, *refs):
+    outs, pieces, total = refs[:dp], refs[dp : 2 * dp], refs[2 * dp]
+    core = lax.rem(lax.axis_index("tensor"), 2)
+    for e in range(total.shape[0]):
+        total[e] = half_blocks(dp, e, core, rows, far, outs, pieces)
+
+
+def blocks_kernel(dp, counts, first, rows, far, *refs):
+    outs, pieces, result = refs[:dp], refs[dp : 2 * dp], refs[2 * dp]
+    core = lax.rem(lax.axis_index("tensor"), 2)
+    for e in range(result.shape[0]):
+        total = first[e] + half_blocks(dp, e, 1 - core, rows, far, outs, pieces)
+        side = total.shape[0] // dp
+        squares = total * total
+        summed = squares[:side]
+        for n in range(1, dp):
+            summed = summed + squares[n * side : (n + 1) * side]
+        result[e] = summed / counts[e].astype(F32)
+
+
+def call(kernel, name, out_shape, specs=None, scratch=()):
+    vmem = pl.BlockSpec(memory_space=pltpu.VMEM)
+    return lambda *args: pl.pallas_call(
+        kernel,
+        out_shape=out_shape,
+        in_specs=specs or [vmem] * len(args),
+        scratch_shapes=scratch,
+        compiler_params=pltpu.CompilerParams(vmem_limit_bytes=VMEM),
+        cost_estimate=pl.CostEstimate(flops=1, bytes_accessed=1, transcendentals=0),
+        name=name,
+    )(*args)
+
+
+def fast(acts, grads, routes, example_ids, expert_counts, basis_in, basis_out):
+    tokens, _, hidden = grads.shape
+    experts, features, width = basis_in.shape
+    cap = tokens // 2
+    dp = lax.axis_size("dp")
+    steps = hidden // CHUNK
+    wide = experts * cap
+    half = wide * width // 256
+    slab = half // dp
+    hbm = pl.BlockSpec(memory_space=pltpu.HBM)
+    vmem = pl.BlockSpec(memory_space=pltpu.VMEM)
+
+    def pin(x):
+        return pltpu.with_memory_space_constraint(x, pltpu.HBM)
+
+    def rows(count, dtype):
+        return jax.ShapeDtypeStruct((count, 128), dtype)
+
+    core = [(t, t ^ 1) for t in range(4)]
+    across = [(t, t ^ 2) for t in range(4)]
+    others = [[(d, d ^ k) for d in range(dp)] for k in range(dp)]
+
+    keep, send, label, pick = call(
+        rotate_in_kernel,
+        "rotate_in",
+        (rows(half, F32), rows(half, F32), rows(LABEL_ROWS, BF16),
+         jax.ShapeDtypeStruct((wide, 2 * tokens), BF16)),
+        [hbm] * 4,
+        [
+            pltpu.VMEM(acts.shape, BF16),
+            pltpu.VMEM((2, tokens), jnp.int32),
+            pltpu.VMEM((1, tokens), jnp.int32),
+            pltpu.VMEM(basis_in.shape, BF16),
+            pltpu.VMEM((experts, cap, width), F32),
+            pltpu.SemaphoreType.DMA((3 + experts,)),
+        ],
+    )(pin(acts), routes.T, example_ids.reshape(1, tokens), pin(basis_in))
+    got = lax.ppermute(send, "tensor", core)
+    pieces = call(pair_in_kernel, "pair_in", [rows(slab + LABEL_ROWS, BF16)] * dp)(keep, got, label)
+    arrived = [pieces[0]] + [lax.ppermute(pieces[k], "dp", others[k]) for k in range(1, dp)]
+
+    acc = call(
+        rotate_out_kernel,
+        "rotate_out",
+        jax.ShapeDtypeStruct((experts, cap, width), F32),
+        [hbm, vmem, hbm, vmem],
+        [
+            pltpu.VMEM((steps, tokens, 2, CHUNK), BF16),
+            pltpu.VMEM((steps, experts, CHUNK, width), BF16),
+            pltpu.SemaphoreType.DMA((2 * steps,)),
+        ],
+    )(pin(grads), pick, pin(basis_out), pieces[0])
+    mine = call(stack_kernel, "stack_in", rows(half, BF16))(*arrived)
+    keep, send = call(split_out_kernel, "split_out", (rows(half, F32), rows(half, F32)))(acc, mine)
+    got = lax.ppermute(send, "tensor", core)
+    keep, send = call(pair_out_kernel, "pair_out", (rows(half // 2, F32), rows(half // 2, BF16)))(
+        keep, got
+    )
+    got = lax.ppermute(send, "tensor", across)
+    out = call(round_kernel, "round_out", rows(half // 2, BF16))(keep, got)
+    outs = [out] + [lax.ppermute(out, "dp", others[k]) for k in range(1, dp)]
+
+    far = lax.ppermute(mine, "tensor", across)
+    first = call(
+        functools.partial(first_blocks_kernel, dp),
+        "first_blocks",
+        jax.ShapeDtypeStruct((experts, dp * 128, 128), F32),
+    )(mine, far, *outs, *arrived)
+    other = lax.ppermute(mine, "tensor", core)
+    other_far = lax.ppermute(far, "tensor", core)
+    return call(
+        functools.partial(blocks_kernel, dp),
+        "blocks",
+        jax.ShapeDtypeStruct((experts, 128, 128), F32),
+        [pl.BlockSpec(memory_space=pltpu.SMEM)] + [vmem] * (2 * dp + 3),
+    )(expert_counts, first, other, other_far, *outs, *arrived)
+
 
 EX_DEV = 1
 
@@ -19,7 +313,7 @@
     return (positions, filled, second_hit[positions])
 
 
-def shards(acts, grads, routes, example_ids, expert_counts, basis_in, basis_out):
+def general(acts, grads, routes, example_ids, expert_counts, basis_in, basis_out):
     capacity = acts.shape[0] // 2
     experts = basis_in.shape[0]
     parts_in, parts_out, label_rows = ([], [], [])
@@ -56,6 +350,12 @@
     return totals / expert_counts.astype(jnp.float32)[:, None, None]
 
 
+def shards(*args):
+    width = args[5].shape[2]
+    fits = lax.axis_size("tensor") == 4 and lax.axis_size("dp") == 4 and width == 512
+    return (fast if fits else general)(*args)
+
+
 def solution(mesh):
     placed = (
         P(("group", "dp"), "tensor"),

time: 224 us -> 42.9 us (0.19)
  waiting for transfers between devices: 108 us -> 14.9 us
  local copies, waits for them, and re-layouts: 37.8 us -> 1.37 us
  blocking collectives: 34.3 us -> 0 us
  other arithmetic: 20.9 us -> 0 us
  starting transfers between devices: 0.04 us -> 14.1 us
  between operations: 13.7 us -> 0.12 us
  Pallas kernels: 0 us -> 12.2 us
  matrix products: 9.33 us -> 0 us
    unnamed x3 -> x0, waiting for transfers between devices: 86.7 us -> none
    gather x8 -> x0, local copies, waits for them, and re-layouts: 36 us -> none  [the longest x2 27.6 us: shards(): chosen = grads[positions]]
    psum x1 -> x0, blocking collectives: 34.3 us -> none  [shards(): summed_in, summed_out = lax.psum((part_in, part_out), 'tensor')]
    reduce_scatter x1 -> x0, waiting for transfers between devices: 20.8 us -> none  [shards(): totals = lax.psum_scatter(squared, 'dp', scatter_dimension=2, tiled=True)]
    ppermute x0 -> x12, waiting for transfers between devices: none -> 14.9 us  [the longest x3 7.6 us: fast(): outs = [out] + [lax.ppermute(out, 'dp', others[k]) for k in range(1, dp)]]
    select_n x6 -> x0, other arithmetic: 14.2 us -> none  [the longest x2 14.2 us: shards(): grad_rows = jnp.where(second[:, None], chosen[:, 1, :], chosen[:, 0, :])]
    ppermute x0 -> x12, starting transfers between devices: none -> 14.1 us  [the longest x3 5.6 us: fast(): lax.ppermute(pieces[k], 'dp', others[k])]
    pallas_call x0 -> x9, Pallas kernels: none -> 12.2 us  [call(): pl.pallas_call(kernel, out_shape=out_shape, in_specs=specs or [vmem] * le...]
  transfers between devices with their start and end apart: 2 -> 12, of which waited for: 2 -> 5; matrix products, arithmetic and copies ran while one was open for 0% -> 0% of each run, Pallas kernels for 0% -> 17%
where the time goes in v2:
time: 42.9 us; the launch traced here: 42.7 us
  waiting for transfers between devices  14.9 us (35%)
  starting transfers between devices  14.1 us (33%)
  Pallas kernels  12.2 us (28%)
  local copies, waits for them, and re-layouts  1.37 us (3%)
    pallas_call x9, Pallas kernels, call(): pl.pallas_call(kernel, out_shape=out_shape, in_specs=specs or [vmem] * le...  12.2 us
    ppermute x3, waiting for transfers between devices, fast(): outs = [out] + [lax.ppermute(out, 'dp', others[k]) for k in range(1, dp)]  7.6 us
    ppermute x3, starting transfers between devices, fast(): lax.ppermute(pieces[k], 'dp', others[k])  5.6 us
    ppermute x3, starting transfers between devices, fast(): outs = [out] + [lax.ppermute(out, 'dp', others[k]) for k in range(1, dp)]  4.46 us
    ppermute x1, waiting for transfers between devices, fast(): far = lax.ppermute(mine, 'tensor', across)  4.24 us
    ppermute x1, starting transfers between devices, fast(): far = lax.ppermute(mine, 'tensor', across)  1.77 us
    ppermute x1, starting transfers between devices, fast(): got = lax.ppermute(send, 'tensor', across)  1.71 us
    ppermute x1, waiting for transfers between devices, fast(): got = lax.ppermute(send, 'tensor', across)  1.65 us
  transfers between devices with their start and end apart: 12, of which 5 were waited for; matrix products, arithmetic and copies ran while one was open for 0% of the time, Pallas kernels for 17%

profile of v2, /device:TPU:0, one launch (start us, length us, event | category | flops | bytes accessed | tf_op | source)
XLA Modules:
  0.0 42.7 jit_solution(9442402101489760761)
XLA Ops:
  0.0 0.7 %reshape.3.ids = s32[1,384]{1,0:T(1,128)S(1)} reshape(s32[384]{0:T(512)} %param.10) | data formatting | bytes 3072 | tf_op jit(solution)/shard_map/reshape | solution.py:258
  0.7 0.0 copy-start
  0.7 0.7 %copy-done = s32[384,2]{0,1:T(2,128)S(1)} copy-done((s32[384,2]{0,1:T(2,128)S(1)}, s32[384,2]{0,1:T(2,128)}, u32[]{:S(2)}) %copy-start) | copy-done | bytes 3096
  1.4 3.1 %rotate_in.1 = (f32[768,128]{1,0:T(8,128)S(1)}, f32[768,128]{1,0:T(8,128)S(1)}, bf16[16,128]{1,0:T(8,128)(2,1)S(1)}, bf16[384,768]{1,0:T(8,128)(2,1)S(1)}) custom-call(bf16[384,1536]{1,0:T(8,128)(2,1)} %acts.1, s32[2,384]{1,0:T(2,128)S(1)} %bitcast.1, s32[1,384]{1,0:T(1,128)S(1)} %reshape.3.ids, bf16[2,1536,512]{2,1,0:T(8,128)(2,1)} %basis_in.1), custom_call_target="tpu_custom_call" | custom-call | flops 1 | bytes 1 | tf_op jit(solution)/shard_map/rotate_in/pallas_call | solution.py:211
  4.5 0.5 %collective-permute-start = (f32[768,128]{1,0:T(8,128)S(1)}, f32[768,128]{1,0:T(8,128)S(1)}, u32[]{:S(2)}, u32[]{:S(2)}) collective-permute-start(f32[768,128]{1,0:T(8,128)S(1)} %get-tuple-element.18), channel_id=1, source_target_pairs={{0,1},{1,0},{2,3},{3,2},{4,5},{5,4},{6,7},{7,6},{8,9},{9,8},{10,11... | collective-permute-start | bytes 1179656 | tf_op jit(solution)/shard_map/ppermute | solution.py:259
  5.0 1.3 %collective-permute-done.got = f32[768,128]{1,0:T(8,128)S(1)} collective-permute-done((f32[768,128]{1,0:T(8,128)S(1)}, f32[768,128]{1,0:T(8,128)S(1)}, u32[]{:S(2)}, u32[]{:S(2)}) %collective-permute-start) | collective-permute-done | bytes 393248 | tf_op jit(solution)/shard_map/ppermute | solution.py:259
  6.4 3.0 %collective-permute-start.1 = (bf16[208,128]{1,0:T(8,128)(2,1)S(1)}, bf16[208,128]{1,0:T(8,128)(2,1)S(1)}, u32[]{:S(2)}, u32[]{:S(2)}) collective-permute-start(bf16[208,128]{1,0:T(8,128)(2,1)S(1)} %get-tuple-element.21), channel_id=1, source_target_pairs={{0,4},{4,0},{8,12},{12,8},{1,5},{5,1},{9,13},{13,9},{2,6},{6,2},{1... | collective-permute-start | bytes 159752 | tf_op jit(solution)/shard_map/ppermute | solution.py:261
  9.4 2.6 %collective-permute-start.2 = (bf16[208,128]{1,0:T(8,128)(2,1)S(1)}, bf16[208,128]{1,0:T(8,128)(2,1)S(1)}, u32[]{:S(2)}, u32[]{:S(2)}) collective-permute-start(bf16[208,128]{1,0:T(8,128)(2,1)S(1)} %get-tuple-element.22), channel_id=1, source_target_pairs={{0,8},{4,12},{8,0},{12,4},{1,9},{5,13},{9,1},{13,5},{2,10},{6,14},... | collective-permute-start | bytes 159752 | tf_op jit(solution)/shard_map/ppermute | solution.py:261
  12.0 0.0 collective-permute-start.3
  12.0 0.0 copy-start.1
  12.0 6.7 %rotate_out.1.acc = f32[2,192,512]{2,1,0:T(8,128)S(1)} custom-call(bf16[384,2,4096]{2,1,0:T(2,128)(2,1)} %grads.1, bf16[384,768]{1,0:T(8,128)(2,1)S(1)} %get-tuple-element.24.pick, bf16[2,4096,512]{2,1,0:T(8,128)(2,1)} %basis_out.1, bf16[208,128]{1,0:T(8,128)(2,1)S(1)} %get-tuple-element.20.refs_0_._.refs_4_), custom_call_target="tpu_custom_call" | custom-call | flops 1 | bytes 1 | tf_op jit(solution)/shard_map/rotate_out/pallas_call | solution.py:211
  18.8 0.0 collective-permute-done.1.refs_1_.refs_5_
  18.8 0.0 collective-permute-done.2.refs_2_.refs_6_
  18.8 0.0 collective-permute-done.3.refs_3_.refs_7_
  18.8 0.1 split_out.1
  19.0 0.1 collective-permute-start.5
  19.0 1.8 %collective-permute-start.4 = (bf16[768,128]{1,0:T(8,128)(2,1)S(1)}, bf16[768,128]{1,0:T(8,128)(2,1)S(1)}, u32[]{:S(2)}, u32[]{:S(2)}) collective-permute-start(bf16[768,128]{1,0:T(8,128)(2,1)S(1)} %stack_in.1._.rows), channel_id=1, source_target_pairs={{0,2},{1,3},{2,0},{3,1},{4,6},{5,7},{6,4},{7,5},{8,10},{9,11},{10,... | collective-permute-start | bytes 589832 | tf_op jit(solution)/shard_map/ppermute | solution.py:284
  20.8 0.0 collective-permute-done.5.got
  20.9 1.7 %collective-permute-start.6 = (bf16[384,128]{1,0:T(8,128)(2,1)S(1)}, bf16[384,128]{1,0:T(8,128)(2,1)S(1)}, u32[]{:S(2)}, u32[]{:S(2)}) collective-permute-start(bf16[384,128]{1,0:T(8,128)(2,1)S(1)} %get-tuple-element.28), channel_id=1, source_target_pairs={{0,2},{1,3},{2,0},{3,1},{4,6},{5,7},{6,4},{7,5},{8,10},{9,11},{10,... | collective-permute-start | bytes 294920 | tf_op jit(solution)/shard_map/ppermute | solution.py:280
  22.6 0.0 collective-permute-start.10
  22.6 4.2 %collective-permute-done.4.far = bf16[768,128]{1,0:T(8,128)(2,1)S(1)} collective-permute-done((bf16[768,128]{1,0:T(8,128)(2,1)S(1)}, bf16[768,128]{1,0:T(8,128)(2,1)S(1)}, u32[]{:S(2)}, u32[]{:S(2)}) %collective-permute-start.4) | collective-permute-done | bytes 196640 | tf_op jit(solution)/shard_map/ppermute | solution.py:284
  26.8 0.0 collective-permute-start.11
  26.8 1.7 %collective-permute-done.6.got = bf16[384,128]{1,0:T(8,128)(2,1)S(1)} collective-permute-done((bf16[384,128]{1,0:T(8,128)(2,1)S(1)}, bf16[384,128]{1,0:T(8,128)(2,1)S(1)}, u32[]{:S(2)}, u32[]{:S(2)}) %collective-permute-start.6) | collective-permute-done | bytes 98336 | tf_op jit(solution)/shard_map/ppermute | solution.py:280
  28.5 1.0 %collective-permute-start.7 = (bf16[384,128]{1,0:T(8,128)(2,1)S(1)}, bf16[384,128]{1,0:T(8,128)(2,1)S(1)}, u32[]{:S(2)}, u32[]{:S(2)}) collective-permute-start(bf16[384,128]{1,0:T(8,128)(2,1)S(1)} %round_out.1.refs_0_), channel_id=1, source_target_pairs={{0,4},{4,0},{8,12},{12,8},{1,5},{5,1},{9,13},{13,9},{2,6},{6,2},{1... | collective-permute-start | bytes 294920 | tf_op jit(solution)/shard_map/ppermute | solution.py:282
  29.5 3.5 %collective-permute-start.8 = (bf16[384,128]{1,0:T(8,128)(2,1)S(1)}, bf16[384,128]{1,0:T(8,128)(2,1)S(1)}, u32[]{:S(2)}, u32[]{:S(2)}) collective-permute-start(bf16[384,128]{1,0:T(8,128)(2,1)S(1)} %round_out.1.refs_0_), channel_id=1, source_target_pairs={{0,8},{4,12},{8,0},{12,4},{1,9},{5,13},{9,1},{13,5},{2,10},{6,14},... | collective-permute-start | bytes 294920 | tf_op jit(solution)/shard_map/ppermute | solution.py:282
  33.0 0.0 collective-permute-start.9
  33.0 0.2 collective-permute-done.7.refs_1_
  33.2 7.4 %collective-permute-done.8.refs_2_ = bf16[384,128]{1,0:T(8,128)(2,1)S(1)} collective-permute-done((bf16[384,128]{1,0:T(8,128)(2,1)S(1)}, bf16[384,128]{1,0:T(8,128)(2,1)S(1)}, u32[]{:S(2)}, u32[]{:S(2)}) %collective-permute-start.8) | collective-permute-done | bytes 98336 | tf_op jit(solution)/shard_map/ppermute | solution.py:282
  40.6 0.0 collective-permute-done.9.refs_3_
  40.6 0.4 %first_blocks.1.first = f32[2,512,128]{2,1,0:T(8,128)S(1)} custom-call(bf16[768,128]{1,0:T(8,128)(2,1)S(1)} %stack_in.1._.rows, bf16[768,128]{1,0:T(8,128)(2,1)S(1)} %collective-permute-done.4.far, bf16[384,128]{1,0:T(8,128)(2,1)S(1)} %round_out.1.refs_0_, bf16[384,128]{1,0:T(8,128)(2,1)S(1)} %collective-permute-done.7.refs_1_, ...), custom_call_target="tpu_custom_call" | custom-call | flops 1 | bytes 1 | tf_op jit(solution)/shard_map/first_blocks/pallas_call | solution.py:211
  41.0 0.0 collective-permute-done.10.rows
  41.0 0.0 collective-permute-done.11.far
  41.0 0.0 copy-done.1
  41.0 1.6 %blocks.1 = f32[2,128,128]{2,1,0:T(8,128)} custom-call(s32[2]{0:T(128)S(1)} %copy-done.1, f32[2,512,128]{2,1,0:T(8,128)S(1)} %first_blocks.1.first, bf16[768,128]{1,0:T(8,128)(2,1)S(1)} %collective-permute-done.10.rows, bf16[768,128]{1,0:T(8,128)(2,1)S(1)} %collective-permute-done.11.far, bf16[384,128]{1,0:T(8,128)(2,1)S(1)} %round_out.1.refs_0_, ...), custom_call_target="tpu_custom_call" | custom-call | flops 1 | bytes 1 | tf_op jit(solution)/shard_map/blocks/pallas_call | solution.py:211
  (4 shorter events, 0.1 us)
Async XLA Ops:
  0.7 0.7 %copy-start = (s32[384,2]{0,1:T(2,128)S(1)}, s32[384,2]{0,1:T(2,128)}, u32[]{:S(2)}) copy-start(s32[384,2]{0,1:T(2,128)} %param.9) | copy-start | bytes 9220
  4.5 1.9 %collective-permute-start = (f32[768,128]{1,0:T(8,128)S(1)}, f32[768,128]{1,0:T(8,128)S(1)}, u32[]{:S(2)}, u32[]{:S(2)}) collective-permute-start(f32[768,128]{1,0:T(8,128)S(1)} %get-tuple-element.18), channel_id=1, source_target_pairs={{0,1},{1,0},{2,3},{3,2},{4,5},{5,4},{6,7},{7,6},{8,9},{9,8},{10,11... | collective-permute-start | bytes 1179656 | tf_op jit(solution)/shard_map/ppermute | solution.py:259
  6.4 12.4 %collective-permute-start.1 = (bf16[208,128]{1,0:T(8,128)(2,1)S(1)}, bf16[208,128]{1,0:T(8,128)(2,1)S(1)}, u32[]{:S(2)}, u32[]{:S(2)}) collective-permute-start(bf16[208,128]{1,0:T(8,128)(2,1)S(1)} %get-tuple-element.21), channel_id=1, source_target_pairs={{0,4},{4,0},{8,12},{12,8},{1,5},{5,1},{9,13},{13,9},{2,6},{6,2},{1... | collective-permute-start | bytes 159752 | tf_op jit(solution)/shard_map/ppermute | solution.py:261
  9.4 9.4 %collective-permute-start.2 = (bf16[208,128]{1,0:T(8,128)(2,1)S(1)}, bf16[208,128]{1,0:T(8,128)(2,1)S(1)}, u32[]{:S(2)}, u32[]{:S(2)}) collective-permute-start(bf16[208,128]{1,0:T(8,128)(2,1)S(1)} %get-tuple-element.22), channel_id=1, source_target_pairs={{0,8},{4,12},{8,0},{12,4},{1,9},{5,13},{9,1},{13,5},{2,10},{6,14},... | collective-permute-start | bytes 159752 | tf_op jit(solution)/shard_map/ppermute | solution.py:261
  12.0 6.8 %collective-permute-start.3 = (bf16[208,128]{1,0:T(8,128)(2,1)S(1)}, bf16[208,128]{1,0:T(8,128)(2,1)S(1)}, u32[]{:S(2)}, u32[]{:S(2)}) collective-permute-start(bf16[208,128]{1,0:T(8,128)(2,1)S(1)} %get-tuple-element.23), channel_id=1, source_target_pairs={{0,12},{4,8},{8,4},{12,0},{1,13},{5,9},{9,5},{13,1},{2,14},{6,10},... | collective-permute-start | bytes 159752 | tf_op jit(solution)/shard_map/ppermute | solution.py:261
  12.0 29.0 %copy-start.1 = (s32[2]{0:T(128)S(1)}, s32[2]{0:T(128)}, u32[]{:S(2)}) copy-start(s32[2]{0:T(128)} %counts.1) | copy-start | bytes 28
  19.0 1.9 %collective-permute-start.5 = (f32[768,128]{1,0:T(8,128)S(1)}, f32[768,128]{1,0:T(8,128)S(1)}, u32[]{:S(2)}, u32[]{:S(2)}) collective-permute-start(f32[768,128]{1,0:T(8,128)S(1)} %get-tuple-element.26), channel_id=1, source_target_pairs={{0,1},{1,0},{2,3},{3,2},{4,5},{5,4},{6,7},{7,6},{8,9},{9,8},{10,11... | collective-permute-start | bytes 1179656 | tf_op jit(solution)/shard_map/ppermute | solution.py:276
  19.0 7.8 %collective-permute-start.4 = (bf16[768,128]{1,0:T(8,128)(2,1)S(1)}, bf16[768,128]{1,0:T(8,128)(2,1)S(1)}, u32[]{:S(2)}, u32[]{:S(2)}) collective-permute-start(bf16[768,128]{1,0:T(8,128)(2,1)S(1)} %stack_in.1._.rows), channel_id=1, source_target_pairs={{0,2},{1,3},{2,0},{3,1},{4,6},{5,7},{6,4},{7,5},{8,10},{9,11},{10,... | collective-permute-start | bytes 589832 | tf_op jit(solution)/shard_map/ppermute | solution.py:284
  20.9 7.6 %collective-permute-start.6 = (bf16[384,128]{1,0:T(8,128)(2,1)S(1)}, bf16[384,128]{1,0:T(8,128)(2,1)S(1)}, u32[]{:S(2)}, u32[]{:S(2)}) collective-permute-start(bf16[384,128]{1,0:T(8,128)(2,1)S(1)} %get-tuple-element.28), channel_id=1, source_target_pairs={{0,2},{1,3},{2,0},{3,1},{4,6},{5,7},{6,4},{7,5},{8,10},{9,11},{10,... | collective-permute-start | bytes 294920 | tf_op jit(solution)/shard_map/ppermute | solution.py:280
  22.6 18.4 %collective-permute-start.10 = (bf16[768,128]{1,0:T(8,128)(2,1)S(1)}, bf16[768,128]{1,0:T(8,128)(2,1)S(1)}, u32[]{:S(2)}, u32[]{:S(2)}) collective-permute-start(bf16[768,128]{1,0:T(8,128)(2,1)S(1)} %stack_in.1._.rows), channel_id=1, source_target_pairs={{0,1},{1,0},{2,3},{3,2},{4,5},{5,4},{6,7},{7,6},{8,9},{9,8},{10,11... | collective-permute-start | bytes 589832 | tf_op jit(solution)/shard_map/ppermute | solution.py:290
  26.8 14.2 %collective-permute-start.11 = (bf16[768,128]{1,0:T(8,128)(2,1)S(1)}, bf16[768,128]{1,0:T(8,128)(2,1)S(1)}, u32[]{:S(2)}, u32[]{:S(2)}) collective-permute-start(bf16[768,128]{1,0:T(8,128)(2,1)S(1)} %collective-permute-done.4.far), channel_id=1, source_target_pairs={{0,1},{1,0},{2,3},{3,2},{4,5},{5,4},{6,7},{7,6},{8,9},{9,8},{10,11... | collective-permute-start | bytes 589832 | tf_op jit(solution)/shard_map/ppermute | solution.py:291
  28.5 4.7 %collective-permute-start.7 = (bf16[384,128]{1,0:T(8,128)(2,1)S(1)}, bf16[384,128]{1,0:T(8,128)(2,1)S(1)}, u32[]{:S(2)}, u32[]{:S(2)}) collective-permute-start(bf16[384,128]{1,0:T(8,128)(2,1)S(1)} %round_out.1.refs_0_), channel_id=1, source_target_pairs={{0,4},{4,0},{8,12},{12,8},{1,5},{5,1},{9,13},{13,9},{2,6},{6,2},{1... | collective-permute-start | bytes 294920 | tf_op jit(solution)/shard_map/ppermute | solution.py:282
  29.5 11.1 %collective-permute-start.8 = (bf16[384,128]{1,0:T(8,128)(2,1)S(1)}, bf16[384,128]{1,0:T(8,128)(2,1)S(1)}, u32[]{:S(2)}, u32[]{:S(2)}) collective-permute-start(bf16[384,128]{1,0:T(8,128)(2,1)S(1)} %round_out.1.refs_0_), channel_id=1, source_target_pairs={{0,8},{4,12},{8,0},{12,4},{1,9},{5,13},{9,1},{13,5},{2,10},{6,14},... | collective-permute-start | bytes 294920 | tf_op jit(solution)/shard_map/ppermute | solution.py:282
  33.0 7.6 %collective-permute-start.9 = (bf16[384,128]{1,0:T(8,128)(2,1)S(1)}, bf16[384,128]{1,0:T(8,128)(2,1)S(1)}, u32[]{:S(2)}, u32[]{:S(2)}) collective-permute-start(bf16[384,128]{1,0:T(8,128)(2,1)S(1)} %round_out.1.refs_0_), channel_id=1, source_target_pairs={{0,12},{4,8},{8,4},{12,0},{1,13},{5,9},{9,5},{13,1},{2,14},{6,10},... | collective-permute-start | bytes 294920 | tf_op jit(solution)/shard_map/ppermute | solution.py:282

commit v3 on v2

--- a/solution.py
+++ b/solution.py
@@ -10,7 +10,8 @@
 F32 = jnp.float32
 BF16 = jnp.bfloat16
 CHUNK = 512
-VMEM = 40 * 2**20
+VMEM = 20 * 2**20
+FAR_FIRST = (2, 3, 1)
 LABEL_ROWS = 16
 
 
@@ -35,8 +36,8 @@
 
 def rotate_in_kernel(
     acts, routes, ids, basis_in,
-    keep, send, label, pick,
-    acts_v, routes_v, ids_v, basis_v, acc, sems,
+    acc, label, pick,
+    acts_v, routes_v, ids_v, basis_v, sems,
 ):
     tokens = acts.shape[0]
     experts, _, width = basis_in.shape
@@ -73,7 +74,7 @@
         pick[e * cap : (e + 1) * cap, :] = (
             (wide[e : e + 1] == slots) & (routed_to == float(e))
         ).astype(BF16)
-    numbers = jnp.broadcast_to(ids_v[...].astype(F32) + 1.0, (8, tokens)).astype(BF16)
+    numbers = jnp.broadcast_to(ids_v[...].reshape(1, tokens).astype(F32) + 1.0, (8, tokens)).astype(BF16)
     named = lax.dot_general(numbers, pick_in, (((1,), (1,)), ((), ())), preferred_element_type=F32)
     block = jnp.zeros((LABEL_ROWS, 128), F32)
     row = iota((LABEL_ROWS, 128), 0)
@@ -89,7 +90,12 @@
     for e in range(experts):
         bases[e].wait()
         acc[e] = dot(chosen[e * cap : (e + 1) * cap], basis_v[e])
+
+
+def split_in_kernel(acc, keep, send):
+    experts, cap, width = acc.shape
     core = lax.rem(lax.axis_index("tensor"), 2)
+    half = cap // 2
     at = 0
     for q in range(width // 128):
         for e in range(experts):
@@ -100,31 +106,23 @@
             at += half
 
 
-def rotate_out_kernel(grads, pick, basis_out, _, acc, grads_v, basis_v, sems):
+def rotate_out_kernel(grads, pick, basis_out, _, acc):
     tokens, _, hidden = grads.shape
-    experts, _, width = basis_out.shape
+    experts = basis_out.shape[0]
     cap = tokens // 2
-    fetch = fetcher(sems)
-    steps = hidden // CHUNK
-    copies = []
-    for s in range(steps):
+    for s in range(hidden // CHUNK):
         cols = pl.ds(s * CHUNK, CHUNK)
-        copies.append(
-            (fetch(grads.at[:, :, cols], grads_v.at[s]), fetch(basis_out.at[:, cols, :], basis_v.at[s]))
-        )
-    for s in range(steps):
-        for copy in copies[s]:
-            copy.wait()
-        chosen = dot(pick[...], grads_v[s].reshape(2 * tokens, CHUNK)).astype(BF16)
+        chosen = dot(pick[...], grads[:, :, cols].reshape(2 * tokens, CHUNK)).astype(BF16)
         for e in range(experts):
-            part = dot(chosen[e * cap : (e + 1) * cap], basis_v[s, e])
+            part = dot(chosen[e * cap : (e + 1) * cap], basis_out[e, cols, :])
             if s == 0:
                 acc[e] = part
             else:
                 acc[e] += part
 
 
-def split_out_kernel(acc, _, keep, send):
+def split_out_kernel(acc, *refs):
+    *_, keep, send = refs
     experts, cap, width = acc.shape
     core = lax.rem(lax.axis_index("tensor"), 2)
     at = 0
@@ -137,13 +135,12 @@
             at += cap
 
 
-def pair_in_kernel(kept, got, label, *pays):
+def pair_in_kernel(kept, got, *pays):
     slab = kept.shape[0] // len(pays)
     d = lax.axis_index("dp")
     for k, pay in enumerate(pays):
         rows = pl.ds(pl.multiple_of((d ^ k) * slab, 16), slab)
-        pay[:slab, :] = (kept[rows, :] + got[rows, :]).astype(BF16)
-        pay[slab:, :] = label[...]
+        pay[...] = (kept[rows, :] + got[rows, :]).astype(BF16)
 
 
 def pair_out_kernel(kept, got, keep, send):
@@ -155,29 +152,29 @@
     send[...] = (kept[other, :] + got[other, :]).astype(BF16)
 
 
-def round_kernel(kept, got, out):
-    out[...] = (kept[...] + got[...].astype(F32)).astype(BF16)
-
-
-def stack_kernel(*refs):
-    *pieces, out = refs
-    slab = pieces[0].shape[0] - LABEL_ROWS
+def round_kernel(kept, got, label, out):
+    outer = kept.shape[0]
+    out[:outer, :] = (kept[...] + got[...].astype(F32)).astype(BF16)
+    out[outer:, :] = label[...]
+
+
+def stack_kernel(experts, *refs):
+    pieces, outs = refs[: -1 - experts], refs[-experts:]
+    half = pieces[0].shape[0] // experts
     for k, piece in enumerate(pieces):
-        out[k * slab : (k + 1) * slab, :] = piece[:slab, :]
-
-
-def half_blocks(dp, e, which, rows, far, outs, pieces):
-    half = rows.shape[0] // (2 * dp)
-    slab = pieces[0].shape[0] - LABEL_ROWS
-    rows_in, rows_out, labels = [], [], []
-    for k in range(dp):
-        at = pl.ds((2 * k + e) * half, half)
-        rows_in.append((rows[at, :].astype(F32) + far[at, :].astype(F32)).astype(BF16))
-        at = pl.ds(pl.multiple_of((2 * e + which) * half, 16), half)
-        rows_out.append(outs[k][at, :])
-        label = pieces[k][slab:, :].astype(F32)[2 * e : 2 * e + 2, :half]
+        for e, out in enumerate(outs):
+            out[k * half : (k + 1) * half, :] = piece[e * half : (e + 1) * half, :]
+
+
+def half_blocks(e, experts, which, near, far, outs):
+    dp = len(outs)
+    half = near.shape[0] // dp
+    rows_out, labels = [], []
+    for ref in outs:
+        rows_out.append(ref[pl.ds(pl.multiple_of((2 * e + which) * half, 16), half), :])
+        label = ref[2 * experts * half :, :].astype(F32)[2 * e : 2 * e + 2, :half]
         labels.append(jnp.where(which == 0, label[0:1], label[1:2]))
-    rows_in = jnp.concatenate(rows_in, axis=0)
+    rows_in = (near[...].astype(F32) + far[...].astype(F32)).astype(BF16)
     rows_out = jnp.concatenate(rows_out, axis=0).T
     labels = jnp.concatenate(labels, axis=1)
     masked = [
@@ -186,50 +183,59 @@
     return dot(jnp.concatenate(masked, axis=0), rows_in)
 
 
-def first_blocks_kernel(dp, rows, far, *refs):
-    outs, pieces, total = refs[:dp], refs[dp : 2 * dp], refs[2 * dp]
+def first_blocks_kernel(experts, dp, counts, *refs):
+    near, far, outs = refs[:experts], refs[experts : 2 * experts], refs[2 * experts : -2]
+    total, divisor = refs[-2:]
     core = lax.rem(lax.axis_index("tensor"), 2)
-    for e in range(total.shape[0]):
-        total[e] = half_blocks(dp, e, core, rows, far, outs, pieces)
-
-
-def blocks_kernel(dp, counts, first, rows, far, *refs):
-    outs, pieces, result = refs[:dp], refs[dp : 2 * dp], refs[2 * dp]
+    for e in range(experts):
+        divisor[e] = jnp.full(divisor.shape[1:], counts[e].astype(F32), F32)
+        total[e] = half_blocks(e, experts, core, near[e], far[e], outs)
+
+
+def blocks_kernel(experts, dp, first, divisor, *refs):
+    near, far, outs = refs[:experts], refs[experts : 2 * experts], refs[2 * experts : -3]
+    result, final, sems = refs[-3:]
     core = lax.rem(lax.axis_index("tensor"), 2)
-    for e in range(result.shape[0]):
-        total = first[e] + half_blocks(dp, e, 1 - core, rows, far, outs, pieces)
+    copies = []
+    for e in range(experts):
+        total = first[e] + half_blocks(e, experts, 1 - core, near[e], far[e], outs)
         side = total.shape[0] // dp
         squares = total * total
         summed = squares[:side]
         for n in range(1, dp):
             summed = summed + squares[n * side : (n + 1) * side]
-        result[e] = summed / counts[e].astype(F32)
-
-
-def call(kernel, name, out_shape, specs=None, scratch=()):
+        final[e] = summed / divisor[e][:1]
+        copies.append(pltpu.make_async_copy(final.at[e], result.at[e], sems.at[e]))
+        copies[e].start()
+    for copy in copies:
+        copy.wait()
+
+
+def call(kernel, name, out_shape, specs=None, scratch=(), out_specs=None, flops=1):
     vmem = pl.BlockSpec(memory_space=pltpu.VMEM)
+    given = {} if out_specs is None else {"out_specs": out_specs}
     return lambda *args: pl.pallas_call(
         kernel,
         out_shape=out_shape,
         in_specs=specs or [vmem] * len(args),
         scratch_shapes=scratch,
         compiler_params=pltpu.CompilerParams(vmem_limit_bytes=VMEM),
-        cost_estimate=pl.CostEstimate(flops=1, bytes_accessed=1, transcendentals=0),
+        cost_estimate=pl.CostEstimate(flops=flops, bytes_accessed=1, transcendentals=0),
         name=name,
+        **given,
     )(*args)
 
 
 def fast(acts, grads, routes, example_ids, expert_counts, basis_in, basis_out):
-    tokens, _, hidden = grads.shape
+    tokens = acts.shape[0]
     experts, features, width = basis_in.shape
     cap = tokens // 2
     dp = lax.axis_size("dp")
-    steps = hidden // CHUNK
     wide = experts * cap
     half = wide * width // 256
-    slab = half // dp
     hbm = pl.BlockSpec(memory_space=pltpu.HBM)
     vmem = pl.BlockSpec(memory_space=pltpu.VMEM)
+    smem = pl.BlockSpec(memory_space=pltpu.SMEM)
 
     def pin(x):
         return pltpu.with_memory_space_constraint(x, pltpu.HBM)
@@ -239,62 +245,67 @@
 
     core = [(t, t ^ 1) for t in range(4)]
     across = [(t, t ^ 2) for t in range(4)]
-    others = [[(d, d ^ k) for d in range(dp)] for k in range(dp)]
-
-    keep, send, label, pick = call(
+
+    def spread(pays):
+        got = {k: lax.ppermute(pays[k], "dp", [(d, d ^ k) for d in range(dp)]) for k in FAR_FIRST}
+        return [pays[0]] + [got[k] for k in range(1, dp)]
+
+    partial = jax.ShapeDtypeStruct((experts, cap, width), F32)
+    acc, label, pick = call(
         rotate_in_kernel,
         "rotate_in",
-        (rows(half, F32), rows(half, F32), rows(LABEL_ROWS, BF16),
-         jax.ShapeDtypeStruct((wide, 2 * tokens), BF16)),
+        (partial, rows(LABEL_ROWS, BF16), jax.ShapeDtypeStruct((wide, 2 * tokens), BF16)),
         [hbm] * 4,
         [
             pltpu.VMEM(acts.shape, BF16),
             pltpu.VMEM((2, tokens), jnp.int32),
-            pltpu.VMEM((1, tokens), jnp.int32),
+            pltpu.VMEM((tokens,), jnp.int32),
             pltpu.VMEM(basis_in.shape, BF16),
-            pltpu.VMEM((experts, cap, width), F32),
             pltpu.SemaphoreType.DMA((3 + experts,)),
         ],
-    )(pin(acts), routes.T, example_ids.reshape(1, tokens), pin(basis_in))
+    )(pin(acts), pin(routes.T), pin(example_ids), pin(basis_in))
+    keep, send = call(
+        split_in_kernel, "split_in", (rows(half, F32), rows(half, F32)), flops=8 * 10**9
+    )(acc)
     got = lax.ppermute(send, "tensor", core)
-    pieces = call(pair_in_kernel, "pair_in", [rows(slab + LABEL_ROWS, BF16)] * dp)(keep, got, label)
-    arrived = [pieces[0]] + [lax.ppermute(pieces[k], "dp", others[k]) for k in range(1, dp)]
-
-    acc = call(
-        rotate_out_kernel,
-        "rotate_out",
-        jax.ShapeDtypeStruct((experts, cap, width), F32),
-        [hbm, vmem, hbm, vmem],
-        [
-            pltpu.VMEM((steps, tokens, 2, CHUNK), BF16),
-            pltpu.VMEM((steps, experts, CHUNK, width), BF16),
-            pltpu.SemaphoreType.DMA((2 * steps,)),
-        ],
-    )(pin(grads), pick, pin(basis_out), pieces[0])
-    mine = call(stack_kernel, "stack_in", rows(half, BF16))(*arrived)
-    keep, send = call(split_out_kernel, "split_out", (rows(half, F32), rows(half, F32)))(acc, mine)
+    pieces = call(pair_in_kernel, "pair_in", [rows(half // dp, BF16)] * dp)(keep, got)
+    arrived = spread(pieces)
+
+    acc = call(rotate_out_kernel, "rotate_out", partial)(grads, pick, basis_out, pieces[0])
+    keep, send = call(split_out_kernel, "split_out", (rows(half, F32), rows(half, F32)))(
+        acc, *arrived[1:]
+    )
     got = lax.ppermute(send, "tensor", core)
     keep, send = call(pair_out_kernel, "pair_out", (rows(half // 2, F32), rows(half // 2, BF16)))(
         keep, got
     )
     got = lax.ppermute(send, "tensor", across)
-    out = call(round_kernel, "round_out", rows(half // 2, BF16))(keep, got)
-    outs = [out] + [lax.ppermute(out, "dp", others[k]) for k in range(1, dp)]
-
-    far = lax.ppermute(mine, "tensor", across)
-    first = call(
-        functools.partial(first_blocks_kernel, dp),
+    out = call(round_kernel, "round_out", rows(half // 2 + LABEL_ROWS, BF16))(keep, got, label)
+
+    near = call(
+        functools.partial(stack_kernel, experts), "stack_in", [rows(half // experts, BF16)] * experts
+    )(*arrived, out)
+    far = [lax.ppermute(x, "tensor", across) for x in near]
+    outs = spread([out] * dp)
+    first, divisor = call(
+        functools.partial(first_blocks_kernel, experts, dp),
         "first_blocks",
-        jax.ShapeDtypeStruct((experts, dp * 128, 128), F32),
-    )(mine, far, *outs, *arrived)
-    other = lax.ppermute(mine, "tensor", core)
-    other_far = lax.ppermute(far, "tensor", core)
+        (
+            jax.ShapeDtypeStruct((experts, dp * 128, 128), F32),
+            jax.ShapeDtypeStruct((experts, 8, 128), F32),
+        ),
+        [smem] + [vmem] * (2 * experts + dp),
+    )(expert_counts, *near, *far, *outs)
+    near = [lax.ppermute(x, "tensor", core) for x in near]
+    far = [lax.ppermute(x, "tensor", core) for x in far]
+    result = jax.ShapeDtypeStruct((experts, 128, 128), F32)
     return call(
-        functools.partial(blocks_kernel, dp),
+        functools.partial(blocks_kernel, experts, dp),
         "blocks",
-        jax.ShapeDtypeStruct((experts, 128, 128), F32),
-        [pl.BlockSpec(memory_space=pltpu.SMEM)] + [vmem] * (2 * dp + 3),
-    )(expert_counts, first, other, other_far, *outs, *arrived)
+        result,
+        scratch=[pltpu.VMEM(result.shape, F32), pltpu.SemaphoreType.DMA((experts,))],
+        out_specs=hbm,
+    )(first, divisor, *near, *far, *outs)
 
 
 EX_DEV = 1

time: 42.9 us -> 37.7 us (0.88)
  waiting for transfers between devices: 14.9 us -> 12 us
  Pallas kernels: 12.2 us -> 10.6 us
  local copies, waits for them, and re-layouts: 1.37 us -> 0.03 us
  starting transfers between devices: 14.1 us -> 14.8 us
    ppermute x9 -> x12, waiting for transfers between devices: 11.9 us -> 5.58 us  [the longest x6 2.85 us: spread(): lax.ppermute(pays[k], 'dp', [(d, d ^ k) for d in range(dp)])]
    ppermute x2, waiting for transfers between devices: 1.35 us -> 3.06 us  [fast(): got = lax.ppermute(send, 'tensor', core)]
    ppermute x1, waiting for transfers between devices: 1.65 us -> 3.35 us  [fast(): got = lax.ppermute(send, 'tensor', across)]
    pallas_call x9 -> x10, Pallas kernels: 12.2 us -> 10.6 us  [call(): pl.pallas_call(kernel, out_shape=out_shape, in_specs=specs or [vmem] * le...]
    ppermute x9 -> x12, starting transfers between devices: 11.8 us -> 12.7 us  [the longest x6 10.1 us: spread(): lax.ppermute(pays[k], 'dp', [(d, d ^ k) for d in range(dp)])]
    reshape x1 -> x0, local copies, waits for them, and re-layouts: 0.68 us -> none  [fast(): example_ids.reshape(1, tokens)]
    unnamed x4 -> x10, local copies, waits for them, and re-layouts: 0.69 us -> 0.03 us
  transfers between devices with their start and end apart: 12 -> 15, of which waited for: 5 -> 8; matrix products, arithmetic and copies ran while one was open for 0% -> 0% of each run, Pallas kernels for 17% -> 16%
where the time goes in v3:
time: 37.7 us; the launch traced here: 37.6 us
  starting transfers between devices  14.8 us (39%)
  waiting for transfers between devices  12 us (32%)
  Pallas kernels  10.6 us (28%)
    pallas_call x10, Pallas kernels, call(): pl.pallas_call(kernel, out_shape=out_shape, in_specs=specs or [vmem] * le...  10.6 us
    ppermute x6, starting transfers between devices, spread(): lax.ppermute(pays[k], 'dp', [(d, d ^ k) for d in range(dp)])  10.1 us
    ppermute x1, waiting for transfers between devices, fast(): got = lax.ppermute(send, 'tensor', across)  3.35 us
    ppermute x2, waiting for transfers between devices, fast(): got = lax.ppermute(send, 'tensor', core)  3.06 us
    ppermute x6, waiting for transfers between devices, spread(): lax.ppermute(pays[k], 'dp', [(d, d ^ k) for d in range(dp)])  2.85 us
    ppermute x2, waiting for transfers between devices, fast(): far = [lax.ppermute(x, 'tensor', across) for x in near]  2.72 us
    ppermute x2, starting transfers between devices, fast(): far = [lax.ppermute(x, 'tensor', across) for x in near]  2.09 us
    ppermute x1, starting transfers between devices, fast(): got = lax.ppermute(send, 'tensor', across)  1.55 us
  transfers between devices with their start and end apart: 15, of which 8 were waited for; matrix products, arithmetic and copies ran while one was open for 0% of the time, Pallas kernels for 16%

profile of v3, /device:TPU:0, one launch (start us, length us, event | category | flops | bytes accessed | tf_op | source)
XLA Modules:
  0.0 37.6 jit_solution(5118193002924646446)
XLA Ops:
  0.0 0.0 slice-start.2
  0.0 3.2 %rotate_in.1 = (f32[2,192,512]{2,1,0:T(8,128)S(1)}, bf16[16,128]{1,0:T(8,128)(2,1)S(1)}, bf16[384,768]{1,0:T(8,128)(2,1)S(1)}) custom-call(bf16[384,1536]{1,0:T(8,128)(2,1)} %acts.1, s32[2,384]{1,0:T(2,128)} %bitcast.5, s32[384]{0:T(512)} %ids.1, bf16[2,1536,512]{2,1,0:T(8,128)(2,1)} %basis_in.1), custom_call_target="tpu_custom_call" | custom-call | flops 1 | bytes 1 | tf_op jit(solution)/shard_map/rotate_in/pallas_call | solution.py:217
  3.2 0.0 slice-start
  3.3 0.0 slice-start.1
  3.3 0.0 slice-start.3
  3.3 0.1 split_in.1
  3.4 0.5 %collective-permute-start = (f32[768,128]{1,0:T(8,128)S(1)}, f32[768,128]{1,0:T(8,128)S(1)}, u32[]{:S(2)}, u32[]{:S(2)}) collective-permute-start(f32[768,128]{1,0:T(8,128)S(1)} %get-tuple-element.24), channel_id=1, source_target_pairs={{0,1},{1,0},{2,3},{3,2},{4,5},{5,4},{6,7},{7,6},{8,9},{9,8},{10,11... | collective-permute-start | bytes 1179656 | tf_op jit(solution)/shard_map/ppermute | solution.py:270
  3.9 1.3 %collective-permute-done.got = f32[768,128]{1,0:T(8,128)S(1)} collective-permute-done((f32[768,128]{1,0:T(8,128)S(1)}, f32[768,128]{1,0:T(8,128)S(1)}, u32[]{:S(2)}, u32[]{:S(2)}) %collective-permute-start) | collective-permute-done | bytes 393248 | tf_op jit(solution)/shard_map/ppermute | solution.py:270
  5.3 3.0 %collective-permute-start.1 = (bf16[192,128]{1,0:T(8,128)(2,1)S(1)}, bf16[192,128]{1,0:T(8,128)(2,1)S(1)}, u32[]{:S(2)}, u32[]{:S(2)}) collective-permute-start(bf16[192,128]{1,0:T(8,128)(2,1)S(1)} %get-tuple-element.26), channel_id=1, source_target_pairs={{0,4},{4,0},{8,12},{12,8},{1,5},{5,1},{9,13},{13,9},{2,6},{6,2},{1... | collective-permute-start | bytes 147464 | tf_op jit(solution)/shard_map/ppermute | solution.py:250
  8.3 2.6 %collective-permute-start.2 = (bf16[192,128]{1,0:T(8,128)(2,1)S(1)}, bf16[192,128]{1,0:T(8,128)(2,1)S(1)}, u32[]{:S(2)}, u32[]{:S(2)}) collective-permute-start(bf16[192,128]{1,0:T(8,128)(2,1)S(1)} %get-tuple-element.27), channel_id=1, source_target_pairs={{0,8},{4,12},{8,0},{12,4},{1,9},{5,13},{9,1},{13,5},{2,10},{6,14},... | collective-permute-start | bytes 147464 | tf_op jit(solution)/shard_map/ppermute | solution.py:250
  10.9 0.0 collective-permute-start.3
  10.9 0.0 slice-done.2
  10.9 0.0 slice-done
  10.9 0.0 slice-done.1
  10.9 0.0 slice-done.3
  10.9 0.0 copy-start
  10.9 5.0 %rotate_out.1.acc = f32[2,192,512]{2,1,0:T(8,128)S(1)} custom-call(bf16[384,2,4096]{2,1,0:T(2,128)(2,1)S(1)} %bitcast.4, bf16[384,768]{1,0:T(8,128)(2,1)S(1)} %get-tuple-element.29.pick, bf16[2,4096,512]{2,1,0:T(8,128)(2,1)S(1)} %bitcast.2, bf16[192,128]{1,0:T(8,128)(2,1)S(1)} %get-tuple-element.25._.refs_0_), custom_call_target="tpu_custom_call" | custom-call | flops 1 | bytes 1 | tf_op jit(solution)/shard_map/rotate_out/pallas_call | solution.py:217
  15.9 0.0 collective-permute-done.1.refs_0_.refs_1_
  15.9 0.0 collective-permute-done.2.refs_1_.refs_2_
  15.9 0.8 %collective-permute-done.3.refs_2_.refs_3_ = bf16[192,128]{1,0:T(8,128)(2,1)S(1)} collective-permute-done((bf16[192,128]{1,0:T(8,128)(2,1)S(1)}, bf16[192,128]{1,0:T(8,128)(2,1)S(1)}, u32[]{:S(2)}, u32[]{:S(2)}) %collective-permute-start.3) | collective-permute-done | bytes 49184 | tf_op jit(solution)/shard_map/ppermute | solution.py:250
  16.8 0.1 split_out.1
  16.9 0.1 collective-permute-start.4
  16.9 1.7 %collective-permute-done.4.got = f32[768,128]{1,0:T(8,128)S(1)} collective-permute-done((f32[768,128]{1,0:T(8,128)S(1)}, f32[768,128]{1,0:T(8,128)S(1)}, u32[]{:S(2)}, u32[]{:S(2)}) %collective-permute-start.4) | collective-permute-done | bytes 393248 | tf_op jit(solution)/shard_map/ppermute | solution.py:278
  18.7 1.6 %collective-permute-start.5 = (bf16[384,128]{1,0:T(8,128)(2,1)S(1)}, bf16[384,128]{1,0:T(8,128)(2,1)S(1)}, u32[]{:S(2)}, u32[]{:S(2)}) collective-permute-start(bf16[384,128]{1,0:T(8,128)(2,1)S(1)} %get-tuple-element.33), channel_id=1, source_target_pairs={{0,2},{1,3},{2,0},{3,1},{4,6},{5,7},{6,4},{7,5},{8,10},{9,11},{10,... | collective-permute-start | bytes 294920 | tf_op jit(solution)/shard_map/ppermute | solution.py:282
  20.3 3.3 %collective-permute-done.5.got = bf16[384,128]{1,0:T(8,128)(2,1)S(1)} collective-permute-done((bf16[384,128]{1,0:T(8,128)(2,1)S(1)}, bf16[384,128]{1,0:T(8,128)(2,1)S(1)}, u32[]{:S(2)}, u32[]{:S(2)}) %collective-permute-start.5) | collective-permute-done | bytes 98336 | tf_op jit(solution)/shard_map/ppermute | solution.py:282
  23.6 3.1 %collective-permute-start.10 = (bf16[400,128]{1,0:T(8,128)(2,1)S(1)}, bf16[400,128]{1,0:T(8,128)(2,1)S(1)}, u32[]{:S(2)}, u32[]{:S(2)}) collective-permute-start(bf16[400,128]{1,0:T(8,128)(2,1)S(1)} %round_out.1.refs_4_), channel_id=1, source_target_pairs={{0,12},{4,8},{8,4},{12,0},{1,13},{5,9},{9,5},{13,1},{2,14},{6,10},... | collective-permute-start | bytes 307208 | tf_op jit(solution)/shard_map/ppermute | solution.py:250
  26.7 0.0 collective-permute-start.9
  26.7 1.6 %collective-permute-start.6 = (bf16[384,128]{1,0:T(8,128)(2,1)S(1)}, bf16[384,128]{1,0:T(8,128)(2,1)S(1)}, u32[]{:S(2)}, u32[]{:S(2)}) collective-permute-start(bf16[384,128]{1,0:T(8,128)(2,1)S(1)} %get-tuple-element.35.refs_0_), channel_id=1, source_target_pairs={{0,2},{1,3},{2,0},{3,1},{4,6},{5,7},{6,4},{7,5},{8,10},{9,11},{10,... | collective-permute-start | bytes 294920 | tf_op jit(solution)/shard_map/ppermute | solution.py:288
  28.3 0.5 %collective-permute-start.7 = (bf16[384,128]{1,0:T(8,128)(2,1)S(1)}, bf16[384,128]{1,0:T(8,128)(2,1)S(1)}, u32[]{:S(2)}, u32[]{:S(2)}) collective-permute-start(bf16[384,128]{1,0:T(8,128)(2,1)S(1)} %get-tuple-element.36.refs_1_), channel_id=1, source_target_pairs={{0,2},{1,3},{2,0},{3,1},{4,6},{5,7},{6,4},{7,5},{8,10},{9,11},{10,... | collective-permute-start | bytes 294920 | tf_op jit(solution)/shard_map/ppermute | solution.py:288
  28.8 1.4 %collective-permute-start.8 = (bf16[400,128]{1,0:T(8,128)(2,1)S(1)}, bf16[400,128]{1,0:T(8,128)(2,1)S(1)}, u32[]{:S(2)}, u32[]{:S(2)}) collective-permute-start(bf16[400,128]{1,0:T(8,128)(2,1)S(1)} %round_out.1.refs_4_), channel_id=1, source_target_pairs={{0,4},{4,0},{8,12},{12,8},{1,5},{5,1},{9,13},{13,9},{2,6},{6,2},{1... | collective-permute-start | bytes 307208 | tf_op jit(solution)/shard_map/ppermute | solution.py:250
  30.2 1.6 %collective-permute-done.6.refs_2_ = bf16[384,128]{1,0:T(8,128)(2,1)S(1)} collective-permute-done((bf16[384,128]{1,0:T(8,128)(2,1)S(1)}, bf16[384,128]{1,0:T(8,128)(2,1)S(1)}, u32[]{:S(2)}, u32[]{:S(2)}) %collective-permute-start.6) | collective-permute-done | bytes 98336 | tf_op jit(solution)/shard_map/ppermute | solution.py:288
  31.7 0.0 collective-permute-start.11
  31.7 1.2 %collective-permute-done.7.refs_3_ = bf16[384,128]{1,0:T(8,128)(2,1)S(1)} collective-permute-done((bf16[384,128]{1,0:T(8,128)(2,1)S(1)}, bf16[384,128]{1,0:T(8,128)(2,1)S(1)}, u32[]{:S(2)}, u32[]{:S(2)}) %collective-permute-start.7) | collective-permute-done | bytes 98336 | tf_op jit(solution)/shard_map/ppermute | solution.py:288
  32.9 0.0 collective-permute-start.12
  32.9 0.0 collective-permute-done.10.refs_7_
  32.9 0.5 %collective-permute-start.13 = (bf16[384,128]{1,0:T(8,128)(2,1)S(1)}, bf16[384,128]{1,0:T(8,128)(2,1)S(1)}, u32[]{:S(2)}, u32[]{:S(2)}) collective-permute-start(bf16[384,128]{1,0:T(8,128)(2,1)S(1)} %collective-permute-done.6.refs_2_), channel_id=1, source_target_pairs={{0,1},{1,0},{2,3},{3,2},{4,5},{5,4},{6,7},{7,6},{8,9},{9,8},{10,11... | collective-permute-start | bytes 294920 | tf_op jit(solution)/shard_map/ppermute | solution.py:300
  33.4 1.1 %collective-permute-done.9.refs_6_ = bf16[400,128]{1,0:T(8,128)(2,1)S(1)} collective-permute-done((bf16[400,128]{1,0:T(8,128)(2,1)S(1)}, bf16[400,128]{1,0:T(8,128)(2,1)S(1)}, u32[]{:S(2)}, u32[]{:S(2)}) %collective-permute-start.9) | collective-permute-done | bytes 102432 | tf_op jit(solution)/shard_map/ppermute | solution.py:250
  34.6 0.0 collective-permute-start.14
  34.6 0.9 %collective-permute-done.8.refs_5_ = bf16[400,128]{1,0:T(8,128)(2,1)S(1)} collective-permute-done((bf16[400,128]{1,0:T(8,128)(2,1)S(1)}, bf16[400,128]{1,0:T(8,128)(2,1)S(1)}, u32[]{:S(2)}, u32[]{:S(2)}) %collective-permute-start.8) | collective-permute-done | bytes 102432 | tf_op jit(solution)/shard_map/ppermute | solution.py:250
  35.5 0.0 copy-done
  35.5 1.0 %first_blocks.1 = (f32[2,512,128]{2,1,0:T(8,128)S(1)}, f32[2,8,128]{2,1,0:T(8,128)S(1)}) custom-call(s32[2]{0:T(128)S(1)} %copy-done, bf16[384,128]{1,0:T(8,128)(2,1)S(1)} %get-tuple-element.35.refs_0_, bf16[384,128]{1,0:T(8,128)(2,1)S(1)} %get-tuple-element.36.refs_1_, bf16[384,128]{1,0:T(8,128)(2,1)S(1)} %collective-permute-done.6.refs_2_, ...), custom_call_target="tpu_custom_call" | custom-call | flops 1 | bytes 1 | tf_op jit(solution)/shard_map/first_blocks/pallas_call | solution.py:217
  36.4 0.0 collective-permute-done.11.refs_0_
  36.5 0.0 collective-permute-done.12.refs_1_
  36.5 0.0 collective-permute-done.13.refs_2_
  36.5 0.0 collective-permute-done.14.refs_3_
  36.5 1.1 %blocks.1 = f32[2,128,128]{2,1,0:T(8,128)} custom-call(f32[2,512,128]{2,1,0:T(8,128)S(1)} %get-tuple-element.37.first, f32[2,8,128]{2,1,0:T(8,128)S(1)} %get-tuple-element.38.divisor, bf16[384,128]{1,0:T(8,128)(2,1)S(1)} %collective-permute-done.11.refs_0_, bf16[384,128]{1,0:T(8,128)(2,1)S(1)} %collective-permute-done.12.refs_1_, ...), custom_call_target="tpu_custom_call" | custom-call | flops 1 | bytes 1 | tf_op jit(solution)/shard_map/blocks/pallas_call | solution.py:217
  (6 shorter events, 0.1 us)
Async XLA Ops:
  0.0 10.9 %slice-start.2 = ((s8[6291456]{0:T(1024)(128)(4,1)}), s8[4194304]{0:T(1024)(128)(4,1)S(1)}, s32[]{:S(2)}) async-start(s8[6291456]{0:T(1024)(128)(4,1)} %bitcast.3), calls=%async_computation.2 | async-start | bytes 8388608
  3.2 7.6 %slice-start = ((s8[8388608]{0:T(1024)(128)(4,1)}), s8[4194304]{0:T(1024)(128)(4,1)S(1)}, s32[]{:S(2)}) async-start(s8[8388608]{0:T(1024)(128)(4,1)} %bitcast.1), calls=%async_computation | async-start | bytes 8388608
  3.3 7.6 %slice-start.1 = ((s8[8388608]{0:T(1024)(128)(4,1)}), s8[4194304]{0:T(1024)(128)(4,1)S(1)}, s32[]{:S(2)}) async-start(s8[8388608]{0:T(1024)(128)(4,1)} %bitcast.1), calls=%async_computation.1 | async-start | bytes 8388608
  3.3 7.6 %slice-start.3 = ((s8[6291456]{0:T(1024)(128)(4,1)}), s8[2097152]{0:T(1024)(128)(4,1)S(1)}, s32[]{:S(2)}) async-start(s8[6291456]{0:T(1024)(128)(4,1)} %bitcast.3), calls=%async_computation.3 | async-start | bytes 4194304
  3.4 1.9 %collective-permute-start = (f32[768,128]{1,0:T(8,128)S(1)}, f32[768,128]{1,0:T(8,128)S(1)}, u32[]{:S(2)}, u32[]{:S(2)}) collective-permute-start(f32[768,128]{1,0:T(8,128)S(1)} %get-tuple-element.24), channel_id=1, source_target_pairs={{0,1},{1,0},{2,3},{3,2},{4,5},{5,4},{6,7},{7,6},{8,9},{9,8},{10,11... | collective-permute-start | bytes 1179656 | tf_op jit(solution)/shard_map/ppermute | solution.py:270
  5.3 10.7 %collective-permute-start.1 = (bf16[192,128]{1,0:T(8,128)(2,1)S(1)}, bf16[192,128]{1,0:T(8,128)(2,1)S(1)}, u32[]{:S(2)}, u32[]{:S(2)}) collective-permute-start(bf16[192,128]{1,0:T(8,128)(2,1)S(1)} %get-tuple-element.26), channel_id=1, source_target_pairs={{0,4},{4,0},{8,12},{12,8},{1,5},{5,1},{9,13},{13,9},{2,6},{6,2},{1... | collective-permute-start | bytes 147464 | tf_op jit(solution)/shard_map/ppermute | solution.py:250
  8.3 7.7 %collective-permute-start.2 = (bf16[192,128]{1,0:T(8,128)(2,1)S(1)}, bf16[192,128]{1,0:T(8,128)(2,1)S(1)}, u32[]{:S(2)}, u32[]{:S(2)}) collective-permute-start(bf16[192,128]{1,0:T(8,128)(2,1)S(1)} %get-tuple-element.27), channel_id=1, source_target_pairs={{0,8},{4,12},{8,0},{12,4},{1,9},{5,13},{9,1},{13,5},{2,10},{6,14},... | collective-permute-start | bytes 147464 | tf_op jit(solution)/shard_map/ppermute | solution.py:250
  10.9 5.9 %collective-permute-start.3 = (bf16[192,128]{1,0:T(8,128)(2,1)S(1)}, bf16[192,128]{1,0:T(8,128)(2,1)S(1)}, u32[]{:S(2)}, u32[]{:S(2)}) collective-permute-start(bf16[192,128]{1,0:T(8,128)(2,1)S(1)} %get-tuple-element.28), channel_id=1, source_target_pairs={{0,12},{4,8},{8,4},{12,0},{1,13},{5,9},{9,5},{13,1},{2,14},{6,10},... | collective-permute-start | bytes 147464 | tf_op jit(solution)/shard_map/ppermute | solution.py:250
  10.9 24.5 %copy-start = (s32[2]{0:T(128)S(1)}, s32[2]{0:T(128)}, u32[]{:S(2)}) copy-start(s32[2]{0:T(128)} %counts.1) | copy-start | bytes 28
  16.9 1.8 %collective-permute-start.4 = (f32[768,128]{1,0:T(8,128)S(1)}, f32[768,128]{1,0:T(8,128)S(1)}, u32[]{:S(2)}, u32[]{:S(2)}) collective-permute-start(f32[768,128]{1,0:T(8,128)S(1)} %get-tuple-element.31), channel_id=1, source_target_pairs={{0,1},{1,0},{2,3},{3,2},{4,5},{5,4},{6,7},{7,6},{8,9},{9,8},{10,11... | collective-permute-start | bytes 1179656 | tf_op jit(solution)/shard_map/ppermute | solution.py:278
  18.7 4.9 %collective-permute-start.5 = (bf16[384,128]{1,0:T(8,128)(2,1)S(1)}, bf16[384,128]{1,0:T(8,128)(2,1)S(1)}, u32[]{:S(2)}, u32[]{:S(2)}) collective-permute-start(bf16[384,128]{1,0:T(8,128)(2,1)S(1)} %get-tuple-element.33), channel_id=1, source_target_pairs={{0,2},{1,3},{2,0},{3,1},{4,6},{5,7},{6,4},{7,5},{8,10},{9,11},{10,... | collective-permute-start | bytes 294920 | tf_op jit(solution)/shard_map/ppermute | solution.py:282
  23.6 9.3 %collective-permute-start.10 = (bf16[400,128]{1,0:T(8,128)(2,1)S(1)}, bf16[400,128]{1,0:T(8,128)(2,1)S(1)}, u32[]{:S(2)}, u32[]{:S(2)}) collective-permute-start(bf16[400,128]{1,0:T(8,128)(2,1)S(1)} %round_out.1.refs_4_), channel_id=1, source_target_pairs={{0,12},{4,8},{8,4},{12,0},{1,13},{5,9},{9,5},{13,1},{2,14},{6,10},... | collective-permute-start | bytes 307208 | tf_op jit(solution)/shard_map/ppermute | solution.py:250
  26.7 7.9 %collective-permute-start.9 = (bf16[400,128]{1,0:T(8,128)(2,1)S(1)}, bf16[400,128]{1,0:T(8,128)(2,1)S(1)}, u32[]{:S(2)}, u32[]{:S(2)}) collective-permute-start(bf16[400,128]{1,0:T(8,128)(2,1)S(1)} %round_out.1.refs_4_), channel_id=1, source_target_pairs={{0,8},{4,12},{8,0},{12,4},{1,9},{5,13},{9,1},{13,5},{2,10},{6,14},... | collective-permute-start | bytes 307208 | tf_op jit(solution)/shard_map/ppermute | solution.py:250
  26.7 5.0 %collective-permute-start.6 = (bf16[384,128]{1,0:T(8,128)(2,1)S(1)}, bf16[384,128]{1,0:T(8,128)(2,1)S(1)}, u32[]{:S(2)}, u32[]{:S(2)}) collective-permute-start(bf16[384,128]{1,0:T(8,128)(2,1)S(1)} %get-tuple-element.35.refs_0_), channel_id=1, source_target_pairs={{0,2},{1,3},{2,0},{3,1},{4,6},{5,7},{6,4},{7,5},{8,10},{9,11},{10,... | collective-permute-start | bytes 294920 | tf_op jit(solution)/shard_map/ppermute | solution.py:288
  28.3 4.6 %collective-permute-start.7 = (bf16[384,128]{1,0:T(8,128)(2,1)S(1)}, bf16[384,128]{1,0:T(8,128)(2,1)S(1)}, u32[]{:S(2)}, u32[]{:S(2)}) collective-permute-start(bf16[384,128]{1,0:T(8,128)(2,1)S(1)} %get-tuple-element.36.refs_1_), channel_id=1, source_target_pairs={{0,2},{1,3},{2,0},{3,1},{4,6},{5,7},{6,4},{7,5},{8,10},{9,11},{10,... | collective-permute-start | bytes 294920 | tf_op jit(solution)/shard_map/ppermute | solution.py:288
  28.8 6.6 %collective-permute-start.8 = (bf16[400,128]{1,0:T(8,128)(2,1)S(1)}, bf16[400,128]{1,0:T(8,128)(2,1)S(1)}, u32[]{:S(2)}, u32[]{:S(2)}) collective-permute-start(bf16[400,128]{1,0:T(8,128)(2,1)S(1)} %round_out.1.refs_4_), channel_id=1, source_target_pairs={{0,4},{4,0},{8,12},{12,8},{1,5},{5,1},{9,13},{13,9},{2,6},{6,2},{1... | collective-permute-start | bytes 307208 | tf_op jit(solution)/shard_map/ppermute | solution.py:250
  31.7 4.7 %collective-permute-start.11 = (bf16[384,128]{1,0:T(8,128)(2,1)S(1)}, bf16[384,128]{1,0:T(8,128)(2,1)S(1)}, u32[]{:S(2)}, u32[]{:S(2)}) collective-permute-start(bf16[384,128]{1,0:T(8,128)(2,1)S(1)} %get-tuple-element.35.refs_0_), channel_id=1, source_target_pairs={{0,1},{1,0},{2,3},{3,2},{4,5},{5,4},{6,7},{7,6},{8,9},{9,8},{10,11... | collective-permute-start | bytes 294920 | tf_op jit(solution)/shard_map/ppermute | solution.py:299
  32.9 3.5 %collective-permute-start.12 = (bf16[384,128]{1,0:T(8,128)(2,1)S(1)}, bf16[384,128]{1,0:T(8,128)(2,1)S(1)}, u32[]{:S(2)}, u32[]{:S(2)}) collective-permute-start(bf16[384,128]{1,0:T(8,128)(2,1)S(1)} %get-tuple-element.36.refs_1_), channel_id=1, source_target_pairs={{0,1},{1,0},{2,3},{3,2},{4,5},{5,4},{6,7},{7,6},{8,9},{9,8},{10,11... | collective-permute-start | bytes 294920 | tf_op jit(solution)/shard_map/ppermute | solution.py:299
  32.9 3.6 %collective-permute-start.13 = (bf16[384,128]{1,0:T(8,128)(2,1)S(1)}, bf16[384,128]{1,0:T(8,128)(2,1)S(1)}, u32[]{:S(2)}, u32[]{:S(2)}) collective-permute-start(bf16[384,128]{1,0:T(8,128)(2,1)S(1)} %collective-permute-done.6.refs_2_), channel_id=1, source_target_pairs={{0,1},{1,0},{2,3},{3,2},{4,5},{5,4},{6,7},{7,6},{8,9},{9,8},{10,11... | collective-permute-start | bytes 294920 | tf_op jit(solution)/shard_map/ppermute | solution.py:300
  34.6 1.9 %collective-permute-start.14 = (bf16[384,128]{1,0:T(8,128)(2,1)S(1)}, bf16[384,128]{1,0:T(8,128)(2,1)S(1)}, u32[]{:S(2)}, u32[]{:S(2)}) collective-permute-start(bf16[384,128]{1,0:T(8,128)(2,1)S(1)} %collective-permute-done.7.refs_3_), channel_id=1, source_target_pairs={{0,1},{1,0},{2,3},{3,2},{4,5},{5,4},{6,7},{7,6},{8,9},{9,8},{10,11... | collective-permute-start | bytes 294920 | tf_op jit(solution)/shard_map/ppermute | solution.py:300

commit v4 on v3

--- a/solution.py
+++ b/solution.py
@@ -106,33 +106,33 @@
             at += half
 
 
-def rotate_out_kernel(grads, pick, basis_out, _, acc):
+def rotate_first_kernel(grads, pick, basis_out, acc, rest):
     tokens, _, hidden = grads.shape
-    experts = basis_out.shape[0]
     cap = tokens // 2
     for s in range(hidden // CHUNK):
         cols = pl.ds(s * CHUNK, CHUNK)
         chosen = dot(pick[...], grads[:, :, cols].reshape(2 * tokens, CHUNK)).astype(BF16)
-        for e in range(experts):
-            part = dot(chosen[e * cap : (e + 1) * cap], basis_out[e, cols, :])
-            if s == 0:
-                acc[e] = part
-            else:
-                acc[e] += part
-
-
-def split_out_kernel(acc, *refs):
-    *_, keep, send = refs
-    experts, cap, width = acc.shape
+        rest[:, cols] = chosen[cap:]
+        part = dot(chosen[:cap], basis_out[0, cols, :])
+        if s == 0:
+            acc[...] = part
+        else:
+            acc[...] += part
+
+
+def rotate_rest_kernel(e, rest, basis_out, acc):
+    cap = acc.shape[0]
+    acc[...] = dot(rest[(e - 1) * cap : e * cap, :], basis_out[e])
+
+
+def split_out_kernel(acc, keep, send):
+    cap, width = acc.shape
     core = lax.rem(lax.axis_index("tensor"), 2)
-    at = 0
     for x in range(width // 256):
-        for e in range(experts):
-            for ref, which in ((keep, core), (send, 1 - core)):
-                ref[at : at + cap, :] = acc[
-                    e, :, pl.ds(pl.multiple_of((2 * x + which) * 128, 128), 128)
-                ]
-            at += cap
+        for ref, which in ((keep, core), (send, 1 - core)):
+            ref[x * cap : (x + 1) * cap, :] = acc[
+                :, pl.ds(pl.multiple_of((2 * x + which) * 128, 128), 128)
+            ]
 
 
 def pair_in_kernel(kept, got, *pays):
@@ -158,72 +158,84 @@
     out[outer:, :] = label[...]
 
 
-def stack_kernel(experts, *refs):
-    pieces, outs = refs[: -1 - experts], refs[-experts:]
-    half = pieces[0].shape[0] // experts
+def stack_kernel(*refs):
+    *pieces, out = refs
+    slab = pieces[0].shape[0]
     for k, piece in enumerate(pieces):
-        for e, out in enumerate(outs):
-            out[k * half : (k + 1) * half, :] = piece[e * half : (e + 1) * half, :]
-
-
-def half_blocks(e, experts, which, near, far, outs):
+        out[k * slab : (k + 1) * slab, :] = piece[...]
+
+
+def sum_kernel(near, far, out):
+    out[...] = (near[...].astype(F32) + far[...].astype(F32)).astype(BF16)
+
+
+def squared_blocks(e, experts, mine, other, outs):
     dp = len(outs)
-    half = near.shape[0] // dp
-    rows_out, labels = [], []
-    for ref in outs:
-        rows_out.append(ref[pl.ds(pl.multiple_of((2 * e + which) * half, 16), half), :])
-        label = ref[2 * experts * half :, :].astype(F32)[2 * e : 2 * e + 2, :half]
-        labels.append(jnp.where(which == 0, label[0:1], label[1:2]))
-    rows_in = (near[...].astype(F32) + far[...].astype(F32)).astype(BF16)
+    half = mine.shape[0] // (dp * experts)
+    core = lax.rem(lax.axis_index("tensor"), 2)
+    rows_in, rows_out, labels = [], [], []
+    for which, ref_in in ((core, mine), (1 - core, other)):
+        for k, ref in enumerate(outs):
+            at = (k * experts + e) * half
+            rows_in.append(ref_in[at : at + half, :])
+            rows_out.append(ref[pl.ds(pl.multiple_of(which * half, 16), half), :])
+            label = ref[2 * half :, :].astype(F32)[2 * e : 2 * e + 2, :half]
+            labels.append(jnp.where(which == 0, label[0:1], label[1:2]))
+    rows_in = jnp.concatenate(rows_in, axis=0)
     rows_out = jnp.concatenate(rows_out, axis=0).T
     labels = jnp.concatenate(labels, axis=1)
     masked = [
         jnp.where(labels == float(n + 1), rows_out, jnp.zeros_like(rows_out)) for n in range(dp)
     ]
-    return dot(jnp.concatenate(masked, axis=0), rows_in)
-
-
-def first_blocks_kernel(experts, dp, counts, *refs):
-    near, far, outs = refs[:experts], refs[experts : 2 * experts], refs[2 * experts : -2]
-    total, divisor = refs[-2:]
-    core = lax.rem(lax.axis_index("tensor"), 2)
-    for e in range(experts):
-        divisor[e] = jnp.full(divisor.shape[1:], counts[e].astype(F32), F32)
-        total[e] = half_blocks(e, experts, core, near[e], far[e], outs)
-
-
-def blocks_kernel(experts, dp, first, divisor, *refs):
-    near, far, outs = refs[:experts], refs[experts : 2 * experts], refs[2 * experts : -3]
+    blocks = dot(jnp.concatenate(masked, axis=0), rows_in)
+    squares = blocks * blocks
+    side = squares.shape[0] // dp
+    summed = squares[:side]
+    for n in range(1, dp):
+        summed = summed + squares[n * side : (n + 1) * side]
+    return summed
+
+
+def blocks_kernel(e, counts, *refs):
+    *given, result, divisor = refs
+    experts = counts.shape[0]
+    result[...] = squared_blocks(e, experts, *given[:2], given[2:]) / counts[e].astype(F32)
+    divisor[...] = jnp.full(divisor.shape, counts[experts - 1].astype(F32), F32)
+
+
+def last_blocks_kernel(experts, divisor, *refs):
+    earlier, given = refs[: experts - 1], refs[experts - 1 : -3]
     result, final, sems = refs[-3:]
-    core = lax.rem(lax.axis_index("tensor"), 2)
-    copies = []
-    for e in range(experts):
-        total = first[e] + half_blocks(e, experts, 1 - core, near[e], far[e], outs)
-        side = total.shape[0] // dp
-        squares = total * total
-        summed = squares[:side]
-        for n in range(1, dp):
-            summed = summed + squares[n * side : (n + 1) * side]
-        final[e] = summed / divisor[e][:1]
-        copies.append(pltpu.make_async_copy(final.at[e], result.at[e], sems.at[e]))
-        copies[e].start()
+    copies = [pltpu.make_async_copy(x, result.at[e], sems.at[e]) for e, x in enumerate(earlier)]
+    for copy in copies:
+        copy.start()
+    final[...] = squared_blocks(experts - 1, experts, *given[:2], given[2:]) / divisor[:1]
+    copies.append(pltpu.make_async_copy(final, result.at[experts - 1], sems.at[experts - 1]))
+    copies[-1].start()
     for copy in copies:
         copy.wait()
 
 
-def call(kernel, name, out_shape, specs=None, scratch=(), out_specs=None, flops=1):
+def call(kernel, name, out_shape, specs=None, scratch=(), out_specs=None, flops=1, after=()):
     vmem = pl.BlockSpec(memory_space=pltpu.VMEM)
     given = {} if out_specs is None else {"out_specs": out_specs}
-    return lambda *args: pl.pallas_call(
-        kernel,
-        out_shape=out_shape,
-        in_specs=specs or [vmem] * len(args),
-        scratch_shapes=scratch,
-        compiler_params=pltpu.CompilerParams(vmem_limit_bytes=VMEM),
-        cost_estimate=pl.CostEstimate(flops=flops, bytes_accessed=1, transcendentals=0),
-        name=name,
-        **given,
-    )(*args)
+
+    def run(*args):
+        def body(*refs):
+            kernel(*refs[: len(args)], *refs[len(args) + len(after) :])
+
+        return pl.pallas_call(
+            body,
+            out_shape=out_shape,
+            in_specs=(specs or [vmem] * len(args)) + [vmem] * len(after),
+            scratch_shapes=scratch,
+            compiler_params=pltpu.CompilerParams(vmem_limit_bytes=VMEM),
+            cost_estimate=pl.CostEstimate(flops=flops, bytes_accessed=1, transcendentals=0),
+            name=name,
+            **given,
+        )(*args, *after)
+
+    return run
 
 
 def fast(acts, grads, routes, example_ids, expert_counts, basis_in, basis_out):
@@ -271,41 +283,63 @@
     pieces = call(pair_in_kernel, "pair_in", [rows(half // dp, BF16)] * dp)(keep, got)
     arrived = spread(pieces)
 
-    acc = call(rotate_out_kernel, "rotate_out", partial)(grads, pick, basis_out, pieces[0])
-    keep, send = call(split_out_kernel, "split_out", (rows(half, F32), rows(half, F32)))(
-        acc, *arrived[1:]
-    )
-    got = lax.ppermute(send, "tensor", core)
-    keep, send = call(pair_out_kernel, "pair_out", (rows(half // 2, F32), rows(half // 2, BF16)))(
-        keep, got
-    )
-    got = lax.ppermute(send, "tensor", across)
-    out = call(round_kernel, "round_out", rows(half // 2 + LABEL_ROWS, BF16))(keep, got, label)
-
-    near = call(
-        functools.partial(stack_kernel, experts), "stack_in", [rows(half // experts, BF16)] * experts
-    )(*arrived, out)
-    far = [lax.ppermute(x, "tensor", across) for x in near]
-    outs = spread([out] * dp)
-    first, divisor = call(
-        functools.partial(first_blocks_kernel, experts, dp),
-        "first_blocks",
+    quarter = half // (2 * experts)
+    split_shape = (rows(2 * quarter, F32), rows(2 * quarter, F32))
+    pair_shape = (rows(quarter, F32), rows(quarter, BF16))
+    out_shape = rows(quarter + LABEL_ROWS, BF16)
+    rotated, rest = call(
+        rotate_first_kernel,
+        "rotate_first",
         (
-            jax.ShapeDtypeStruct((experts, dp * 128, 128), F32),
-            jax.ShapeDtypeStruct((experts, 8, 128), F32),
+            jax.ShapeDtypeStruct((cap, width), F32),
+            jax.ShapeDtypeStruct((wide - cap, grads.shape[2]), BF16),
         ),
-        [smem] + [vmem] * (2 * experts + dp),
-    )(expert_counts, *near, *far, *outs)
-    near = [lax.ppermute(x, "tensor", core) for x in near]
-    far = [lax.ppermute(x, "tensor", core) for x in far]
+        after=pieces[:1],
+    )(grads, pick, basis_out)
+    near = call(stack_kernel, "stack_in", rows(half, BF16))(*arrived)
+    far = lax.ppermute(near, "tensor", across)
+    keeps, gots, sends = [], [], []
+    for e in range(experts):
+        if e > 0:
+            rotated = call(
+                functools.partial(rotate_rest_kernel, e),
+                "rotate_rest",
+                jax.ShapeDtypeStruct((cap, width), F32),
+                flops=10**9,
+            )(rest, basis_out)
+        keep, send = call(
+            split_out_kernel, "split_out", split_shape, after=sends[-1:] or [near]
+        )(rotated)
+        got = lax.ppermute(send, "tensor", core)
+        keep, send = call(pair_out_kernel, "pair_out", pair_shape)(keep, got)
+        keeps.append(keep)
+        sends.append(send)
+        gots.append(lax.ppermute(send, "tensor", across))
+    mine = call(sum_kernel, "sum_in", rows(half, BF16), after=gots[:1])(near, far)
+    other = lax.ppermute(mine, "tensor", core)
+    outs = []
+    for e in range(experts):
+        early = [mine, sends[-1]] if e == 0 else [outs[-1][1]]
+        out = call(round_kernel, "round_out", out_shape, after=early)(keeps[e], gots[e], label)
+        outs.append(spread([out] * dp))
+
     result = jax.ShapeDtypeStruct((experts, 128, 128), F32)
+    done = []
+    for e in range(experts - 1):
+        block, divisor = call(
+            functools.partial(blocks_kernel, e),
+            "blocks",
+            (rows(128, F32), rows(8, F32)),
+            [smem] + [vmem] * (2 + dp),
+        )(expert_counts, mine, other, *outs[e])
+        done.append(block)
     return call(
-        functools.partial(blocks_kernel, experts, dp),
-        "blocks",
+        functools.partial(last_blocks_kernel, experts),
+        "last_blocks",
         result,
-        scratch=[pltpu.VMEM(result.shape, F32), pltpu.SemaphoreType.DMA((experts,))],
+        scratch=[pltpu.VMEM(result.shape[1:], F32), pltpu.SemaphoreType.DMA((experts,))],
         out_specs=hbm,
-    )(first, divisor, *near, *far, *outs)
+    )(divisor, *done, mine, other, *outs[-1])
 
 
 EX_DEV = 1

time: 37.7 us -> 41.3 us (1.095)
  starting transfers between devices: 14.8 us -> 19 us
  waiting for transfers between devices: 12 us -> 11.3 us
    ppermute x6 -> x9, starting transfers between devices: 10.1 us -> 14.4 us  [spread(): lax.ppermute(pays[k], 'dp', [(d, d ^ k) for d in range(dp)])]
    ppermute x6 -> x9, waiting for transfers between devices: 2.85 us -> 5.04 us  [spread(): lax.ppermute(pays[k], 'dp', [(d, d ^ k) for d in range(dp)])]
    ppermute x2 -> x3, waiting for transfers between devices: 3.06 us -> 1.35 us  [fast(): got = lax.ppermute(send, 'tensor', core)]
    ppermute x7 -> x4, waiting for transfers between devices: 6.08 us -> 4.95 us  [the longest x1 4.34 us: fast(): far = lax.ppermute(near, 'tensor', across)]
    ppermute x7 -> x4, starting transfers between devices: 4.16 us -> 3.72 us  [the longest x2 2.09 us: fast(): gots.append(lax.ppermute(send, 'tensor', across))]
    ppermute x2 -> x3, starting transfers between devices: 0.59 us -> 0.83 us  [fast(): got = lax.ppermute(send, 'tensor', core)]
    pallas_call x10 -> x15, Pallas kernels: 10.6 us -> 10.5 us  [run(): pl.pallas_call(body, out_shape=out_shape, in_specs=(specs or [vmem] * len...]
  transfers between devices with their start and end apart: 15 -> 16, of which waited for: 8 -> 6; matrix products, arithmetic and copies ran while one was open for 0% -> 0% of each run, Pallas kernels for 16% -> 15%
where the time goes in v4:
time: 41.3 us; the launch traced here: 41.1 us
  starting transfers between devices  19 us (46%)
  waiting for transfers between devices  11.3 us (27%)
  Pallas kernels  10.5 us (25%)
    ppermute x9, starting transfers between devices, spread(): lax.ppermute(pays[k], 'dp', [(d, d ^ k) for d in range(dp)])  14.4 us
    pallas_call x15, Pallas kernels, run(): pl.pallas_call(body, out_shape=out_shape, in_specs=(specs or [vmem] * len...  10.5 us
    ppermute x9, waiting for transfers between devices, spread(): lax.ppermute(pays[k], 'dp', [(d, d ^ k) for d in range(dp)])  5.04 us
    ppermute x1, waiting for transfers between devices, fast(): far = lax.ppermute(near, 'tensor', across)  4.34 us
    ppermute x2, starting transfers between devices, fast(): gots.append(lax.ppermute(send, 'tensor', across))  2.09 us
    ppermute x1, starting transfers between devices, fast(): far = lax.ppermute(near, 'tensor', across)  1.55 us
    ppermute x3, waiting for transfers between devices, fast(): got = lax.ppermute(send, 'tensor', core)  1.35 us
    ppermute x3, starting transfers between devices, fast(): got = lax.ppermute(send, 'tensor', core)  0.83 us
  transfers between devices with their start and end apart: 16, of which 6 were waited for; matrix products, arithmetic and copies ran while one was open for 0% of the time, Pallas kernels for 15%

profile of v4, /device:TPU:0, one launch (start us, length us, event | category | flops | bytes accessed | tf_op | source)
XLA Modules:
  0.0 41.1 jit_solution(16370943617421681905)
XLA Ops:
  0.0 3.1 %rotate_in.1 = (f32[2,192,512]{2,1,0:T(8,128)S(1)}, bf16[16,128]{1,0:T(8,128)(2,1)S(1)}, bf16[384,768]{1,0:T(8,128)(2,1)S(1)}) custom-call(bf16[384,1536]{1,0:T(8,128)(2,1)} %refs_0_.3, s32[2,384]{1,0:T(2,128)} %bitcast.5, s32[384]{0:T(512)} %refs_2_.2, bf16[2,1536,512]{2,1,0:T(8,128)(2,1)} %refs_3_.1), custom_call_target="tpu_custom_call" | custom-call | flops 1 | bytes 1 | tf_op jit(solution)/shard_map/rotate_in/pallas_call | solution.py:227
  3.1 0.0 slice-start
  3.1 0.0 slice-start.2
  3.1 0.0 slice-start.1
  3.1 0.0 slice-start.3
  3.1 0.1 split_in.1
  3.2 0.5 %collective-permute-start = (f32[768,128]{1,0:T(8,128)S(1)}, f32[768,128]{1,0:T(8,128)S(1)}, u32[]{:S(2)}, u32[]{:S(2)}) collective-permute-start(f32[768,128]{1,0:T(8,128)S(1)} %get-tuple-element.28), channel_id=1, source_target_pairs={{0,1},{1,0},{2,3},{3,2},{4,5},{5,4},{6,7},{7,6},{8,9},{9,8},{10,11... | collective-permute-start | bytes 1179656 | tf_op jit(solution)/shard_map/ppermute | solution.py:282
  3.7 1.3 %collective-permute-done.refs_1_ = f32[768,128]{1,0:T(8,128)S(1)} collective-permute-done((f32[768,128]{1,0:T(8,128)S(1)}, f32[768,128]{1,0:T(8,128)S(1)}, u32[]{:S(2)}, u32[]{:S(2)}) %collective-permute-start) | collective-permute-done | bytes 393248 | tf_op jit(solution)/shard_map/ppermute | solution.py:282
  5.1 3.0 %collective-permute-start.1 = (bf16[192,128]{1,0:T(8,128)(2,1)S(1)}, bf16[192,128]{1,0:T(8,128)(2,1)S(1)}, u32[]{:S(2)}, u32[]{:S(2)}) collective-permute-start(bf16[192,128]{1,0:T(8,128)(2,1)S(1)} %get-tuple-element.30), channel_id=1, source_target_pairs={{0,4},{4,0},{8,12},{12,8},{1,5},{5,1},{9,13},{13,9},{2,6},{6,2},{1... | collective-permute-start | bytes 147464 | tf_op jit(solution)/shard_map/ppermute | solution.py:262
  8.1 2.6 %collective-permute-start.2 = (bf16[192,128]{1,0:T(8,128)(2,1)S(1)}, bf16[192,128]{1,0:T(8,128)(2,1)S(1)}, u32[]{:S(2)}, u32[]{:S(2)}) collective-permute-start(bf16[192,128]{1,0:T(8,128)(2,1)S(1)} %get-tuple-element.31), channel_id=1, source_target_pairs={{0,8},{4,12},{8,0},{12,4},{1,9},{5,13},{9,1},{13,5},{2,10},{6,14},... | collective-permute-start | bytes 147464 | tf_op jit(solution)/shard_map/ppermute | solution.py:262
  10.7 0.0 collective-permute-start.3
  10.7 0.0 slice-done
  10.7 0.0 slice-done.2
  10.7 0.0 slice-done.1
  10.8 0.0 slice-done.3
  10.8 4.0 %rotate_first.1 = (f32[192,512]{1,0:T(8,128)S(1)}, bf16[192,4096]{1,0:T(8,128)(2,1)S(1)}) custom-call(bf16[384,2,4096]{2,1,0:T(2,128)(2,1)S(1)} %bitcast.4, bf16[384,768]{1,0:T(8,128)(2,1)S(1)} %get-tuple-element.33.refs_1_, bf16[2,4096,512]{2,1,0:T(8,128)(2,1)S(1)} %bitcast.2, bf16[192,128]{1,0:T(8,128)(2,1)S(1)} %get-tuple-element.29.refs_0_.refs_3_), custom_call_target="tpu_custom_call" | custom-call | flops 1 | bytes 1 | tf_op jit(solution)/shard_map/rotate_first/pallas_call | solution.py:227
  14.8 0.0 collective-permute-done.1.refs_1_
  14.8 0.0 collective-permute-done.2.refs_2_
  14.8 1.8 %collective-permute-done.3.refs_3_ = bf16[192,128]{1,0:T(8,128)(2,1)S(1)} collective-permute-done((bf16[192,128]{1,0:T(8,128)(2,1)S(1)}, bf16[192,128]{1,0:T(8,128)(2,1)S(1)}, u32[]{:S(2)}, u32[]{:S(2)}) %collective-permute-start.3) | collective-permute-done | bytes 49184 | tf_op jit(solution)/shard_map/ppermute | solution.py:262
  16.6 0.1 split_out.2
  16.7 0.1 collective-permute-start.5
  16.8 1.6 %collective-permute-start.4 = (bf16[768,128]{1,0:T(8,128)(2,1)S(1)}, bf16[768,128]{1,0:T(8,128)(2,1)S(1)}, u32[]{:S(2)}, u32[]{:S(2)}) collective-permute-start(bf16[768,128]{1,0:T(8,128)(2,1)S(1)} %stack_in.1.refs_1_.refs_0_), channel_id=1, source_target_pairs={{0,2},{1,3},{2,0},{3,1},{4,6},{5,7},{6,4},{7,5},{8,10},{9,11},{10,... | collective-permute-start | bytes 589832 | tf_op jit(solution)/shard_map/ppermute | solution.py:300
  18.3 1.0 %rotate_rest.1.refs_0_ = f32[192,512]{1,0:T(8,128)S(1)} custom-call(bf16[192,4096]{1,0:T(8,128)(2,1)S(1)} %get-tuple-element.40.refs_0_, bf16[2,4096,512]{2,1,0:T(8,128)(2,1)S(1)} %bitcast.2), custom_call_target="tpu_custom_call" | custom-call | flops 1000000000 | bytes 1 | tf_op jit(solution)/shard_map/rotate_rest/pallas_call | solution.py:227
  19.3 0.0 collective-permute-done.5.refs_1_
  19.4 0.1 split_out.3
  19.4 0.2 collective-permute-start.8
  19.7 0.5 %collective-permute-start.6 = (bf16[192,128]{1,0:T(8,128)(2,1)S(1)}, bf16[192,128]{1,0:T(8,128)(2,1)S(1)}, u32[]{:S(2)}, u32[]{:S(2)}) collective-permute-start(bf16[192,128]{1,0:T(8,128)(2,1)S(1)} %get-tuple-element.37.refs_1_), channel_id=1, source_target_pairs={{0,2},{1,3},{2,0},{3,1},{4,6},{5,7},{6,4},{7,5},{8,10},{9,11},{10,... | collective-permute-start | bytes 147464 | tf_op jit(solution)/shard_map/ppermute | solution.py:317
  20.2 4.3 %collective-permute-done.4.refs_1_ = bf16[768,128]{1,0:T(8,128)(2,1)S(1)} collective-permute-done((bf16[768,128]{1,0:T(8,128)(2,1)S(1)}, bf16[768,128]{1,0:T(8,128)(2,1)S(1)}, u32[]{:S(2)}, u32[]{:S(2)}) %collective-permute-start.4) | collective-permute-done | bytes 196640 | tf_op jit(solution)/shard_map/ppermute | solution.py:300
  24.6 0.6 %collective-permute-done.6.refs_2_.refs_1_ = bf16[192,128]{1,0:T(8,128)(2,1)S(1)} collective-permute-done((bf16[192,128]{1,0:T(8,128)(2,1)S(1)}, bf16[192,128]{1,0:T(8,128)(2,1)S(1)}, u32[]{:S(2)}, u32[]{:S(2)}) %collective-permute-start.6) | collective-permute-done | bytes 49184 | tf_op jit(solution)/shard_map/ppermute | solution.py:317
  25.2 0.1 collective-permute-start.7
  25.3 0.0 collective-permute-done.8.refs_1_
  25.4 0.1 collective-permute-start.9
  25.4 1.6 %collective-permute-start.12 = (bf16[192,128]{1,0:T(8,128)(2,1)S(1)}, bf16[192,128]{1,0:T(8,128)(2,1)S(1)}, u32[]{:S(2)}, u32[]{:S(2)}) collective-permute-start(bf16[192,128]{1,0:T(8,128)(2,1)S(1)} %get-tuple-element.43.refs_4_), channel_id=1, source_target_pairs={{0,2},{1,3},{2,0},{3,1},{4,6},{5,7},{6,4},{7,5},{8,10},{9,11},{10,... | collective-permute-start | bytes 147464 | tf_op jit(solution)/shard_map/ppermute | solution.py:317
  27.0 2.5 %collective-permute-start.10 = (bf16[208,128]{1,0:T(8,128)(2,1)S(1)}, bf16[208,128]{1,0:T(8,128)(2,1)S(1)}, u32[]{:S(2)}, u32[]{:S(2)}) collective-permute-start(bf16[208,128]{1,0:T(8,128)(2,1)S(1)} %round_out.2.refs_3_), channel_id=1, source_target_pairs={{0,8},{4,12},{8,0},{12,4},{1,9},{5,13},{9,1},{13,5},{2,10},{6,14},... | collective-permute-start | bytes 159752 | tf_op jit(solution)/shard_map/ppermute | solution.py:262
  29.5 1.8 %collective-permute-start.11 = (bf16[208,128]{1,0:T(8,128)(2,1)S(1)}, bf16[208,128]{1,0:T(8,128)(2,1)S(1)}, u32[]{:S(2)}, u32[]{:S(2)}) collective-permute-start(bf16[208,128]{1,0:T(8,128)(2,1)S(1)} %round_out.2.refs_3_), channel_id=1, source_target_pairs={{0,12},{4,8},{8,4},{12,0},{1,13},{5,9},{9,5},{13,1},{2,14},{6,10},... | collective-permute-start | bytes 159752 | tf_op jit(solution)/shard_map/ppermute | solution.py:262
  31.3 0.0 collective-permute-done.12.refs_1_
  31.3 0.0 collective-permute-done.9.refs_4_.refs_3_
  31.3 0.3 collective-permute-start.13
  31.6 2.3 %collective-permute-start.14 = (bf16[208,128]{1,0:T(8,128)(2,1)S(1)}, bf16[208,128]{1,0:T(8,128)(2,1)S(1)}, u32[]{:S(2)}, u32[]{:S(2)}) collective-permute-start(bf16[208,128]{1,0:T(8,128)(2,1)S(1)} %round_out.3.refs_4_), channel_id=1, source_target_pairs={{0,8},{4,12},{8,0},{12,4},{1,9},{5,13},{9,1},{13,5},{2,10},{6,14},... | collective-permute-start | bytes 159752 | tf_op jit(solution)/shard_map/ppermute | solution.py:262
  34.0 0.0 collective-permute-done.7.refs_2_.refs_3_
  34.0 1.8 %collective-permute-start.15 = (bf16[208,128]{1,0:T(8,128)(2,1)S(1)}, bf16[208,128]{1,0:T(8,128)(2,1)S(1)}, u32[]{:S(2)}, u32[]{:S(2)}) collective-permute-start(bf16[208,128]{1,0:T(8,128)(2,1)S(1)} %round_out.3.refs_4_), channel_id=1, source_target_pairs={{0,12},{4,8},{8,4},{12,0},{1,13},{5,9},{9,5},{13,1},{2,14},{6,10},... | collective-permute-start | bytes 159752 | tf_op jit(solution)/shard_map/ppermute | solution.py:262
  35.8 0.0 collective-permute-done.10.refs_5_
  35.8 0.0 collective-permute-done.11.refs_6_
  35.8 1.0 %blocks.1 = (f32[128,128]{1,0:T(8,128)S(1)}, f32[8,128]{1,0:T(8,128)S(1)}) custom-call(s32[2]{0:T(128)S(1)} %copy-done, bf16[768,128]{1,0:T(8,128)(2,1)S(1)} %sum_in.1.refs_3_.refs_1_.refs_2_, bf16[768,128]{1,0:T(8,128)(2,1)S(1)} %collective-permute-done.7.refs_2_.refs_3_, bf16[208,128]{1,0:T(8,128)(2,1)S(1)} %round_out.2.refs_3_, ...), custom_call_target="tpu_custom_call" | custom-call | flops 1 | bytes 1 | tf_op jit(solution)/shard_map/blocks/pallas_call | solution.py:227
  36.8 0.0 collective-permute-done.13.refs_5_
  36.8 2.0 %collective-permute-done.14.refs_6_ = bf16[208,128]{1,0:T(8,128)(2,1)S(1)} collective-permute-done((bf16[208,128]{1,0:T(8,128)(2,1)S(1)}, bf16[208,128]{1,0:T(8,128)(2,1)S(1)}, u32[]{:S(2)}, u32[]{:S(2)}) %collective-permute-start.14) | collective-permute-done | bytes 53280 | tf_op jit(solution)/shard_map/ppermute | solution.py:262
  38.8 1.2 %collective-permute-done.15.refs_7_ = bf16[208,128]{1,0:T(8,128)(2,1)S(1)} collective-permute-done((bf16[208,128]{1,0:T(8,128)(2,1)S(1)}, bf16[208,128]{1,0:T(8,128)(2,1)S(1)}, u32[]{:S(2)}, u32[]{:S(2)}) %collective-permute-start.15) | collective-permute-done | bytes 53280 | tf_op jit(solution)/shard_map/ppermute | solution.py:262
  40.0 1.1 %last_blocks.1 = f32[2,128,128]{2,1,0:T(8,128)} custom-call(f32[8,128]{1,0:T(8,128)S(1)} %get-tuple-element.44.refs_0_, f32[128,128]{1,0:T(8,128)S(1)} %get-tuple-element.45.refs_1_, bf16[768,128]{1,0:T(8,128)(2,1)S(1)} %sum_in.1.refs_3_.refs_1_.refs_2_, bf16[768,128]{1,0:T(8,128)(2,1)S(1)} %collective-permute-done.7.refs_2_.refs_3_, ...), custom_call_target="tpu_custom_call" | custom-call | flops 1 | bytes 1 | tf_op jit(solution)/shard_map/last_blocks/pallas_call | solution.py:227
  (11 shorter events, 0.2 us)
Async XLA Ops:
  3.1 7.6 %slice-start = ((s8[8388608]{0:T(1024)(128)(4,1)}), s8[4194304]{0:T(1024)(128)(4,1)S(1)}, s32[]{:S(2)}) async-start(s8[8388608]{0:T(1024)(128)(4,1)} %bitcast.1), calls=%async_computation | async-start | bytes 8388608
  3.1 7.6 %slice-start.2 = ((s8[6291456]{0:T(1024)(128)(4,1)}), s8[4194304]{0:T(1024)(128)(4,1)S(1)}, s32[]{:S(2)}) async-start(s8[6291456]{0:T(1024)(128)(4,1)} %bitcast.3), calls=%async_computation.2 | async-start | bytes 8388608
  3.1 7.6 %slice-start.1 = ((s8[8388608]{0:T(1024)(128)(4,1)}), s8[4194304]{0:T(1024)(128)(4,1)S(1)}, s32[]{:S(2)}) async-start(s8[8388608]{0:T(1024)(128)(4,1)} %bitcast.1), calls=%async_computation.1 | async-start | bytes 8388608
  3.1 7.6 %slice-start.3 = ((s8[6291456]{0:T(1024)(128)(4,1)}), s8[2097152]{0:T(1024)(128)(4,1)S(1)}, s32[]{:S(2)}) async-start(s8[6291456]{0:T(1024)(128)(4,1)} %bitcast.3), calls=%async_computation.3 | async-start | bytes 4194304
  3.2 1.9 %collective-permute-start = (f32[768,128]{1,0:T(8,128)S(1)}, f32[768,128]{1,0:T(8,128)S(1)}, u32[]{:S(2)}, u32[]{:S(2)}) collective-permute-start(f32[768,128]{1,0:T(8,128)S(1)} %get-tuple-element.28), channel_id=1, source_target_pairs={{0,1},{1,0},{2,3},{3,2},{4,5},{5,4},{6,7},{7,6},{8,9},{9,8},{10,11... | collective-permute-start | bytes 1179656 | tf_op jit(solution)/shard_map/ppermute | solution.py:282
  5.1 9.7 %collective-permute-start.1 = (bf16[192,128]{1,0:T(8,128)(2,1)S(1)}, bf16[192,128]{1,0:T(8,128)(2,1)S(1)}, u32[]{:S(2)}, u32[]{:S(2)}) collective-permute-start(bf16[192,128]{1,0:T(8,128)(2,1)S(1)} %get-tuple-element.30), channel_id=1, source_target_pairs={{0,4},{4,0},{8,12},{12,8},{1,5},{5,1},{9,13},{13,9},{2,6},{6,2},{1... | collective-permute-start | bytes 147464 | tf_op jit(solution)/shard_map/ppermute | solution.py:262
  8.1 6.7 %collective-permute-start.2 = (bf16[192,128]{1,0:T(8,128)(2,1)S(1)}, bf16[192,128]{1,0:T(8,128)(2,1)S(1)}, u32[]{:S(2)}, u32[]{:S(2)}) collective-permute-start(bf16[192,128]{1,0:T(8,128)(2,1)S(1)} %get-tuple-element.31), channel_id=1, source_target_pairs={{0,8},{4,12},{8,0},{12,4},{1,9},{5,13},{9,1},{13,5},{2,10},{6,14},... | collective-permute-start | bytes 147464 | tf_op jit(solution)/shard_map/ppermute | solution.py:262
  10.7 5.9 %collective-permute-start.3 = (bf16[192,128]{1,0:T(8,128)(2,1)S(1)}, bf16[192,128]{1,0:T(8,128)(2,1)S(1)}, u32[]{:S(2)}, u32[]{:S(2)}) collective-permute-start(bf16[192,128]{1,0:T(8,128)(2,1)S(1)} %get-tuple-element.32), channel_id=1, source_target_pairs={{0,12},{4,8},{8,4},{12,0},{1,13},{5,9},{9,5},{13,1},{2,14},{6,10},... | collective-permute-start | bytes 147464 | tf_op jit(solution)/shard_map/ppermute | solution.py:262
  16.7 2.6 %collective-permute-start.5 = (f32[384,128]{1,0:T(8,128)S(1)}, f32[384,128]{1,0:T(8,128)S(1)}, u32[]{:S(2)}, u32[]{:S(2)}) collective-permute-start(f32[384,128]{1,0:T(8,128)S(1)} %get-tuple-element.36), channel_id=1, source_target_pairs={{0,1},{1,0},{2,3},{3,2},{4,5},{5,4},{6,7},{7,6},{8,9},{9,8},{10,11... | collective-permute-start | bytes 589832 | tf_op jit(solution)/shard_map/ppermute | solution.py:313
  16.8 7.8 %collective-permute-start.4 = (bf16[768,128]{1,0:T(8,128)(2,1)S(1)}, bf16[768,128]{1,0:T(8,128)(2,1)S(1)}, u32[]{:S(2)}, u32[]{:S(2)}) collective-permute-start(bf16[768,128]{1,0:T(8,128)(2,1)S(1)} %stack_in.1.refs_1_.refs_0_), channel_id=1, source_target_pairs={{0,2},{1,3},{2,0},{3,1},{4,6},{5,7},{6,4},{7,5},{8,10},{9,11},{10,... | collective-permute-start | bytes 589832 | tf_op jit(solution)/shard_map/ppermute | solution.py:300
  18.3 17.5 %copy-start = (s32[2]{0:T(128)S(1)}, s32[2]{0:T(128)}, u32[]{:S(2)}) copy-start(s32[2]{0:T(128)} %refs_0_.5) | copy-start | bytes 28
  19.4 5.8 %collective-permute-start.8 = (f32[384,128]{1,0:T(8,128)S(1)}, f32[384,128]{1,0:T(8,128)S(1)}, u32[]{:S(2)}, u32[]{:S(2)}) collective-permute-start(f32[384,128]{1,0:T(8,128)S(1)} %get-tuple-element.42), channel_id=1, source_target_pairs={{0,1},{1,0},{2,3},{3,2},{4,5},{5,4},{6,7},{7,6},{8,9},{9,8},{10,11... | collective-permute-start | bytes 589832 | tf_op jit(solution)/shard_map/ppermute | solution.py:313
  19.7 5.5 %collective-permute-start.6 = (bf16[192,128]{1,0:T(8,128)(2,1)S(1)}, bf16[192,128]{1,0:T(8,128)(2,1)S(1)}, u32[]{:S(2)}, u32[]{:S(2)}) collective-permute-start(bf16[192,128]{1,0:T(8,128)(2,1)S(1)} %get-tuple-element.37.refs_1_), channel_id=1, source_target_pairs={{0,2},{1,3},{2,0},{3,1},{4,6},{5,7},{6,4},{7,5},{8,10},{9,11},{10,... | collective-permute-start | bytes 147464 | tf_op jit(solution)/shard_map/ppermute | solution.py:317
  25.2 8.8 %collective-permute-start.7 = (bf16[768,128]{1,0:T(8,128)(2,1)S(1)}, bf16[768,128]{1,0:T(8,128)(2,1)S(1)}, u32[]{:S(2)}, u32[]{:S(2)}) collective-permute-start(bf16[768,128]{1,0:T(8,128)(2,1)S(1)} %sum_in.1.refs_3_.refs_1_.refs_2_), channel_id=1, source_target_pairs={{0,1},{1,0},{2,3},{3,2},{4,5},{5,4},{6,7},{7,6},{8,9},{9,8},{10,11... | collective-permute-start | bytes 589832 | tf_op jit(solution)/shard_map/ppermute | solution.py:319
  25.4 5.9 %collective-permute-start.9 = (bf16[208,128]{1,0:T(8,128)(2,1)S(1)}, bf16[208,128]{1,0:T(8,128)(2,1)S(1)}, u32[]{:S(2)}, u32[]{:S(2)}) collective-permute-start(bf16[208,128]{1,0:T(8,128)(2,1)S(1)} %round_out.2.refs_3_), channel_id=1, source_target_pairs={{0,4},{4,0},{8,12},{12,8},{1,5},{5,1},{9,13},{13,9},{2,6},{6,2},{1... | collective-permute-start | bytes 159752 | tf_op jit(solution)/shard_map/ppermute | solution.py:262
  25.4 5.9 %collective-permute-start.12 = (bf16[192,128]{1,0:T(8,128)(2,1)S(1)}, bf16[192,128]{1,0:T(8,128)(2,1)S(1)}, u32[]{:S(2)}, u32[]{:S(2)}) collective-permute-start(bf16[192,128]{1,0:T(8,128)(2,1)S(1)} %get-tuple-element.43.refs_4_), channel_id=1, source_target_pairs={{0,2},{1,3},{2,0},{3,1},{4,6},{5,7},{6,4},{7,5},{8,10},{9,11},{10,... | collective-permute-start | bytes 147464 | tf_op jit(solution)/shard_map/ppermute | solution.py:317
  27.0 8.8 %collective-permute-start.10 = (bf16[208,128]{1,0:T(8,128)(2,1)S(1)}, bf16[208,128]{1,0:T(8,128)(2,1)S(1)}, u32[]{:S(2)}, u32[]{:S(2)}) collective-permute-start(bf16[208,128]{1,0:T(8,128)(2,1)S(1)} %round_out.2.refs_3_), channel_id=1, source_target_pairs={{0,8},{4,12},{8,0},{12,4},{1,9},{5,13},{9,1},{13,5},{2,10},{6,14},... | collective-permute-start | bytes 159752 | tf_op jit(solution)/shard_map/ppermute | solution.py:262
  29.5 6.3 %collective-permute-start.11 = (bf16[208,128]{1,0:T(8,128)(2,1)S(1)}, bf16[208,128]{1,0:T(8,128)(2,1)S(1)}, u32[]{:S(2)}, u32[]{:S(2)}) collective-permute-start(bf16[208,128]{1,0:T(8,128)(2,1)S(1)} %round_out.2.refs_3_), channel_id=1, source_target_pairs={{0,12},{4,8},{8,4},{12,0},{1,13},{5,9},{9,5},{13,1},{2,14},{6,10},... | collective-permute-start | bytes 159752 | tf_op jit(solution)/shard_map/ppermute | solution.py:262
  31.3 5.5 %collective-permute-start.13 = (bf16[208,128]{1,0:T(8,128)(2,1)S(1)}, bf16[208,128]{1,0:T(8,128)(2,1)S(1)}, u32[]{:S(2)}, u32[]{:S(2)}) collective-permute-start(bf16[208,128]{1,0:T(8,128)(2,1)S(1)} %round_out.3.refs_4_), channel_id=1, source_target_pairs={{0,4},{4,0},{8,12},{12,8},{1,5},{5,1},{9,13},{13,9},{2,6},{6,2},{1... | collective-permute-start | bytes 159752 | tf_op jit(solution)/shard_map/ppermute | solution.py:262
  31.6 7.2 %collective-permute-start.14 = (bf16[208,128]{1,0:T(8,128)(2,1)S(1)}, bf16[208,128]{1,0:T(8,128)(2,1)S(1)}, u32[]{:S(2)}, u32[]{:S(2)}) collective-permute-start(bf16[208,128]{1,0:T(8,128)(2,1)S(1)} %round_out.3.refs_4_), channel_id=1, source_target_pairs={{0,8},{4,12},{8,0},{12,4},{1,9},{5,13},{9,1},{13,5},{2,10},{6,14},... | collective-permute-start | bytes 159752 | tf_op jit(solution)/shard_map/ppermute | solution.py:262
  34.0 6.0 %collective-permute-start.15 = (bf16[208,128]{1,0:T(8,128)(2,1)S(1)}, bf16[208,128]{1,0:T(8,128)(2,1)S(1)}, u32[]{:S(2)}, u32[]{:S(2)}) collective-permute-start(bf16[208,128]{1,0:T(8,128)(2,1)S(1)} %round_out.3.refs_4_), channel_id=1, source_target_pairs={{0,12},{4,8},{8,4},{12,0},{1,13},{5,9},{9,5},{13,1},{2,14},{6,10},... | collective-permute-start | bytes 159752 | tf_op jit(solution)/shard_map/ppermute | solution.py:262

commit v5 on v4

--- a/solution.py
+++ b/solution.py
@@ -11,7 +11,7 @@
 BF16 = jnp.bfloat16
 CHUNK = 512
 VMEM = 20 * 2**20
-FAR_FIRST = (2, 3, 1)
+ARRIVAL = (0, 2, 1, 3)
 LABEL_ROWS = 16
 
 
@@ -135,12 +135,13 @@
             ]
 
 
-def pair_in_kernel(kept, got, *pays):
+def pair_in_kernel(kept, got, label, *pays):
     slab = kept.shape[0] // len(pays)
     d = lax.axis_index("dp")
     for k, pay in enumerate(pays):
         rows = pl.ds(pl.multiple_of((d ^ k) * slab, 16), slab)
-        pay[...] = (kept[rows, :] + got[rows, :]).astype(BF16)
+        pay[:slab, :] = (kept[rows, :] + got[rows, :]).astype(BF16)
+        pay[slab:, :] = label[...]
 
 
 def pair_out_kernel(kept, got, keep, send):
@@ -152,64 +153,78 @@
     send[...] = (kept[other, :] + got[other, :]).astype(BF16)
 
 
-def round_kernel(kept, got, label, out):
-    outer = kept.shape[0]
-    out[:outer, :] = (kept[...] + got[...].astype(F32)).astype(BF16)
-    out[outer:, :] = label[...]
+def round_kernel(kept, got, out):
+    out[...] = (kept[...] + got[...].astype(F32)).astype(BF16)
+
+
+def pile_kernel(near, far, out):
+    out[: near.shape[0], :] = near[...]
+    out[near.shape[0] :, :] = far[...]
 
 
 def stack_kernel(*refs):
     *pieces, out = refs
-    slab = pieces[0].shape[0]
+    slab = pieces[0].shape[0] - LABEL_ROWS
     for k, piece in enumerate(pieces):
-        out[k * slab : (k + 1) * slab, :] = piece[...]
+        out[k * slab : (k + 1) * slab, :] = piece[:slab, :]
 
 
 def sum_kernel(near, far, out):
     out[...] = (near[...].astype(F32) + far[...].astype(F32)).astype(BF16)
 
 
-def squared_blocks(e, experts, mine, other, outs):
-    dp = len(outs)
-    half = mine.shape[0] // (dp * experts)
+def mask_kernel(experts, mine, other, *refs):
+    pieces, out = refs[:-1], refs[-1]
+    dp = len(pieces)
+    slab = pieces[0].shape[0] - LABEL_ROWS
+    half = slab // experts
     core = lax.rem(lax.axis_index("tensor"), 2)
-    rows_in, rows_out, labels = [], [], []
-    for which, ref_in in ((core, mine), (1 - core, other)):
-        for k, ref in enumerate(outs):
-            at = (k * experts + e) * half
-            rows_in.append(ref_in[at : at + half, :])
-            rows_out.append(ref[pl.ds(pl.multiple_of(which * half, 16), half), :])
-            label = ref[2 * half :, :].astype(F32)[2 * e : 2 * e + 2, :half]
-            labels.append(jnp.where(which == 0, label[0:1], label[1:2]))
-    rows_in = jnp.concatenate(rows_in, axis=0)
-    rows_out = jnp.concatenate(rows_out, axis=0).T
-    labels = jnp.concatenate(labels, axis=1)
-    masked = [
-        jnp.where(labels == float(n + 1), rows_out, jnp.zeros_like(rows_out)) for n in range(dp)
+    for e in range(experts):
+        rows, labels = [], []
+        for which, ref in ((core, mine), (1 - core, other)):
+            for k, piece in enumerate(pieces):
+                at = (k * experts + e) * half
+                rows.append(ref[at : at + half, :])
+                label = piece[slab:, :].astype(F32)[2 * e : 2 * e + 2, :half]
+                labels.append(jnp.where(which == 0, label[0:1], label[1:2]))
+        rows = jnp.concatenate(rows, axis=0).astype(F32)
+        labels = jnp.concatenate(labels, axis=1)
+        labels = jnp.broadcast_to(labels, (128, labels.shape[1])).T
+        for n in range(dp):
+            out[e, :, n * 128 : (n + 1) * 128] = jnp.where(
+                labels == float(n + 1), rows, 0.0
+            ).astype(BF16)
+
+
+def squared_blocks(e, masked, *outs):
+    cap = masked.shape[1] * 128 // masked.shape[2]
+    half = cap // 2
+    core = lax.rem(lax.axis_index("tensor"), 2)
+    rows = [
+        ref[pl.ds(pl.multiple_of(at + which * half, 16), half), :]
+        for which in (core, 1 - core)
+        for ref in outs
+        for at in range(0, ref.shape[0], cap)
     ]
-    blocks = dot(jnp.concatenate(masked, axis=0), rows_in)
+    blocks = dot(jnp.concatenate(rows, axis=0).T, masked[e])
     squares = blocks * blocks
-    side = squares.shape[0] // dp
-    summed = squares[:side]
-    for n in range(1, dp):
-        summed = summed + squares[n * side : (n + 1) * side]
+    summed = squares[:, :128]
+    for at in range(128, squares.shape[1], 128):
+        summed = summed + squares[:, at : at + 128]
     return summed
 
 
-def blocks_kernel(e, counts, *refs):
-    *given, result, divisor = refs
-    experts = counts.shape[0]
-    result[...] = squared_blocks(e, experts, *given[:2], given[2:]) / counts[e].astype(F32)
-    divisor[...] = jnp.full(divisor.shape, counts[experts - 1].astype(F32), F32)
-
-
-def last_blocks_kernel(experts, divisor, *refs):
-    earlier, given = refs[: experts - 1], refs[experts - 1 : -3]
-    result, final, sems = refs[-3:]
+def blocks_kernel(e, counts, masked, near, far, result, divisor):
+    result[...] = squared_blocks(e, masked, near, far) / counts[e].astype(F32)
+    divisor[...] = jnp.full(divisor.shape, counts[counts.shape[0] - 1].astype(F32), F32)
+
+
+def last_blocks_kernel(experts, divisor, masked, near, far, *refs):
+    *earlier, result, final, sems = refs
     copies = [pltpu.make_async_copy(x, result.at[e], sems.at[e]) for e, x in enumerate(earlier)]
     for copy in copies:
         copy.start()
-    final[...] = squared_blocks(experts - 1, experts, *given[:2], given[2:]) / divisor[:1]
+    final[...] = squared_blocks(experts - 1, masked, near, far) / divisor[:1]
     copies.append(pltpu.make_async_copy(final, result.at[experts - 1], sems.at[experts - 1]))
     copies[-1].start()
     for copy in copies:
@@ -258,9 +273,8 @@
     core = [(t, t ^ 1) for t in range(4)]
     across = [(t, t ^ 2) for t in range(4)]
 
-    def spread(pays):
-        got = {k: lax.ppermute(pays[k], "dp", [(d, d ^ k) for d in range(dp)]) for k in FAR_FIRST}
-        return [pays[0]] + [got[k] for k in range(1, dp)]
+    def swap(x, k):
+        return lax.ppermute(x, "dp", [(d, d ^ k) for d in range(dp)])
 
     partial = jax.ShapeDtypeStruct((experts, cap, width), F32)
     acc, label, pick = call(
@@ -280,8 +294,11 @@
         split_in_kernel, "split_in", (rows(half, F32), rows(half, F32)), flops=8 * 10**9
     )(acc)
     got = lax.ppermute(send, "tensor", core)
-    pieces = call(pair_in_kernel, "pair_in", [rows(half // dp, BF16)] * dp)(keep, got)
-    arrived = spread(pieces)
+    pieces = call(pair_in_kernel, "pair_in", [rows(half // dp + LABEL_ROWS, BF16)] * dp)(
+        keep, got, label
+    )
+    arrived = [pieces[0]] + [swap(pieces[k], k) for k in range(1, dp)]
+    arrived = [arrived[k] for k in ARRIVAL]
 
     quarter = half // (2 * experts)
     split_shape = (rows(2 * quarter, F32), rows(2 * quarter, F32))
@@ -296,8 +313,6 @@
         ),
         after=pieces[:1],
     )(grads, pick, basis_out)
-    near = call(stack_kernel, "stack_in", rows(half, BF16))(*arrived)
-    far = lax.ppermute(near, "tensor", across)
     keeps, gots, sends = [], [], []
     for e in range(experts):
         if e > 0:
@@ -308,20 +323,31 @@
                 flops=10**9,
             )(rest, basis_out)
         keep, send = call(
-            split_out_kernel, "split_out", split_shape, after=sends[-1:] or [near]
+            split_out_kernel, "split_out", split_shape, after=sends[-1:] or arrived[1:]
         )(rotated)
         got = lax.ppermute(send, "tensor", core)
         keep, send = call(pair_out_kernel, "pair_out", pair_shape)(keep, got)
         keeps.append(keep)
         sends.append(send)
         gots.append(lax.ppermute(send, "tensor", across))
-    mine = call(sum_kernel, "sum_in", rows(half, BF16), after=gots[:1])(near, far)
-    other = lax.ppermute(mine, "tensor", core)
+    near = call(stack_kernel, "stack_in", rows(half, BF16), after=[gots[0], sends[-1]])(
+        *arrived
+    )
+    far = lax.ppermute(near, "tensor", across)
     outs = []
     for e in range(experts):
-        early = [mine, sends[-1]] if e == 0 else [outs[-1][1]]
-        out = call(round_kernel, "round_out", out_shape, after=early)(keeps[e], gots[e], label)
-        outs.append(spread([out] * dp))
+        out = call(round_kernel, "round_out", rows(quarter, BF16), after=sends[-1:])(
+            keeps[e], gots[e]
+        )
+        pair = call(pile_kernel, "pile_out", rows(2 * quarter, BF16))(out, swap(out, 2))
+        outs.append((pair, swap(pair, 1)))
+    mine = call(sum_kernel, "sum_in", rows(half, BF16), after=outs[0][:1])(near, far)
+    other = lax.ppermute(mine, "tensor", core)
+    masked = call(
+        functools.partial(mask_kernel, experts),
+        "mask_in",
+        jax.ShapeDtypeStruct((experts, dp * cap, dp * 128), BF16),
+    )(mine, other, *arrived)
 
     result = jax.ShapeDtypeStruct((experts, 128, 128), F32)
     done = []
@@ -330,8 +356,8 @@
             functools.partial(blocks_kernel, e),
             "blocks",
             (rows(128, F32), rows(8, F32)),
-            [smem] + [vmem] * (2 + dp),
-        )(expert_counts, mine, other, *outs[e])
+            [smem] + [vmem] * 3,
+        )(expert_counts, masked, *outs[e])
         done.append(block)
     return call(
         functools.partial(last_blocks_kernel, experts),
@@ -339,7 +365,7 @@
         result,
         scratch=[pltpu.VMEM(result.shape[1:], F32), pltpu.SemaphoreType.DMA((experts,))],
         out_specs=hbm,
-    )(divisor, *done, mine, other, *outs[-1])
+    )(divisor, masked, *outs[-1], *done)
 
 
 EX_DEV = 1

time: 41.3 us -> 40.8 us (0.988)
  starting transfers between devices: 19 us -> 15.1 us
  waiting for transfers between devices: 11.3 us -> 14.5 us
    ppermute x9 -> x7, waiting for transfers between devices: 5.04 us -> 9.75 us  [swap(): return lax.ppermute(x, 'dp', [(d, d ^ k) for d in range(dp)])]
    ppermute x1, waiting for transfers between devices: 4.34 us -> 0.01 us  [fast(): far = lax.ppermute(near, 'tensor', across)]
    ppermute x9 -> x7, starting transfers between devices: 14.4 us -> 10.6 us  [swap(): return lax.ppermute(x, 'dp', [(d, d ^ k) for d in range(dp)])]
    ppermute x2, waiting for transfers between devices: 0.61 us -> 2.92 us  [fast(): gots.append(lax.ppermute(send, 'tensor', across))]
    ppermute x3, waiting for transfers between devices: 1.35 us -> 1.79 us  [fast(): got = lax.ppermute(send, 'tensor', core)]
    pallas_call x15 -> x18, Pallas kernels: 10.5 us -> 10.8 us  [run(): pl.pallas_call(body, out_shape=out_shape, in_specs=(specs or [vmem] * len...]
  transfers between devices with their start and end apart: 16 -> 14, of which waited for: 6 -> 8; matrix products, arithmetic and copies ran while one was open for 0% -> 0% of each run, Pallas kernels for 15% -> 16%
where the time goes in v5:
time: 40.8 us; the launch traced here: 40.6 us
  starting transfers between devices  15.1 us (37%)
  waiting for transfers between devices  14.5 us (36%)
  Pallas kernels  10.8 us (26%)
    pallas_call x18, Pallas kernels, run(): pl.pallas_call(body, out_shape=out_shape, in_specs=(specs or [vmem] * len...  10.8 us
    ppermute x7, starting transfers between devices, swap(): return lax.ppermute(x, 'dp', [(d, d ^ k) for d in range(dp)])  10.6 us
    ppermute x7, waiting for transfers between devices, swap(): return lax.ppermute(x, 'dp', [(d, d ^ k) for d in range(dp)])  9.75 us
    ppermute x2, waiting for transfers between devices, fast(): gots.append(lax.ppermute(send, 'tensor', across))  2.92 us
    ppermute x2, starting transfers between devices, fast(): gots.append(lax.ppermute(send, 'tensor', across))  2.04 us
    ppermute x3, waiting for transfers between devices, fast(): got = lax.ppermute(send, 'tensor', core)  1.79 us
    ppermute x1, starting transfers between devices, fast(): far = lax.ppermute(near, 'tensor', across)  1.55 us
  transfers between devices with their start and end apart: 14, of which 8 were waited for; matrix products, arithmetic and copies ran while one was open for 0% of the time, Pallas kernels for 16%

profile of v5, /device:TPU:0, one launch (start us, length us, event | category | flops | bytes accessed | tf_op | source)
XLA Modules:
  0.0 40.6 jit_solution(14745967557113466144)
XLA Ops:
  0.0 3.1 %rotate_in.1 = (f32[2,192,512]{2,1,0:T(8,128)S(1)}, bf16[16,128]{1,0:T(8,128)(2,1)S(1)}, bf16[384,768]{1,0:T(8,128)(2,1)S(1)}) custom-call(bf16[384,1536]{1,0:T(8,128)(2,1)} %refs_0_.3, s32[2,384]{1,0:T(2,128)} %bitcast.5, s32[384]{0:T(512)} %refs_2_.2, bf16[2,1536,512]{2,1,0:T(8,128)(2,1)} %refs_3_.1), custom_call_target="tpu_custom_call" | custom-call | flops 1 | bytes 1 | tf_op jit(solution)/shard_map/rotate_in/pallas_call | solution.py:242
  3.1 0.0 slice-start
  3.1 0.0 slice-start.2
  3.1 0.0 slice-start.1
  3.1 0.0 slice-start.3
  3.1 0.1 split_in.1
  3.2 0.5 %collective-permute-start = (f32[768,128]{1,0:T(8,128)S(1)}, f32[768,128]{1,0:T(8,128)S(1)}, u32[]{:S(2)}, u32[]{:S(2)}) collective-permute-start(f32[768,128]{1,0:T(8,128)S(1)} %get-tuple-element.28), channel_id=1, source_target_pairs={{0,1},{1,0},{2,3},{3,2},{4,5},{5,4},{6,7},{7,6},{8,9},{9,8},{10,11... | collective-permute-start | bytes 1179656 | tf_op jit(solution)/shard_map/ppermute | solution.py:296
  3.7 1.3 %collective-permute-done.refs_1_ = f32[768,128]{1,0:T(8,128)S(1)} collective-permute-done((f32[768,128]{1,0:T(8,128)S(1)}, f32[768,128]{1,0:T(8,128)S(1)}, u32[]{:S(2)}, u32[]{:S(2)}) %collective-permute-start) | collective-permute-done | bytes 393248 | tf_op jit(solution)/shard_map/ppermute | solution.py:296
  5.1 0.1 pair_in.1
  5.2 4.0 %collective-permute-start.1 = (bf16[208,128]{1,0:T(8,128)(2,1)S(1)}, bf16[208,128]{1,0:T(8,128)(2,1)S(1)}, u32[]{:S(2)}, u32[]{:S(2)}) collective-permute-start(bf16[208,128]{1,0:T(8,128)(2,1)S(1)} %get-tuple-element.31), channel_id=1, source_target_pairs={{0,8},{4,12},{8,0},{12,4},{1,9},{5,13},{9,1},{13,5},{2,10},{6,14},... | collective-permute-start | bytes 159752 | tf_op jit(solution)/shard_map/ppermute | solution.py:277
  9.2 1.6 %collective-permute-start.2 = (bf16[208,128]{1,0:T(8,128)(2,1)S(1)}, bf16[208,128]{1,0:T(8,128)(2,1)S(1)}, u32[]{:S(2)}, u32[]{:S(2)}) collective-permute-start(bf16[208,128]{1,0:T(8,128)(2,1)S(1)} %get-tuple-element.32), channel_id=1, source_target_pairs={{0,4},{4,0},{8,12},{12,8},{1,5},{5,1},{9,13},{13,9},{2,6},{6,2},{1... | collective-permute-start | bytes 159752 | tf_op jit(solution)/shard_map/ppermute | solution.py:277
  10.8 0.0 collective-permute-start.3
  10.8 0.0 slice-done
  10.8 0.0 slice-done.2
  10.8 0.0 slice-done.1
  10.8 0.0 slice-done.3
  10.8 4.0 %rotate_first.1 = (f32[192,512]{1,0:T(8,128)S(1)}, bf16[192,4096]{1,0:T(8,128)(2,1)S(1)}) custom-call(bf16[384,2,4096]{2,1,0:T(2,128)(2,1)S(1)} %bitcast.4, bf16[384,768]{1,0:T(8,128)(2,1)S(1)} %get-tuple-element.34.refs_1_, bf16[2,4096,512]{2,1,0:T(8,128)(2,1)S(1)} %bitcast.2, bf16[208,128]{1,0:T(8,128)(2,1)S(1)} %get-tuple-element.30.refs_3_.refs_0_.refs_2_), custom_call_target="tpu_custom_call" | custom-call | flops 1 | bytes 1 | tf_op jit(solution)/shard_map/rotate_first/pallas_call | solution.py:242
  14.8 0.0 collective-permute-done.1.refs_1_.refs_3_
  14.8 0.0 collective-permute-done.2.refs_2_.refs_4_
  14.8 1.9 %collective-permute-done.3.refs_3_.refs_5_ = bf16[208,128]{1,0:T(8,128)(2,1)S(1)} collective-permute-done((bf16[208,128]{1,0:T(8,128)(2,1)S(1)}, bf16[208,128]{1,0:T(8,128)(2,1)S(1)}, u32[]{:S(2)}, u32[]{:S(2)}) %collective-permute-start.3) | collective-permute-done | bytes 53280 | tf_op jit(solution)/shard_map/ppermute | solution.py:277
  16.7 0.1 split_out.2
  16.7 0.1 collective-permute-start.4
  16.8 1.0 %rotate_rest.1.refs_0_ = f32[192,512]{1,0:T(8,128)S(1)} custom-call(bf16[192,4096]{1,0:T(8,128)(2,1)S(1)} %get-tuple-element.39.refs_0_, bf16[2,4096,512]{2,1,0:T(8,128)(2,1)S(1)} %bitcast.2), custom_call_target="tpu_custom_call" | custom-call | flops 1000000000 | bytes 1 | tf_op jit(solution)/shard_map/rotate_rest/pallas_call | solution.py:242
  17.8 0.0 copy-start
  17.8 0.4 %collective-permute-done.4.refs_1_ = f32[384,128]{1,0:T(8,128)S(1)} collective-permute-done((f32[384,128]{1,0:T(8,128)S(1)}, f32[384,128]{1,0:T(8,128)S(1)}, u32[]{:S(2)}, u32[]{:S(2)}) %collective-permute-start.4) | collective-permute-done | bytes 196640 | tf_op jit(solution)/shard_map/ppermute | solution.py:328
  18.3 0.1 split_out.3
  18.4 0.2 collective-permute-start.6
  18.6 1.5 %collective-permute-start.5 = (bf16[192,128]{1,0:T(8,128)(2,1)S(1)}, bf16[192,128]{1,0:T(8,128)(2,1)S(1)}, u32[]{:S(2)}, u32[]{:S(2)}) collective-permute-start(bf16[192,128]{1,0:T(8,128)(2,1)S(1)} %get-tuple-element.38.refs_1_), channel_id=1, source_target_pairs={{0,2},{1,3},{2,0},{3,1},{4,6},{5,7},{6,4},{7,5},{8,10},{9,11},{10,... | collective-permute-start | bytes 147464 | tf_op jit(solution)/shard_map/ppermute | solution.py:332
  20.1 0.0 collective-permute-done.6.refs_1_
  20.1 2.6 %collective-permute-done.5.refs_4_.refs_1_ = bf16[192,128]{1,0:T(8,128)(2,1)S(1)} collective-permute-done((bf16[192,128]{1,0:T(8,128)(2,1)S(1)}, bf16[192,128]{1,0:T(8,128)(2,1)S(1)}, u32[]{:S(2)}, u32[]{:S(2)}) %collective-permute-start.5) | collective-permute-done | bytes 49184 | tf_op jit(solution)/shard_map/ppermute | solution.py:332
  22.7 1.6 %collective-permute-start.7 = (bf16[768,128]{1,0:T(8,128)(2,1)S(1)}, bf16[768,128]{1,0:T(8,128)(2,1)S(1)}, u32[]{:S(2)}, u32[]{:S(2)}) collective-permute-start(bf16[768,128]{1,0:T(8,128)(2,1)S(1)} %stack_in.1.refs_0_), channel_id=1, source_target_pairs={{0,2},{1,3},{2,0},{3,1},{4,6},{5,7},{6,4},{7,5},{8,10},{9,11},{10,... | collective-permute-start | bytes 589832 | tf_op jit(solution)/shard_map/ppermute | solution.py:336
  24.2 0.7 %collective-permute-start.8 = (bf16[192,128]{1,0:T(8,128)(2,1)S(1)}, bf16[192,128]{1,0:T(8,128)(2,1)S(1)}, u32[]{:S(2)}, u32[]{:S(2)}) collective-permute-start(bf16[192,128]{1,0:T(8,128)(2,1)S(1)} %round_out.2.refs_0_), channel_id=1, source_target_pairs={{0,8},{4,12},{8,0},{12,4},{1,9},{5,13},{9,1},{13,5},{2,10},{6,14},... | collective-permute-start | bytes 147464 | tf_op jit(solution)/shard_map/ppermute | solution.py:277
  25.0 0.5 %collective-permute-start.11 = (bf16[192,128]{1,0:T(8,128)(2,1)S(1)}, bf16[192,128]{1,0:T(8,128)(2,1)S(1)}, u32[]{:S(2)}, u32[]{:S(2)}) collective-permute-start(bf16[192,128]{1,0:T(8,128)(2,1)S(1)} %get-tuple-element.42.refs_5_.refs_2_), channel_id=1, source_target_pairs={{0,2},{1,3},{2,0},{3,1},{4,6},{5,7},{6,4},{7,5},{8,10},{9,11},{10,... | collective-permute-start | bytes 147464 | tf_op jit(solution)/shard_map/ppermute | solution.py:332
  25.5 3.8 %collective-permute-done.8.refs_1_ = bf16[192,128]{1,0:T(8,128)(2,1)S(1)} collective-permute-done((bf16[192,128]{1,0:T(8,128)(2,1)S(1)}, bf16[192,128]{1,0:T(8,128)(2,1)S(1)}, u32[]{:S(2)}, u32[]{:S(2)}) %collective-permute-start.8) | collective-permute-done | bytes 49184 | tf_op jit(solution)/shard_map/ppermute | solution.py:277
  29.3 0.0 collective-permute-done.7.refs_1_
  29.3 0.1 sum_in.1.refs_0_
  29.4 0.1 collective-permute-start.9
  29.5 0.4 collective-permute-done.11.refs_1_
  29.8 1.6 %collective-permute-start.12 = (bf16[192,128]{1,0:T(8,128)(2,1)S(1)}, bf16[192,128]{1,0:T(8,128)(2,1)S(1)}, u32[]{:S(2)}, u32[]{:S(2)}) collective-permute-start(bf16[192,128]{1,0:T(8,128)(2,1)S(1)} %round_out.3.refs_0_), channel_id=1, source_target_pairs={{0,8},{4,12},{8,0},{12,4},{1,9},{5,13},{9,1},{13,5},{2,10},{6,14},... | collective-permute-start | bytes 147464 | tf_op jit(solution)/shard_map/ppermute | solution.py:277
  31.4 1.0 %collective-permute-start.10 = (bf16[384,128]{1,0:T(8,128)(2,1)S(1)}, bf16[384,128]{1,0:T(8,128)(2,1)S(1)}, u32[]{:S(2)}, u32[]{:S(2)}) collective-permute-start(bf16[384,128]{1,0:T(8,128)(2,1)S(1)} %pile_out.2.refs_2_), channel_id=1, source_target_pairs={{0,4},{4,0},{8,12},{12,8},{1,5},{5,1},{9,13},{13,9},{2,6},{6,2},{1... | collective-permute-start | bytes 294920 | tf_op jit(solution)/shard_map/ppermute | solution.py:277
  32.4 2.5 %collective-permute-done.12.refs_1_ = bf16[192,128]{1,0:T(8,128)(2,1)S(1)} collective-permute-done((bf16[192,128]{1,0:T(8,128)(2,1)S(1)}, bf16[192,128]{1,0:T(8,128)(2,1)S(1)}, u32[]{:S(2)}, u32[]{:S(2)}) %collective-permute-start.12) | collective-permute-done | bytes 49184 | tf_op jit(solution)/shard_map/ppermute | solution.py:277
  35.0 1.7 %collective-permute-start.13 = (bf16[384,128]{1,0:T(8,128)(2,1)S(1)}, bf16[384,128]{1,0:T(8,128)(2,1)S(1)}, u32[]{:S(2)}, u32[]{:S(2)}) collective-permute-start(bf16[384,128]{1,0:T(8,128)(2,1)S(1)} %pile_out.3.refs_2_), channel_id=1, source_target_pairs={{0,4},{4,0},{8,12},{12,8},{1,5},{5,1},{9,13},{13,9},{2,6},{6,2},{1... | collective-permute-start | bytes 294920 | tf_op jit(solution)/shard_map/ppermute | solution.py:277
  36.6 0.0 collective-permute-done.9.refs_1_
  36.6 0.5 %mask_in.1.refs_1_ = bf16[2,768,512]{2,1,0:T(8,128)(2,1)S(1)} custom-call(bf16[768,128]{1,0:T(8,128)(2,1)S(1)} %sum_in.1.refs_0_, bf16[768,128]{1,0:T(8,128)(2,1)S(1)} %collective-permute-done.9.refs_1_, bf16[208,128]{1,0:T(8,128)(2,1)S(1)} %get-tuple-element.30.refs_3_.refs_0_.refs_2_, bf16[208,128]{1,0:T(8,128)(2,1)S(1)} %collective-permute-done.1.refs_1_.refs_3_, ...), custom_call_target="tpu_custom_call" | custom-call | flops 1 | bytes 1 | tf_op jit(solution)/shard_map/mask_in/pallas_call | solution.py:242
  37.2 0.0 collective-permute-done.10.refs_3_
  37.2 0.8 %blocks.1 = (f32[128,128]{1,0:T(8,128)S(1)}, f32[8,128]{1,0:T(8,128)S(1)}) custom-call(s32[2]{0:T(128)S(1)} %copy-done, bf16[2,768,512]{2,1,0:T(8,128)(2,1)S(1)} %mask_in.1.refs_1_, bf16[384,128]{1,0:T(8,128)(2,1)S(1)} %pile_out.2.refs_2_, bf16[384,128]{1,0:T(8,128)(2,1)S(1)} %collective-permute-done.10.refs_3_), custom_call_target="tpu_custom_call" | custom-call | flops 1 | bytes 1 | tf_op jit(solution)/shard_map/blocks/pallas_call | solution.py:242
  38.0 1.6 %collective-permute-done.13.refs_3_ = bf16[384,128]{1,0:T(8,128)(2,1)S(1)} collective-permute-done((bf16[384,128]{1,0:T(8,128)(2,1)S(1)}, bf16[384,128]{1,0:T(8,128)(2,1)S(1)}, u32[]{:S(2)}, u32[]{:S(2)}) %collective-permute-start.13) | collective-permute-done | bytes 98336 | tf_op jit(solution)/shard_map/ppermute | solution.py:277
  39.6 1.0 %last_blocks.1 = f32[2,128,128]{2,1,0:T(8,128)} custom-call(f32[8,128]{1,0:T(8,128)S(1)} %get-tuple-element.44.refs_0_, bf16[2,768,512]{2,1,0:T(8,128)(2,1)S(1)} %mask_in.1.refs_1_, bf16[384,128]{1,0:T(8,128)(2,1)S(1)} %pile_out.3.refs_2_, bf16[384,128]{1,0:T(8,128)(2,1)S(1)} %collective-permute-done.13.refs_3_, f32[128,128]{1,0:T(8,128)S(1)} %get-tuple-element.46.refs_4_), custom_call_target="tpu_custom_call" | custom-call | flops 1 | bytes 1 | tf_op jit(solution)/shard_map/last_blocks/pallas_call | solution.py:242
  (10 shorter events, 0.1 us)
Async XLA Ops:
  3.1 7.7 %slice-start = ((s8[8388608]{0:T(1024)(128)(4,1)}), s8[4194304]{0:T(1024)(128)(4,1)S(1)}, s32[]{:S(2)}) async-start(s8[8388608]{0:T(1024)(128)(4,1)} %bitcast.1), calls=%async_computation | async-start | bytes 8388608
  3.1 7.7 %slice-start.2 = ((s8[6291456]{0:T(1024)(128)(4,1)}), s8[4194304]{0:T(1024)(128)(4,1)S(1)}, s32[]{:S(2)}) async-start(s8[6291456]{0:T(1024)(128)(4,1)} %bitcast.3), calls=%async_computation.2 | async-start | bytes 8388608
  3.1 7.6 %slice-start.1 = ((s8[8388608]{0:T(1024)(128)(4,1)}), s8[4194304]{0:T(1024)(128)(4,1)S(1)}, s32[]{:S(2)}) async-start(s8[8388608]{0:T(1024)(128)(4,1)} %bitcast.1), calls=%async_computation.1 | async-start | bytes 8388608
  3.1 7.6 %slice-start.3 = ((s8[6291456]{0:T(1024)(128)(4,1)}), s8[2097152]{0:T(1024)(128)(4,1)S(1)}, s32[]{:S(2)}) async-start(s8[6291456]{0:T(1024)(128)(4,1)} %bitcast.3), calls=%async_computation.3 | async-start | bytes 4194304
  3.2 1.9 %collective-permute-start = (f32[768,128]{1,0:T(8,128)S(1)}, f32[768,128]{1,0:T(8,128)S(1)}, u32[]{:S(2)}, u32[]{:S(2)}) collective-permute-start(f32[768,128]{1,0:T(8,128)S(1)} %get-tuple-element.28), channel_id=1, source_target_pairs={{0,1},{1,0},{2,3},{3,2},{4,5},{5,4},{6,7},{7,6},{8,9},{9,8},{10,11... | collective-permute-start | bytes 1179656 | tf_op jit(solution)/shard_map/ppermute | solution.py:296
  5.2 9.6 %collective-permute-start.1 = (bf16[208,128]{1,0:T(8,128)(2,1)S(1)}, bf16[208,128]{1,0:T(8,128)(2,1)S(1)}, u32[]{:S(2)}, u32[]{:S(2)}) collective-permute-start(bf16[208,128]{1,0:T(8,128)(2,1)S(1)} %get-tuple-element.31), channel_id=1, source_target_pairs={{0,8},{4,12},{8,0},{12,4},{1,9},{5,13},{9,1},{13,5},{2,10},{6,14},... | collective-permute-start | bytes 159752 | tf_op jit(solution)/shard_map/ppermute | solution.py:277
  9.2 5.6 %collective-permute-start.2 = (bf16[208,128]{1,0:T(8,128)(2,1)S(1)}, bf16[208,128]{1,0:T(8,128)(2,1)S(1)}, u32[]{:S(2)}, u32[]{:S(2)}) collective-permute-start(bf16[208,128]{1,0:T(8,128)(2,1)S(1)} %get-tuple-element.32), channel_id=1, source_target_pairs={{0,4},{4,0},{8,12},{12,8},{1,5},{5,1},{9,13},{13,9},{2,6},{6,2},{1... | collective-permute-start | bytes 159752 | tf_op jit(solution)/shard_map/ppermute | solution.py:277
  10.8 5.9 %collective-permute-start.3 = (bf16[208,128]{1,0:T(8,128)(2,1)S(1)}, bf16[208,128]{1,0:T(8,128)(2,1)S(1)}, u32[]{:S(2)}, u32[]{:S(2)}) collective-permute-start(bf16[208,128]{1,0:T(8,128)(2,1)S(1)} %get-tuple-element.33), channel_id=1, source_target_pairs={{0,12},{4,8},{8,4},{12,0},{1,13},{5,9},{9,5},{13,1},{2,14},{6,10},... | collective-permute-start | bytes 159752 | tf_op jit(solution)/shard_map/ppermute | solution.py:277
  16.7 1.5 %collective-permute-start.4 = (f32[384,128]{1,0:T(8,128)S(1)}, f32[384,128]{1,0:T(8,128)S(1)}, u32[]{:S(2)}, u32[]{:S(2)}) collective-permute-start(f32[384,128]{1,0:T(8,128)S(1)} %get-tuple-element.37), channel_id=1, source_target_pairs={{0,1},{1,0},{2,3},{3,2},{4,5},{5,4},{6,7},{7,6},{8,9},{9,8},{10,11... | collective-permute-start | bytes 589832 | tf_op jit(solution)/shard_map/ppermute | solution.py:328
  17.8 19.4 %copy-start = (s32[2]{0:T(128)S(1)}, s32[2]{0:T(128)}, u32[]{:S(2)}) copy-start(s32[2]{0:T(128)} %refs_0_.5) | copy-start | bytes 28
  18.4 1.7 %collective-permute-start.6 = (f32[384,128]{1,0:T(8,128)S(1)}, f32[384,128]{1,0:T(8,128)S(1)}, u32[]{:S(2)}, u32[]{:S(2)}) collective-permute-start(f32[384,128]{1,0:T(8,128)S(1)} %get-tuple-element.41), channel_id=1, source_target_pairs={{0,1},{1,0},{2,3},{3,2},{4,5},{5,4},{6,7},{7,6},{8,9},{9,8},{10,11... | collective-permute-start | bytes 589832 | tf_op jit(solution)/shard_map/ppermute | solution.py:328
  18.6 4.1 %collective-permute-start.5 = (bf16[192,128]{1,0:T(8,128)(2,1)S(1)}, bf16[192,128]{1,0:T(8,128)(2,1)S(1)}, u32[]{:S(2)}, u32[]{:S(2)}) collective-permute-start(bf16[192,128]{1,0:T(8,128)(2,1)S(1)} %get-tuple-element.38.refs_1_), channel_id=1, source_target_pairs={{0,2},{1,3},{2,0},{3,1},{4,6},{5,7},{6,4},{7,5},{8,10},{9,11},{10,... | collective-permute-start | bytes 147464 | tf_op jit(solution)/shard_map/ppermute | solution.py:332
  22.7 6.6 %collective-permute-start.7 = (bf16[768,128]{1,0:T(8,128)(2,1)S(1)}, bf16[768,128]{1,0:T(8,128)(2,1)S(1)}, u32[]{:S(2)}, u32[]{:S(2)}) collective-permute-start(bf16[768,128]{1,0:T(8,128)(2,1)S(1)} %stack_in.1.refs_0_), channel_id=1, source_target_pairs={{0,2},{1,3},{2,0},{3,1},{4,6},{5,7},{6,4},{7,5},{8,10},{9,11},{10,... | collective-permute-start | bytes 589832 | tf_op jit(solution)/shard_map/ppermute | solution.py:336
  24.2 5.1 %collective-permute-start.8 = (bf16[192,128]{1,0:T(8,128)(2,1)S(1)}, bf16[192,128]{1,0:T(8,128)(2,1)S(1)}, u32[]{:S(2)}, u32[]{:S(2)}) collective-permute-start(bf16[192,128]{1,0:T(8,128)(2,1)S(1)} %round_out.2.refs_0_), channel_id=1, source_target_pairs={{0,8},{4,12},{8,0},{12,4},{1,9},{5,13},{9,1},{13,5},{2,10},{6,14},... | collective-permute-start | bytes 147464 | tf_op jit(solution)/shard_map/ppermute | solution.py:277
  25.0 4.8 %collective-permute-start.11 = (bf16[192,128]{1,0:T(8,128)(2,1)S(1)}, bf16[192,128]{1,0:T(8,128)(2,1)S(1)}, u32[]{:S(2)}, u32[]{:S(2)}) collective-permute-start(bf16[192,128]{1,0:T(8,128)(2,1)S(1)} %get-tuple-element.42.refs_5_.refs_2_), channel_id=1, source_target_pairs={{0,2},{1,3},{2,0},{3,1},{4,6},{5,7},{6,4},{7,5},{8,10},{9,11},{10,... | collective-permute-start | bytes 147464 | tf_op jit(solution)/shard_map/ppermute | solution.py:332
  29.4 7.2 %collective-permute-start.9 = (bf16[768,128]{1,0:T(8,128)(2,1)S(1)}, bf16[768,128]{1,0:T(8,128)(2,1)S(1)}, u32[]{:S(2)}, u32[]{:S(2)}) collective-permute-start(bf16[768,128]{1,0:T(8,128)(2,1)S(1)} %sum_in.1.refs_0_), channel_id=1, source_target_pairs={{0,1},{1,0},{2,3},{3,2},{4,5},{5,4},{6,7},{7,6},{8,9},{9,8},{10,11... | collective-permute-start | bytes 589832 | tf_op jit(solution)/shard_map/ppermute | solution.py:345
  29.8 5.1 %collective-permute-start.12 = (bf16[192,128]{1,0:T(8,128)(2,1)S(1)}, bf16[192,128]{1,0:T(8,128)(2,1)S(1)}, u32[]{:S(2)}, u32[]{:S(2)}) collective-permute-start(bf16[192,128]{1,0:T(8,128)(2,1)S(1)} %round_out.3.refs_0_), channel_id=1, source_target_pairs={{0,8},{4,12},{8,0},{12,4},{1,9},{5,13},{9,1},{13,5},{2,10},{6,14},... | collective-permute-start | bytes 147464 | tf_op jit(solution)/shard_map/ppermute | solution.py:277
  31.4 5.7 %collective-permute-start.10 = (bf16[384,128]{1,0:T(8,128)(2,1)S(1)}, bf16[384,128]{1,0:T(8,128)(2,1)S(1)}, u32[]{:S(2)}, u32[]{:S(2)}) collective-permute-start(bf16[384,128]{1,0:T(8,128)(2,1)S(1)} %pile_out.2.refs_2_), channel_id=1, source_target_pairs={{0,4},{4,0},{8,12},{12,8},{1,5},{5,1},{9,13},{13,9},{2,6},{6,2},{1... | collective-permute-start | bytes 294920 | tf_op jit(solution)/shard_map/ppermute | solution.py:277
  35.0 4.7 %collective-permute-start.13 = (bf16[384,128]{1,0:T(8,128)(2,1)S(1)}, bf16[384,128]{1,0:T(8,128)(2,1)S(1)}, u32[]{:S(2)}, u32[]{:S(2)}) collective-permute-start(bf16[384,128]{1,0:T(8,128)(2,1)S(1)} %pile_out.3.refs_2_), channel_id=1, source_target_pairs={{0,4},{4,0},{8,12},{12,8},{1,5},{5,1},{9,13},{13,9},{2,6},{6,2},{1... | collective-permute-start | bytes 294920 | tf_op jit(solution)/shard_map/ppermute | solution.py:277

commit v6 on v5

--- a/solution.py
+++ b/solution.py
@@ -9,9 +9,11 @@
 
 F32 = jnp.float32
 BF16 = jnp.bfloat16
-CHUNK = 512
+CHUNK = 1024
+EARLY = 1024
+PARTS = 3
 VMEM = 20 * 2**20
-ARRIVAL = (0, 2, 1, 3)
+ARRIVAL = (0, 1, 3, 2)
 LABEL_ROWS = 16
 
 
@@ -35,17 +37,19 @@
 
 
 def rotate_in_kernel(
-    acts, routes, ids, basis_in,
-    acc, label, pick,
+    acts, routes, ids, basis_in, grads,
+    acc, label, pick, early,
     acts_v, routes_v, ids_v, basis_v, sems,
 ):
-    tokens = acts.shape[0]
-    experts, _, width = basis_in.shape
+    tokens, features = acts.shape
+    experts = basis_in.shape[0]
     cap = tokens // 2
+    parts = [pl.ds(at, features // PARTS) for at in range(0, features, features // PARTS)]
     fetch = fetcher(sems)
     first = [fetch(routes, routes_v), fetch(ids, ids_v)]
-    acts_in = fetch(acts, acts_v)
-    bases = [fetch(basis_in.at[e], basis_v.at[e]) for e in range(experts)]
+    acts_in = [fetch(acts.at[:, part], acts_v.at[:, part]) for part in parts]
+    bases = [fetch(basis_in.at[:, part, :], basis_v.at[:, part, :]) for part in parts]
+    grads_in = fetch(grads.at[:, :, pl.ds(0, early.shape[2])], early)
     for copy in first:
         copy.wait()
     hits = [
@@ -85,11 +89,16 @@
         block = jnp.where(row == at, mine, block)
     label[...] = block.astype(BF16)
 
-    acts_in.wait()
-    chosen = dot(pick_in, acts_v[...]).astype(BF16)
-    for e in range(experts):
-        bases[e].wait()
-        acc[e] = dot(chosen[e * cap : (e + 1) * cap], basis_v[e])
+    chosen = []
+    for part, copy in zip(parts, acts_in):
+        copy.wait()
+        chosen.append(dot(pick_in, acts_v[:, part]).astype(BF16))
+    for n, part in enumerate(parts):
+        bases[n].wait()
+        for e in range(experts):
+            more = dot(chosen[n][e * cap : (e + 1) * cap], basis_v[e, part, :])
+            acc[e] = more if n == 0 else acc[e] + more
+    grads_in.wait()
 
 
 def split_in_kernel(acc, keep, send):
@@ -106,18 +115,25 @@
             at += half
 
 
-def rotate_first_kernel(grads, pick, basis_out, acc, rest):
-    tokens, _, hidden = grads.shape
-    cap = tokens // 2
-    for s in range(hidden // CHUNK):
-        cols = pl.ds(s * CHUNK, CHUNK)
-        chosen = dot(pick[...], grads[:, :, cols].reshape(2 * tokens, CHUNK)).astype(BF16)
+def choose(pick, grads, cols):
+    rows = grads[:, :, cols]
+    return dot(pick[...], rows.reshape(rows.shape[0] * 2, rows.shape[2])).astype(BF16)
+
+
+def choose_kernel(grads, pick, out):
+    out[...] = choose(pick, grads, slice(None))
+
+
+def rotate_first_kernel(grads, pick, basis_out, early, acc, rest):
+    cap, width = acc.shape
+    done = early.shape[1]
+    rest[:, :done] = early[cap:, :]
+    acc[...] = dot(early[:cap, :], basis_out[0, :done, :])
+    for at in range(done, grads.shape[2], CHUNK):
+        cols = pl.ds(at, CHUNK)
+        chosen = choose(pick, grads, cols)
         rest[:, cols] = chosen[cap:]
-        part = dot(chosen[:cap], basis_out[0, cols, :])
-        if s == 0:
-            acc[...] = part
-        else:
-            acc[...] += part
+        acc[...] += dot(chosen[:cap], basis_out[0, cols, :])
 
 
 def rotate_rest_kernel(e, rest, basis_out, acc):
@@ -153,80 +169,82 @@
     send[...] = (kept[other, :] + got[other, :]).astype(BF16)
 
 
-def round_kernel(kept, got, out):
-    out[...] = (kept[...] + got[...].astype(F32)).astype(BF16)
-
-
-def pile_kernel(near, far, out):
-    out[: near.shape[0], :] = near[...]
-    out[near.shape[0] :, :] = far[...]
-
-
-def stack_kernel(*refs):
-    *pieces, out = refs
-    slab = pieces[0].shape[0] - LABEL_ROWS
+def round_kernel(*refs):
+    *given, out = refs
+    cap = given[0].shape[0]
+    for e in range(len(given) // 2):
+        kept, got = given[2 * e : 2 * e + 2]
+        out[e * cap : (e + 1) * cap, :] = (kept[...] + got[...].astype(F32)).astype(BF16)
+
+
+def stack_kernel(experts, *refs):
+    pieces, outs = refs[:-experts], refs[-experts:]
+    half = (pieces[0].shape[0] - LABEL_ROWS) // experts
     for k, piece in enumerate(pieces):
-        out[k * slab : (k + 1) * slab, :] = piece[:slab, :]
-
-
-def sum_kernel(near, far, out):
-    out[...] = (near[...].astype(F32) + far[...].astype(F32)).astype(BF16)
-
-
-def mask_kernel(experts, mine, other, *refs):
-    pieces, out = refs[:-1], refs[-1]
+        for e, out in enumerate(outs):
+            out[k * half : (k + 1) * half, :] = piece[e * half : (e + 1) * half, :]
+
+
+def sum_kernel(near, far, *outs):
+    piece = outs[0].shape[0]
+    for n, out in enumerate(outs):
+        at = pl.ds(n * piece, piece)
+        out[...] = (near[at, :].astype(F32) + far[at, :].astype(F32)).astype(BF16)
+
+
+def mask(e, which, rows, pieces):
     dp = len(pieces)
-    slab = pieces[0].shape[0] - LABEL_ROWS
-    half = slab // experts
+    rows = jnp.concatenate([row[...] for row in rows], axis=0).astype(F32)
+    half = rows.shape[0] // dp
+    labels = []
+    for piece in pieces:
+        label = piece[-LABEL_ROWS:, :].astype(F32)[2 * e : 2 * e + 2, :half]
+        labels.append(jnp.where(which == 0, label[0:1], label[1:2]))
+    labels = jnp.concatenate(labels, axis=1)
+    labels = jnp.broadcast_to(labels, (128, labels.shape[1])).T
+    return jnp.concatenate(
+        [jnp.where(labels == float(n + 1), rows, 0.0).astype(BF16) for n in range(dp)], axis=1
+    )
+
+
+def mask_kernel(experts, *refs):
+    mine, pieces, out = refs[: 2 * experts], refs[2 * experts : -1], refs[-1]
     core = lax.rem(lax.axis_index("tensor"), 2)
     for e in range(experts):
-        rows, labels = [], []
-        for which, ref in ((core, mine), (1 - core, other)):
-            for k, piece in enumerate(pieces):
-                at = (k * experts + e) * half
-                rows.append(ref[at : at + half, :])
-                label = piece[slab:, :].astype(F32)[2 * e : 2 * e + 2, :half]
-                labels.append(jnp.where(which == 0, label[0:1], label[1:2]))
-        rows = jnp.concatenate(rows, axis=0).astype(F32)
-        labels = jnp.concatenate(labels, axis=1)
-        labels = jnp.broadcast_to(labels, (128, labels.shape[1])).T
-        for n in range(dp):
-            out[e, :, n * 128 : (n + 1) * 128] = jnp.where(
-                labels == float(n + 1), rows, 0.0
-            ).astype(BF16)
-
-
-def squared_blocks(e, masked, *outs):
-    cap = masked.shape[1] * 128 // masked.shape[2]
+        out[e] = mask(e, core, mine[2 * e : 2 * e + 2], pieces)
+
+
+def gather_kernel(*refs):
+    *given, out = refs
+    experts = out.shape[0]
+    cap = given[0].shape[0] // experts
     half = cap // 2
     core = lax.rem(lax.axis_index("tensor"), 2)
-    rows = [
-        ref[pl.ds(pl.multiple_of(at + which * half, 16), half), :]
-        for which in (core, 1 - core)
-        for ref in outs
-        for at in range(0, ref.shape[0], cap)
-    ]
-    blocks = dot(jnp.concatenate(rows, axis=0).T, masked[e])
-    squares = blocks * blocks
-    summed = squares[:, :128]
-    for at in range(128, squares.shape[1], 128):
-        summed = summed + squares[:, at : at + 128]
-    return summed
-
-
-def blocks_kernel(e, counts, masked, near, far, result, divisor):
-    result[...] = squared_blocks(e, masked, near, far) / counts[e].astype(F32)
-    divisor[...] = jnp.full(divisor.shape, counts[counts.shape[0] - 1].astype(F32), F32)
-
-
-def last_blocks_kernel(experts, divisor, masked, near, far, *refs):
-    *earlier, result, final, sems = refs
-    copies = [pltpu.make_async_copy(x, result.at[e], sems.at[e]) for e, x in enumerate(earlier)]
-    for copy in copies:
-        copy.start()
-    final[...] = squared_blocks(experts - 1, masked, near, far) / divisor[:1]
-    copies.append(pltpu.make_async_copy(final, result.at[experts - 1], sems.at[experts - 1]))
-    copies[-1].start()
+    for e in range(experts):
+        rows = [
+            ref[pl.ds(pl.multiple_of(e * cap + which * half, 16), half), :]
+            for which in (core, 1 - core)
+            for ref in given
+        ]
+        out[e] = jnp.concatenate(rows, axis=0).T
+
+
+def blocks_kernel(counts, rows_out, masked, *refs):
+    experts, half = masked.shape[:2]
+    other, pieces = refs[: 2 * experts], refs[2 * experts : -3]
+    result, final, sems = refs[-3:]
+    core = lax.rem(lax.axis_index("tensor"), 2)
+    copies = []
+    for e in range(experts):
+        blocks = dot(rows_out[e, :, :half], masked[e])
+        blocks += dot(rows_out[e, :, half:], mask(e, 1 - core, other[2 * e : 2 * e + 2], pieces))
+        squares = blocks * blocks
+        summed = squares[:, :128]
+        for at in range(128, squares.shape[1], 128):
+            summed = summed + squares[:, at : at + 128]
+        final[e] = summed / counts[e].astype(F32)
+        copies.append(pltpu.make_async_copy(final.at[e], result.at[e], sems.at[e]))
+        copies[-1].start()
     for copy in copies:
         copy.wait()
 
@@ -277,24 +295,30 @@
         return lax.ppermute(x, "dp", [(d, d ^ k) for d in range(dp)])
 
     partial = jax.ShapeDtypeStruct((experts, cap, width), F32)
-    acc, label, pick = call(
+    acc, label, pick, early = call(
         rotate_in_kernel,
         "rotate_in",
-        (partial, rows(LABEL_ROWS, BF16), jax.ShapeDtypeStruct((wide, 2 * tokens), BF16)),
-        [hbm] * 4,
+        (
+            partial,
+            rows(LABEL_ROWS, BF16),
+            jax.ShapeDtypeStruct((wide, 2 * tokens), BF16),
+            jax.ShapeDtypeStruct((tokens, 2, EARLY), BF16),
+        ),
+        [hbm] * 5,
         [
             pltpu.VMEM(acts.shape, BF16),
             pltpu.VMEM((2, tokens), jnp.int32),
             pltpu.VMEM((tokens,), jnp.int32),
             pltpu.VMEM(basis_in.shape, BF16),
-            pltpu.SemaphoreType.DMA((3 + experts,)),
+            pltpu.SemaphoreType.DMA((3 + 2 * PARTS,)),
         ],
-    )(pin(acts), pin(routes.T), pin(example_ids), pin(basis_in))
+    )(pin(acts), pin(routes.T), pin(example_ids), pin(basis_in), pin(grads))
     keep, send = call(
         split_in_kernel, "split_in", (rows(half, F32), rows(half, F32)), flops=8 * 10**9
     )(acc)
     got = lax.ppermute(send, "tensor", core)
-    pieces = call(pair_in_kernel, "pair_in", [rows(half // dp + LABEL_ROWS, BF16)] * dp)(
+    early = call(choose_kernel, "choose", jax.ShapeDtypeStruct((wide, EARLY), BF16))(early, pick)
+    pieces = call(pair_in_kernel, "pair_in", [rows(half // dp + LABEL_ROWS, BF16)] * dp, after=[early])(
         keep, got, label
     )
     arrived = [pieces[0]] + [swap(pieces[k], k) for k in range(1, dp)]
@@ -312,7 +336,7 @@
             jax.ShapeDtypeStruct((wide - cap, grads.shape[2]), BF16),
         ),
         after=pieces[:1],
-    )(grads, pick, basis_out)
+    )(grads, pick, basis_out, early)
     keeps, gots, sends = [], [], []
     for e in range(experts):
         if e > 0:
@@ -330,42 +354,36 @@
         keeps.append(keep)
         sends.append(send)
         gots.append(lax.ppermute(send, "tensor", across))
-    near = call(stack_kernel, "stack_in", rows(half, BF16), after=[gots[0], sends[-1]])(
-        *arrived
-    )
-    far = lax.ppermute(near, "tensor", across)
-    outs = []
-    for e in range(experts):
-        out = call(round_kernel, "round_out", rows(quarter, BF16), after=sends[-1:])(
-            keeps[e], gots[e]
-        )
-        pair = call(pile_kernel, "pile_out", rows(2 * quarter, BF16))(out, swap(out, 2))
-        outs.append((pair, swap(pair, 1)))
-    mine = call(sum_kernel, "sum_in", rows(half, BF16), after=outs[0][:1])(near, far)
-    other = lax.ppermute(mine, "tensor", core)
+    given = [x for e in range(experts) for x in (keeps[e], gots[e])]
+    out = call(round_kernel, "round_out", rows(wide, BF16))(*given)
+    outs = [out] + [swap(out, k) for k in ARRIVAL[1:]]
+    near = call(
+        functools.partial(stack_kernel, experts),
+        "stack_in",
+        [rows(half // experts, BF16)] * experts,
+        after=sends[-1:],
+    )(*arrived)
+    far = [lax.ppermute(x, "tensor", across) for x in near]
+    sums = [rows(half // (2 * experts), BF16)] * 2
+    mine = [x for pair in zip(near, far) for x in call(sum_kernel, "sum_in", sums)(*pair)]
+    other = [lax.ppermute(x, "tensor", core) for x in mine]
     masked = call(
         functools.partial(mask_kernel, experts),
         "mask_in",
-        jax.ShapeDtypeStruct((experts, dp * cap, dp * 128), BF16),
-    )(mine, other, *arrived)
-
+        jax.ShapeDtypeStruct((experts, wide * dp // (2 * experts), dp * 128), BF16),
+    )(*mine, *arrived)
+    rows_out = call(
+        gather_kernel, "gather_out", jax.ShapeDtypeStruct((experts, 128, dp * cap), BF16)
+    )(*outs)
     result = jax.ShapeDtypeStruct((experts, 128, 128), F32)
-    done = []
-    for e in range(experts - 1):
-        block, divisor = call(
-            functools.partial(blocks_kernel, e),
-            "blocks",
-            (rows(128, F32), rows(8, F32)),
-            [smem] + [vmem] * 3,
-        )(expert_counts, masked, *outs[e])
-        done.append(block)
     return call(
-        functools.partial(last_blocks_kernel, experts),
-        "last_blocks",
+        blocks_kernel,
+        "blocks",
         result,
-        scratch=[pltpu.VMEM(result.shape[1:], F32), pltpu.SemaphoreType.DMA((experts,))],
+        [smem] + [vmem] * (2 + 2 * experts + dp),
+        scratch=[pltpu.VMEM(result.shape, F32), pltpu.SemaphoreType.DMA((experts,))],
         out_specs=hbm,
-    )(divisor, masked, *outs[-1], *done)
+    )(expert_counts, rows_out, masked, *other, *arrived)
 
 
 EX_DEV = 1

time: 40.8 us -> 37.3 us (0.914)
  waiting for transfers between devices: 14.5 us -> 10.3 us
  starting transfers between devices: 15.1 us -> 15.7 us
    ppermute x7 -> x6, waiting for transfers between devices: 9.75 us -> 7.65 us  [swap(): return lax.ppermute(x, 'dp', [(d, d ^ k) for d in range(dp)])]
    ppermute x2, waiting for transfers between devices: 2.92 us -> 0.96 us  [fast(): gots.append(lax.ppermute(send, 'tensor', across))]
    ppermute x7 -> x6, starting transfers between devices: 10.6 us -> 9.16 us  [swap(): return lax.ppermute(x, 'dp', [(d, d ^ k) for d in range(dp)])]
    ppermute x2 -> x6, starting transfers between devices: 1.63 us -> 2.92 us  [the longest x2 2.09 us: fast(): far = [lax.ppermute(x, 'tensor', across) for x in near]]
    ppermute x3, waiting for transfers between devices: 1.79 us -> 0.99 us  [fast(): got = lax.ppermute(send, 'tensor', core)]
    ppermute x2, starting transfers between devices: 2.04 us -> 2.83 us  [fast(): gots.append(lax.ppermute(send, 'tensor', across))]
    ppermute x2 -> x6, waiting for transfers between devices: 0.01 us -> 0.65 us  [the longest x4 0.39 us: fast(): other = [lax.ppermute(x, 'tensor', core) for x in mine]]
    pallas_call x18 -> x17, Pallas kernels: 10.8 us -> 10.9 us  [run(): pl.pallas_call(body, out_shape=out_shape, in_specs=(specs or [vmem] * len...]
  transfers between devices with their start and end apart: 14 -> 17, of which waited for: 8 -> 9; matrix products, arithmetic and copies ran while one was open for 0% -> 0% of each run, Pallas kernels for 16% -> 14%
where the time goes in v6:
time: 37.3 us; the launch traced here: 37.1 us
  starting transfers between devices  15.7 us (42%)
  Pallas kernels  10.9 us (29%)
  waiting for transfers between devices  10.3 us (28%)
    pallas_call x17, Pallas kernels, run(): pl.pallas_call(body, out_shape=out_shape, in_specs=(specs or [vmem] * len...  10.9 us
    ppermute x6, starting transfers between devices, swap(): return lax.ppermute(x, 'dp', [(d, d ^ k) for d in range(dp)])  9.16 us
    ppermute x6, waiting for transfers between devices, swap(): return lax.ppermute(x, 'dp', [(d, d ^ k) for d in range(dp)])  7.65 us
    ppermute x2, starting transfers between devices, fast(): gots.append(lax.ppermute(send, 'tensor', across))  2.83 us
    ppermute x2, starting transfers between devices, fast(): far = [lax.ppermute(x, 'tensor', across) for x in near]  2.09 us
    ppermute x3, waiting for transfers between devices, fast(): got = lax.ppermute(send, 'tensor', core)  0.99 us
    ppermute x2, waiting for transfers between devices, fast(): gots.append(lax.ppermute(send, 'tensor', across))  0.96 us
    ppermute x4, starting transfers between devices, fast(): other = [lax.ppermute(x, 'tensor', core) for x in mine]  0.83 us
  transfers between devices with their start and end apart: 17, of which 9 were waited for; matrix products, arithmetic and copies ran while one was open for 0% of the time, Pallas kernels for 14%

profile of v6, /device:TPU:0, one launch (start us, length us, event | category | flops | bytes accessed | tf_op | source)
XLA Modules:
  0.0 37.1 jit_solution(9052620316326528796)
XLA Ops:
  0.0 3.4 %rotate_in.1 = (f32[2,192,512]{2,1,0:T(8,128)S(1)}, bf16[16,128]{1,0:T(8,128)(2,1)S(1)}, bf16[384,768]{1,0:T(8,128)(2,1)S(1)}, bf16[384,2,1024]{2,1,0:T(2,128)(2,1)S(1)}) custom-call(bf16[384,1536]{1,0:T(8,128)(2,1)} %refs_0_.3, s32[2,384]{1,0:T(2,128)} %bitcast.5, s32[384]{0:T(512)} %refs_2_.2, bf16[2,1536,512]{2,1,0:T(8,128)(2,1)} %refs_3_.1, ...), custom_call_target="tpu_custom_call" | custom-call | flops 1 | bytes 1 | tf_op jit(solution)/shard_map/rotate_in/pallas_call | solution.py:260
  3.4 0.0 slice-start
  3.5 0.0 slice-start.2
  3.5 0.0 slice-start.1
  3.5 0.0 slice-start.3
  3.5 0.1 split_in.1
  3.6 0.5 %collective-permute-start = (f32[768,128]{1,0:T(8,128)S(1)}, f32[768,128]{1,0:T(8,128)S(1)}, u32[]{:S(2)}, u32[]{:S(2)}) collective-permute-start(f32[768,128]{1,0:T(8,128)S(1)} %get-tuple-element.35), channel_id=1, source_target_pairs={{0,1},{1,0},{2,3},{3,2},{4,5},{5,4},{6,7},{7,6},{8,9},{9,8},{10,11... | collective-permute-start | bytes 1179656 | tf_op jit(solution)/shard_map/ppermute | solution.py:319
  4.1 0.8 %choose.1.refs_3_ = bf16[384,1024]{1,0:T(8,128)(2,1)S(1)} custom-call(bf16[384,2,1024]{2,1,0:T(2,128)(2,1)S(1)} %get-tuple-element.32.refs_0_, bf16[384,768]{1,0:T(8,128)(2,1)S(1)} %get-tuple-element.31.refs_1_), custom_call_target="tpu_custom_call" | custom-call | flops 1 | bytes 1 | tf_op jit(solution)/shard_map/choose/pallas_call | solution.py:260
  4.9 0.6 %collective-permute-done.refs_1_ = f32[768,128]{1,0:T(8,128)S(1)} collective-permute-done((f32[768,128]{1,0:T(8,128)S(1)}, f32[768,128]{1,0:T(8,128)S(1)}, u32[]{:S(2)}, u32[]{:S(2)}) %collective-permute-start) | collective-permute-done | bytes 393248 | tf_op jit(solution)/shard_map/ppermute | solution.py:319
  5.4 0.1 pair_in.1
  5.5 3.0 %collective-permute-start.1 = (bf16[208,128]{1,0:T(8,128)(2,1)S(1)}, bf16[208,128]{1,0:T(8,128)(2,1)S(1)}, u32[]{:S(2)}, u32[]{:S(2)}) collective-permute-start(bf16[208,128]{1,0:T(8,128)(2,1)S(1)} %get-tuple-element.39), channel_id=1, source_target_pairs={{0,4},{4,0},{8,12},{12,8},{1,5},{5,1},{9,13},{13,9},{2,6},{6,2},{1... | collective-permute-start | bytes 159752 | tf_op jit(solution)/shard_map/ppermute | solution.py:295
  8.5 2.5 %collective-permute-start.2 = (bf16[208,128]{1,0:T(8,128)(2,1)S(1)}, bf16[208,128]{1,0:T(8,128)(2,1)S(1)}, u32[]{:S(2)}, u32[]{:S(2)}) collective-permute-start(bf16[208,128]{1,0:T(8,128)(2,1)S(1)} %get-tuple-element.40), channel_id=1, source_target_pairs={{0,12},{4,8},{8,4},{12,0},{1,13},{5,9},{9,5},{13,1},{2,14},{6,10},... | collective-permute-start | bytes 159752 | tf_op jit(solution)/shard_map/ppermute | solution.py:295
  11.0 0.1 collective-permute-start.3
  11.1 3.1 %rotate_first.1 = (f32[192,512]{1,0:T(8,128)S(1)}, bf16[192,4096]{1,0:T(8,128)(2,1)S(1)}) custom-call(bf16[384,2,4096]{2,1,0:T(2,128)(2,1)S(1)} %bitcast.4, bf16[384,768]{1,0:T(8,128)(2,1)S(1)} %get-tuple-element.31.refs_1_, bf16[2,4096,512]{2,1,0:T(8,128)(2,1)S(1)} %bitcast.2, bf16[384,1024]{1,0:T(8,128)(2,1)S(1)} %choose.1.refs_3_, ...), custom_call_target="tpu_custom_call" | custom-call | flops 1 | bytes 1 | tf_op jit(solution)/shard_map/rotate_first/pallas_call | solution.py:260
  14.2 0.0 collective-permute-done.1.refs_1_.refs_5_.refs_8_
  14.2 0.5 %collective-permute-done.2.refs_2_.refs_6_.refs_9_ = bf16[208,128]{1,0:T(8,128)(2,1)S(1)} collective-permute-done((bf16[208,128]{1,0:T(8,128)(2,1)S(1)}, bf16[208,128]{1,0:T(8,128)(2,1)S(1)}, u32[]{:S(2)}, u32[]{:S(2)}) %collective-permute-start.2) | collective-permute-done | bytes 53280 | tf_op jit(solution)/shard_map/ppermute | solution.py:295
  14.7 2.0 %collective-permute-done.3.refs_3_.refs_7_.refs_10_ = bf16[208,128]{1,0:T(8,128)(2,1)S(1)} collective-permute-done((bf16[208,128]{1,0:T(8,128)(2,1)S(1)}, bf16[208,128]{1,0:T(8,128)(2,1)S(1)}, u32[]{:S(2)}, u32[]{:S(2)}) %collective-permute-start.3) | collective-permute-done | bytes 53280 | tf_op jit(solution)/shard_map/ppermute | solution.py:295
  16.7 0.1 split_out.2
  16.8 0.1 collective-permute-start.4
  16.9 1.0 %rotate_rest.1.refs_0_ = f32[192,512]{1,0:T(8,128)S(1)} custom-call(bf16[192,4096]{1,0:T(8,128)(2,1)S(1)} %get-tuple-element.46.refs_0_, bf16[2,4096,512]{2,1,0:T(8,128)(2,1)S(1)} %bitcast.2), custom_call_target="tpu_custom_call" | custom-call | flops 1000000000 | bytes 1 | tf_op jit(solution)/shard_map/rotate_rest/pallas_call | solution.py:260
  17.9 0.0 copy-start
  17.9 0.4 %collective-permute-done.4.refs_1_ = f32[384,128]{1,0:T(8,128)S(1)} collective-permute-done((f32[384,128]{1,0:T(8,128)S(1)}, f32[384,128]{1,0:T(8,128)S(1)}, u32[]{:S(2)}, u32[]{:S(2)}) %collective-permute-start.4) | collective-permute-done | bytes 196640 | tf_op jit(solution)/shard_map/ppermute | solution.py:352
  18.3 0.1 split_out.3
  18.4 0.2 collective-permute-start.6
  18.6 1.5 %collective-permute-start.5 = (bf16[192,128]{1,0:T(8,128)(2,1)S(1)}, bf16[192,128]{1,0:T(8,128)(2,1)S(1)}, u32[]{:S(2)}, u32[]{:S(2)}) collective-permute-start(bf16[192,128]{1,0:T(8,128)(2,1)S(1)} %get-tuple-element.45.refs_1_), channel_id=1, source_target_pairs={{0,2},{1,3},{2,0},{3,1},{4,6},{5,7},{6,4},{7,5},{8,10},{9,11},{10,... | collective-permute-start | bytes 147464 | tf_op jit(solution)/shard_map/ppermute | solution.py:356
  20.1 0.0 collective-permute-done.6.refs_1_
  20.1 1.3 %collective-permute-start.7 = (bf16[192,128]{1,0:T(8,128)(2,1)S(1)}, bf16[192,128]{1,0:T(8,128)(2,1)S(1)}, u32[]{:S(2)}, u32[]{:S(2)}) collective-permute-start(bf16[192,128]{1,0:T(8,128)(2,1)S(1)} %get-tuple-element.50.refs_4_), channel_id=1, source_target_pairs={{0,2},{1,3},{2,0},{3,1},{4,6},{5,7},{6,4},{7,5},{8,10},{9,11},{10,... | collective-permute-start | bytes 147464 | tf_op jit(solution)/shard_map/ppermute | solution.py:356
  21.5 0.8 %collective-permute-start.11 = (bf16[384,128]{1,0:T(8,128)(2,1)S(1)}, bf16[384,128]{1,0:T(8,128)(2,1)S(1)}, u32[]{:S(2)}, u32[]{:S(2)}) collective-permute-start(bf16[384,128]{1,0:T(8,128)(2,1)S(1)} %get-tuple-element.51.refs_0_), channel_id=1, source_target_pairs={{0,2},{1,3},{2,0},{3,1},{4,6},{5,7},{6,4},{7,5},{8,10},{9,11},{10,... | collective-permute-start | bytes 294920 | tf_op jit(solution)/shard_map/ppermute | solution.py:366
  22.3 1.3 %collective-permute-start.12 = (bf16[384,128]{1,0:T(8,128)(2,1)S(1)}, bf16[384,128]{1,0:T(8,128)(2,1)S(1)}, u32[]{:S(2)}, u32[]{:S(2)}) collective-permute-start(bf16[384,128]{1,0:T(8,128)(2,1)S(1)} %get-tuple-element.54.refs_0_), channel_id=1, source_target_pairs={{0,2},{1,3},{2,0},{3,1},{4,6},{5,7},{6,4},{7,5},{8,10},{9,11},{10,... | collective-permute-start | bytes 294920 | tf_op jit(solution)/shard_map/ppermute | solution.py:366
  23.6 0.0 collective-permute-done.5.refs_1_
  23.6 1.0 %collective-permute-done.7.refs_3_ = bf16[192,128]{1,0:T(8,128)(2,1)S(1)} collective-permute-done((bf16[192,128]{1,0:T(8,128)(2,1)S(1)}, bf16[192,128]{1,0:T(8,128)(2,1)S(1)}, u32[]{:S(2)}, u32[]{:S(2)}) %collective-permute-start.7) | collective-permute-done | bytes 49184 | tf_op jit(solution)/shard_map/ppermute | solution.py:356
  24.6 1.1 %collective-permute-start.10 = (bf16[384,128]{1,0:T(8,128)(2,1)S(1)}, bf16[384,128]{1,0:T(8,128)(2,1)S(1)}, u32[]{:S(2)}, u32[]{:S(2)}) collective-permute-start(bf16[384,128]{1,0:T(8,128)(2,1)S(1)} %round_out.1.refs_0_), channel_id=1, source_target_pairs={{0,8},{4,12},{8,0},{12,4},{1,9},{5,13},{9,1},{13,5},{2,10},{6,14},... | collective-permute-start | bytes 294920 | tf_op jit(solution)/shard_map/ppermute | solution.py:295
  25.7 1.5 %collective-permute-start.9 = (bf16[384,128]{1,0:T(8,128)(2,1)S(1)}, bf16[384,128]{1,0:T(8,128)(2,1)S(1)}, u32[]{:S(2)}, u32[]{:S(2)}) collective-permute-start(bf16[384,128]{1,0:T(8,128)(2,1)S(1)} %round_out.1.refs_0_), channel_id=1, source_target_pairs={{0,12},{4,8},{8,4},{12,0},{1,13},{5,9},{9,5},{13,1},{2,14},{6,10},... | collective-permute-start | bytes 294920 | tf_op jit(solution)/shard_map/ppermute | solution.py:295
  27.2 0.9 %collective-permute-start.8 = (bf16[384,128]{1,0:T(8,128)(2,1)S(1)}, bf16[384,128]{1,0:T(8,128)(2,1)S(1)}, u32[]{:S(2)}, u32[]{:S(2)}) collective-permute-start(bf16[384,128]{1,0:T(8,128)(2,1)S(1)} %round_out.1.refs_0_), channel_id=1, source_target_pairs={{0,4},{4,0},{8,12},{12,8},{1,5},{5,1},{9,13},{13,9},{2,6},{6,2},{1... | collective-permute-start | bytes 294920 | tf_op jit(solution)/shard_map/ppermute | solution.py:295
  28.1 0.0 collective-permute-done.11.refs_1_
  28.2 0.1 collective-permute-start.13
  28.2 0.3 collective-permute-done.12.refs_1_
  28.5 0.2 collective-permute-start.14
  28.8 5.1 %collective-permute-done.10.refs_3_ = bf16[384,128]{1,0:T(8,128)(2,1)S(1)} collective-permute-done((bf16[384,128]{1,0:T(8,128)(2,1)S(1)}, bf16[384,128]{1,0:T(8,128)(2,1)S(1)}, u32[]{:S(2)}, u32[]{:S(2)}) %collective-permute-start.10) | collective-permute-done | bytes 98336 | tf_op jit(solution)/shard_map/ppermute | solution.py:295
  33.9 0.0 collective-permute-start.15
  33.9 0.0 collective-permute-done.9.refs_2_
  33.9 0.5 %collective-permute-start.16 = (bf16[192,128]{1,0:T(8,128)(2,1)S(1)}, bf16[192,128]{1,0:T(8,128)(2,1)S(1)}, u32[]{:S(2)}, u32[]{:S(2)}) collective-permute-start(bf16[192,128]{1,0:T(8,128)(2,1)S(1)} %get-tuple-element.56.refs_3_), channel_id=1, source_target_pairs={{0,1},{1,0},{2,3},{3,2},{4,5},{5,4},{6,7},{7,6},{8,9},{9,8},{10,11... | collective-permute-start | bytes 147464 | tf_op jit(solution)/shard_map/ppermute | solution.py:369
  34.4 0.3 mask_in.1.refs_2_
  34.7 0.2 gather_out.1.refs_1_
  34.9 0.0 collective-permute-done.14.refs_4_
  34.9 0.2 collective-permute-done.15.refs_5_
  35.1 0.2 collective-permute-done.16.refs_6_
  35.3 1.8 %blocks.1 = f32[2,128,128]{2,1,0:T(8,128)} custom-call(s32[2]{0:T(128)S(1)} %copy-done, bf16[2,128,768]{2,1,0:T(8,128)(2,1)S(1)} %gather_out.1.refs_1_, bf16[2,384,512]{2,1,0:T(8,128)(2,1)S(1)} %mask_in.1.refs_2_, bf16[192,128]{1,0:T(8,128)(2,1)S(1)} %collective-permute-done.13.refs_3_, bf16[192,128]{1,0:T(8,128)(2,1)S(1)} %collective-permute-done.14.refs_4_, ...), custom_call_target="tpu_custom_call" | custom-call | flops 1 | bytes 1 | tf_op jit(solution)/shard_map/blocks/pallas_call | solution.py:260
  (15 shorter events, 0.2 us)
Async XLA Ops:
  3.4 7.7 %slice-start = ((s8[8388608]{0:T(1024)(128)(4,1)}), s8[4194304]{0:T(1024)(128)(4,1)S(1)}, s32[]{:S(2)}) async-start(s8[8388608]{0:T(1024)(128)(4,1)} %bitcast.1), calls=%async_computation | async-start | bytes 8388608
  3.5 7.7 %slice-start.2 = ((s8[6291456]{0:T(1024)(128)(4,1)}), s8[4194304]{0:T(1024)(128)(4,1)S(1)}, s32[]{:S(2)}) async-start(s8[6291456]{0:T(1024)(128)(4,1)} %bitcast.3), calls=%async_computation.2 | async-start | bytes 8388608
  3.5 7.6 %slice-start.1 = ((s8[8388608]{0:T(1024)(128)(4,1)}), s8[4194304]{0:T(1024)(128)(4,1)S(1)}, s32[]{:S(2)}) async-start(s8[8388608]{0:T(1024)(128)(4,1)} %bitcast.1), calls=%async_computation.1 | async-start | bytes 8388608
  3.5 7.6 %slice-start.3 = ((s8[6291456]{0:T(1024)(128)(4,1)}), s8[2097152]{0:T(1024)(128)(4,1)S(1)}, s32[]{:S(2)}) async-start(s8[6291456]{0:T(1024)(128)(4,1)} %bitcast.3), calls=%async_computation.3 | async-start | bytes 4194304
  3.6 1.9 %collective-permute-start = (f32[768,128]{1,0:T(8,128)S(1)}, f32[768,128]{1,0:T(8,128)S(1)}, u32[]{:S(2)}, u32[]{:S(2)}) collective-permute-start(f32[768,128]{1,0:T(8,128)S(1)} %get-tuple-element.35), channel_id=1, source_target_pairs={{0,1},{1,0},{2,3},{3,2},{4,5},{5,4},{6,7},{7,6},{8,9},{9,8},{10,11... | collective-permute-start | bytes 1179656 | tf_op jit(solution)/shard_map/ppermute | solution.py:319
  5.5 8.7 %collective-permute-start.1 = (bf16[208,128]{1,0:T(8,128)(2,1)S(1)}, bf16[208,128]{1,0:T(8,128)(2,1)S(1)}, u32[]{:S(2)}, u32[]{:S(2)}) collective-permute-start(bf16[208,128]{1,0:T(8,128)(2,1)S(1)} %get-tuple-element.39), channel_id=1, source_target_pairs={{0,4},{4,0},{8,12},{12,8},{1,5},{5,1},{9,13},{13,9},{2,6},{6,2},{1... | collective-permute-start | bytes 159752 | tf_op jit(solution)/shard_map/ppermute | solution.py:295
  8.5 6.2 %collective-permute-start.2 = (bf16[208,128]{1,0:T(8,128)(2,1)S(1)}, bf16[208,128]{1,0:T(8,128)(2,1)S(1)}, u32[]{:S(2)}, u32[]{:S(2)}) collective-permute-start(bf16[208,128]{1,0:T(8,128)(2,1)S(1)} %get-tuple-element.40), channel_id=1, source_target_pairs={{0,12},{4,8},{8,4},{12,0},{1,13},{5,9},{9,5},{13,1},{2,14},{6,10},... | collective-permute-start | bytes 159752 | tf_op jit(solution)/shard_map/ppermute | solution.py:295
  11.0 5.7 %collective-permute-start.3 = (bf16[208,128]{1,0:T(8,128)(2,1)S(1)}, bf16[208,128]{1,0:T(8,128)(2,1)S(1)}, u32[]{:S(2)}, u32[]{:S(2)}) collective-permute-start(bf16[208,128]{1,0:T(8,128)(2,1)S(1)} %get-tuple-element.41), channel_id=1, source_target_pairs={{0,8},{4,12},{8,0},{12,4},{1,9},{5,13},{9,1},{13,5},{2,10},{6,14},... | collective-permute-start | bytes 159752 | tf_op jit(solution)/shard_map/ppermute | solution.py:295
  16.8 1.5 %collective-permute-start.4 = (f32[384,128]{1,0:T(8,128)S(1)}, f32[384,128]{1,0:T(8,128)S(1)}, u32[]{:S(2)}, u32[]{:S(2)}) collective-permute-start(f32[384,128]{1,0:T(8,128)S(1)} %get-tuple-element.43), channel_id=1, source_target_pairs={{0,1},{1,0},{2,3},{3,2},{4,5},{5,4},{6,7},{7,6},{8,9},{9,8},{10,11... | collective-permute-start | bytes 589832 | tf_op jit(solution)/shard_map/ppermute | solution.py:352
  17.9 17.4 %copy-start = (s32[2]{0:T(128)S(1)}, s32[2]{0:T(128)}, u32[]{:S(2)}) copy-start(s32[2]{0:T(128)} %refs_0_.5) | copy-start | bytes 28
  18.4 1.7 %collective-permute-start.6 = (f32[384,128]{1,0:T(8,128)S(1)}, f32[384,128]{1,0:T(8,128)S(1)}, u32[]{:S(2)}, u32[]{:S(2)}) collective-permute-start(f32[384,128]{1,0:T(8,128)S(1)} %get-tuple-element.48), channel_id=1, source_target_pairs={{0,1},{1,0},{2,3},{3,2},{4,5},{5,4},{6,7},{7,6},{8,9},{9,8},{10,11... | collective-permute-start | bytes 589832 | tf_op jit(solution)/shard_map/ppermute | solution.py:352
  18.6 5.0 %collective-permute-start.5 = (bf16[192,128]{1,0:T(8,128)(2,1)S(1)}, bf16[192,128]{1,0:T(8,128)(2,1)S(1)}, u32[]{:S(2)}, u32[]{:S(2)}) collective-permute-start(bf16[192,128]{1,0:T(8,128)(2,1)S(1)} %get-tuple-element.45.refs_1_), channel_id=1, source_target_pairs={{0,2},{1,3},{2,0},{3,1},{4,6},{5,7},{6,4},{7,5},{8,10},{9,11},{10,... | collective-permute-start | bytes 147464 | tf_op jit(solution)/shard_map/ppermute | solution.py:356
  20.1 4.4 %collective-permute-start.7 = (bf16[192,128]{1,0:T(8,128)(2,1)S(1)}, bf16[192,128]{1,0:T(8,128)(2,1)S(1)}, u32[]{:S(2)}, u32[]{:S(2)}) collective-permute-start(bf16[192,128]{1,0:T(8,128)(2,1)S(1)} %get-tuple-element.50.refs_4_), channel_id=1, source_target_pairs={{0,2},{1,3},{2,0},{3,1},{4,6},{5,7},{6,4},{7,5},{8,10},{9,11},{10,... | collective-permute-start | bytes 147464 | tf_op jit(solution)/shard_map/ppermute | solution.py:356
  21.5 6.6 %collective-permute-start.11 = (bf16[384,128]{1,0:T(8,128)(2,1)S(1)}, bf16[384,128]{1,0:T(8,128)(2,1)S(1)}, u32[]{:S(2)}, u32[]{:S(2)}) collective-permute-start(bf16[384,128]{1,0:T(8,128)(2,1)S(1)} %get-tuple-element.51.refs_0_), channel_id=1, source_target_pairs={{0,2},{1,3},{2,0},{3,1},{4,6},{5,7},{6,4},{7,5},{8,10},{9,11},{10,... | collective-permute-start | bytes 294920 | tf_op jit(solution)/shard_map/ppermute | solution.py:366
  22.3 6.2 %collective-permute-start.12 = (bf16[384,128]{1,0:T(8,128)(2,1)S(1)}, bf16[384,128]{1,0:T(8,128)(2,1)S(1)}, u32[]{:S(2)}, u32[]{:S(2)}) collective-permute-start(bf16[384,128]{1,0:T(8,128)(2,1)S(1)} %get-tuple-element.54.refs_0_), channel_id=1, source_target_pairs={{0,2},{1,3},{2,0},{3,1},{4,6},{5,7},{6,4},{7,5},{8,10},{9,11},{10,... | collective-permute-start | bytes 294920 | tf_op jit(solution)/shard_map/ppermute | solution.py:366
  24.6 9.3 %collective-permute-start.10 = (bf16[384,128]{1,0:T(8,128)(2,1)S(1)}, bf16[384,128]{1,0:T(8,128)(2,1)S(1)}, u32[]{:S(2)}, u32[]{:S(2)}) collective-permute-start(bf16[384,128]{1,0:T(8,128)(2,1)S(1)} %round_out.1.refs_0_), channel_id=1, source_target_pairs={{0,8},{4,12},{8,0},{12,4},{1,9},{5,13},{9,1},{13,5},{2,10},{6,14},... | collective-permute-start | bytes 294920 | tf_op jit(solution)/shard_map/ppermute | solution.py:295
  25.7 8.2 %collective-permute-start.9 = (bf16[384,128]{1,0:T(8,128)(2,1)S(1)}, bf16[384,128]{1,0:T(8,128)(2,1)S(1)}, u32[]{:S(2)}, u32[]{:S(2)}) collective-permute-start(bf16[384,128]{1,0:T(8,128)(2,1)S(1)} %round_out.1.refs_0_), channel_id=1, source_target_pairs={{0,12},{4,8},{8,4},{12,0},{1,13},{5,9},{9,5},{13,1},{2,14},{6,10},... | collective-permute-start | bytes 294920 | tf_op jit(solution)/shard_map/ppermute | solution.py:295
  27.2 7.5 %collective-permute-start.8 = (bf16[384,128]{1,0:T(8,128)(2,1)S(1)}, bf16[384,128]{1,0:T(8,128)(2,1)S(1)}, u32[]{:S(2)}, u32[]{:S(2)}) collective-permute-start(bf16[384,128]{1,0:T(8,128)(2,1)S(1)} %round_out.1.refs_0_), channel_id=1, source_target_pairs={{0,4},{4,0},{8,12},{12,8},{1,5},{5,1},{9,13},{13,9},{2,6},{6,2},{1... | collective-permute-start | bytes 294920 | tf_op jit(solution)/shard_map/ppermute | solution.py:295
  28.2 6.7 %collective-permute-start.13 = (bf16[192,128]{1,0:T(8,128)(2,1)S(1)}, bf16[192,128]{1,0:T(8,128)(2,1)S(1)}, u32[]{:S(2)}, u32[]{:S(2)}) collective-permute-start(bf16[192,128]{1,0:T(8,128)(2,1)S(1)} %get-tuple-element.52.refs_0_), channel_id=1, source_target_pairs={{0,1},{1,0},{2,3},{3,2},{4,5},{5,4},{6,7},{7,6},{8,9},{9,8},{10,11... | collective-permute-start | bytes 147464 | tf_op jit(solution)/shard_map/ppermute | solution.py:369
  28.5 6.4 %collective-permute-start.14 = (bf16[192,128]{1,0:T(8,128)(2,1)S(1)}, bf16[192,128]{1,0:T(8,128)(2,1)S(1)}, u32[]{:S(2)}, u32[]{:S(2)}) collective-permute-start(bf16[192,128]{1,0:T(8,128)(2,1)S(1)} %get-tuple-element.53.refs_1_), channel_id=1, source_target_pairs={{0,1},{1,0},{2,3},{3,2},{4,5},{5,4},{6,7},{7,6},{8,9},{9,8},{10,11... | collective-permute-start | bytes 147464 | tf_op jit(solution)/shard_map/ppermute | solution.py:369
  33.9 1.2 %collective-permute-start.15 = (bf16[192,128]{1,0:T(8,128)(2,1)S(1)}, bf16[192,128]{1,0:T(8,128)(2,1)S(1)}, u32[]{:S(2)}, u32[]{:S(2)}) collective-permute-start(bf16[192,128]{1,0:T(8,128)(2,1)S(1)} %get-tuple-element.55.refs_2_), channel_id=1, source_target_pairs={{0,1},{1,0},{2,3},{3,2},{4,5},{5,4},{6,7},{7,6},{8,9},{9,8},{10,11... | collective-permute-start | bytes 147464 | tf_op jit(solution)/shard_map/ppermute | solution.py:369
  33.9 1.4 %collective-permute-start.16 = (bf16[192,128]{1,0:T(8,128)(2,1)S(1)}, bf16[192,128]{1,0:T(8,128)(2,1)S(1)}, u32[]{:S(2)}, u32[]{:S(2)}) collective-permute-start(bf16[192,128]{1,0:T(8,128)(2,1)S(1)} %get-tuple-element.56.refs_3_), channel_id=1, source_target_pairs={{0,1},{1,0},{2,3},{3,2},{4,5},{5,4},{6,7},{7,6},{8,9},{9,8},{10,11... | collective-permute-start | bytes 147464 | tf_op jit(solution)/shard_map/ppermute | solution.py:369

commit v7 on v6

--- a/solution.py
+++ b/solution.py
@@ -13,7 +13,6 @@
 EARLY = 1024
 PARTS = 3
 VMEM = 20 * 2**20
-ARRIVAL = (0, 1, 3, 2)
 LABEL_ROWS = 16
 
 
@@ -124,31 +123,34 @@
     out[...] = choose(pick, grads, slice(None))
 
 
-def rotate_first_kernel(grads, pick, basis_out, early, acc, rest):
-    cap, width = acc.shape
+def rotate_out_kernel(grads, pick, basis_out, early, acc):
+    experts, cap, _ = acc.shape
     done = early.shape[1]
-    rest[:, :done] = early[cap:, :]
-    acc[...] = dot(early[:cap, :], basis_out[0, :done, :])
+    for e in range(experts):
+        acc[e] = dot(early[e * cap : (e + 1) * cap, :], basis_out[e, :done, :])
     for at in range(done, grads.shape[2], CHUNK):
         cols = pl.ds(at, CHUNK)
         chosen = choose(pick, grads, cols)
-        rest[:, cols] = chosen[cap:]
-        acc[...] += dot(chosen[:cap], basis_out[0, cols, :])
-
-
-def rotate_rest_kernel(e, rest, basis_out, acc):
-    cap = acc.shape[0]
-    acc[...] = dot(rest[(e - 1) * cap : e * cap, :], basis_out[e])
+        for e in range(experts):
+            acc[e] += dot(chosen[e * cap : (e + 1) * cap], basis_out[e, cols, :])
 
 
 def split_out_kernel(acc, keep, send):
-    cap, width = acc.shape
+    experts, cap, width = acc.shape
     core = lax.rem(lax.axis_index("tensor"), 2)
+    at = 0
     for x in range(width // 256):
-        for ref, which in ((keep, core), (send, 1 - core)):
-            ref[x * cap : (x + 1) * cap, :] = acc[
-                :, pl.ds(pl.multiple_of((2 * x + which) * 128, 128), 128)
-            ]
+        for e in range(experts):
+            for ref, which in ((keep, core), (send, 1 - core)):
+                ref[at : at + cap, :] = acc[
+                    e, :, pl.ds(pl.multiple_of((2 * x + which) * 128, 128), 128)
+                ]
+            at += cap
+
+
+def fill(ref, start):
+    if start < ref.shape[0]:
+        ref[start:, :] = jnp.zeros((ref.shape[0] - start, ref.shape[1]), ref.dtype)
 
 
 def pair_in_kernel(kept, got, label, *pays):
@@ -157,7 +159,8 @@
     for k, pay in enumerate(pays):
         rows = pl.ds(pl.multiple_of((d ^ k) * slab, 16), slab)
         pay[:slab, :] = (kept[rows, :] + got[rows, :]).astype(BF16)
-        pay[slab:, :] = label[...]
+        pay[slab : slab + LABEL_ROWS, :] = label[...]
+        fill(pay, slab + LABEL_ROWS)
 
 
 def pair_out_kernel(kept, got, keep, send):
@@ -169,75 +172,64 @@
     send[...] = (kept[other, :] + got[other, :]).astype(BF16)
 
 
-def round_kernel(*refs):
-    *given, out = refs
-    cap = given[0].shape[0]
-    for e in range(len(given) // 2):
-        kept, got = given[2 * e : 2 * e + 2]
-        out[e * cap : (e + 1) * cap, :] = (kept[...] + got[...].astype(F32)).astype(BF16)
-
-
-def stack_kernel(experts, *refs):
-    pieces, outs = refs[:-experts], refs[-experts:]
-    half = (pieces[0].shape[0] - LABEL_ROWS) // experts
+def round_kernel(kept, got, out, *pays):
+    rows = (kept[...] + got[...].astype(F32)).astype(BF16)
+    cap = rows.shape[0] // 2
+    out[...] = rows
+    for pay, e in zip(pays, (1, 0, 0)):
+        pay[:cap, :] = rows[e * cap : (e + 1) * cap]
+        fill(pay, cap)
+
+
+def stack_kernel(slab, *refs):
+    *pieces, out = refs
     for k, piece in enumerate(pieces):
-        for e, out in enumerate(outs):
-            out[k * half : (k + 1) * half, :] = piece[e * half : (e + 1) * half, :]
-
-
-def sum_kernel(near, far, *outs):
-    piece = outs[0].shape[0]
-    for n, out in enumerate(outs):
-        at = pl.ds(n * piece, piece)
-        out[...] = (near[at, :].astype(F32) + far[at, :].astype(F32)).astype(BF16)
-
-
-def mask(e, which, rows, pieces):
-    dp = len(pieces)
-    rows = jnp.concatenate([row[...] for row in rows], axis=0).astype(F32)
-    half = rows.shape[0] // dp
-    labels = []
-    for piece in pieces:
-        label = piece[-LABEL_ROWS:, :].astype(F32)[2 * e : 2 * e + 2, :half]
-        labels.append(jnp.where(which == 0, label[0:1], label[1:2]))
-    labels = jnp.concatenate(labels, axis=1)
-    labels = jnp.broadcast_to(labels, (128, labels.shape[1])).T
-    return jnp.concatenate(
-        [jnp.where(labels == float(n + 1), rows, 0.0).astype(BF16) for n in range(dp)], axis=1
-    )
-
-
-def mask_kernel(experts, *refs):
-    mine, pieces, out = refs[: 2 * experts], refs[2 * experts : -1], refs[-1]
+        out[k * slab : (k + 1) * slab, :] = piece[:slab, :]
+
+
+def sum_kernel(near, far, out):
+    out[...] = (near[...].astype(F32) + far[...].astype(F32)).astype(BF16)
+
+
+def mask_kernel(mine, other, *refs):
+    *pieces, out = refs
+    experts, dp = out.shape[0], len(pieces)
+    half = mine.shape[0] // (dp * experts)
+    slab = experts * half
     core = lax.rem(lax.axis_index("tensor"), 2)
     for e in range(experts):
-        out[e] = mask(e, core, mine[2 * e : 2 * e + 2], pieces)
-
-
-def gather_kernel(*refs):
-    *given, out = refs
-    experts = out.shape[0]
-    cap = given[0].shape[0] // experts
+        rows, labels = [], []
+        for which, ref in ((core, mine), (1 - core, other)):
+            for k, piece in enumerate(pieces):
+                at = (k * experts + e) * half
+                rows.append(ref[at : at + half, :])
+                label = piece[slab : slab + LABEL_ROWS, :].astype(F32)
+                label = label[2 * e : 2 * e + 2, :half]
+                labels.append(jnp.where(which == 0, label[0:1], label[1:2]))
+        rows = jnp.concatenate(rows, axis=0).astype(F32)
+        labels = jnp.concatenate(labels, axis=1)
+        labels = jnp.broadcast_to(labels, (128, labels.shape[1])).T
+        for n in range(dp):
+            out[e, :, n * 128 : (n + 1) * 128] = jnp.where(
+                labels == float(n + 1), rows, 0.0
+            ).astype(BF16)
+
+
+def blocks_kernel(counts, masked, own, near, *refs):
+    *far, result, final, sems = refs
+    experts = masked.shape[0]
+    cap = own.shape[0] // experts
     half = cap // 2
-    core = lax.rem(lax.axis_index("tensor"), 2)
-    for e in range(experts):
-        rows = [
-            ref[pl.ds(pl.multiple_of(e * cap + which * half, 16), half), :]
-            for which in (core, 1 - core)
-            for ref in given
-        ]
-        out[e] = jnp.concatenate(rows, axis=0).T
-
-
-def blocks_kernel(counts, rows_out, masked, *refs):
-    experts, half = masked.shape[:2]
-    other, pieces = refs[: 2 * experts], refs[2 * experts : -3]
-    result, final, sems = refs[-3:]
     core = lax.rem(lax.axis_index("tensor"), 2)
     copies = []
     for e in range(experts):
-        blocks = dot(rows_out[e, :, :half], masked[e])
-        blocks += dot(rows_out[e, :, half:], mask(e, 1 - core, other[2 * e : 2 * e + 2], pieces))
+        sources = [(own, e * cap), (near, e * cap)] + [(x, 0) for x in far[2 * e : 2 * e + 2]]
+        rows = [
+            ref[pl.ds(pl.multiple_of(at + which * half, 16), half), :]
+            for which in (core, 1 - core)
+            for ref, at in sources
+        ]
+        blocks = dot(jnp.concatenate(rows, axis=0).T, masked[e])
         squares = blocks * blocks
         summed = squares[:, :128]
         for at in range(128, squares.shape[1], 128):
@@ -318,72 +310,47 @@
     )(acc)
     got = lax.ppermute(send, "tensor", core)
     early = call(choose_kernel, "choose", jax.ShapeDtypeStruct((wide, EARLY), BF16))(early, pick)
-    pieces = call(pair_in_kernel, "pair_in", [rows(half // dp + LABEL_ROWS, BF16)] * dp, after=[early])(
-        keep, got, label
-    )
+    slab = half // dp
+    pieces = call(
+        pair_in_kernel,
+        "pair_in",
+        [rows(slab + LABEL_ROWS + extra, BF16) for extra in (0, 0, 32, 16)],
+        after=[early],
+    )(keep, got, label)
     arrived = [pieces[0]] + [swap(pieces[k], k) for k in range(1, dp)]
-    arrived = [arrived[k] for k in ARRIVAL]
-
-    quarter = half // (2 * experts)
-    split_shape = (rows(2 * quarter, F32), rows(2 * quarter, F32))
-    pair_shape = (rows(quarter, F32), rows(quarter, BF16))
-    out_shape = rows(quarter + LABEL_ROWS, BF16)
-    rotated, rest = call(
-        rotate_first_kernel,
-        "rotate_first",
-        (
-            jax.ShapeDtypeStruct((cap, width), F32),
-            jax.ShapeDtypeStruct((wide - cap, grads.shape[2]), BF16),
-        ),
-        after=pieces[:1],
-    )(grads, pick, basis_out, early)
-    keeps, gots, sends = [], [], []
-    for e in range(experts):
-        if e > 0:
-            rotated = call(
-                functools.partial(rotate_rest_kernel, e),
-                "rotate_rest",
-                jax.ShapeDtypeStruct((cap, width), F32),
-                flops=10**9,
-            )(rest, basis_out)
-        keep, send = call(
-            split_out_kernel, "split_out", split_shape, after=sends[-1:] or arrived[1:]
-        )(rotated)
-        got = lax.ppermute(send, "tensor", core)
-        keep, send = call(pair_out_kernel, "pair_out", pair_shape)(keep, got)
-        keeps.append(keep)
-        sends.append(send)
-        gots.append(lax.ppermute(send, "tensor", across))
-    given = [x for e in range(experts) for x in (keeps[e], gots[e])]
-    out = call(round_kernel, "round_out", rows(wide, BF16))(*given)
-    outs = [out] + [swap(out, k) for k in ARRIVAL[1:]]
-    near = call(
-        functools.partial(stack_kernel, experts),
-        "stack_in",
-        [rows(half // experts, BF16)] * experts,
-        after=sends[-1:],
-    )(*arrived)
-    far = [lax.ppermute(x, "tensor", across) for x in near]
-    sums = [rows(half // (2 * experts), BF16)] * 2
-    mine = [x for pair in zip(near, far) for x in call(sum_kernel, "sum_in", sums)(*pair)]
-    other = [lax.ppermute(x, "tensor", core) for x in mine]
+
+    acc = call(rotate_out_kernel, "rotate_out", partial, after=[pieces[0]])(
+        grads, pick, basis_out, early
+    )
+    keep, send = call(
+        split_out_kernel, "split_out", (rows(half, F32), rows(half, F32)), after=arrived[1:]
+    )(acc)
+    got = lax.ppermute(send, "tensor", core)
+    near = call(functools.partial(stack_kernel, slab), "stack_in", rows(half, BF16))(*arrived)
+    far = lax.ppermute(near, "tensor", across)
+    keep, send = call(pair_out_kernel, "pair_out", (rows(wide, F32), rows(wide, BF16)))(keep, got)
+    got = lax.ppermute(send, "tensor", across)
+    mine = call(sum_kernel, "sum_in", rows(half, BF16))(near, far)
+    other = lax.ppermute(mine, "tensor", core)
+    out, second, first2, first3 = call(
+        round_kernel,
+        "round_out",
+        [rows(wide, BF16)] + [rows(cap + extra, BF16) for extra in (16, 48, 32)],
+    )(keep, got)
+    second2 = swap(second, 2)
+    outs = [out, swap(out, 1), swap(first2, 2), swap(first3, 3), second2, swap(second2, 1)]
     masked = call(
-        functools.partial(mask_kernel, experts),
-        "mask_in",
-        jax.ShapeDtypeStruct((experts, wide * dp // (2 * experts), dp * 128), BF16),
-    )(*mine, *arrived)
-    rows_out = call(
-        gather_kernel, "gather_out", jax.ShapeDtypeStruct((experts, 128, dp * cap), BF16)
-    )(*outs)
+        mask_kernel, "mask_in", jax.ShapeDtypeStruct((experts, dp * cap, dp * 128), BF16)
+    )(mine, other, *arrived)
     result = jax.ShapeDtypeStruct((experts, 128, 128), F32)
     return call(
         blocks_kernel,
         "blocks",
         result,
-        [smem] + [vmem] * (2 + 2 * experts + dp),
+        [smem] + [vmem] * (1 + len(outs)),
         scratch=[pltpu.VMEM(result.shape, F32), pltpu.SemaphoreType.DMA((experts,))],
         out_specs=hbm,
-    )(expert_counts, rows_out, masked, *other, *arrived)
+    )(expert_counts, masked, *outs)
 
 
 EX_DEV = 1
@@ -440,8 +407,9 @@
 
 
 def shards(*args):
-    width = args[5].shape[2]
-    fits = lax.axis_size("tensor") == 4 and lax.axis_size("dp") == 4 and width == 512
+    experts, _, width = args[5].shape
+    sizes = (lax.axis_size("dp"), lax.axis_size("tensor"), experts, width)
+    fits = sizes == (4, 4, 2, 512) and args[0].shape[0] == 384
     return (fast if fits else general)(*args)
 
 

time: 37.3 us -> 38.7 us (1.038)
  starting transfers between devices: 15.7 us -> 16.9 us
  waiting for transfers between devices: 10.3 us -> 10.8 us
    ppermute x8 -> x3, waiting for transfers between devices: 1.61 us -> 5.94 us  [the longest x1 4.36 us: fast(): far = lax.ppermute(near, 'tensor', across)]
    ppermute x6 -> x8, starting transfers between devices: 9.16 us -> 12.9 us  [swap(): return lax.ppermute(x, 'dp', [(d, d ^ k) for d in range(dp)])]
    ppermute x6 -> x8, waiting for transfers between devices: 7.65 us -> 4.24 us  [swap(): return lax.ppermute(x, 'dp', [(d, d ^ k) for d in range(dp)])]
    ppermute x8 -> x3, starting transfers between devices: 5.75 us -> 3.38 us  [the longest x1 1.66 us: fast(): far = lax.ppermute(near, 'tensor', across)]
    ppermute x3 -> x2, waiting for transfers between devices: 0.99 us -> 0.59 us  [fast(): got = lax.ppermute(send, 'tensor', core)]
    pallas_call x17 -> x12, Pallas kernels: 10.9 us -> 10.6 us  [run(): pl.pallas_call(body, out_shape=out_shape, in_specs=(specs or [vmem] * len...]
    ppermute x3 -> x2, starting transfers between devices: 0.79 us -> 0.59 us  [fast(): got = lax.ppermute(send, 'tensor', core)]
  transfers between devices with their start and end apart: 17 -> 13, of which waited for: 9 -> 7; matrix products, arithmetic and copies ran while one was open for 0% -> 0% of each run, Pallas kernels for 14% -> 14%
where the time goes in v7:
time: 38.7 us; the launch traced here: 38.5 us
  starting transfers between devices  16.9 us (44%)
  waiting for transfers between devices  10.8 us (28%)
  Pallas kernels  10.6 us (27%)
    ppermute x8, starting transfers between devices, swap(): return lax.ppermute(x, 'dp', [(d, d ^ k) for d in range(dp)])  12.9 us
    pallas_call x12, Pallas kernels, run(): pl.pallas_call(body, out_shape=out_shape, in_specs=(specs or [vmem] * len...  10.6 us
    ppermute x1, waiting for transfers between devices, fast(): far = lax.ppermute(near, 'tensor', across)  4.36 us
    ppermute x8, waiting for transfers between devices, swap(): return lax.ppermute(x, 'dp', [(d, d ^ k) for d in range(dp)])  4.24 us
    ppermute x1, starting transfers between devices, fast(): far = lax.ppermute(near, 'tensor', across)  1.66 us
    ppermute x1, starting transfers between devices, fast(): got = lax.ppermute(send, 'tensor', across)  1.65 us
    ppermute x1, waiting for transfers between devices, fast(): got = lax.ppermute(send, 'tensor', across)  1.58 us
  transfers between devices with their start and end apart: 13, of which 7 were waited for; matrix products, arithmetic and copies ran while one was open for 0% of the time, Pallas kernels for 14%

profile of v7, /device:TPU:0, one launch (start us, length us, event | category | flops | bytes accessed | tf_op | source)
XLA Modules:
  0.0 38.5 jit_solution(8432627775617118184)
XLA Ops:
  0.0 3.4 %rotate_in.1 = (f32[2,192,512]{2,1,0:T(8,128)S(1)}, bf16[16,128]{1,0:T(8,128)(2,1)S(1)}, bf16[384,768]{1,0:T(8,128)(2,1)S(1)}, bf16[384,2,1024]{2,1,0:T(2,128)(2,1)S(1)}) custom-call(bf16[384,1536]{1,0:T(8,128)(2,1)} %refs_0_.3, s32[2,384]{1,0:T(2,128)} %bitcast.5, s32[384]{0:T(512)} %refs_2_.2, bf16[2,1536,512]{2,1,0:T(8,128)(2,1)} %refs_3_.1, ...), custom_call_target="tpu_custom_call" | custom-call | flops 1 | bytes 1 | tf_op jit(solution)/shard_map/rotate_in/pallas_call | solution.py:252
  3.4 0.0 slice-start
  3.5 0.0 slice-start.2
  3.5 0.0 slice-start.1
  3.5 0.0 slice-start.3
  3.5 0.1 split_in.1
  3.6 0.5 %collective-permute-start = (f32[768,128]{1,0:T(8,128)S(1)}, f32[768,128]{1,0:T(8,128)S(1)}, u32[]{:S(2)}, u32[]{:S(2)}) collective-permute-start(f32[768,128]{1,0:T(8,128)S(1)} %get-tuple-element.25), channel_id=1, source_target_pairs={{0,1},{1,0},{2,3},{3,2},{4,5},{5,4},{6,7},{7,6},{8,9},{9,8},{10,11... | collective-permute-start | bytes 1179656 | tf_op jit(solution)/shard_map/ppermute | solution.py:311
  4.1 0.8 %choose.1.refs_3_ = bf16[384,1024]{1,0:T(8,128)(2,1)S(1)} custom-call(bf16[384,2,1024]{2,1,0:T(2,128)(2,1)S(1)} %get-tuple-element.27.refs_0_, bf16[384,768]{1,0:T(8,128)(2,1)S(1)} %get-tuple-element.28.refs_1_), custom_call_target="tpu_custom_call" | custom-call | flops 1 | bytes 1 | tf_op jit(solution)/shard_map/choose/pallas_call | solution.py:252
  4.9 0.6 %collective-permute-done.refs_1_ = f32[768,128]{1,0:T(8,128)S(1)} collective-permute-done((f32[768,128]{1,0:T(8,128)S(1)}, f32[768,128]{1,0:T(8,128)S(1)}, u32[]{:S(2)}, u32[]{:S(2)}) %collective-permute-start) | collective-permute-done | bytes 393248 | tf_op jit(solution)/shard_map/ppermute | solution.py:311
  5.4 0.1 pair_in.1
  5.5 4.0 %collective-permute-start.2 = (bf16[240,128]{1,0:T(8,128)(2,1)S(1)}, bf16[240,128]{1,0:T(8,128)(2,1)S(1)}, u32[]{:S(2)}, u32[]{:S(2)}) collective-permute-start(bf16[240,128]{1,0:T(8,128)(2,1)S(1)} %get-tuple-element.31), channel_id=1, source_target_pairs={{0,8},{4,12},{8,0},{12,4},{1,9},{5,13},{9,1},{13,5},{2,10},{6,14},... | collective-permute-start | bytes 184328 | tf_op jit(solution)/shard_map/ppermute | solution.py:287
  9.5 1.4 %collective-permute-start.3 = (bf16[224,128]{1,0:T(8,128)(2,1)S(1)}, bf16[224,128]{1,0:T(8,128)(2,1)S(1)}, u32[]{:S(2)}, u32[]{:S(2)}) collective-permute-start(bf16[224,128]{1,0:T(8,128)(2,1)S(1)} %get-tuple-element.32), channel_id=1, source_target_pairs={{0,12},{4,8},{8,4},{12,0},{1,13},{5,9},{9,5},{13,1},{2,14},{6,10},... | collective-permute-start | bytes 172040 | tf_op jit(solution)/shard_map/ppermute | solution.py:287
  10.9 0.2 collective-permute-start.1
  11.1 0.0 slice-done
  11.1 0.0 slice-done.2
  11.1 0.0 slice-done.1
  11.1 0.0 slice-done.3
  11.1 3.9 %rotate_out.1.refs_0_ = f32[2,192,512]{2,1,0:T(8,128)S(1)} custom-call(bf16[384,2,4096]{2,1,0:T(2,128)(2,1)S(1)} %bitcast.2, bf16[384,768]{1,0:T(8,128)(2,1)S(1)} %get-tuple-element.28.refs_1_, bf16[2,4096,512]{2,1,0:T(8,128)(2,1)S(1)} %bitcast.4, bf16[384,1024]{1,0:T(8,128)(2,1)S(1)} %choose.1.refs_3_, ...), custom_call_target="tpu_custom_call" | custom-call | flops 1 | bytes 1 | tf_op jit(solution)/shard_map/rotate_out/pallas_call | solution.py:252
  15.0 0.0 copy-start
  15.1 0.0 collective-permute-done.1.refs_1_.refs_3_
  15.1 0.5 %collective-permute-done.3.refs_3_.refs_5_ = bf16[224,128]{1,0:T(8,128)(2,1)S(1)} collective-permute-done((bf16[224,128]{1,0:T(8,128)(2,1)S(1)}, bf16[224,128]{1,0:T(8,128)(2,1)S(1)}, u32[]{:S(2)}, u32[]{:S(2)}) %collective-permute-start.3) | collective-permute-done | bytes 57376 | tf_op jit(solution)/shard_map/ppermute | solution.py:287
  15.6 0.0 collective-permute-done.2.refs_2_.refs_4_
  15.6 0.1 split_out.1
  15.8 0.1 collective-permute-start.6
  15.9 1.7 %collective-permute-start.4 = (bf16[768,128]{1,0:T(8,128)(2,1)S(1)}, bf16[768,128]{1,0:T(8,128)(2,1)S(1)}, u32[]{:S(2)}, u32[]{:S(2)}) collective-permute-start(bf16[768,128]{1,0:T(8,128)(2,1)S(1)} %stack_in.1.refs_0_), channel_id=1, source_target_pairs={{0,2},{1,3},{2,0},{3,1},{4,6},{5,7},{6,4},{7,5},{8,10},{9,11},{10,... | collective-permute-start | bytes 589832 | tf_op jit(solution)/shard_map/ppermute | solution.py:330
  17.5 0.0 collective-permute-done.6.refs_1_
  17.5 0.1 pair_out.1
  17.6 1.7 %collective-permute-start.7 = (bf16[384,128]{1,0:T(8,128)(2,1)S(1)}, bf16[384,128]{1,0:T(8,128)(2,1)S(1)}, u32[]{:S(2)}, u32[]{:S(2)}) collective-permute-start(bf16[384,128]{1,0:T(8,128)(2,1)S(1)} %get-tuple-element.36), channel_id=1, source_target_pairs={{0,2},{1,3},{2,0},{3,1},{4,6},{5,7},{6,4},{7,5},{8,10},{9,11},{10,... | collective-permute-start | bytes 294920 | tf_op jit(solution)/shard_map/ppermute | solution.py:332
  19.3 4.4 %collective-permute-done.4.refs_1_ = bf16[768,128]{1,0:T(8,128)(2,1)S(1)} collective-permute-done((bf16[768,128]{1,0:T(8,128)(2,1)S(1)}, bf16[768,128]{1,0:T(8,128)(2,1)S(1)}, u32[]{:S(2)}, u32[]{:S(2)}) %collective-permute-start.4) | collective-permute-done | bytes 196640 | tf_op jit(solution)/shard_map/ppermute | solution.py:330
  23.7 0.1 collective-permute-start.5
  23.7 1.6 %collective-permute-done.7.refs_1_ = bf16[384,128]{1,0:T(8,128)(2,1)S(1)} collective-permute-done((bf16[384,128]{1,0:T(8,128)(2,1)S(1)}, bf16[384,128]{1,0:T(8,128)(2,1)S(1)}, u32[]{:S(2)}, u32[]{:S(2)}) %collective-permute-start.7) | collective-permute-done | bytes 98336 | tf_op jit(solution)/shard_map/ppermute | solution.py:332
  25.4 2.7 %collective-permute-start.11 = (bf16[208,128]{1,0:T(8,128)(2,1)S(1)}, bf16[208,128]{1,0:T(8,128)(2,1)S(1)}, u32[]{:S(2)}, u32[]{:S(2)}) collective-permute-start(bf16[208,128]{1,0:T(8,128)(2,1)S(1)} %get-tuple-element.40), channel_id=1, source_target_pairs={{0,8},{4,12},{8,0},{12,4},{1,9},{5,13},{9,1},{13,5},{2,10},{6,14},... | collective-permute-start | bytes 159752 | tf_op jit(solution)/shard_map/ppermute | solution.py:287
  28.1 1.1 %collective-permute-start.8 = (bf16[384,128]{1,0:T(8,128)(2,1)S(1)}, bf16[384,128]{1,0:T(8,128)(2,1)S(1)}, u32[]{:S(2)}, u32[]{:S(2)}) collective-permute-start(bf16[384,128]{1,0:T(8,128)(2,1)S(1)} %get-tuple-element.37.refs_2_), channel_id=1, source_target_pairs={{0,4},{4,0},{8,12},{12,8},{1,5},{5,1},{9,13},{13,9},{2,6},{6,2},{1... | collective-permute-start | bytes 294920 | tf_op jit(solution)/shard_map/ppermute | solution.py:287
  29.2 0.4 %collective-permute-start.9 = (bf16[240,128]{1,0:T(8,128)(2,1)S(1)}, bf16[240,128]{1,0:T(8,128)(2,1)S(1)}, u32[]{:S(2)}, u32[]{:S(2)}) collective-permute-start(bf16[240,128]{1,0:T(8,128)(2,1)S(1)} %get-tuple-element.38), channel_id=1, source_target_pairs={{0,8},{4,12},{8,0},{12,4},{1,9},{5,13},{9,1},{13,5},{2,10},{6,14},... | collective-permute-start | bytes 184328 | tf_op jit(solution)/shard_map/ppermute | solution.py:287
  29.6 2.8 %collective-permute-start.10 = (bf16[224,128]{1,0:T(8,128)(2,1)S(1)}, bf16[224,128]{1,0:T(8,128)(2,1)S(1)}, u32[]{:S(2)}, u32[]{:S(2)}) collective-permute-start(bf16[224,128]{1,0:T(8,128)(2,1)S(1)} %get-tuple-element.39), channel_id=1, source_target_pairs={{0,12},{4,8},{8,4},{12,0},{1,13},{5,9},{9,5},{13,1},{2,14},{6,10},... | collective-permute-start | bytes 172040 | tf_op jit(solution)/shard_map/ppermute | solution.py:287
  32.5 0.0 collective-permute-done.11.refs_6_
  32.5 0.2 collective-permute-start.12
  32.7 0.0 collective-permute-done.5.refs_1_
  32.7 0.5 %mask_in.1.refs_1_ = bf16[2,768,512]{2,1,0:T(8,128)(2,1)S(1)} custom-call(bf16[768,128]{1,0:T(8,128)(2,1)S(1)} %sum_in.1.refs_0_, bf16[768,128]{1,0:T(8,128)(2,1)S(1)} %collective-permute-done.5.refs_1_, bf16[208,128]{1,0:T(8,128)(2,1)S(1)} %get-tuple-element.29.refs_0_.refs_2_.refs_4_, bf16[208,128]{1,0:T(8,128)(2,1)S(1)} %collective-permute-done.1.refs_1_.refs_3_, ...), custom_call_target="tpu_custom_call" | custom-call | flops 1 | bytes 1 | tf_op jit(solution)/shard_map/mask_in/pallas_call | solution.py:252
  33.2 2.5 %collective-permute-done.10.refs_5_ = bf16[224,128]{1,0:T(8,128)(2,1)S(1)} collective-permute-done((bf16[224,128]{1,0:T(8,128)(2,1)S(1)}, bf16[224,128]{1,0:T(8,128)(2,1)S(1)}, u32[]{:S(2)}, u32[]{:S(2)}) %collective-permute-start.10) | collective-permute-done | bytes 57376 | tf_op jit(solution)/shard_map/ppermute | solution.py:287
  35.7 0.6 %collective-permute-done.9.refs_4_ = bf16[240,128]{1,0:T(8,128)(2,1)S(1)} collective-permute-done((bf16[240,128]{1,0:T(8,128)(2,1)S(1)}, bf16[240,128]{1,0:T(8,128)(2,1)S(1)}, u32[]{:S(2)}, u32[]{:S(2)}) %collective-permute-start.9) | collective-permute-done | bytes 61472 | tf_op jit(solution)/shard_map/ppermute | solution.py:287
  36.3 0.0 collective-permute-done.8.refs_3_
  36.3 0.5 %collective-permute-done.12.refs_7_ = bf16[208,128]{1,0:T(8,128)(2,1)S(1)} collective-permute-done((bf16[208,128]{1,0:T(8,128)(2,1)S(1)}, bf16[208,128]{1,0:T(8,128)(2,1)S(1)}, u32[]{:S(2)}, u32[]{:S(2)}) %collective-permute-start.12) | collective-permute-done | bytes 53280 | tf_op jit(solution)/shard_map/ppermute | solution.py:287
  36.9 0.0 copy-done
  36.9 1.6 %blocks.1 = f32[2,128,128]{2,1,0:T(8,128)} custom-call(s32[2]{0:T(128)S(1)} %copy-done, bf16[2,768,512]{2,1,0:T(8,128)(2,1)S(1)} %mask_in.1.refs_1_, bf16[384,128]{1,0:T(8,128)(2,1)S(1)} %get-tuple-element.37.refs_2_, bf16[384,128]{1,0:T(8,128)(2,1)S(1)} %collective-permute-done.8.refs_3_, bf16[240,128]{1,0:T(8,128)(2,1)S(1)} %collective-permute-done.9.refs_4_, ...), custom_call_target="tpu_custom_call" | custom-call | flops 1 | bytes 1 | tf_op jit(solution)/shard_map/blocks/pallas_call | solution.py:252
  (5 shorter events, 0.1 us)
Async XLA Ops:
  3.4 7.7 %slice-start = ((s8[6291456]{0:T(1024)(128)(4,1)}), s8[4194304]{0:T(1024)(128)(4,1)S(1)}, s32[]{:S(2)}) async-start(s8[6291456]{0:T(1024)(128)(4,1)} %bitcast.1), calls=%async_computation | async-start | bytes 8388608
  3.5 7.7 %slice-start.2 = ((s8[8388608]{0:T(1024)(128)(4,1)}), s8[4194304]{0:T(1024)(128)(4,1)S(1)}, s32[]{:S(2)}) async-start(s8[8388608]{0:T(1024)(128)(4,1)} %bitcast.3), calls=%async_computation.2 | async-start | bytes 8388608
  3.5 7.7 %slice-start.1 = ((s8[6291456]{0:T(1024)(128)(4,1)}), s8[2097152]{0:T(1024)(128)(4,1)S(1)}, s32[]{:S(2)}) async-start(s8[6291456]{0:T(1024)(128)(4,1)} %bitcast.1), calls=%async_computation.1 | async-start | bytes 4194304
  3.5 7.6 %slice-start.3 = ((s8[8388608]{0:T(1024)(128)(4,1)}), s8[4194304]{0:T(1024)(128)(4,1)S(1)}, s32[]{:S(2)}) async-start(s8[8388608]{0:T(1024)(128)(4,1)} %bitcast.3), calls=%async_computation.3 | async-start | bytes 8388608
  3.6 1.9 %collective-permute-start = (f32[768,128]{1,0:T(8,128)S(1)}, f32[768,128]{1,0:T(8,128)S(1)}, u32[]{:S(2)}, u32[]{:S(2)}) collective-permute-start(f32[768,128]{1,0:T(8,128)S(1)} %get-tuple-element.25), channel_id=1, source_target_pairs={{0,1},{1,0},{2,3},{3,2},{4,5},{5,4},{6,7},{7,6},{8,9},{9,8},{10,11... | collective-permute-start | bytes 1179656 | tf_op jit(solution)/shard_map/ppermute | solution.py:311
  5.5 10.1 %collective-permute-start.2 = (bf16[240,128]{1,0:T(8,128)(2,1)S(1)}, bf16[240,128]{1,0:T(8,128)(2,1)S(1)}, u32[]{:S(2)}, u32[]{:S(2)}) collective-permute-start(bf16[240,128]{1,0:T(8,128)(2,1)S(1)} %get-tuple-element.31), channel_id=1, source_target_pairs={{0,8},{4,12},{8,0},{12,4},{1,9},{5,13},{9,1},{13,5},{2,10},{6,14},... | collective-permute-start | bytes 184328 | tf_op jit(solution)/shard_map/ppermute | solution.py:287
  9.5 6.1 %collective-permute-start.3 = (bf16[224,128]{1,0:T(8,128)(2,1)S(1)}, bf16[224,128]{1,0:T(8,128)(2,1)S(1)}, u32[]{:S(2)}, u32[]{:S(2)}) collective-permute-start(bf16[224,128]{1,0:T(8,128)(2,1)S(1)} %get-tuple-element.32), channel_id=1, source_target_pairs={{0,12},{4,8},{8,4},{12,0},{1,13},{5,9},{9,5},{13,1},{2,14},{6,10},... | collective-permute-start | bytes 172040 | tf_op jit(solution)/shard_map/ppermute | solution.py:287
  10.9 4.2 %collective-permute-start.1 = (bf16[208,128]{1,0:T(8,128)(2,1)S(1)}, bf16[208,128]{1,0:T(8,128)(2,1)S(1)}, u32[]{:S(2)}, u32[]{:S(2)}) collective-permute-start(bf16[208,128]{1,0:T(8,128)(2,1)S(1)} %get-tuple-element.30), channel_id=1, source_target_pairs={{0,4},{4,0},{8,12},{12,8},{1,5},{5,1},{9,13},{13,9},{2,6},{6,2},{1... | collective-permute-start | bytes 159752 | tf_op jit(solution)/shard_map/ppermute | solution.py:287
  15.0 21.8 %copy-start = (s32[2]{0:T(128)S(1)}, s32[2]{0:T(128)}, u32[]{:S(2)}) copy-start(s32[2]{0:T(128)} %refs_0_.5) | copy-start | bytes 28
  15.8 1.8 %collective-permute-start.6 = (f32[768,128]{1,0:T(8,128)S(1)}, f32[768,128]{1,0:T(8,128)S(1)}, u32[]{:S(2)}, u32[]{:S(2)}) collective-permute-start(f32[768,128]{1,0:T(8,128)S(1)} %get-tuple-element.34), channel_id=1, source_target_pairs={{0,1},{1,0},{2,3},{3,2},{4,5},{5,4},{6,7},{7,6},{8,9},{9,8},{10,11... | collective-permute-start | bytes 1179656 | tf_op jit(solution)/shard_map/ppermute | solution.py:328
  15.9 7.8 %collective-permute-start.4 = (bf16[768,128]{1,0:T(8,128)(2,1)S(1)}, bf16[768,128]{1,0:T(8,128)(2,1)S(1)}, u32[]{:S(2)}, u32[]{:S(2)}) collective-permute-start(bf16[768,128]{1,0:T(8,128)(2,1)S(1)} %stack_in.1.refs_0_), channel_id=1, source_target_pairs={{0,2},{1,3},{2,0},{3,1},{4,6},{5,7},{6,4},{7,5},{8,10},{9,11},{10,... | collective-permute-start | bytes 589832 | tf_op jit(solution)/shard_map/ppermute | solution.py:330
  17.6 7.7 %collective-permute-start.7 = (bf16[384,128]{1,0:T(8,128)(2,1)S(1)}, bf16[384,128]{1,0:T(8,128)(2,1)S(1)}, u32[]{:S(2)}, u32[]{:S(2)}) collective-permute-start(bf16[384,128]{1,0:T(8,128)(2,1)S(1)} %get-tuple-element.36), channel_id=1, source_target_pairs={{0,2},{1,3},{2,0},{3,1},{4,6},{5,7},{6,4},{7,5},{8,10},{9,11},{10,... | collective-permute-start | bytes 294920 | tf_op jit(solution)/shard_map/ppermute | solution.py:332
  23.7 9.0 %collective-permute-start.5 = (bf16[768,128]{1,0:T(8,128)(2,1)S(1)}, bf16[768,128]{1,0:T(8,128)(2,1)S(1)}, u32[]{:S(2)}, u32[]{:S(2)}) collective-permute-start(bf16[768,128]{1,0:T(8,128)(2,1)S(1)} %sum_in.1.refs_0_), channel_id=1, source_target_pairs={{0,1},{1,0},{2,3},{3,2},{4,5},{5,4},{6,7},{7,6},{8,9},{9,8},{10,11... | collective-permute-start | bytes 589832 | tf_op jit(solution)/shard_map/ppermute | solution.py:334
  25.4 7.1 %collective-permute-start.11 = (bf16[208,128]{1,0:T(8,128)(2,1)S(1)}, bf16[208,128]{1,0:T(8,128)(2,1)S(1)}, u32[]{:S(2)}, u32[]{:S(2)}) collective-permute-start(bf16[208,128]{1,0:T(8,128)(2,1)S(1)} %get-tuple-element.40), channel_id=1, source_target_pairs={{0,8},{4,12},{8,0},{12,4},{1,9},{5,13},{9,1},{13,5},{2,10},{6,14},... | collective-permute-start | bytes 159752 | tf_op jit(solution)/shard_map/ppermute | solution.py:287
  28.1 8.3 %collective-permute-start.8 = (bf16[384,128]{1,0:T(8,128)(2,1)S(1)}, bf16[384,128]{1,0:T(8,128)(2,1)S(1)}, u32[]{:S(2)}, u32[]{:S(2)}) collective-permute-start(bf16[384,128]{1,0:T(8,128)(2,1)S(1)} %get-tuple-element.37.refs_2_), channel_id=1, source_target_pairs={{0,4},{4,0},{8,12},{12,8},{1,5},{5,1},{9,13},{13,9},{2,6},{6,2},{1... | collective-permute-start | bytes 294920 | tf_op jit(solution)/shard_map/ppermute | solution.py:287
  29.2 7.1 %collective-permute-start.9 = (bf16[240,128]{1,0:T(8,128)(2,1)S(1)}, bf16[240,128]{1,0:T(8,128)(2,1)S(1)}, u32[]{:S(2)}, u32[]{:S(2)}) collective-permute-start(bf16[240,128]{1,0:T(8,128)(2,1)S(1)} %get-tuple-element.38), channel_id=1, source_target_pairs={{0,8},{4,12},{8,0},{12,4},{1,9},{5,13},{9,1},{13,5},{2,10},{6,14},... | collective-permute-start | bytes 184328 | tf_op jit(solution)/shard_map/ppermute | solution.py:287
  29.6 6.1 %collective-permute-start.10 = (bf16[224,128]{1,0:T(8,128)(2,1)S(1)}, bf16[224,128]{1,0:T(8,128)(2,1)S(1)}, u32[]{:S(2)}, u32[]{:S(2)}) collective-permute-start(bf16[224,128]{1,0:T(8,128)(2,1)S(1)} %get-tuple-element.39), channel_id=1, source_target_pairs={{0,12},{4,8},{8,4},{12,0},{1,13},{5,9},{9,5},{13,1},{2,14},{6,10},... | collective-permute-start | bytes 172040 | tf_op jit(solution)/shard_map/ppermute | solution.py:287
  32.5 4.4 %collective-permute-start.12 = (bf16[208,128]{1,0:T(8,128)(2,1)S(1)}, bf16[208,128]{1,0:T(8,128)(2,1)S(1)}, u32[]{:S(2)}, u32[]{:S(2)}) collective-permute-start(bf16[208,128]{1,0:T(8,128)(2,1)S(1)} %collective-permute-done.11.refs_6_), channel_id=1, source_target_pairs={{0,4},{4,0},{8,12},{12,8},{1,5},{5,1},{9,13},{13,9},{2,6},{6,2},{1... | collective-permute-start | bytes 159752 | tf_op jit(solution)/shard_map/ppermute | solution.py:287

commit v8 on v7

--- a/solution.py
+++ b/solution.py
@@ -10,7 +10,6 @@
 F32 = jnp.float32
 BF16 = jnp.bfloat16
 CHUNK = 1024
-EARLY = 1024
 PARTS = 3
 VMEM = 20 * 2**20
 LABEL_ROWS = 16
@@ -36,8 +35,8 @@
 
 
 def rotate_in_kernel(
-    acts, routes, ids, basis_in, grads,
-    acc, label, pick, early,
+    acts, routes, ids, basis_in,
+    acc, label, pick,
     acts_v, routes_v, ids_v, basis_v, sems,
 ):
     tokens, features = acts.shape
@@ -48,7 +47,6 @@
     first = [fetch(routes, routes_v), fetch(ids, ids_v)]
     acts_in = [fetch(acts.at[:, part], acts_v.at[:, part]) for part in parts]
     bases = [fetch(basis_in.at[:, part, :], basis_v.at[:, part, :]) for part in parts]
-    grads_in = fetch(grads.at[:, :, pl.ds(0, early.shape[2])], early)
     for copy in first:
         copy.wait()
     hits = [
@@ -97,7 +95,6 @@
         for e in range(experts):
             more = dot(chosen[n][e * cap : (e + 1) * cap], basis_v[e, part, :])
             acc[e] = more if n == 0 else acc[e] + more
-    grads_in.wait()
 
 
 def split_in_kernel(acc, keep, send):
@@ -114,25 +111,15 @@
             at += half
 
 
-def choose(pick, grads, cols):
-    rows = grads[:, :, cols]
-    return dot(pick[...], rows.reshape(rows.shape[0] * 2, rows.shape[2])).astype(BF16)
-
-
-def choose_kernel(grads, pick, out):
-    out[...] = choose(pick, grads, slice(None))
-
-
-def rotate_out_kernel(grads, pick, basis_out, early, acc):
+def rotate_out_kernel(grads, pick, basis_out, acc):
+    tokens, _, hidden = grads.shape
     experts, cap, _ = acc.shape
-    done = early.shape[1]
-    for e in range(experts):
-        acc[e] = dot(early[e * cap : (e + 1) * cap, :], basis_out[e, :done, :])
-    for at in range(done, grads.shape[2], CHUNK):
+    for at in range(0, hidden, CHUNK):
         cols = pl.ds(at, CHUNK)
-        chosen = choose(pick, grads, cols)
+        chosen = dot(pick[...], grads[:, :, cols].reshape(2 * tokens, CHUNK)).astype(BF16)
         for e in range(experts):
-            acc[e] += dot(chosen[e * cap : (e + 1) * cap], basis_out[e, cols, :])
+            part = dot(chosen[e * cap : (e + 1) * cap], basis_out[e, cols, :])
+            acc[e] = part if at == 0 else acc[e] + part
 
 
 def split_out_kernel(acc, keep, send):
@@ -172,13 +159,12 @@
     send[...] = (kept[other, :] + got[other, :]).astype(BF16)
 
 
-def round_kernel(kept, got, out, *pays):
+def round_kernel(kept, got, *pays):
+    outer = kept.shape[0]
     rows = (kept[...] + got[...].astype(F32)).astype(BF16)
-    cap = rows.shape[0] // 2
-    out[...] = rows
-    for pay, e in zip(pays, (1, 0, 0)):
-        pay[:cap, :] = rows[e * cap : (e + 1) * cap]
-        fill(pay, cap)
+    for pay in pays:
+        pay[:outer, :] = rows
+        fill(pay, outer)
 
 
 def stack_kernel(slab, *refs):
@@ -187,22 +173,27 @@
         out[k * slab : (k + 1) * slab, :] = piece[:slab, :]
 
 
-def sum_kernel(near, far, out):
-    out[...] = (near[...].astype(F32) + far[...].astype(F32)).astype(BF16)
-
-
-def mask_kernel(mine, other, *refs):
-    *pieces, out = refs
+def sum_kernel(near, far, *outs):
+    piece = outs[0].shape[0]
+    for n, out in enumerate(outs):
+        rows = pl.ds(n * piece, piece)
+        out[...] = (near[rows, :].astype(F32) + far[rows, :].astype(F32)).astype(BF16)
+
+
+def mask_kernel(counts, *refs):
+    mine, other, pieces = refs[:2], refs[2:4], refs[4:-2]
+    out, divisor = refs[-2:]
     experts, dp = out.shape[0], len(pieces)
-    half = mine.shape[0] // (dp * experts)
+    half = 2 * mine[0].shape[0] // (dp * experts)
     slab = experts * half
     core = lax.rem(lax.axis_index("tensor"), 2)
     for e in range(experts):
+        divisor[e] = jnp.full(divisor.shape[1:], counts[e].astype(F32), F32)
         rows, labels = [], []
-        for which, ref in ((core, mine), (1 - core, other)):
+        for which, refs in ((core, mine), (1 - core, other)):
             for k, piece in enumerate(pieces):
-                at = (k * experts + e) * half
-                rows.append(ref[at : at + half, :])
+                at = (k % (dp // 2) * experts + e) * half
+                rows.append(refs[k // (dp // 2)][at : at + half, :])
                 label = piece[slab : slab + LABEL_ROWS, :].astype(F32)
                 label = label[2 * e : 2 * e + 2, :half]
                 labels.append(jnp.where(which == 0, label[0:1], label[1:2]))
@@ -215,26 +206,24 @@
             ).astype(BF16)
 
 
-def blocks_kernel(counts, masked, own, near, *refs):
-    *far, result, final, sems = refs
-    experts = masked.shape[0]
-    cap = own.shape[0] // experts
-    half = cap // 2
+def blocks_kernel(divisor, masked, *refs):
+    *outs, result, final, sems = refs
+    experts, slots, _ = masked.shape
+    half = slots // (2 * len(outs))
     core = lax.rem(lax.axis_index("tensor"), 2)
     copies = []
     for e in range(experts):
-        sources = [(own, e * cap), (near, e * cap)] + [(x, 0) for x in far[2 * e : 2 * e + 2]]
         rows = [
-            ref[pl.ds(pl.multiple_of(at + which * half, 16), half), :]
+            ref[pl.ds(pl.multiple_of((2 * e + which) * half, 16), half), :]
             for which in (core, 1 - core)
-            for ref, at in sources
+            for ref in outs
         ]
         blocks = dot(jnp.concatenate(rows, axis=0).T, masked[e])
         squares = blocks * blocks
         summed = squares[:, :128]
         for at in range(128, squares.shape[1], 128):
             summed = summed + squares[:, at : at + 128]
-        final[e] = summed / counts[e].astype(F32)
+        final[e] = summed / divisor[e][:1]
         copies.append(pltpu.make_async_copy(final.at[e], result.at[e], sems.at[e]))
         copies[-1].start()
     for copy in copies:
@@ -287,16 +276,15 @@
         return lax.ppermute(x, "dp", [(d, d ^ k) for d in range(dp)])
 
     partial = jax.ShapeDtypeStruct((experts, cap, width), F32)
-    acc, label, pick, early = call(
+    acc, label, pick = call(
         rotate_in_kernel,
         "rotate_in",
         (
             partial,
             rows(LABEL_ROWS, BF16),
             jax.ShapeDtypeStruct((wide, 2 * tokens), BF16),
-            jax.ShapeDtypeStruct((tokens, 2, EARLY), BF16),
         ),
-        [hbm] * 5,
+        [hbm] * 4,
         [
             pltpu.VMEM(acts.shape, BF16),
             pltpu.VMEM((2, tokens), jnp.int32),
@@ -304,53 +292,56 @@
             pltpu.VMEM(basis_in.shape, BF16),
             pltpu.SemaphoreType.DMA((3 + 2 * PARTS,)),
         ],
-    )(pin(acts), pin(routes.T), pin(example_ids), pin(basis_in), pin(grads))
+    )(pin(acts), pin(routes.T), pin(example_ids), pin(basis_in))
     keep, send = call(
         split_in_kernel, "split_in", (rows(half, F32), rows(half, F32)), flops=8 * 10**9
     )(acc)
     got = lax.ppermute(send, "tensor", core)
-    early = call(choose_kernel, "choose", jax.ShapeDtypeStruct((wide, EARLY), BF16))(early, pick)
     slab = half // dp
     pieces = call(
         pair_in_kernel,
         "pair_in",
         [rows(slab + LABEL_ROWS + extra, BF16) for extra in (0, 0, 32, 16)],
-        after=[early],
     )(keep, got, label)
     arrived = [pieces[0]] + [swap(pieces[k], k) for k in range(1, dp)]
 
     acc = call(rotate_out_kernel, "rotate_out", partial, after=[pieces[0]])(
-        grads, pick, basis_out, early
+        grads, pick, basis_out
     )
     keep, send = call(
         split_out_kernel, "split_out", (rows(half, F32), rows(half, F32)), after=arrived[1:]
     )(acc)
     got = lax.ppermute(send, "tensor", core)
-    near = call(functools.partial(stack_kernel, slab), "stack_in", rows(half, BF16))(*arrived)
-    far = lax.ppermute(near, "tensor", across)
     keep, send = call(pair_out_kernel, "pair_out", (rows(wide, F32), rows(wide, BF16)))(keep, got)
     got = lax.ppermute(send, "tensor", across)
-    mine = call(sum_kernel, "sum_in", rows(half, BF16))(near, far)
-    other = lax.ppermute(mine, "tensor", core)
-    out, second, first2, first3 = call(
-        round_kernel,
-        "round_out",
-        [rows(wide, BF16)] + [rows(cap + extra, BF16) for extra in (16, 48, 32)],
+    outs = call(
+        round_kernel, "round_out", [rows(wide + extra, BF16) for extra in (0, 16, 48, 32)]
     )(keep, got)
-    second2 = swap(second, 2)
-    outs = [out, swap(out, 1), swap(first2, 2), swap(first3, 3), second2, swap(second2, 1)]
-    masked = call(
-        mask_kernel, "mask_in", jax.ShapeDtypeStruct((experts, dp * cap, dp * 128), BF16)
-    )(mine, other, *arrived)
+    outs = [outs[0]] + [swap(outs[k], k) for k in range(1, dp)]
+
+    near = call(
+        functools.partial(stack_kernel, slab), "stack_in", rows(half, BF16), after=[got]
+    )(*arrived)
+    far = lax.ppermute(near, "tensor", across)
+    mine = call(sum_kernel, "sum_in", [rows(half // 2, BF16)] * 2)(near, far)
+    other = [lax.ppermute(x, "tensor", core) for x in mine]
+    masked, divisor = call(
+        mask_kernel,
+        "mask_in",
+        (
+            jax.ShapeDtypeStruct((experts, dp * cap, dp * 128), BF16),
+            jax.ShapeDtypeStruct((experts, 8, 128), F32),
+        ),
+        [smem] + [vmem] * (4 + dp),
+    )(expert_counts, *mine, *other, *arrived)
     result = jax.ShapeDtypeStruct((experts, 128, 128), F32)
     return call(
         blocks_kernel,
         "blocks",
         result,
-        [smem] + [vmem] * (1 + len(outs)),
         scratch=[pltpu.VMEM(result.shape, F32), pltpu.SemaphoreType.DMA((experts,))],
         out_specs=hbm,
-    )(expert_counts, masked, *outs)
+    )(divisor, masked, *outs)
 
 
 EX_DEV = 1

time: 38.7 us -> 36.7 us (0.948)
  starting transfers between devices: 16.9 us -> 14.1 us
  waiting for transfers between devices: 10.8 us -> 11.6 us
    ppermute x1, waiting for transfers between devices: 4.36 us -> 0.37 us  [fast(): far = lax.ppermute(near, 'tensor', across)]
    ppermute x8 -> x6, starting transfers between devices: 12.9 us -> 9.82 us  [swap(): return lax.ppermute(x, 'dp', [(d, d ^ k) for d in range(dp)])]
    ppermute x2, waiting for transfers between devices: 0.59 us -> 3.06 us  [fast(): got = lax.ppermute(send, 'tensor', core)]
    ppermute x1, waiting for transfers between devices: 1.58 us -> 3.33 us  [fast(): got = lax.ppermute(send, 'tensor', across)]
    ppermute x1 -> x2, waiting for transfers between devices: 0.01 us -> 0.94 us  [fast(): other = [lax.ppermute(x, 'tensor', core) for x in mine]]
    ppermute x1 -> x2, starting transfers between devices: 0.07 us -> 0.57 us  [fast(): other = [lax.ppermute(x, 'tensor', core) for x in mine]]
    ppermute x8 -> x6, waiting for transfers between devices: 4.24 us -> 3.94 us  [swap(): return lax.ppermute(x, 'dp', [(d, d ^ k) for d in range(dp)])]
    pallas_call x12 -> x11, Pallas kernels: 10.6 us -> 10.5 us  [run(): pl.pallas_call(body, out_shape=out_shape, in_specs=(specs or [vmem] * len...]
  transfers between devices with their start and end apart: 13 -> 12, of which waited for: 7 -> 7; matrix products, arithmetic and copies ran while one was open for 0% -> 0% of each run, Pallas kernels for 14% -> 16%
where the time goes in v8:
time: 36.7 us; the launch traced here: 36.5 us
  starting transfers between devices  14.1 us (38%)
  waiting for transfers between devices  11.6 us (32%)
  Pallas kernels  10.5 us (29%)
    pallas_call x11, Pallas kernels, run(): pl.pallas_call(body, out_shape=out_shape, in_specs=(specs or [vmem] * len...  10.5 us
    ppermute x6, starting transfers between devices, swap(): return lax.ppermute(x, 'dp', [(d, d ^ k) for d in range(dp)])  9.82 us
    ppermute x6, waiting for transfers between devices, swap(): return lax.ppermute(x, 'dp', [(d, d ^ k) for d in range(dp)])  3.94 us
    ppermute x1, waiting for transfers between devices, fast(): got = lax.ppermute(send, 'tensor', across)  3.33 us
    ppermute x2, waiting for transfers between devices, fast(): got = lax.ppermute(send, 'tensor', core)  3.06 us
    ppermute x1, starting transfers between devices, fast(): got = lax.ppermute(send, 'tensor', across)  1.57 us
    ppermute x1, starting transfers between devices, fast(): far = lax.ppermute(near, 'tensor', across)  1.57 us
    ppermute x2, waiting for transfers between devices, fast(): other = [lax.ppermute(x, 'tensor', core) for x in mine]  0.94 us
  transfers between devices with their start and end apart: 12, of which 7 were waited for; matrix products, arithmetic and copies ran while one was open for 0% of the time, Pallas kernels for 16%

profile of v8, /device:TPU:0, one launch (start us, length us, event | category | flops | bytes accessed | tf_op | source)
XLA Modules:
  0.0 36.5 jit_solution(4065700598736974326)
XLA Ops:
  0.0 3.4 %rotate_in.1 = (f32[2,192,512]{2,1,0:T(8,128)S(1)}, bf16[16,128]{1,0:T(8,128)(2,1)S(1)}, bf16[384,768]{1,0:T(8,128)(2,1)S(1)}) custom-call(bf16[384,1536]{1,0:T(8,128)(2,1)} %refs_0_.3, s32[2,384]{1,0:T(2,128)} %bitcast.5, s32[384]{0:T(512)} %refs_2_.2, bf16[2,1536,512]{2,1,0:T(8,128)(2,1)} %refs_3_.1), custom_call_target="tpu_custom_call" | custom-call | flops 1 | bytes 1 | tf_op jit(solution)/shard_map/rotate_in/pallas_call | solution.py:241
  3.4 0.0 slice-start
  3.5 0.0 slice-start.2
  3.5 0.0 slice-start.1
  3.5 0.0 slice-start.3
  3.5 0.1 split_in.1
  3.6 0.5 %collective-permute-start = (f32[768,128]{1,0:T(8,128)S(1)}, f32[768,128]{1,0:T(8,128)S(1)}, u32[]{:S(2)}, u32[]{:S(2)}) collective-permute-start(f32[768,128]{1,0:T(8,128)S(1)} %get-tuple-element.28), channel_id=1, source_target_pairs={{0,1},{1,0},{2,3},{3,2},{4,5},{5,4},{6,7},{7,6},{8,9},{9,8},{10,11... | collective-permute-start | bytes 1179656 | tf_op jit(solution)/shard_map/ppermute | solution.py:299
  4.1 1.3 %collective-permute-done.refs_1_ = f32[768,128]{1,0:T(8,128)S(1)} collective-permute-done((f32[768,128]{1,0:T(8,128)S(1)}, f32[768,128]{1,0:T(8,128)S(1)}, u32[]{:S(2)}, u32[]{:S(2)}) %collective-permute-start) | collective-permute-done | bytes 393248 | tf_op jit(solution)/shard_map/ppermute | solution.py:299
  5.5 4.0 %collective-permute-start.2 = (bf16[240,128]{1,0:T(8,128)(2,1)S(1)}, bf16[240,128]{1,0:T(8,128)(2,1)S(1)}, u32[]{:S(2)}, u32[]{:S(2)}) collective-permute-start(bf16[240,128]{1,0:T(8,128)(2,1)S(1)} %get-tuple-element.32), channel_id=1, source_target_pairs={{0,8},{4,12},{8,0},{12,4},{1,9},{5,13},{9,1},{13,5},{2,10},{6,14},... | collective-permute-start | bytes 184328 | tf_op jit(solution)/shard_map/ppermute | solution.py:276
  9.5 1.4 %collective-permute-start.3 = (bf16[224,128]{1,0:T(8,128)(2,1)S(1)}, bf16[224,128]{1,0:T(8,128)(2,1)S(1)}, u32[]{:S(2)}, u32[]{:S(2)}) collective-permute-start(bf16[224,128]{1,0:T(8,128)(2,1)S(1)} %get-tuple-element.33), channel_id=1, source_target_pairs={{0,12},{4,8},{8,4},{12,0},{1,13},{5,9},{9,5},{13,1},{2,14},{6,10},... | collective-permute-start | bytes 172040 | tf_op jit(solution)/shard_map/ppermute | solution.py:276
  10.9 0.2 collective-permute-start.1
  11.1 0.0 slice-done
  11.1 0.0 slice-done.2
  11.1 0.0 slice-done.1
  11.1 0.0 slice-done.3
  11.1 0.0 copy-start
  11.1 4.6 %rotate_out.1.refs_0_ = f32[2,192,512]{2,1,0:T(8,128)S(1)} custom-call(bf16[384,2,4096]{2,1,0:T(2,128)(2,1)S(1)} %bitcast.4, bf16[384,768]{1,0:T(8,128)(2,1)S(1)} %get-tuple-element.34.refs_1_, bf16[2,4096,512]{2,1,0:T(8,128)(2,1)S(1)} %bitcast.2, bf16[208,128]{1,0:T(8,128)(2,1)S(1)} %get-tuple-element.30.refs_3_.refs_0_.refs_5_), custom_call_target="tpu_custom_call" | custom-call | flops 1 | bytes 1 | tf_op jit(solution)/shard_map/rotate_out/pallas_call | solution.py:241
  15.7 0.0 collective-permute-done.1.refs_1_.refs_6_
  15.8 0.0 collective-permute-done.3.refs_3_.refs_8_
  15.8 0.0 collective-permute-done.2.refs_2_.refs_7_
  15.8 0.1 split_out.1
  15.9 0.1 collective-permute-start.4
  16.0 1.7 %collective-permute-done.4.refs_1_ = f32[768,128]{1,0:T(8,128)S(1)} collective-permute-done((f32[768,128]{1,0:T(8,128)S(1)}, f32[768,128]{1,0:T(8,128)S(1)}, u32[]{:S(2)}, u32[]{:S(2)}) %collective-permute-start.4) | collective-permute-done | bytes 393248 | tf_op jit(solution)/shard_map/ppermute | solution.py:314
  17.7 1.6 %collective-permute-start.5 = (bf16[384,128]{1,0:T(8,128)(2,1)S(1)}, bf16[384,128]{1,0:T(8,128)(2,1)S(1)}, u32[]{:S(2)}, u32[]{:S(2)}) collective-permute-start(bf16[384,128]{1,0:T(8,128)(2,1)S(1)} %get-tuple-element.37), channel_id=1, source_target_pairs={{0,2},{1,3},{2,0},{3,1},{4,6},{5,7},{6,4},{7,5},{8,10},{9,11},{10,... | collective-permute-start | bytes 294920 | tf_op jit(solution)/shard_map/ppermute | solution.py:316
  19.3 3.3 %collective-permute-done.5.refs_4_.refs_1_ = bf16[384,128]{1,0:T(8,128)(2,1)S(1)} collective-permute-done((bf16[384,128]{1,0:T(8,128)(2,1)S(1)}, bf16[384,128]{1,0:T(8,128)(2,1)S(1)}, u32[]{:S(2)}, u32[]{:S(2)}) %collective-permute-start.5) | collective-permute-done | bytes 98336 | tf_op jit(solution)/shard_map/ppermute | solution.py:316
  22.7 1.6 %collective-permute-start.6 = (bf16[768,128]{1,0:T(8,128)(2,1)S(1)}, bf16[768,128]{1,0:T(8,128)(2,1)S(1)}, u32[]{:S(2)}, u32[]{:S(2)}) collective-permute-start(bf16[768,128]{1,0:T(8,128)(2,1)S(1)} %stack_in.1.refs_0_), channel_id=1, source_target_pairs={{0,2},{1,3},{2,0},{3,1},{4,6},{5,7},{6,4},{7,5},{8,10},{9,11},{10,... | collective-permute-start | bytes 589832 | tf_op jit(solution)/shard_map/ppermute | solution.py:325
  24.3 2.9 %collective-permute-start.10 = (bf16[432,128]{1,0:T(8,128)(2,1)S(1)}, bf16[432,128]{1,0:T(8,128)(2,1)S(1)}, u32[]{:S(2)}, u32[]{:S(2)}) collective-permute-start(bf16[432,128]{1,0:T(8,128)(2,1)S(1)} %get-tuple-element.45), channel_id=1, source_target_pairs={{0,8},{4,12},{8,0},{12,4},{1,9},{5,13},{9,1},{13,5},{2,10},{6,14},... | collective-permute-start | bytes 331784 | tf_op jit(solution)/shard_map/ppermute | solution.py:276
  27.1 1.3 %collective-permute-start.11 = (bf16[416,128]{1,0:T(8,128)(2,1)S(1)}, bf16[416,128]{1,0:T(8,128)(2,1)S(1)}, u32[]{:S(2)}, u32[]{:S(2)}) collective-permute-start(bf16[416,128]{1,0:T(8,128)(2,1)S(1)} %get-tuple-element.46), channel_id=1, source_target_pairs={{0,12},{4,8},{8,4},{12,0},{1,13},{5,9},{9,5},{13,1},{2,14},{6,10},... | collective-permute-start | bytes 319496 | tf_op jit(solution)/shard_map/ppermute | solution.py:276
  28.5 0.0 collective-permute-start.9
  28.5 0.4 %collective-permute-done.6.refs_1_ = bf16[768,128]{1,0:T(8,128)(2,1)S(1)} collective-permute-done((bf16[768,128]{1,0:T(8,128)(2,1)S(1)}, bf16[768,128]{1,0:T(8,128)(2,1)S(1)}, u32[]{:S(2)}, u32[]{:S(2)}) %collective-permute-start.6) | collective-permute-done | bytes 196640 | tf_op jit(solution)/shard_map/ppermute | solution.py:325
  28.9 0.1 collective-permute-start.7
  29.0 0.5 %collective-permute-start.8 = (bf16[384,128]{1,0:T(8,128)(2,1)S(1)}, bf16[384,128]{1,0:T(8,128)(2,1)S(1)}, u32[]{:S(2)}, u32[]{:S(2)}) collective-permute-start(bf16[384,128]{1,0:T(8,128)(2,1)S(1)} %get-tuple-element.39.refs_2_), channel_id=1, source_target_pairs={{0,1},{1,0},{2,3},{3,2},{4,5},{5,4},{6,7},{7,6},{8,9},{9,8},{10,11... | collective-permute-start | bytes 294920 | tf_op jit(solution)/shard_map/ppermute | solution.py:327
  29.5 0.8 %collective-permute-done.7.refs_3_ = bf16[384,128]{1,0:T(8,128)(2,1)S(1)} collective-permute-done((bf16[384,128]{1,0:T(8,128)(2,1)S(1)}, bf16[384,128]{1,0:T(8,128)(2,1)S(1)}, u32[]{:S(2)}, u32[]{:S(2)}) %collective-permute-start.7) | collective-permute-done | bytes 98336 | tf_op jit(solution)/shard_map/ppermute | solution.py:327
  30.3 0.2 collective-permute-done.8.refs_4_
  30.4 0.0 copy-done
  30.4 1.1 %mask_in.1 = (bf16[2,768,512]{2,1,0:T(8,128)(2,1)S(1)}, f32[2,8,128]{2,1,0:T(8,128)S(1)}) custom-call(s32[2]{0:T(128)S(1)} %copy-done, bf16[384,128]{1,0:T(8,128)(2,1)S(1)} %get-tuple-element.38.refs_1_, bf16[384,128]{1,0:T(8,128)(2,1)S(1)} %get-tuple-element.39.refs_2_, bf16[384,128]{1,0:T(8,128)(2,1)S(1)} %collective-permute-done.7.refs_3_, ...), custom_call_target="tpu_custom_call" | custom-call | flops 1 | bytes 1 | tf_op jit(solution)/shard_map/mask_in/pallas_call | solution.py:241
  31.5 3.9 %collective-permute-done.9.refs_3_ = bf16[400,128]{1,0:T(8,128)(2,1)S(1)} collective-permute-done((bf16[400,128]{1,0:T(8,128)(2,1)S(1)}, bf16[400,128]{1,0:T(8,128)(2,1)S(1)}, u32[]{:S(2)}, u32[]{:S(2)}) %collective-permute-start.9) | collective-permute-done | bytes 102432 | tf_op jit(solution)/shard_map/ppermute | solution.py:276
  35.4 0.0 collective-permute-done.11.refs_5_
  35.4 0.0 collective-permute-done.10.refs_4_
  35.4 1.1 %blocks.1 = f32[2,128,128]{2,1,0:T(8,128)} custom-call(f32[2,8,128]{2,1,0:T(8,128)S(1)} %get-tuple-element.40.refs_0_, bf16[2,768,512]{2,1,0:T(8,128)(2,1)S(1)} %get-tuple-element.41.refs_1_, bf16[384,128]{1,0:T(8,128)(2,1)S(1)} %get-tuple-element.43.refs_2_, bf16[400,128]{1,0:T(8,128)(2,1)S(1)} %collective-permute-done.9.refs_3_, ...), custom_call_target="tpu_custom_call" | custom-call | flops 1 | bytes 1 | tf_op jit(solution)/shard_map/blocks/pallas_call | solution.py:241
  (7 shorter events, 0.2 us)
Async XLA Ops:
  3.4 7.6 %slice-start = ((s8[8388608]{0:T(1024)(128)(4,1)}), s8[4194304]{0:T(1024)(128)(4,1)S(1)}, s32[]{:S(2)}) async-start(s8[8388608]{0:T(1024)(128)(4,1)} %bitcast.1), calls=%async_computation | async-start | bytes 8388608
  3.5 7.6 %slice-start.2 = ((s8[6291456]{0:T(1024)(128)(4,1)}), s8[4194304]{0:T(1024)(128)(4,1)S(1)}, s32[]{:S(2)}) async-start(s8[6291456]{0:T(1024)(128)(4,1)} %bitcast.3), calls=%async_computation.2 | async-start | bytes 8388608
  3.5 7.6 %slice-start.1 = ((s8[8388608]{0:T(1024)(128)(4,1)}), s8[4194304]{0:T(1024)(128)(4,1)S(1)}, s32[]{:S(2)}) async-start(s8[8388608]{0:T(1024)(128)(4,1)} %bitcast.1), calls=%async_computation.1 | async-start | bytes 8388608
  3.5 7.6 %slice-start.3 = ((s8[6291456]{0:T(1024)(128)(4,1)}), s8[2097152]{0:T(1024)(128)(4,1)S(1)}, s32[]{:S(2)}) async-start(s8[6291456]{0:T(1024)(128)(4,1)} %bitcast.3), calls=%async_computation.3 | async-start | bytes 4194304
  3.6 1.9 %collective-permute-start = (f32[768,128]{1,0:T(8,128)S(1)}, f32[768,128]{1,0:T(8,128)S(1)}, u32[]{:S(2)}, u32[]{:S(2)}) collective-permute-start(f32[768,128]{1,0:T(8,128)S(1)} %get-tuple-element.28), channel_id=1, source_target_pairs={{0,1},{1,0},{2,3},{3,2},{4,5},{5,4},{6,7},{7,6},{8,9},{9,8},{10,11... | collective-permute-start | bytes 1179656 | tf_op jit(solution)/shard_map/ppermute | solution.py:299
  5.5 10.3 %collective-permute-start.2 = (bf16[240,128]{1,0:T(8,128)(2,1)S(1)}, bf16[240,128]{1,0:T(8,128)(2,1)S(1)}, u32[]{:S(2)}, u32[]{:S(2)}) collective-permute-start(bf16[240,128]{1,0:T(8,128)(2,1)S(1)} %get-tuple-element.32), channel_id=1, source_target_pairs={{0,8},{4,12},{8,0},{12,4},{1,9},{5,13},{9,1},{13,5},{2,10},{6,14},... | collective-permute-start | bytes 184328 | tf_op jit(solution)/shard_map/ppermute | solution.py:276
  9.5 6.3 %collective-permute-start.3 = (bf16[224,128]{1,0:T(8,128)(2,1)S(1)}, bf16[224,128]{1,0:T(8,128)(2,1)S(1)}, u32[]{:S(2)}, u32[]{:S(2)}) collective-permute-start(bf16[224,128]{1,0:T(8,128)(2,1)S(1)} %get-tuple-element.33), channel_id=1, source_target_pairs={{0,12},{4,8},{8,4},{12,0},{1,13},{5,9},{9,5},{13,1},{2,14},{6,10},... | collective-permute-start | bytes 172040 | tf_op jit(solution)/shard_map/ppermute | solution.py:276
  10.9 4.9 %collective-permute-start.1 = (bf16[208,128]{1,0:T(8,128)(2,1)S(1)}, bf16[208,128]{1,0:T(8,128)(2,1)S(1)}, u32[]{:S(2)}, u32[]{:S(2)}) collective-permute-start(bf16[208,128]{1,0:T(8,128)(2,1)S(1)} %get-tuple-element.31), channel_id=1, source_target_pairs={{0,4},{4,0},{8,12},{12,8},{1,5},{5,1},{9,13},{13,9},{2,6},{6,2},{1... | collective-permute-start | bytes 159752 | tf_op jit(solution)/shard_map/ppermute | solution.py:276
  11.1 19.3 %copy-start = (s32[2]{0:T(128)S(1)}, s32[2]{0:T(128)}, u32[]{:S(2)}) copy-start(s32[2]{0:T(128)} %refs_0_.5) | copy-start | bytes 28
  15.9 1.8 %collective-permute-start.4 = (f32[768,128]{1,0:T(8,128)S(1)}, f32[768,128]{1,0:T(8,128)S(1)}, u32[]{:S(2)}, u32[]{:S(2)}) collective-permute-start(f32[768,128]{1,0:T(8,128)S(1)} %get-tuple-element.36), channel_id=1, source_target_pairs={{0,1},{1,0},{2,3},{3,2},{4,5},{5,4},{6,7},{7,6},{8,9},{9,8},{10,11... | collective-permute-start | bytes 1179656 | tf_op jit(solution)/shard_map/ppermute | solution.py:314
  17.7 4.9 %collective-permute-start.5 = (bf16[384,128]{1,0:T(8,128)(2,1)S(1)}, bf16[384,128]{1,0:T(8,128)(2,1)S(1)}, u32[]{:S(2)}, u32[]{:S(2)}) collective-permute-start(bf16[384,128]{1,0:T(8,128)(2,1)S(1)} %get-tuple-element.37), channel_id=1, source_target_pairs={{0,2},{1,3},{2,0},{3,1},{4,6},{5,7},{6,4},{7,5},{8,10},{9,11},{10,... | collective-permute-start | bytes 294920 | tf_op jit(solution)/shard_map/ppermute | solution.py:316
  22.7 6.2 %collective-permute-start.6 = (bf16[768,128]{1,0:T(8,128)(2,1)S(1)}, bf16[768,128]{1,0:T(8,128)(2,1)S(1)}, u32[]{:S(2)}, u32[]{:S(2)}) collective-permute-start(bf16[768,128]{1,0:T(8,128)(2,1)S(1)} %stack_in.1.refs_0_), channel_id=1, source_target_pairs={{0,2},{1,3},{2,0},{3,1},{4,6},{5,7},{6,4},{7,5},{8,10},{9,11},{10,... | collective-permute-start | bytes 589832 | tf_op jit(solution)/shard_map/ppermute | solution.py:325
  24.3 11.2 %collective-permute-start.10 = (bf16[432,128]{1,0:T(8,128)(2,1)S(1)}, bf16[432,128]{1,0:T(8,128)(2,1)S(1)}, u32[]{:S(2)}, u32[]{:S(2)}) collective-permute-start(bf16[432,128]{1,0:T(8,128)(2,1)S(1)} %get-tuple-element.45), channel_id=1, source_target_pairs={{0,8},{4,12},{8,0},{12,4},{1,9},{5,13},{9,1},{13,5},{2,10},{6,14},... | collective-permute-start | bytes 331784 | tf_op jit(solution)/shard_map/ppermute | solution.py:276
  27.1 8.3 %collective-permute-start.11 = (bf16[416,128]{1,0:T(8,128)(2,1)S(1)}, bf16[416,128]{1,0:T(8,128)(2,1)S(1)}, u32[]{:S(2)}, u32[]{:S(2)}) collective-permute-start(bf16[416,128]{1,0:T(8,128)(2,1)S(1)} %get-tuple-element.46), channel_id=1, source_target_pairs={{0,12},{4,8},{8,4},{12,0},{1,13},{5,9},{9,5},{13,1},{2,14},{6,10},... | collective-permute-start | bytes 319496 | tf_op jit(solution)/shard_map/ppermute | solution.py:276
  28.5 6.9 %collective-permute-start.9 = (bf16[400,128]{1,0:T(8,128)(2,1)S(1)}, bf16[400,128]{1,0:T(8,128)(2,1)S(1)}, u32[]{:S(2)}, u32[]{:S(2)}) collective-permute-start(bf16[400,128]{1,0:T(8,128)(2,1)S(1)} %get-tuple-element.44), channel_id=1, source_target_pairs={{0,4},{4,0},{8,12},{12,8},{1,5},{5,1},{9,13},{13,9},{2,6},{6,2},{1... | collective-permute-start | bytes 307208 | tf_op jit(solution)/shard_map/ppermute | solution.py:276
  28.9 1.4 %collective-permute-start.7 = (bf16[384,128]{1,0:T(8,128)(2,1)S(1)}, bf16[384,128]{1,0:T(8,128)(2,1)S(1)}, u32[]{:S(2)}, u32[]{:S(2)}) collective-permute-start(bf16[384,128]{1,0:T(8,128)(2,1)S(1)} %get-tuple-element.38.refs_1_), channel_id=1, source_target_pairs={{0,1},{1,0},{2,3},{3,2},{4,5},{5,4},{6,7},{7,6},{8,9},{9,8},{10,11... | collective-permute-start | bytes 294920 | tf_op jit(solution)/shard_map/ppermute | solution.py:327
  29.0 1.4 %collective-permute-start.8 = (bf16[384,128]{1,0:T(8,128)(2,1)S(1)}, bf16[384,128]{1,0:T(8,128)(2,1)S(1)}, u32[]{:S(2)}, u32[]{:S(2)}) collective-permute-start(bf16[384,128]{1,0:T(8,128)(2,1)S(1)} %get-tuple-element.39.refs_2_), channel_id=1, source_target_pairs={{0,1},{1,0},{2,3},{3,2},{4,5},{5,4},{6,7},{7,6},{8,9},{9,8},{10,11... | collective-permute-start | bytes 294920 | tf_op jit(solution)/shard_map/ppermute | solution.py:327

commit v9 on v8

--- a/solution.py
+++ b/solution.py
@@ -10,8 +10,8 @@
 F32 = jnp.float32
 BF16 = jnp.bfloat16
 CHUNK = 1024
-PARTS = 3
 VMEM = 20 * 2**20
+FAR_FIRST = (2, 3, 1)
 LABEL_ROWS = 16
 
 
@@ -39,14 +39,13 @@
     acc, label, pick,
     acts_v, routes_v, ids_v, basis_v, sems,
 ):
-    tokens, features = acts.shape
+    tokens = acts.shape[0]
     experts = basis_in.shape[0]
     cap = tokens // 2
-    parts = [pl.ds(at, features // PARTS) for at in range(0, features, features // PARTS)]
     fetch = fetcher(sems)
     first = [fetch(routes, routes_v), fetch(ids, ids_v)]
-    acts_in = [fetch(acts.at[:, part], acts_v.at[:, part]) for part in parts]
-    bases = [fetch(basis_in.at[:, part, :], basis_v.at[:, part, :]) for part in parts]
+    acts_in = fetch(acts, acts_v)
+    bases = [fetch(basis_in.at[e], basis_v.at[e]) for e in range(experts)]
     for copy in first:
         copy.wait()
     hits = [
@@ -86,15 +85,11 @@
         block = jnp.where(row == at, mine, block)
     label[...] = block.astype(BF16)
 
-    chosen = []
-    for part, copy in zip(parts, acts_in):
-        copy.wait()
-        chosen.append(dot(pick_in, acts_v[:, part]).astype(BF16))
-    for n, part in enumerate(parts):
-        bases[n].wait()
-        for e in range(experts):
-            more = dot(chosen[n][e * cap : (e + 1) * cap], basis_v[e, part, :])
-            acc[e] = more if n == 0 else acc[e] + more
+    acts_in.wait()
+    chosen = dot(pick_in, acts_v[...]).astype(BF16)
+    for e in range(experts):
+        bases[e].wait()
+        acc[e] = dot(chosen[e * cap : (e + 1) * cap], basis_v[e])
 
 
 def split_in_kernel(acc, keep, send):
@@ -135,19 +130,13 @@
             at += cap
 
 
-def fill(ref, start):
-    if start < ref.shape[0]:
-        ref[start:, :] = jnp.zeros((ref.shape[0] - start, ref.shape[1]), ref.dtype)
-
-
 def pair_in_kernel(kept, got, label, *pays):
     slab = kept.shape[0] // len(pays)
     d = lax.axis_index("dp")
     for k, pay in enumerate(pays):
         rows = pl.ds(pl.multiple_of((d ^ k) * slab, 16), slab)
         pay[:slab, :] = (kept[rows, :] + got[rows, :]).astype(BF16)
-        pay[slab : slab + LABEL_ROWS, :] = label[...]
-        fill(pay, slab + LABEL_ROWS)
+        pay[slab:, :] = label[...]
 
 
 def pair_out_kernel(kept, got, keep, send):
@@ -159,12 +148,10 @@
     send[...] = (kept[other, :] + got[other, :]).astype(BF16)
 
 
-def round_kernel(kept, got, *pays):
+def round_kernel(kept, got, out):
     outer = kept.shape[0]
-    rows = (kept[...] + got[...].astype(F32)).astype(BF16)
-    for pay in pays:
-        pay[:outer, :] = rows
-        fill(pay, outer)
+    out[:outer, :] = (kept[...] + got[...].astype(F32)).astype(BF16)
+    out[outer:, :] = jnp.zeros((out.shape[0] - outer, 128), BF16)
 
 
 def stack_kernel(slab, *refs):
@@ -184,18 +171,17 @@
     mine, other, pieces = refs[:2], refs[2:4], refs[4:-2]
     out, divisor = refs[-2:]
     experts, dp = out.shape[0], len(pieces)
-    half = 2 * mine[0].shape[0] // (dp * experts)
-    slab = experts * half
+    slab = 2 * mine[0].shape[0] // dp
+    half = slab // experts
     core = lax.rem(lax.axis_index("tensor"), 2)
     for e in range(experts):
         divisor[e] = jnp.full(divisor.shape[1:], counts[e].astype(F32), F32)
         rows, labels = [], []
-        for which, refs in ((core, mine), (1 - core, other)):
+        for which, parts in ((core, mine), (1 - core, other)):
             for k, piece in enumerate(pieces):
-                at = (k % (dp // 2) * experts + e) * half
-                rows.append(refs[k // (dp // 2)][at : at + half, :])
-                label = piece[slab : slab + LABEL_ROWS, :].astype(F32)
-                label = label[2 * e : 2 * e + 2, :half]
+                at = k % (dp // 2) * slab + e * half
+                rows.append(parts[k // (dp // 2)][at : at + half, :])
+                label = piece[slab:, :].astype(F32)[2 * e : 2 * e + 2, :half]
                 labels.append(jnp.where(which == 0, label[0:1], label[1:2]))
         rows = jnp.concatenate(rows, axis=0).astype(F32)
         labels = jnp.concatenate(labels, axis=1)
@@ -290,7 +276,7 @@
             pltpu.VMEM((2, tokens), jnp.int32),
             pltpu.VMEM((tokens,), jnp.int32),
             pltpu.VMEM(basis_in.shape, BF16),
-            pltpu.SemaphoreType.DMA((3 + 2 * PARTS,)),
+            pltpu.SemaphoreType.DMA((3 + experts,)),
         ],
     )(pin(acts), pin(routes.T), pin(example_ids), pin(basis_in))
     keep, send = call(
@@ -298,12 +284,10 @@
     )(acc)
     got = lax.ppermute(send, "tensor", core)
     slab = half // dp
-    pieces = call(
-        pair_in_kernel,
-        "pair_in",
-        [rows(slab + LABEL_ROWS + extra, BF16) for extra in (0, 0, 32, 16)],
-    )(keep, got, label)
-    arrived = [pieces[0]] + [swap(pieces[k], k) for k in range(1, dp)]
+    pieces = call(pair_in_kernel, "pair_in", [rows(slab + LABEL_ROWS, BF16)] * dp)(
+        keep, got, label
+    )
+    arrived = [pieces[0]] + [swap(pieces[k], k) for k in FAR_FIRST]
 
     acc = call(rotate_out_kernel, "rotate_out", partial, after=[pieces[0]])(
         grads, pick, basis_out
@@ -314,10 +298,8 @@
     got = lax.ppermute(send, "tensor", core)
     keep, send = call(pair_out_kernel, "pair_out", (rows(wide, F32), rows(wide, BF16)))(keep, got)
     got = lax.ppermute(send, "tensor", across)
-    outs = call(
-        round_kernel, "round_out", [rows(wide + extra, BF16) for extra in (0, 16, 48, 32)]
-    )(keep, got)
-    outs = [outs[0]] + [swap(outs[k], k) for k in range(1, dp)]
+    out = call(round_kernel, "round_out", rows(wide + 16, BF16))(keep, got)
+    outs = [out] + [swap(out, k) for k in FAR_FIRST]
 
     near = call(
         functools.partial(stack_kernel, slab), "stack_in", rows(half, BF16), after=[got]

time: 36.7 us -> 36 us (0.981)
  transfers between devices with their start and end apart: 12 -> 12, of which waited for: 7 -> 8; matrix products, arithmetic and copies ran while one was open for 0% -> 0% of each run, Pallas kernels for 16% -> 16%
where the time goes in v9:
time: 36 us; the launch traced here: 35.8 us
  starting transfers between devices  14.1 us (39%)
  waiting for transfers between devices  11.4 us (32%)
  Pallas kernels  10.2 us (28%)
    pallas_call x11, Pallas kernels, run(): pl.pallas_call(body, out_shape=out_shape, in_specs=(specs or [vmem] * len...  10.2 us
    ppermute x6, starting transfers between devices, swap(): return lax.ppermute(x, 'dp', [(d, d ^ k) for d in range(dp)])  9.82 us
    ppermute x6, waiting for transfers between devices, swap(): return lax.ppermute(x, 'dp', [(d, d ^ k) for d in range(dp)])  3.64 us
    ppermute x1, waiting for transfers between devices, fast(): got = lax.ppermute(send, 'tensor', across)  3.35 us
    ppermute x2, waiting for transfers between devices, fast(): got = lax.ppermute(send, 'tensor', core)  3.06 us
    ppermute x1, starting transfers between devices, fast(): got = lax.ppermute(send, 'tensor', across)  1.55 us
    ppermute x1, starting transfers between devices, fast(): far = lax.ppermute(near, 'tensor', across)  1.55 us
    ppermute x2, waiting for transfers between devices, fast(): other = [lax.ppermute(x, 'tensor', core) for x in mine]  0.94 us
  transfers between devices with their start and end apart: 12, of which 8 were waited for; matrix products, arithmetic and copies ran while one was open for 0% of the time, Pallas kernels for 16%

profile of v9, /device:TPU:0, one launch (start us, length us, event | category | flops | bytes accessed | tf_op | source)
XLA Modules:
  0.0 35.8 jit_solution(1892761797781384789)
XLA Ops:
  0.0 3.1 %rotate_in.1 = (f32[2,192,512]{2,1,0:T(8,128)S(1)}, bf16[16,128]{1,0:T(8,128)(2,1)S(1)}, bf16[384,768]{1,0:T(8,128)(2,1)S(1)}) custom-call(bf16[384,1536]{1,0:T(8,128)(2,1)} %refs_0_.3, s32[2,384]{1,0:T(2,128)} %bitcast.5, s32[384]{0:T(512)} %refs_2_.2, bf16[2,1536,512]{2,1,0:T(8,128)(2,1)} %refs_3_.1), custom_call_target="tpu_custom_call" | custom-call | flops 1 | bytes 1 | tf_op jit(solution)/shard_map/rotate_in/pallas_call | solution.py:227
  3.1 0.0 slice-start
  3.1 0.0 slice-start.2
  3.1 0.0 slice-start.1
  3.1 0.0 slice-start.3
  3.1 0.1 split_in.1
  3.2 0.5 %collective-permute-start = (f32[768,128]{1,0:T(8,128)S(1)}, f32[768,128]{1,0:T(8,128)S(1)}, u32[]{:S(2)}, u32[]{:S(2)}) collective-permute-start(f32[768,128]{1,0:T(8,128)S(1)} %get-tuple-element.24), channel_id=1, source_target_pairs={{0,1},{1,0},{2,3},{3,2},{4,5},{5,4},{6,7},{7,6},{8,9},{9,8},{10,11... | collective-permute-start | bytes 1179656 | tf_op jit(solution)/shard_map/ppermute | solution.py:285
  3.7 1.3 %collective-permute-done.refs_1_ = f32[768,128]{1,0:T(8,128)S(1)} collective-permute-done((f32[768,128]{1,0:T(8,128)S(1)}, f32[768,128]{1,0:T(8,128)S(1)}, u32[]{:S(2)}, u32[]{:S(2)}) %collective-permute-start) | collective-permute-done | bytes 393248 | tf_op jit(solution)/shard_map/ppermute | solution.py:285
  5.1 4.0 %collective-permute-start.1 = (bf16[208,128]{1,0:T(8,128)(2,1)S(1)}, bf16[208,128]{1,0:T(8,128)(2,1)S(1)}, u32[]{:S(2)}, u32[]{:S(2)}) collective-permute-start(bf16[208,128]{1,0:T(8,128)(2,1)S(1)} %get-tuple-element.27), channel_id=1, source_target_pairs={{0,8},{4,12},{8,0},{12,4},{1,9},{5,13},{9,1},{13,5},{2,10},{6,14},... | collective-permute-start | bytes 159752 | tf_op jit(solution)/shard_map/ppermute | solution.py:262
  9.2 1.3 %collective-permute-start.2 = (bf16[208,128]{1,0:T(8,128)(2,1)S(1)}, bf16[208,128]{1,0:T(8,128)(2,1)S(1)}, u32[]{:S(2)}, u32[]{:S(2)}) collective-permute-start(bf16[208,128]{1,0:T(8,128)(2,1)S(1)} %get-tuple-element.28), channel_id=1, source_target_pairs={{0,12},{4,8},{8,4},{12,0},{1,13},{5,9},{9,5},{13,1},{2,14},{6,10},... | collective-permute-start | bytes 159752 | tf_op jit(solution)/shard_map/ppermute | solution.py:262
  10.5 0.2 collective-permute-start.3
  10.7 0.0 slice-done
  10.7 0.0 slice-done.2
  10.7 0.0 slice-done.1
  10.7 0.0 slice-done.3
  10.8 0.0 copy-start
  10.8 4.6 %rotate_out.1.refs_0_ = f32[2,192,512]{2,1,0:T(8,128)S(1)} custom-call(bf16[384,2,4096]{2,1,0:T(2,128)(2,1)S(1)} %bitcast.4, bf16[384,768]{1,0:T(8,128)(2,1)S(1)} %get-tuple-element.30.refs_1_, bf16[2,4096,512]{2,1,0:T(8,128)(2,1)S(1)} %bitcast.2, bf16[208,128]{1,0:T(8,128)(2,1)S(1)} %get-tuple-element.26.refs_3_.refs_0_.refs_5_), custom_call_target="tpu_custom_call" | custom-call | flops 1 | bytes 1 | tf_op jit(solution)/shard_map/rotate_out/pallas_call | solution.py:227
  15.4 0.0 collective-permute-done.1.refs_1_.refs_6_
  15.4 0.0 collective-permute-done.2.refs_2_.refs_7_
  15.4 0.0 collective-permute-done.3.refs_3_.refs_8_
  15.4 0.1 split_out.1
  15.6 0.1 collective-permute-start.4
  15.6 1.7 %collective-permute-done.4.refs_1_ = f32[768,128]{1,0:T(8,128)S(1)} collective-permute-done((f32[768,128]{1,0:T(8,128)S(1)}, f32[768,128]{1,0:T(8,128)S(1)}, u32[]{:S(2)}, u32[]{:S(2)}) %collective-permute-start.4) | collective-permute-done | bytes 393248 | tf_op jit(solution)/shard_map/ppermute | solution.py:298
  17.4 1.6 %collective-permute-start.5 = (bf16[384,128]{1,0:T(8,128)(2,1)S(1)}, bf16[384,128]{1,0:T(8,128)(2,1)S(1)}, u32[]{:S(2)}, u32[]{:S(2)}) collective-permute-start(bf16[384,128]{1,0:T(8,128)(2,1)S(1)} %get-tuple-element.33), channel_id=1, source_target_pairs={{0,2},{1,3},{2,0},{3,1},{4,6},{5,7},{6,4},{7,5},{8,10},{9,11},{10,... | collective-permute-start | bytes 294920 | tf_op jit(solution)/shard_map/ppermute | solution.py:300
  18.9 3.3 %collective-permute-done.5.refs_4_.refs_1_ = bf16[384,128]{1,0:T(8,128)(2,1)S(1)} collective-permute-done((bf16[384,128]{1,0:T(8,128)(2,1)S(1)}, bf16[384,128]{1,0:T(8,128)(2,1)S(1)}, u32[]{:S(2)}, u32[]{:S(2)}) %collective-permute-start.5) | collective-permute-done | bytes 98336 | tf_op jit(solution)/shard_map/ppermute | solution.py:300
  22.3 1.6 %collective-permute-start.6 = (bf16[768,128]{1,0:T(8,128)(2,1)S(1)}, bf16[768,128]{1,0:T(8,128)(2,1)S(1)}, u32[]{:S(2)}, u32[]{:S(2)}) collective-permute-start(bf16[768,128]{1,0:T(8,128)(2,1)S(1)} %stack_in.1.refs_0_), channel_id=1, source_target_pairs={{0,2},{1,3},{2,0},{3,1},{4,6},{5,7},{6,4},{7,5},{8,10},{9,11},{10,... | collective-permute-start | bytes 589832 | tf_op jit(solution)/shard_map/ppermute | solution.py:307
  23.9 2.9 %collective-permute-start.9 = (bf16[400,128]{1,0:T(8,128)(2,1)S(1)}, bf16[400,128]{1,0:T(8,128)(2,1)S(1)}, u32[]{:S(2)}, u32[]{:S(2)}) collective-permute-start(bf16[400,128]{1,0:T(8,128)(2,1)S(1)} %round_out.1.refs_2_), channel_id=1, source_target_pairs={{0,8},{4,12},{8,0},{12,4},{1,9},{5,13},{9,1},{13,5},{2,10},{6,14},... | collective-permute-start | bytes 307208 | tf_op jit(solution)/shard_map/ppermute | solution.py:262
  26.8 1.3 %collective-permute-start.10 = (bf16[400,128]{1,0:T(8,128)(2,1)S(1)}, bf16[400,128]{1,0:T(8,128)(2,1)S(1)}, u32[]{:S(2)}, u32[]{:S(2)}) collective-permute-start(bf16[400,128]{1,0:T(8,128)(2,1)S(1)} %round_out.1.refs_2_), channel_id=1, source_target_pairs={{0,12},{4,8},{8,4},{12,0},{1,13},{5,9},{9,5},{13,1},{2,14},{6,10},... | collective-permute-start | bytes 307208 | tf_op jit(solution)/shard_map/ppermute | solution.py:262
  28.1 0.0 collective-permute-start.11
  28.1 0.4 %collective-permute-done.6.refs_1_ = bf16[768,128]{1,0:T(8,128)(2,1)S(1)} collective-permute-done((bf16[768,128]{1,0:T(8,128)(2,1)S(1)}, bf16[768,128]{1,0:T(8,128)(2,1)S(1)}, u32[]{:S(2)}, u32[]{:S(2)}) %collective-permute-start.6) | collective-permute-done | bytes 196640 | tf_op jit(solution)/shard_map/ppermute | solution.py:307
  28.5 0.1 collective-permute-start.7
  28.6 0.5 %collective-permute-start.8 = (bf16[384,128]{1,0:T(8,128)(2,1)S(1)}, bf16[384,128]{1,0:T(8,128)(2,1)S(1)}, u32[]{:S(2)}, u32[]{:S(2)}) collective-permute-start(bf16[384,128]{1,0:T(8,128)(2,1)S(1)} %get-tuple-element.35.refs_2_), channel_id=1, source_target_pairs={{0,1},{1,0},{2,3},{3,2},{4,5},{5,4},{6,7},{7,6},{8,9},{9,8},{10,11... | collective-permute-start | bytes 294920 | tf_op jit(solution)/shard_map/ppermute | solution.py:309
  29.1 0.8 %collective-permute-done.7.refs_3_ = bf16[384,128]{1,0:T(8,128)(2,1)S(1)} collective-permute-done((bf16[384,128]{1,0:T(8,128)(2,1)S(1)}, bf16[384,128]{1,0:T(8,128)(2,1)S(1)}, u32[]{:S(2)}, u32[]{:S(2)}) %collective-permute-start.7) | collective-permute-done | bytes 98336 | tf_op jit(solution)/shard_map/ppermute | solution.py:309
  29.9 0.2 collective-permute-done.8.refs_4_
  30.1 0.0 copy-done
  30.1 1.1 %mask_in.1 = (bf16[2,768,512]{2,1,0:T(8,128)(2,1)S(1)}, f32[2,8,128]{2,1,0:T(8,128)S(1)}) custom-call(s32[2]{0:T(128)S(1)} %copy-done, bf16[384,128]{1,0:T(8,128)(2,1)S(1)} %get-tuple-element.34.refs_1_, bf16[384,128]{1,0:T(8,128)(2,1)S(1)} %get-tuple-element.35.refs_2_, bf16[384,128]{1,0:T(8,128)(2,1)S(1)} %collective-permute-done.7.refs_3_, ...), custom_call_target="tpu_custom_call" | custom-call | flops 1 | bytes 1 | tf_op jit(solution)/shard_map/mask_in/pallas_call | solution.py:227
  31.1 3.2 %collective-permute-done.9.refs_3_ = bf16[400,128]{1,0:T(8,128)(2,1)S(1)} collective-permute-done((bf16[400,128]{1,0:T(8,128)(2,1)S(1)}, bf16[400,128]{1,0:T(8,128)(2,1)S(1)}, u32[]{:S(2)}, u32[]{:S(2)}) %collective-permute-start.9) | collective-permute-done | bytes 102432 | tf_op jit(solution)/shard_map/ppermute | solution.py:262
  34.3 0.0 collective-permute-done.10.refs_4_
  34.3 0.4 %collective-permute-done.11.refs_5_ = bf16[400,128]{1,0:T(8,128)(2,1)S(1)} collective-permute-done((bf16[400,128]{1,0:T(8,128)(2,1)S(1)}, bf16[400,128]{1,0:T(8,128)(2,1)S(1)}, u32[]{:S(2)}, u32[]{:S(2)}) %collective-permute-start.11) | collective-permute-done | bytes 102432 | tf_op jit(solution)/shard_map/ppermute | solution.py:262
  34.8 1.1 %blocks.1 = f32[2,128,128]{2,1,0:T(8,128)} custom-call(f32[2,8,128]{2,1,0:T(8,128)S(1)} %get-tuple-element.36.refs_0_, bf16[2,768,512]{2,1,0:T(8,128)(2,1)S(1)} %get-tuple-element.37.refs_1_, bf16[400,128]{1,0:T(8,128)(2,1)S(1)} %round_out.1.refs_2_, bf16[400,128]{1,0:T(8,128)(2,1)S(1)} %collective-permute-done.9.refs_3_, ...), custom_call_target="tpu_custom_call" | custom-call | flops 1 | bytes 1 | tf_op jit(solution)/shard_map/blocks/pallas_call | solution.py:227
  (7 shorter events, 0.2 us)
Async XLA Ops:
  3.1 7.6 %slice-start = ((s8[8388608]{0:T(1024)(128)(4,1)}), s8[4194304]{0:T(1024)(128)(4,1)S(1)}, s32[]{:S(2)}) async-start(s8[8388608]{0:T(1024)(128)(4,1)} %bitcast.1), calls=%async_computation | async-start | bytes 8388608
  3.1 7.6 %slice-start.2 = ((s8[6291456]{0:T(1024)(128)(4,1)}), s8[4194304]{0:T(1024)(128)(4,1)S(1)}, s32[]{:S(2)}) async-start(s8[6291456]{0:T(1024)(128)(4,1)} %bitcast.3), calls=%async_computation.2 | async-start | bytes 8388608
  3.1 7.6 %slice-start.1 = ((s8[8388608]{0:T(1024)(128)(4,1)}), s8[4194304]{0:T(1024)(128)(4,1)S(1)}, s32[]{:S(2)}) async-start(s8[8388608]{0:T(1024)(128)(4,1)} %bitcast.1), calls=%async_computation.1 | async-start | bytes 8388608
  3.1 7.6 %slice-start.3 = ((s8[6291456]{0:T(1024)(128)(4,1)}), s8[2097152]{0:T(1024)(128)(4,1)S(1)}, s32[]{:S(2)}) async-start(s8[6291456]{0:T(1024)(128)(4,1)} %bitcast.3), calls=%async_computation.3 | async-start | bytes 4194304
  3.2 1.9 %collective-permute-start = (f32[768,128]{1,0:T(8,128)S(1)}, f32[768,128]{1,0:T(8,128)S(1)}, u32[]{:S(2)}, u32[]{:S(2)}) collective-permute-start(f32[768,128]{1,0:T(8,128)S(1)} %get-tuple-element.24), channel_id=1, source_target_pairs={{0,1},{1,0},{2,3},{3,2},{4,5},{5,4},{6,7},{7,6},{8,9},{9,8},{10,11... | collective-permute-start | bytes 1179656 | tf_op jit(solution)/shard_map/ppermute | solution.py:285
  5.1 10.3 %collective-permute-start.1 = (bf16[208,128]{1,0:T(8,128)(2,1)S(1)}, bf16[208,128]{1,0:T(8,128)(2,1)S(1)}, u32[]{:S(2)}, u32[]{:S(2)}) collective-permute-start(bf16[208,128]{1,0:T(8,128)(2,1)S(1)} %get-tuple-element.27), channel_id=1, source_target_pairs={{0,8},{4,12},{8,0},{12,4},{1,9},{5,13},{9,1},{13,5},{2,10},{6,14},... | collective-permute-start | bytes 159752 | tf_op jit(solution)/shard_map/ppermute | solution.py:262
  9.2 6.3 %collective-permute-start.2 = (bf16[208,128]{1,0:T(8,128)(2,1)S(1)}, bf16[208,128]{1,0:T(8,128)(2,1)S(1)}, u32[]{:S(2)}, u32[]{:S(2)}) collective-permute-start(bf16[208,128]{1,0:T(8,128)(2,1)S(1)} %get-tuple-element.28), channel_id=1, source_target_pairs={{0,12},{4,8},{8,4},{12,0},{1,13},{5,9},{9,5},{13,1},{2,14},{6,10},... | collective-permute-start | bytes 159752 | tf_op jit(solution)/shard_map/ppermute | solution.py:262
  10.5 4.9 %collective-permute-start.3 = (bf16[208,128]{1,0:T(8,128)(2,1)S(1)}, bf16[208,128]{1,0:T(8,128)(2,1)S(1)}, u32[]{:S(2)}, u32[]{:S(2)}) collective-permute-start(bf16[208,128]{1,0:T(8,128)(2,1)S(1)} %get-tuple-element.29), channel_id=1, source_target_pairs={{0,4},{4,0},{8,12},{12,8},{1,5},{5,1},{9,13},{13,9},{2,6},{6,2},{1... | collective-permute-start | bytes 159752 | tf_op jit(solution)/shard_map/ppermute | solution.py:262
  10.8 19.3 %copy-start = (s32[2]{0:T(128)S(1)}, s32[2]{0:T(128)}, u32[]{:S(2)}) copy-start(s32[2]{0:T(128)} %refs_0_.5) | copy-start | bytes 28
  15.6 1.8 %collective-permute-start.4 = (f32[768,128]{1,0:T(8,128)S(1)}, f32[768,128]{1,0:T(8,128)S(1)}, u32[]{:S(2)}, u32[]{:S(2)}) collective-permute-start(f32[768,128]{1,0:T(8,128)S(1)} %get-tuple-element.32), channel_id=1, source_target_pairs={{0,1},{1,0},{2,3},{3,2},{4,5},{5,4},{6,7},{7,6},{8,9},{9,8},{10,11... | collective-permute-start | bytes 1179656 | tf_op jit(solution)/shard_map/ppermute | solution.py:298
  17.4 4.9 %collective-permute-start.5 = (bf16[384,128]{1,0:T(8,128)(2,1)S(1)}, bf16[384,128]{1,0:T(8,128)(2,1)S(1)}, u32[]{:S(2)}, u32[]{:S(2)}) collective-permute-start(bf16[384,128]{1,0:T(8,128)(2,1)S(1)} %get-tuple-element.33), channel_id=1, source_target_pairs={{0,2},{1,3},{2,0},{3,1},{4,6},{5,7},{6,4},{7,5},{8,10},{9,11},{10,... | collective-permute-start | bytes 294920 | tf_op jit(solution)/shard_map/ppermute | solution.py:300
  22.3 6.2 %collective-permute-start.6 = (bf16[768,128]{1,0:T(8,128)(2,1)S(1)}, bf16[768,128]{1,0:T(8,128)(2,1)S(1)}, u32[]{:S(2)}, u32[]{:S(2)}) collective-permute-start(bf16[768,128]{1,0:T(8,128)(2,1)S(1)} %stack_in.1.refs_0_), channel_id=1, source_target_pairs={{0,2},{1,3},{2,0},{3,1},{4,6},{5,7},{6,4},{7,5},{8,10},{9,11},{10,... | collective-permute-start | bytes 589832 | tf_op jit(solution)/shard_map/ppermute | solution.py:307
  23.9 10.4 %collective-permute-start.9 = (bf16[400,128]{1,0:T(8,128)(2,1)S(1)}, bf16[400,128]{1,0:T(8,128)(2,1)S(1)}, u32[]{:S(2)}, u32[]{:S(2)}) collective-permute-start(bf16[400,128]{1,0:T(8,128)(2,1)S(1)} %round_out.1.refs_2_), channel_id=1, source_target_pairs={{0,8},{4,12},{8,0},{12,4},{1,9},{5,13},{9,1},{13,5},{2,10},{6,14},... | collective-permute-start | bytes 307208 | tf_op jit(solution)/shard_map/ppermute | solution.py:262
  26.8 7.6 %collective-permute-start.10 = (bf16[400,128]{1,0:T(8,128)(2,1)S(1)}, bf16[400,128]{1,0:T(8,128)(2,1)S(1)}, u32[]{:S(2)}, u32[]{:S(2)}) collective-permute-start(bf16[400,128]{1,0:T(8,128)(2,1)S(1)} %round_out.1.refs_2_), channel_id=1, source_target_pairs={{0,12},{4,8},{8,4},{12,0},{1,13},{5,9},{9,5},{13,1},{2,14},{6,10},... | collective-permute-start | bytes 307208 | tf_op jit(solution)/shard_map/ppermute | solution.py:262
  28.1 6.7 %collective-permute-start.11 = (bf16[400,128]{1,0:T(8,128)(2,1)S(1)}, bf16[400,128]{1,0:T(8,128)(2,1)S(1)}, u32[]{:S(2)}, u32[]{:S(2)}) collective-permute-start(bf16[400,128]{1,0:T(8,128)(2,1)S(1)} %round_out.1.refs_2_), channel_id=1, source_target_pairs={{0,4},{4,0},{8,12},{12,8},{1,5},{5,1},{9,13},{13,9},{2,6},{6,2},{1... | collective-permute-start | bytes 307208 | tf_op jit(solution)/shard_map/ppermute | solution.py:262
  28.5 1.4 %collective-permute-start.7 = (bf16[384,128]{1,0:T(8,128)(2,1)S(1)}, bf16[384,128]{1,0:T(8,128)(2,1)S(1)}, u32[]{:S(2)}, u32[]{:S(2)}) collective-permute-start(bf16[384,128]{1,0:T(8,128)(2,1)S(1)} %get-tuple-element.34.refs_1_), channel_id=1, source_target_pairs={{0,1},{1,0},{2,3},{3,2},{4,5},{5,4},{6,7},{7,6},{8,9},{9,8},{10,11... | collective-permute-start | bytes 294920 | tf_op jit(solution)/shard_map/ppermute | solution.py:309
  28.6 1.4 %collective-permute-start.8 = (bf16[384,128]{1,0:T(8,128)(2,1)S(1)}, bf16[384,128]{1,0:T(8,128)(2,1)S(1)}, u32[]{:S(2)}, u32[]{:S(2)}) collective-permute-start(bf16[384,128]{1,0:T(8,128)(2,1)S(1)} %get-tuple-element.35.refs_2_), channel_id=1, source_target_pairs={{0,1},{1,0},{2,3},{3,2},{4,5},{5,4},{6,7},{7,6},{8,9},{9,8},{10,11... | collective-permute-start | bytes 294920 | tf_op jit(solution)/shard_map/ppermute | solution.py:309

commit v10 on v9

--- a/solution.py
+++ b/solution.py
@@ -106,15 +106,20 @@
             at += half
 
 
-def rotate_out_kernel(grads, pick, basis_out, acc):
+def rotate_out_kernel(grads, pick, basis_out, acc, grads_v, sems):
     tokens, _, hidden = grads.shape
     experts, cap, _ = acc.shape
-    for at in range(0, hidden, CHUNK):
-        cols = pl.ds(at, CHUNK)
-        chosen = dot(pick[...], grads[:, :, cols].reshape(2 * tokens, CHUNK)).astype(BF16)
+    fetch = fetcher(sems)
+    cuts = sorted({0, CHUNK // 2, *range(CHUNK, hidden + 1, CHUNK)})
+    parts = [pl.ds(at, end - at) for at, end in zip(cuts, cuts[1:])]
+    copies = [fetch(grads.at[:, :, part], grads_v.at[:, :, part]) for part in parts]
+    for n, (part, copy) in enumerate(zip(parts, copies)):
+        copy.wait()
+        rows = grads_v[:, :, part].reshape(2 * tokens, part.size)
+        chosen = dot(pick[...], rows).astype(BF16)
         for e in range(experts):
-            part = dot(chosen[e * cap : (e + 1) * cap], basis_out[e, cols, :])
-            acc[e] = part if at == 0 else acc[e] + part
+            more = dot(chosen[e * cap : (e + 1) * cap], basis_out[e, part, :])
+            acc[e] = more if n == 0 else acc[e] + more
 
 
 def split_out_kernel(acc, keep, send):
@@ -130,12 +135,18 @@
             at += cap
 
 
-def pair_in_kernel(kept, got, label, *pays):
+def pair_in_kernel(kept, got, keep, send):
+    total = kept[...] + got[...]
+    keep[...] = total
+    send[...] = total.astype(BF16)
+
+
+def round_in_kernel(kept, got, label, *pays):
     slab = kept.shape[0] // len(pays)
     d = lax.axis_index("dp")
     for k, pay in enumerate(pays):
         rows = pl.ds(pl.multiple_of((d ^ k) * slab, 16), slab)
-        pay[:slab, :] = (kept[rows, :] + got[rows, :]).astype(BF16)
+        pay[:slab, :] = (kept[rows, :] + got[rows, :].astype(F32)).astype(BF16)
         pay[slab:, :] = label[...]
 
 
@@ -154,17 +165,13 @@
     out[outer:, :] = jnp.zeros((out.shape[0] - outer, 128), BF16)
 
 
-def stack_kernel(slab, *refs):
-    *pieces, out = refs
+def stack_kernel(*refs):
+    *pieces, first, second = refs
+    slab = pieces[0].shape[0] - LABEL_ROWS
     for k, piece in enumerate(pieces):
-        out[k * slab : (k + 1) * slab, :] = piece[:slab, :]
-
-
-def sum_kernel(near, far, *outs):
-    piece = outs[0].shape[0]
-    for n, out in enumerate(outs):
-        rows = pl.ds(n * piece, piece)
-        out[...] = (near[rows, :].astype(F32) + far[rows, :].astype(F32)).astype(BF16)
+        out = (first, second)[k * 2 // len(pieces)]
+        at = k * slab % out.shape[0]
+        out[at : at + slab, :] = piece[:slab, :]
 
 
 def mask_kernel(counts, *refs):
@@ -192,8 +199,9 @@
             ).astype(BF16)
 
 
-def blocks_kernel(divisor, masked, *refs):
-    *outs, result, final, sems = refs
+def blocks_kernel(divisor, masked, own, *refs):
+    *far, result, final, sems = refs
+    outs = [own, *reversed(far)]
     experts, slots, _ = masked.shape
     half = slots // (2 * len(outs))
     core = lax.rem(lax.axis_index("tensor"), 2)
@@ -284,28 +292,34 @@
     )(acc)
     got = lax.ppermute(send, "tensor", core)
     slab = half // dp
-    pieces = call(pair_in_kernel, "pair_in", [rows(slab + LABEL_ROWS, BF16)] * dp)(
-        keep, got, label
-    )
-    arrived = [pieces[0]] + [swap(pieces[k], k) for k in FAR_FIRST]
-
-    acc = call(rotate_out_kernel, "rotate_out", partial, after=[pieces[0]])(
-        grads, pick, basis_out
-    )
+    keep_in, send_in = call(pair_in_kernel, "pair_in", (rows(half, F32), rows(half, BF16)))(
+        keep, got
+    )
+    got_in = lax.ppermute(send_in, "tensor", across)
+
+    acc = call(
+        rotate_out_kernel,
+        "rotate_out",
+        partial,
+        [hbm, vmem, vmem],
+        [pltpu.VMEM(grads.shape, BF16), pltpu.SemaphoreType.DMA((grads.shape[2] // CHUNK + 1,))],
+        after=[send_in],
+    )(pin(grads), pick, basis_out)
     keep, send = call(
-        split_out_kernel, "split_out", (rows(half, F32), rows(half, F32)), after=arrived[1:]
+        split_out_kernel, "split_out", (rows(half, F32), rows(half, F32)), after=[got_in]
     )(acc)
     got = lax.ppermute(send, "tensor", core)
     keep, send = call(pair_out_kernel, "pair_out", (rows(wide, F32), rows(wide, BF16)))(keep, got)
     got = lax.ppermute(send, "tensor", across)
+
+    slab = half // dp
+    pieces = call(round_in_kernel, "round_in", [rows(slab + LABEL_ROWS, BF16)] * dp)(
+        keep_in, got_in, label
+    )
+    pieces = [pieces[0]] + [swap(pieces[k], k) for k in FAR_FIRST]
     out = call(round_kernel, "round_out", rows(wide + 16, BF16))(keep, got)
-    outs = [out] + [swap(out, k) for k in FAR_FIRST]
-
-    near = call(
-        functools.partial(stack_kernel, slab), "stack_in", rows(half, BF16), after=[got]
-    )(*arrived)
-    far = lax.ppermute(near, "tensor", across)
-    mine = call(sum_kernel, "sum_in", [rows(half // 2, BF16)] * 2)(near, far)
+    outs = [swap(out, k) for k in reversed(FAR_FIRST)]
+    mine = call(stack_kernel, "stack_in", [rows(half // 2, BF16)] * 2)(*pieces)
     other = [lax.ppermute(x, "tensor", core) for x in mine]
     masked, divisor = call(
         mask_kernel,
@@ -315,7 +329,7 @@
             jax.ShapeDtypeStruct((experts, 8, 128), F32),
         ),
         [smem] + [vmem] * (4 + dp),
-    )(expert_counts, *mine, *other, *arrived)
+    )(expert_counts, *mine, *other, *pieces)
     result = jax.ShapeDtypeStruct((experts, 128, 128), F32)
     return call(
         blocks_kernel,
@@ -323,7 +337,7 @@
         result,
         scratch=[pltpu.VMEM(result.shape, F32), pltpu.SemaphoreType.DMA((experts,))],
         out_specs=hbm,
-    )(divisor, masked, *outs)
+    )(divisor, masked, out, *outs)
 
 
 EX_DEV = 1

time: 36 us -> 34.9 us (0.969)
  waiting for transfers between devices: 11.4 us -> 8.79 us
  Pallas kernels: 10.2 us -> 11.8 us
    ppermute x1, waiting for transfers between devices: 3.35 us -> 0.01 us  [fast(): got = lax.ppermute(send, 'tensor', across)]
    pallas_call x11, Pallas kernels: 10.2 us -> 11.8 us  [run(): pl.pallas_call(body, out_shape=out_shape, in_specs=(specs or [vmem] * len...]
    ppermute x1, starting transfers between devices: 1.55 us -> 2.92 us  [fast(): got_in = lax.ppermute(send_in, 'tensor', across)]
    ppermute x6, starting transfers between devices: 9.82 us -> 8.47 us  [swap(): return lax.ppermute(x, 'dp', [(d, d ^ k) for d in range(dp)])]
    ppermute x6, waiting for transfers between devices: 3.64 us -> 4.78 us  [swap(): return lax.ppermute(x, 'dp', [(d, d ^ k) for d in range(dp)])]
    ppermute x1, waiting for transfers between devices: 0.38 us -> 0.01 us  [fast(): got_in = lax.ppermute(send_in, 'tensor', across)]
  transfers between devices with their start and end apart: 12 -> 12, of which waited for: 8 -> 7; matrix products, arithmetic and copies ran while one was open for 0% -> 0% of each run, Pallas kernels for 16% -> 21%
where the time goes in v10:
time: 34.9 us; the launch traced here: 34.7 us
  starting transfers between devices  14.1 us (40%)
  Pallas kernels  11.8 us (34%)
  waiting for transfers between devices  8.79 us (25%)
    pallas_call x11, Pallas kernels, run(): pl.pallas_call(body, out_shape=out_shape, in_specs=(specs or [vmem] * len...  11.8 us
    ppermute x6, starting transfers between devices, swap(): return lax.ppermute(x, 'dp', [(d, d ^ k) for d in range(dp)])  8.47 us
    ppermute x6, waiting for transfers between devices, swap(): return lax.ppermute(x, 'dp', [(d, d ^ k) for d in range(dp)])  4.78 us
    ppermute x2, waiting for transfers between devices, fast(): got = lax.ppermute(send, 'tensor', core)  3.06 us
    ppermute x1, starting transfers between devices, fast(): got_in = lax.ppermute(send_in, 'tensor', across)  2.92 us
    ppermute x1, starting transfers between devices, fast(): got = lax.ppermute(send, 'tensor', across)  1.51 us
    ppermute x2, waiting for transfers between devices, fast(): other = [lax.ppermute(x, 'tensor', core) for x in mine]  0.94 us
  transfers between devices with their start and end apart: 12, of which 7 were waited for; matrix products, arithmetic and copies ran while one was open for 0% of the time, Pallas kernels for 21%

profile of v10, /device:TPU:0, one launch (start us, length us, event | category | flops | bytes accessed | tf_op | source)
XLA Modules:
  0.0 34.7 jit_solution(15948004199815312787)
XLA Ops:
  0.0 3.1 %rotate_in.1 = (f32[2,192,512]{2,1,0:T(8,128)S(1)}, bf16[16,128]{1,0:T(8,128)(2,1)S(1)}, bf16[384,768]{1,0:T(8,128)(2,1)S(1)}) custom-call(bf16[384,1536]{1,0:T(8,128)(2,1)} %refs_0_.3, s32[2,384]{1,0:T(2,128)} %bitcast.3, s32[384]{0:T(512)} %refs_2_.2, bf16[2,1536,512]{2,1,0:T(8,128)(2,1)} %refs_3_.1), custom_call_target="tpu_custom_call" | custom-call | flops 1 | bytes 1 | tf_op jit(solution)/shard_map/rotate_in/pallas_call | solution.py:235
  3.1 0.0 slice-start
  3.1 0.0 slice-start.1
  3.1 0.1 split_in.1
  3.2 0.5 %collective-permute-start = (f32[768,128]{1,0:T(8,128)S(1)}, f32[768,128]{1,0:T(8,128)S(1)}, u32[]{:S(2)}, u32[]{:S(2)}) collective-permute-start(f32[768,128]{1,0:T(8,128)S(1)} %get-tuple-element.26), channel_id=1, source_target_pairs={{0,1},{1,0},{2,3},{3,2},{4,5},{5,4},{6,7},{7,6},{8,9},{9,8},{10,11... | collective-permute-start | bytes 1179656 | tf_op jit(solution)/shard_map/ppermute | solution.py:293
  3.7 1.3 %collective-permute-done.refs_1_ = f32[768,128]{1,0:T(8,128)S(1)} collective-permute-done((f32[768,128]{1,0:T(8,128)S(1)}, f32[768,128]{1,0:T(8,128)S(1)}, u32[]{:S(2)}, u32[]{:S(2)}) %collective-permute-start) | collective-permute-done | bytes 393248 | tf_op jit(solution)/shard_map/ppermute | solution.py:293
  5.1 2.9 %collective-permute-start.1 = (bf16[768,128]{1,0:T(8,128)(2,1)S(1)}, bf16[768,128]{1,0:T(8,128)(2,1)S(1)}, u32[]{:S(2)}, u32[]{:S(2)}) collective-permute-start(bf16[768,128]{1,0:T(8,128)(2,1)S(1)} %get-tuple-element.28.refs_3_), channel_id=1, source_target_pairs={{0,2},{1,3},{2,0},{3,1},{4,6},{5,7},{6,4},{7,5},{8,10},{9,11},{10,... | collective-permute-start | bytes 589832 | tf_op jit(solution)/shard_map/ppermute | solution.py:298
  8.0 0.0 slice-done
  8.0 0.0 slice-done.1
  8.1 0.0 copy-start
  8.1 6.2 %rotate_out.1.refs_0_ = f32[2,192,512]{2,1,0:T(8,128)S(1)} custom-call(bf16[384,2,4096]{2,1,0:T(2,128)(2,1)} %refs_0_.5, bf16[384,768]{1,0:T(8,128)(2,1)S(1)} %get-tuple-element.38.refs_1_, bf16[2,4096,512]{2,1,0:T(8,128)(2,1)S(1)} %bitcast.2, bf16[768,128]{1,0:T(8,128)(2,1)S(1)} %get-tuple-element.28.refs_3_), custom_call_target="tpu_custom_call" | custom-call | flops 1 | bytes 1 | tf_op jit(solution)/shard_map/rotate_out/pallas_call | solution.py:235
  14.2 0.0 collective-permute-done.1.refs_1_
  14.3 0.1 split_out.1
  14.4 0.1 collective-permute-start.7
  14.5 1.7 %collective-permute-done.7.refs_1_ = f32[768,128]{1,0:T(8,128)S(1)} collective-permute-done((f32[768,128]{1,0:T(8,128)S(1)}, f32[768,128]{1,0:T(8,128)S(1)}, u32[]{:S(2)}, u32[]{:S(2)}) %collective-permute-start.7) | collective-permute-done | bytes 393248 | tf_op jit(solution)/shard_map/ppermute | solution.py:311
  16.2 1.5 %collective-permute-start.8 = (bf16[384,128]{1,0:T(8,128)(2,1)S(1)}, bf16[384,128]{1,0:T(8,128)(2,1)S(1)}, u32[]{:S(2)}, u32[]{:S(2)}) collective-permute-start(bf16[384,128]{1,0:T(8,128)(2,1)S(1)} %get-tuple-element.42), channel_id=1, source_target_pairs={{0,2},{1,3},{2,0},{3,1},{4,6},{5,7},{6,4},{7,5},{8,10},{9,11},{10,... | collective-permute-start | bytes 294920 | tf_op jit(solution)/shard_map/ppermute | solution.py:313
  17.8 2.7 %collective-permute-start.2 = (bf16[208,128]{1,0:T(8,128)(2,1)S(1)}, bf16[208,128]{1,0:T(8,128)(2,1)S(1)}, u32[]{:S(2)}, u32[]{:S(2)}) collective-permute-start(bf16[208,128]{1,0:T(8,128)(2,1)S(1)} %get-tuple-element.31), channel_id=1, source_target_pairs={{0,8},{4,12},{8,0},{12,4},{1,9},{5,13},{9,1},{13,5},{2,10},{6,14},... | collective-permute-start | bytes 159752 | tf_op jit(solution)/shard_map/ppermute | solution.py:270
  20.4 1.3 %collective-permute-start.3 = (bf16[208,128]{1,0:T(8,128)(2,1)S(1)}, bf16[208,128]{1,0:T(8,128)(2,1)S(1)}, u32[]{:S(2)}, u32[]{:S(2)}) collective-permute-start(bf16[208,128]{1,0:T(8,128)(2,1)S(1)} %get-tuple-element.32), channel_id=1, source_target_pairs={{0,12},{4,8},{8,4},{12,0},{1,13},{5,9},{9,5},{13,1},{2,14},{6,10},... | collective-permute-start | bytes 159752 | tf_op jit(solution)/shard_map/ppermute | solution.py:270
  21.8 0.2 collective-permute-start.4
  22.0 0.0 collective-permute-done.8.refs_1_
  22.0 2.9 %collective-permute-start.11 = (bf16[400,128]{1,0:T(8,128)(2,1)S(1)}, bf16[400,128]{1,0:T(8,128)(2,1)S(1)}, u32[]{:S(2)}, u32[]{:S(2)}) collective-permute-start(bf16[400,128]{1,0:T(8,128)(2,1)S(1)} %round_out.1.refs_2_), channel_id=1, source_target_pairs={{0,8},{4,12},{8,0},{12,4},{1,9},{5,13},{9,1},{13,5},{2,10},{6,14},... | collective-permute-start | bytes 307208 | tf_op jit(solution)/shard_map/ppermute | solution.py:270
  24.9 1.3 %collective-permute-start.10 = (bf16[400,128]{1,0:T(8,128)(2,1)S(1)}, bf16[400,128]{1,0:T(8,128)(2,1)S(1)}, u32[]{:S(2)}, u32[]{:S(2)}) collective-permute-start(bf16[400,128]{1,0:T(8,128)(2,1)S(1)} %round_out.1.refs_2_), channel_id=1, source_target_pairs={{0,12},{4,8},{8,4},{12,0},{1,13},{5,9},{9,5},{13,1},{2,14},{6,10},... | collective-permute-start | bytes 307208 | tf_op jit(solution)/shard_map/ppermute | solution.py:270
  26.3 0.0 collective-permute-done.2.refs_1_.refs_6_
  26.3 0.0 collective-permute-start.9
  26.3 0.7 %collective-permute-done.3.refs_2_.refs_7_ = bf16[208,128]{1,0:T(8,128)(2,1)S(1)} collective-permute-done((bf16[208,128]{1,0:T(8,128)(2,1)S(1)}, bf16[208,128]{1,0:T(8,128)(2,1)S(1)}, u32[]{:S(2)}, u32[]{:S(2)}) %collective-permute-start.3) | collective-permute-done | bytes 53280 | tf_op jit(solution)/shard_map/ppermute | solution.py:270
  26.9 0.0 collective-permute-done.4.refs_3_.refs_8_
  27.0 0.1 collective-permute-start.5
  27.0 0.5 %collective-permute-start.6 = (bf16[384,128]{1,0:T(8,128)(2,1)S(1)}, bf16[384,128]{1,0:T(8,128)(2,1)S(1)}, u32[]{:S(2)}, u32[]{:S(2)}) collective-permute-start(bf16[384,128]{1,0:T(8,128)(2,1)S(1)} %get-tuple-element.35.refs_2_), channel_id=1, source_target_pairs={{0,1},{1,0},{2,3},{3,2},{4,5},{5,4},{6,7},{7,6},{8,9},{9,8},{10,11... | collective-permute-start | bytes 294920 | tf_op jit(solution)/shard_map/ppermute | solution.py:323
  27.5 0.8 %collective-permute-done.5.refs_3_ = bf16[384,128]{1,0:T(8,128)(2,1)S(1)} collective-permute-done((bf16[384,128]{1,0:T(8,128)(2,1)S(1)}, bf16[384,128]{1,0:T(8,128)(2,1)S(1)}, u32[]{:S(2)}, u32[]{:S(2)}) %collective-permute-start.5) | collective-permute-done | bytes 98336 | tf_op jit(solution)/shard_map/ppermute | solution.py:323
  28.3 0.2 collective-permute-done.6.refs_4_
  28.5 0.0 copy-done
  28.5 1.1 %mask_in.1 = (bf16[2,768,512]{2,1,0:T(8,128)(2,1)S(1)}, f32[2,8,128]{2,1,0:T(8,128)S(1)}) custom-call(s32[2]{0:T(128)S(1)} %copy-done, bf16[384,128]{1,0:T(8,128)(2,1)S(1)} %get-tuple-element.34.refs_1_, bf16[384,128]{1,0:T(8,128)(2,1)S(1)} %get-tuple-element.35.refs_2_, bf16[384,128]{1,0:T(8,128)(2,1)S(1)} %collective-permute-done.5.refs_3_, ...), custom_call_target="tpu_custom_call" | custom-call | flops 1 | bytes 1 | tf_op jit(solution)/shard_map/mask_in/pallas_call | solution.py:235
  29.6 3.8 %collective-permute-done.11.refs_5_ = bf16[400,128]{1,0:T(8,128)(2,1)S(1)} collective-permute-done((bf16[400,128]{1,0:T(8,128)(2,1)S(1)}, bf16[400,128]{1,0:T(8,128)(2,1)S(1)}, u32[]{:S(2)}, u32[]{:S(2)}) %collective-permute-start.11) | collective-permute-done | bytes 102432 | tf_op jit(solution)/shard_map/ppermute | solution.py:270
  33.3 0.0 collective-permute-done.10.refs_4_
  33.4 0.3 collective-permute-done.9.refs_3_
  33.7 1.1 %blocks.1 = f32[2,128,128]{2,1,0:T(8,128)} custom-call(f32[2,8,128]{2,1,0:T(8,128)S(1)} %get-tuple-element.36.refs_0_, bf16[2,768,512]{2,1,0:T(8,128)(2,1)S(1)} %get-tuple-element.37.refs_1_, bf16[400,128]{1,0:T(8,128)(2,1)S(1)} %round_out.1.refs_2_, bf16[400,128]{1,0:T(8,128)(2,1)S(1)} %collective-permute-done.9.refs_3_, ...), custom_call_target="tpu_custom_call" | custom-call | flops 1 | bytes 1 | tf_op jit(solution)/shard_map/blocks/pallas_call | solution.py:235
  (6 shorter events, 0.2 us)
Async XLA Ops:
  3.1 5.0 %slice-start = ((s8[8388608]{0:T(1024)(128)(4,1)}), s8[4194304]{0:T(1024)(128)(4,1)S(1)}, s32[]{:S(2)}) async-start(s8[8388608]{0:T(1024)(128)(4,1)} %bitcast.1), calls=%async_computation | async-start | bytes 8388608
  3.1 4.9 %slice-start.1 = ((s8[8388608]{0:T(1024)(128)(4,1)}), s8[4194304]{0:T(1024)(128)(4,1)S(1)}, s32[]{:S(2)}) async-start(s8[8388608]{0:T(1024)(128)(4,1)} %bitcast.1), calls=%async_computation.1 | async-start | bytes 8388608
  3.2 1.9 %collective-permute-start = (f32[768,128]{1,0:T(8,128)S(1)}, f32[768,128]{1,0:T(8,128)S(1)}, u32[]{:S(2)}, u32[]{:S(2)}) collective-permute-start(f32[768,128]{1,0:T(8,128)S(1)} %get-tuple-element.26), channel_id=1, source_target_pairs={{0,1},{1,0},{2,3},{3,2},{4,5},{5,4},{6,7},{7,6},{8,9},{9,8},{10,11... | collective-permute-start | bytes 1179656 | tf_op jit(solution)/shard_map/ppermute | solution.py:293
  5.1 9.1 %collective-permute-start.1 = (bf16[768,128]{1,0:T(8,128)(2,1)S(1)}, bf16[768,128]{1,0:T(8,128)(2,1)S(1)}, u32[]{:S(2)}, u32[]{:S(2)}) collective-permute-start(bf16[768,128]{1,0:T(8,128)(2,1)S(1)} %get-tuple-element.28.refs_3_), channel_id=1, source_target_pairs={{0,2},{1,3},{2,0},{3,1},{4,6},{5,7},{6,4},{7,5},{8,10},{9,11},{10,... | collective-permute-start | bytes 589832 | tf_op jit(solution)/shard_map/ppermute | solution.py:298
  8.1 20.4 %copy-start = (s32[2]{0:T(128)S(1)}, s32[2]{0:T(128)}, u32[]{:S(2)}) copy-start(s32[2]{0:T(128)} %refs_0_.4) | copy-start | bytes 28
  14.4 1.8 %collective-permute-start.7 = (f32[768,128]{1,0:T(8,128)S(1)}, f32[768,128]{1,0:T(8,128)S(1)}, u32[]{:S(2)}, u32[]{:S(2)}) collective-permute-start(f32[768,128]{1,0:T(8,128)S(1)} %get-tuple-element.40), channel_id=1, source_target_pairs={{0,1},{1,0},{2,3},{3,2},{4,5},{5,4},{6,7},{7,6},{8,9},{9,8},{10,11... | collective-permute-start | bytes 1179656 | tf_op jit(solution)/shard_map/ppermute | solution.py:311
  16.2 5.8 %collective-permute-start.8 = (bf16[384,128]{1,0:T(8,128)(2,1)S(1)}, bf16[384,128]{1,0:T(8,128)(2,1)S(1)}, u32[]{:S(2)}, u32[]{:S(2)}) collective-permute-start(bf16[384,128]{1,0:T(8,128)(2,1)S(1)} %get-tuple-element.42), channel_id=1, source_target_pairs={{0,2},{1,3},{2,0},{3,1},{4,6},{5,7},{6,4},{7,5},{8,10},{9,11},{10,... | collective-permute-start | bytes 294920 | tf_op jit(solution)/shard_map/ppermute | solution.py:313
  17.8 8.5 %collective-permute-start.2 = (bf16[208,128]{1,0:T(8,128)(2,1)S(1)}, bf16[208,128]{1,0:T(8,128)(2,1)S(1)}, u32[]{:S(2)}, u32[]{:S(2)}) collective-permute-start(bf16[208,128]{1,0:T(8,128)(2,1)S(1)} %get-tuple-element.31), channel_id=1, source_target_pairs={{0,8},{4,12},{8,0},{12,4},{1,9},{5,13},{9,1},{13,5},{2,10},{6,14},... | collective-permute-start | bytes 159752 | tf_op jit(solution)/shard_map/ppermute | solution.py:270
  20.4 6.5 %collective-permute-start.3 = (bf16[208,128]{1,0:T(8,128)(2,1)S(1)}, bf16[208,128]{1,0:T(8,128)(2,1)S(1)}, u32[]{:S(2)}, u32[]{:S(2)}) collective-permute-start(bf16[208,128]{1,0:T(8,128)(2,1)S(1)} %get-tuple-element.32), channel_id=1, source_target_pairs={{0,12},{4,8},{8,4},{12,0},{1,13},{5,9},{9,5},{13,1},{2,14},{6,10},... | collective-permute-start | bytes 159752 | tf_op jit(solution)/shard_map/ppermute | solution.py:270
  21.8 5.2 %collective-permute-start.4 = (bf16[208,128]{1,0:T(8,128)(2,1)S(1)}, bf16[208,128]{1,0:T(8,128)(2,1)S(1)}, u32[]{:S(2)}, u32[]{:S(2)}) collective-permute-start(bf16[208,128]{1,0:T(8,128)(2,1)S(1)} %get-tuple-element.33), channel_id=1, source_target_pairs={{0,4},{4,0},{8,12},{12,8},{1,5},{5,1},{9,13},{13,9},{2,6},{6,2},{1... | collective-permute-start | bytes 159752 | tf_op jit(solution)/shard_map/ppermute | solution.py:270
  22.0 11.3 %collective-permute-start.11 = (bf16[400,128]{1,0:T(8,128)(2,1)S(1)}, bf16[400,128]{1,0:T(8,128)(2,1)S(1)}, u32[]{:S(2)}, u32[]{:S(2)}) collective-permute-start(bf16[400,128]{1,0:T(8,128)(2,1)S(1)} %round_out.1.refs_2_), channel_id=1, source_target_pairs={{0,8},{4,12},{8,0},{12,4},{1,9},{5,13},{9,1},{13,5},{2,10},{6,14},... | collective-permute-start | bytes 307208 | tf_op jit(solution)/shard_map/ppermute | solution.py:270
  24.9 8.4 %collective-permute-start.10 = (bf16[400,128]{1,0:T(8,128)(2,1)S(1)}, bf16[400,128]{1,0:T(8,128)(2,1)S(1)}, u32[]{:S(2)}, u32[]{:S(2)}) collective-permute-start(bf16[400,128]{1,0:T(8,128)(2,1)S(1)} %round_out.1.refs_2_), channel_id=1, source_target_pairs={{0,12},{4,8},{8,4},{12,0},{1,13},{5,9},{9,5},{13,1},{2,14},{6,10},... | collective-permute-start | bytes 307208 | tf_op jit(solution)/shard_map/ppermute | solution.py:270
  26.3 7.4 %collective-permute-start.9 = (bf16[400,128]{1,0:T(8,128)(2,1)S(1)}, bf16[400,128]{1,0:T(8,128)(2,1)S(1)}, u32[]{:S(2)}, u32[]{:S(2)}) collective-permute-start(bf16[400,128]{1,0:T(8,128)(2,1)S(1)} %round_out.1.refs_2_), channel_id=1, source_target_pairs={{0,4},{4,0},{8,12},{12,8},{1,5},{5,1},{9,13},{13,9},{2,6},{6,2},{1... | collective-permute-start | bytes 307208 | tf_op jit(solution)/shard_map/ppermute | solution.py:270
  27.0 1.4 %collective-permute-start.5 = (bf16[384,128]{1,0:T(8,128)(2,1)S(1)}, bf16[384,128]{1,0:T(8,128)(2,1)S(1)}, u32[]{:S(2)}, u32[]{:S(2)}) collective-permute-start(bf16[384,128]{1,0:T(8,128)(2,1)S(1)} %get-tuple-element.34.refs_1_), channel_id=1, source_target_pairs={{0,1},{1,0},{2,3},{3,2},{4,5},{5,4},{6,7},{7,6},{8,9},{9,8},{10,11... | collective-permute-start | bytes 294920 | tf_op jit(solution)/shard_map/ppermute | solution.py:323
  27.0 1.4 %collective-permute-start.6 = (bf16[384,128]{1,0:T(8,128)(2,1)S(1)}, bf16[384,128]{1,0:T(8,128)(2,1)S(1)}, u32[]{:S(2)}, u32[]{:S(2)}) collective-permute-start(bf16[384,128]{1,0:T(8,128)(2,1)S(1)} %get-tuple-element.35.refs_2_), channel_id=1, source_target_pairs={{0,1},{1,0},{2,3},{3,2},{4,5},{5,4},{6,7},{7,6},{8,9},{9,8},{10,11... | collective-permute-start | bytes 294920 | tf_op jit(solution)/shard_map/ppermute | solution.py:323

commit v11 on v10

--- a/solution.py
+++ b/solution.py
@@ -11,7 +11,9 @@
 BF16 = jnp.bfloat16
 CHUNK = 1024
 VMEM = 20 * 2**20
-FAR_FIRST = (2, 3, 1)
+EARLY = 1024
+DISTANCES = (1, 2, 3)
+LATEST = (1, 3, 2)
 LABEL_ROWS = 16
 
 
@@ -35,8 +37,8 @@
 
 
 def rotate_in_kernel(
-    acts, routes, ids, basis_in,
-    acc, label, pick,
+    acts, routes, ids, basis_in, grads,
+    acc, label, pick, early,
     acts_v, routes_v, ids_v, basis_v, sems,
 ):
     tokens = acts.shape[0]
@@ -46,6 +48,7 @@
     first = [fetch(routes, routes_v), fetch(ids, ids_v)]
     acts_in = fetch(acts, acts_v)
     bases = [fetch(basis_in.at[e], basis_v.at[e]) for e in range(experts)]
+    grads_in = fetch(grads.at[:, :, pl.ds(0, early.shape[2])], early)
     for copy in first:
         copy.wait()
     hits = [
@@ -90,6 +93,7 @@
     for e in range(experts):
         bases[e].wait()
         acc[e] = dot(chosen[e * cap : (e + 1) * cap], basis_v[e])
+    grads_in.wait()
 
 
 def split_in_kernel(acc, keep, send):
@@ -106,20 +110,32 @@
             at += half
 
 
-def rotate_out_kernel(grads, pick, basis_out, acc, grads_v, sems):
-    tokens, _, hidden = grads.shape
+def choose(pick, rows):
+    return dot(pick[...], rows.reshape(2 * rows.shape[0], rows.shape[2])).astype(BF16)
+
+
+def choose_kernel(grads, pick, out):
+    out[...] = choose(pick, grads[...])
+
+
+def rotate_out_kernel(grads, pick, basis_out, early, acc, grads_v, sems):
+    hidden = grads.shape[2]
     experts, cap, _ = acc.shape
     fetch = fetcher(sems)
-    cuts = sorted({0, CHUNK // 2, *range(CHUNK, hidden + 1, CHUNK)})
-    parts = [pl.ds(at, end - at) for at, end in zip(cuts, cuts[1:])]
-    copies = [fetch(grads.at[:, :, part], grads_v.at[:, :, part]) for part in parts]
-    for n, (part, copy) in enumerate(zip(parts, copies)):
+    done = early.shape[1]
+    cuts = sorted({done, done + CHUNK // 2, *range(done + CHUNK, hidden + 1, CHUNK)})
+    parts = [(at, pl.ds(at, end - at)) for at, end in zip(cuts, cuts[1:])]
+    copies = [
+        fetch(grads.at[:, :, part], grads_v.at[:, :, pl.ds(at - done, part.size)])
+        for at, part in parts
+    ]
+    for e in range(experts):
+        acc[e] = dot(early[e * cap : (e + 1) * cap, :], basis_out[e, :done, :])
+    for (at, part), copy in zip(parts, copies):
         copy.wait()
-        rows = grads_v[:, :, part].reshape(2 * tokens, part.size)
-        chosen = dot(pick[...], rows).astype(BF16)
+        chosen = choose(pick, grads_v[:, :, pl.ds(at - done, part.size)])
         for e in range(experts):
-            more = dot(chosen[e * cap : (e + 1) * cap], basis_out[e, part, :])
-            acc[e] = more if n == 0 else acc[e] + more
+            acc[e] += dot(chosen[e * cap : (e + 1) * cap], basis_out[e, part, :])
 
 
 def split_out_kernel(acc, keep, send):
@@ -201,7 +217,7 @@
 
 def blocks_kernel(divisor, masked, own, *refs):
     *far, result, final, sems = refs
-    outs = [own, *reversed(far)]
+    outs = [own] + [far[LATEST.index(k)] for k in DISTANCES]
     experts, slots, _ = masked.shape
     half = slots // (2 * len(outs))
     core = lax.rem(lax.axis_index("tensor"), 2)
@@ -270,41 +286,46 @@
         return lax.ppermute(x, "dp", [(d, d ^ k) for d in range(dp)])
 
     partial = jax.ShapeDtypeStruct((experts, cap, width), F32)
-    acc, label, pick = call(
+    acc, label, pick, early = call(
         rotate_in_kernel,
         "rotate_in",
         (
             partial,
             rows(LABEL_ROWS, BF16),
             jax.ShapeDtypeStruct((wide, 2 * tokens), BF16),
+            jax.ShapeDtypeStruct((tokens, 2, EARLY), BF16),
         ),
-        [hbm] * 4,
+        [hbm] * 5,
         [
             pltpu.VMEM(acts.shape, BF16),
             pltpu.VMEM((2, tokens), jnp.int32),
             pltpu.VMEM((tokens,), jnp.int32),
             pltpu.VMEM(basis_in.shape, BF16),
-            pltpu.SemaphoreType.DMA((3 + experts,)),
+            pltpu.SemaphoreType.DMA((4 + experts,)),
         ],
-    )(pin(acts), pin(routes.T), pin(example_ids), pin(basis_in))
+    )(pin(acts), pin(routes.T), pin(example_ids), pin(basis_in), pin(grads))
     keep, send = call(
         split_in_kernel, "split_in", (rows(half, F32), rows(half, F32)), flops=8 * 10**9
     )(acc)
     got = lax.ppermute(send, "tensor", core)
     slab = half // dp
-    keep_in, send_in = call(pair_in_kernel, "pair_in", (rows(half, F32), rows(half, BF16)))(
-        keep, got
-    )
+    early = call(choose_kernel, "choose", jax.ShapeDtypeStruct((wide, EARLY), BF16))(early, pick)
+    keep_in, send_in = call(
+        pair_in_kernel, "pair_in", (rows(half, F32), rows(half, BF16)), after=[early]
+    )(keep, got)
     got_in = lax.ppermute(send_in, "tensor", across)
 
     acc = call(
         rotate_out_kernel,
         "rotate_out",
         partial,
-        [hbm, vmem, vmem],
-        [pltpu.VMEM(grads.shape, BF16), pltpu.SemaphoreType.DMA((grads.shape[2] // CHUNK + 1,))],
+        [hbm, vmem, vmem, vmem],
+        [
+            pltpu.VMEM((tokens, 2, grads.shape[2] - EARLY), BF16),
+            pltpu.SemaphoreType.DMA((grads.shape[2] // CHUNK,)),
+        ],
         after=[send_in],
-    )(pin(grads), pick, basis_out)
+    )(pin(grads), pick, basis_out, early)
     keep, send = call(
         split_out_kernel, "split_out", (rows(half, F32), rows(half, F32)), after=[got_in]
     )(acc)
@@ -316,9 +337,9 @@
     pieces = call(round_in_kernel, "round_in", [rows(slab + LABEL_ROWS, BF16)] * dp)(
         keep_in, got_in, label
     )
-    pieces = [pieces[0]] + [swap(pieces[k], k) for k in FAR_FIRST]
+    pieces = [pieces[0]] + [swap(pieces[k], k) for k in DISTANCES]
     out = call(round_kernel, "round_out", rows(wide + 16, BF16))(keep, got)
-    outs = [swap(out, k) for k in reversed(FAR_FIRST)]
+    outs = [swap(out, k) for k in LATEST]
     mine = call(stack_kernel, "stack_in", [rows(half // 2, BF16)] * 2)(*pieces)
     other = [lax.ppermute(x, "tensor", core) for x in mine]
     masked, divisor = call(

time: 34.9 us -> 35 us (level)
  Pallas kernels: 11.8 us -> 11 us
  starting transfers between devices: 14.1 us -> 14.6 us
    ppermute x2, waiting for transfers between devices: 3.06 us -> 2.27 us  [fast(): got = lax.ppermute(send, 'tensor', core)]
    pallas_call x11 -> x12, Pallas kernels: 11.8 us -> 11 us  [run(): pl.pallas_call(body, out_shape=out_shape, in_specs=(specs or [vmem] * len...]
    ppermute x6, waiting for transfers between devices: 4.78 us -> 5.38 us  [swap(): return lax.ppermute(x, 'dp', [(d, d ^ k) for d in range(dp)])]
    ppermute x1, waiting for transfers between devices: 0.01 us -> 0.51 us  [fast(): got_in = lax.ppermute(send_in, 'tensor', across)]
  transfers between devices with their start and end apart: 12 -> 12, of which waited for: 7 -> 7; matrix products, arithmetic and copies ran while one was open for 0% -> 0% of each run, Pallas kernels for 21% -> 19%
where the time goes in v11:
time: 35 us; the launch traced here: 34.8 us
  starting transfers between devices  14.6 us (42%)
  Pallas kernels  11 us (31%)
  waiting for transfers between devices  9.11 us (26%)
    pallas_call x12, Pallas kernels, run(): pl.pallas_call(body, out_shape=out_shape, in_specs=(specs or [vmem] * len...  11 us
    ppermute x6, starting transfers between devices, swap(): return lax.ppermute(x, 'dp', [(d, d ^ k) for d in range(dp)])  8.68 us
    ppermute x6, waiting for transfers between devices, swap(): return lax.ppermute(x, 'dp', [(d, d ^ k) for d in range(dp)])  5.38 us
    ppermute x1, starting transfers between devices, fast(): got_in = lax.ppermute(send_in, 'tensor', across)  2.92 us
    ppermute x2, waiting for transfers between devices, fast(): got = lax.ppermute(send, 'tensor', core)  2.27 us
    ppermute x1, starting transfers between devices, fast(): got = lax.ppermute(send, 'tensor', across)  1.81 us
    ppermute x2, waiting for transfers between devices, fast(): other = [lax.ppermute(x, 'tensor', core) for x in mine]  0.94 us
  transfers between devices with their start and end apart: 12, of which 7 were waited for; matrix products, arithmetic and copies ran while one was open for 0% of the time, Pallas kernels for 19%

profile of v11, /device:TPU:0, one launch (start us, length us, event | category | flops | bytes accessed | tf_op | source)
XLA Modules:
  0.0 34.8 jit_solution(2810239841114932815)
XLA Ops:
  0.0 3.1 %rotate_in.1 = (f32[2,192,512]{2,1,0:T(8,128)S(1)}, bf16[16,128]{1,0:T(8,128)(2,1)S(1)}, bf16[384,768]{1,0:T(8,128)(2,1)S(1)}, bf16[384,2,1024]{2,1,0:T(2,128)(2,1)S(1)}) custom-call(bf16[384,1536]{1,0:T(8,128)(2,1)} %refs_0_.3, s32[2,384]{1,0:T(2,128)} %bitcast.3, s32[384]{0:T(512)} %refs_2_.2, bf16[2,1536,512]{2,1,0:T(8,128)(2,1)} %refs_3_.1, ...), custom_call_target="tpu_custom_call" | custom-call | flops 1 | bytes 1 | tf_op jit(solution)/shard_map/rotate_in/pallas_call | solution.py:251
  3.1 0.0 slice-start
  3.1 0.0 slice-start.1
  3.1 0.1 split_in.1
  3.2 0.5 %collective-permute-start = (f32[768,128]{1,0:T(8,128)S(1)}, f32[768,128]{1,0:T(8,128)S(1)}, u32[]{:S(2)}, u32[]{:S(2)}) collective-permute-start(f32[768,128]{1,0:T(8,128)S(1)} %get-tuple-element.27), channel_id=1, source_target_pairs={{0,1},{1,0},{2,3},{3,2},{4,5},{5,4},{6,7},{7,6},{8,9},{9,8},{10,11... | collective-permute-start | bytes 1179656 | tf_op jit(solution)/shard_map/ppermute | solution.py:310
  3.7 0.8 %choose.1.refs_2_.refs_3_ = bf16[384,1024]{1,0:T(8,128)(2,1)S(1)} custom-call(bf16[384,2,1024]{2,1,0:T(2,128)(2,1)S(1)} %get-tuple-element.28.refs_0_, bf16[384,768]{1,0:T(8,128)(2,1)S(1)} %get-tuple-element.29.refs_1_), custom_call_target="tpu_custom_call" | custom-call | flops 1 | bytes 1 | tf_op jit(solution)/shard_map/choose/pallas_call | solution.py:251
  4.5 0.6 %collective-permute-done.refs_1_ = f32[768,128]{1,0:T(8,128)S(1)} collective-permute-done((f32[768,128]{1,0:T(8,128)S(1)}, f32[768,128]{1,0:T(8,128)S(1)}, u32[]{:S(2)}, u32[]{:S(2)}) %collective-permute-start) | collective-permute-done | bytes 393248 | tf_op jit(solution)/shard_map/ppermute | solution.py:310
  5.1 0.0 copy-start
  5.1 2.9 %collective-permute-start.1 = (bf16[768,128]{1,0:T(8,128)(2,1)S(1)}, bf16[768,128]{1,0:T(8,128)(2,1)S(1)}, u32[]{:S(2)}, u32[]{:S(2)}) collective-permute-start(bf16[768,128]{1,0:T(8,128)(2,1)S(1)} %get-tuple-element.31.refs_4_), channel_id=1, source_target_pairs={{0,2},{1,3},{2,0},{3,1},{4,6},{5,7},{6,4},{7,5},{8,10},{9,11},{10,... | collective-permute-start | bytes 589832 | tf_op jit(solution)/shard_map/ppermute | solution.py:316
  8.1 0.0 slice-done
  8.1 0.0 slice-done.1
  8.1 4.7 %rotate_out.1.refs_0_ = f32[2,192,512]{2,1,0:T(8,128)S(1)} custom-call(bf16[384,2,4096]{2,1,0:T(2,128)(2,1)} %refs_0_.5, bf16[384,768]{1,0:T(8,128)(2,1)S(1)} %get-tuple-element.29.refs_1_, bf16[2,4096,512]{2,1,0:T(8,128)(2,1)S(1)} %bitcast.2, bf16[384,1024]{1,0:T(8,128)(2,1)S(1)} %choose.1.refs_2_.refs_3_, bf16[768,128]{1,0:T(8,128)(2,1)S(1)} %get-tuple-element.31.refs_4_), custom_call_target="tpu_custom_call" | custom-call | flops 1 | bytes 1 | tf_op jit(solution)/shard_map/rotate_out/pallas_call | solution.py:251
  12.8 0.5 %collective-permute-done.1.refs_1_ = bf16[768,128]{1,0:T(8,128)(2,1)S(1)} collective-permute-done((bf16[768,128]{1,0:T(8,128)(2,1)S(1)}, bf16[768,128]{1,0:T(8,128)(2,1)S(1)}, u32[]{:S(2)}, u32[]{:S(2)}) %collective-permute-start.1) | collective-permute-done | bytes 196640 | tf_op jit(solution)/shard_map/ppermute | solution.py:316
  13.3 0.1 split_out.1
  13.4 0.1 collective-permute-start.7
  13.5 1.7 %collective-permute-done.7.refs_1_ = f32[768,128]{1,0:T(8,128)S(1)} collective-permute-done((f32[768,128]{1,0:T(8,128)S(1)}, f32[768,128]{1,0:T(8,128)S(1)}, u32[]{:S(2)}, u32[]{:S(2)}) %collective-permute-start.7) | collective-permute-done | bytes 393248 | tf_op jit(solution)/shard_map/ppermute | solution.py:332
  15.2 1.8 %collective-permute-start.8 = (bf16[384,128]{1,0:T(8,128)(2,1)S(1)}, bf16[384,128]{1,0:T(8,128)(2,1)S(1)}, u32[]{:S(2)}, u32[]{:S(2)}) collective-permute-start(bf16[384,128]{1,0:T(8,128)(2,1)S(1)} %get-tuple-element.44), channel_id=1, source_target_pairs={{0,2},{1,3},{2,0},{3,1},{4,6},{5,7},{6,4},{7,5},{8,10},{9,11},{10,... | collective-permute-start | bytes 294920 | tf_op jit(solution)/shard_map/ppermute | solution.py:334
  17.1 1.6 %collective-permute-start.2 = (bf16[208,128]{1,0:T(8,128)(2,1)S(1)}, bf16[208,128]{1,0:T(8,128)(2,1)S(1)}, u32[]{:S(2)}, u32[]{:S(2)}) collective-permute-start(bf16[208,128]{1,0:T(8,128)(2,1)S(1)} %get-tuple-element.34), channel_id=1, source_target_pairs={{0,4},{4,0},{8,12},{12,8},{1,5},{5,1},{9,13},{13,9},{2,6},{6,2},{1... | collective-permute-start | bytes 159752 | tf_op jit(solution)/shard_map/ppermute | solution.py:286
  18.7 2.6 %collective-permute-start.3 = (bf16[208,128]{1,0:T(8,128)(2,1)S(1)}, bf16[208,128]{1,0:T(8,128)(2,1)S(1)}, u32[]{:S(2)}, u32[]{:S(2)}) collective-permute-start(bf16[208,128]{1,0:T(8,128)(2,1)S(1)} %get-tuple-element.35), channel_id=1, source_target_pairs={{0,8},{4,12},{8,0},{12,4},{1,9},{5,13},{9,1},{13,5},{2,10},{6,14},... | collective-permute-start | bytes 159752 | tf_op jit(solution)/shard_map/ppermute | solution.py:286
  21.3 0.2 collective-permute-start.4
  21.5 0.0 collective-permute-done.8.refs_1_
  21.5 1.7 %collective-permute-start.11 = (bf16[400,128]{1,0:T(8,128)(2,1)S(1)}, bf16[400,128]{1,0:T(8,128)(2,1)S(1)}, u32[]{:S(2)}, u32[]{:S(2)}) collective-permute-start(bf16[400,128]{1,0:T(8,128)(2,1)S(1)} %round_out.1.refs_2_), channel_id=1, source_target_pairs={{0,8},{4,12},{8,0},{12,4},{1,9},{5,13},{9,1},{13,5},{2,10},{6,14},... | collective-permute-start | bytes 307208 | tf_op jit(solution)/shard_map/ppermute | solution.py:286
  23.3 2.0 %collective-permute-start.10 = (bf16[400,128]{1,0:T(8,128)(2,1)S(1)}, bf16[400,128]{1,0:T(8,128)(2,1)S(1)}, u32[]{:S(2)}, u32[]{:S(2)}) collective-permute-start(bf16[400,128]{1,0:T(8,128)(2,1)S(1)} %round_out.1.refs_2_), channel_id=1, source_target_pairs={{0,12},{4,8},{8,4},{12,0},{1,13},{5,9},{9,5},{13,1},{2,14},{6,10},... | collective-permute-start | bytes 307208 | tf_op jit(solution)/shard_map/ppermute | solution.py:286
  25.3 0.0 collective-permute-done.2.refs_1_.refs_6_
  25.3 0.5 %collective-permute-start.9 = (bf16[400,128]{1,0:T(8,128)(2,1)S(1)}, bf16[400,128]{1,0:T(8,128)(2,1)S(1)}, u32[]{:S(2)}, u32[]{:S(2)}) collective-permute-start(bf16[400,128]{1,0:T(8,128)(2,1)S(1)} %round_out.1.refs_2_), channel_id=1, source_target_pairs={{0,4},{4,0},{8,12},{12,8},{1,5},{5,1},{9,13},{13,9},{2,6},{6,2},{1... | collective-permute-start | bytes 307208 | tf_op jit(solution)/shard_map/ppermute | solution.py:286
  25.8 0.0 collective-permute-done.3.refs_2_.refs_7_
  25.8 2.2 %collective-permute-done.4.refs_3_.refs_8_ = bf16[208,128]{1,0:T(8,128)(2,1)S(1)} collective-permute-done((bf16[208,128]{1,0:T(8,128)(2,1)S(1)}, bf16[208,128]{1,0:T(8,128)(2,1)S(1)}, u32[]{:S(2)}, u32[]{:S(2)}) %collective-permute-start.4) | collective-permute-done | bytes 53280 | tf_op jit(solution)/shard_map/ppermute | solution.py:286
  28.0 0.1 collective-permute-start.5
  28.1 0.5 %collective-permute-start.6 = (bf16[384,128]{1,0:T(8,128)(2,1)S(1)}, bf16[384,128]{1,0:T(8,128)(2,1)S(1)}, u32[]{:S(2)}, u32[]{:S(2)}) collective-permute-start(bf16[384,128]{1,0:T(8,128)(2,1)S(1)} %get-tuple-element.38.refs_2_), channel_id=1, source_target_pairs={{0,1},{1,0},{2,3},{3,2},{4,5},{5,4},{6,7},{7,6},{8,9},{9,8},{10,11... | collective-permute-start | bytes 294920 | tf_op jit(solution)/shard_map/ppermute | solution.py:344
  28.6 0.8 %collective-permute-done.5.refs_3_ = bf16[384,128]{1,0:T(8,128)(2,1)S(1)} collective-permute-done((bf16[384,128]{1,0:T(8,128)(2,1)S(1)}, bf16[384,128]{1,0:T(8,128)(2,1)S(1)}, u32[]{:S(2)}, u32[]{:S(2)}) %collective-permute-start.5) | collective-permute-done | bytes 98336 | tf_op jit(solution)/shard_map/ppermute | solution.py:344
  29.4 0.2 collective-permute-done.6.refs_4_
  29.5 0.0 copy-done
  29.5 1.1 %mask_in.1 = (bf16[2,768,512]{2,1,0:T(8,128)(2,1)S(1)}, f32[2,8,128]{2,1,0:T(8,128)S(1)}) custom-call(s32[2]{0:T(128)S(1)} %copy-done, bf16[384,128]{1,0:T(8,128)(2,1)S(1)} %get-tuple-element.37.refs_1_, bf16[384,128]{1,0:T(8,128)(2,1)S(1)} %get-tuple-element.38.refs_2_, bf16[384,128]{1,0:T(8,128)(2,1)S(1)} %collective-permute-done.5.refs_3_, ...), custom_call_target="tpu_custom_call" | custom-call | flops 1 | bytes 1 | tf_op jit(solution)/shard_map/mask_in/pallas_call | solution.py:251
  30.6 3.1 %collective-permute-done.11.refs_5_ = bf16[400,128]{1,0:T(8,128)(2,1)S(1)} collective-permute-done((bf16[400,128]{1,0:T(8,128)(2,1)S(1)}, bf16[400,128]{1,0:T(8,128)(2,1)S(1)}, u32[]{:S(2)}, u32[]{:S(2)}) %collective-permute-start.11) | collective-permute-done | bytes 102432 | tf_op jit(solution)/shard_map/ppermute | solution.py:286
  33.8 0.0 collective-permute-done.10.refs_4_
  33.8 0.0 collective-permute-done.9.refs_3_
  33.8 1.1 %blocks.1 = f32[2,128,128]{2,1,0:T(8,128)} custom-call(f32[2,8,128]{2,1,0:T(8,128)S(1)} %get-tuple-element.39.refs_0_, bf16[2,768,512]{2,1,0:T(8,128)(2,1)S(1)} %get-tuple-element.40.refs_1_, bf16[400,128]{1,0:T(8,128)(2,1)S(1)} %round_out.1.refs_2_, bf16[400,128]{1,0:T(8,128)(2,1)S(1)} %collective-permute-done.9.refs_3_, ...), custom_call_target="tpu_custom_call" | custom-call | flops 1 | bytes 1 | tf_op jit(solution)/shard_map/blocks/pallas_call | solution.py:251
  (6 shorter events, 0.2 us)
Async XLA Ops:
  3.1 5.0 %slice-start = ((s8[8388608]{0:T(1024)(128)(4,1)}), s8[4194304]{0:T(1024)(128)(4,1)S(1)}, s32[]{:S(2)}) async-start(s8[8388608]{0:T(1024)(128)(4,1)} %bitcast.1), calls=%async_computation | async-start | bytes 8388608
  3.1 5.0 %slice-start.1 = ((s8[8388608]{0:T(1024)(128)(4,1)}), s8[4194304]{0:T(1024)(128)(4,1)S(1)}, s32[]{:S(2)}) async-start(s8[8388608]{0:T(1024)(128)(4,1)} %bitcast.1), calls=%async_computation.1 | async-start | bytes 8388608
  3.2 1.9 %collective-permute-start = (f32[768,128]{1,0:T(8,128)S(1)}, f32[768,128]{1,0:T(8,128)S(1)}, u32[]{:S(2)}, u32[]{:S(2)}) collective-permute-start(f32[768,128]{1,0:T(8,128)S(1)} %get-tuple-element.27), channel_id=1, source_target_pairs={{0,1},{1,0},{2,3},{3,2},{4,5},{5,4},{6,7},{7,6},{8,9},{9,8},{10,11... | collective-permute-start | bytes 1179656 | tf_op jit(solution)/shard_map/ppermute | solution.py:310
  5.1 24.4 %copy-start = (s32[2]{0:T(128)S(1)}, s32[2]{0:T(128)}, u32[]{:S(2)}) copy-start(s32[2]{0:T(128)} %refs_0_.4) | copy-start | bytes 28
  5.1 8.1 %collective-permute-start.1 = (bf16[768,128]{1,0:T(8,128)(2,1)S(1)}, bf16[768,128]{1,0:T(8,128)(2,1)S(1)}, u32[]{:S(2)}, u32[]{:S(2)}) collective-permute-start(bf16[768,128]{1,0:T(8,128)(2,1)S(1)} %get-tuple-element.31.refs_4_), channel_id=1, source_target_pairs={{0,2},{1,3},{2,0},{3,1},{4,6},{5,7},{6,4},{7,5},{8,10},{9,11},{10,... | collective-permute-start | bytes 589832 | tf_op jit(solution)/shard_map/ppermute | solution.py:316
  13.4 1.8 %collective-permute-start.7 = (f32[768,128]{1,0:T(8,128)S(1)}, f32[768,128]{1,0:T(8,128)S(1)}, u32[]{:S(2)}, u32[]{:S(2)}) collective-permute-start(f32[768,128]{1,0:T(8,128)S(1)} %get-tuple-element.42), channel_id=1, source_target_pairs={{0,1},{1,0},{2,3},{3,2},{4,5},{5,4},{6,7},{7,6},{8,9},{9,8},{10,11... | collective-permute-start | bytes 1179656 | tf_op jit(solution)/shard_map/ppermute | solution.py:332
  15.2 6.3 %collective-permute-start.8 = (bf16[384,128]{1,0:T(8,128)(2,1)S(1)}, bf16[384,128]{1,0:T(8,128)(2,1)S(1)}, u32[]{:S(2)}, u32[]{:S(2)}) collective-permute-start(bf16[384,128]{1,0:T(8,128)(2,1)S(1)} %get-tuple-element.44), channel_id=1, source_target_pairs={{0,2},{1,3},{2,0},{3,1},{4,6},{5,7},{6,4},{7,5},{8,10},{9,11},{10,... | collective-permute-start | bytes 294920 | tf_op jit(solution)/shard_map/ppermute | solution.py:334
  17.1 8.2 %collective-permute-start.2 = (bf16[208,128]{1,0:T(8,128)(2,1)S(1)}, bf16[208,128]{1,0:T(8,128)(2,1)S(1)}, u32[]{:S(2)}, u32[]{:S(2)}) collective-permute-start(bf16[208,128]{1,0:T(8,128)(2,1)S(1)} %get-tuple-element.34), channel_id=1, source_target_pairs={{0,4},{4,0},{8,12},{12,8},{1,5},{5,1},{9,13},{13,9},{2,6},{6,2},{1... | collective-permute-start | bytes 159752 | tf_op jit(solution)/shard_map/ppermute | solution.py:286
  18.7 7.1 %collective-permute-start.3 = (bf16[208,128]{1,0:T(8,128)(2,1)S(1)}, bf16[208,128]{1,0:T(8,128)(2,1)S(1)}, u32[]{:S(2)}, u32[]{:S(2)}) collective-permute-start(bf16[208,128]{1,0:T(8,128)(2,1)S(1)} %get-tuple-element.35), channel_id=1, source_target_pairs={{0,8},{4,12},{8,0},{12,4},{1,9},{5,13},{9,1},{13,5},{2,10},{6,14},... | collective-permute-start | bytes 159752 | tf_op jit(solution)/shard_map/ppermute | solution.py:286
  21.3 6.7 %collective-permute-start.4 = (bf16[208,128]{1,0:T(8,128)(2,1)S(1)}, bf16[208,128]{1,0:T(8,128)(2,1)S(1)}, u32[]{:S(2)}, u32[]{:S(2)}) collective-permute-start(bf16[208,128]{1,0:T(8,128)(2,1)S(1)} %get-tuple-element.36), channel_id=1, source_target_pairs={{0,12},{4,8},{8,4},{12,0},{1,13},{5,9},{9,5},{13,1},{2,14},{6,10},... | collective-permute-start | bytes 159752 | tf_op jit(solution)/shard_map/ppermute | solution.py:286
  21.5 12.2 %collective-permute-start.11 = (bf16[400,128]{1,0:T(8,128)(2,1)S(1)}, bf16[400,128]{1,0:T(8,128)(2,1)S(1)}, u32[]{:S(2)}, u32[]{:S(2)}) collective-permute-start(bf16[400,128]{1,0:T(8,128)(2,1)S(1)} %round_out.1.refs_2_), channel_id=1, source_target_pairs={{0,8},{4,12},{8,0},{12,4},{1,9},{5,13},{9,1},{13,5},{2,10},{6,14},... | collective-permute-start | bytes 307208 | tf_op jit(solution)/shard_map/ppermute | solution.py:286
  23.3 10.5 %collective-permute-start.10 = (bf16[400,128]{1,0:T(8,128)(2,1)S(1)}, bf16[400,128]{1,0:T(8,128)(2,1)S(1)}, u32[]{:S(2)}, u32[]{:S(2)}) collective-permute-start(bf16[400,128]{1,0:T(8,128)(2,1)S(1)} %round_out.1.refs_2_), channel_id=1, source_target_pairs={{0,12},{4,8},{8,4},{12,0},{1,13},{5,9},{9,5},{13,1},{2,14},{6,10},... | collective-permute-start | bytes 307208 | tf_op jit(solution)/shard_map/ppermute | solution.py:286
  25.3 8.5 %collective-permute-start.9 = (bf16[400,128]{1,0:T(8,128)(2,1)S(1)}, bf16[400,128]{1,0:T(8,128)(2,1)S(1)}, u32[]{:S(2)}, u32[]{:S(2)}) collective-permute-start(bf16[400,128]{1,0:T(8,128)(2,1)S(1)} %round_out.1.refs_2_), channel_id=1, source_target_pairs={{0,4},{4,0},{8,12},{12,8},{1,5},{5,1},{9,13},{13,9},{2,6},{6,2},{1... | collective-permute-start | bytes 307208 | tf_op jit(solution)/shard_map/ppermute | solution.py:286
  28.0 1.4 %collective-permute-start.5 = (bf16[384,128]{1,0:T(8,128)(2,1)S(1)}, bf16[384,128]{1,0:T(8,128)(2,1)S(1)}, u32[]{:S(2)}, u32[]{:S(2)}) collective-permute-start(bf16[384,128]{1,0:T(8,128)(2,1)S(1)} %get-tuple-element.37.refs_1_), channel_id=1, source_target_pairs={{0,1},{1,0},{2,3},{3,2},{4,5},{5,4},{6,7},{7,6},{8,9},{9,8},{10,11... | collective-permute-start | bytes 294920 | tf_op jit(solution)/shard_map/ppermute | solution.py:344
  28.1 1.4 %collective-permute-start.6 = (bf16[384,128]{1,0:T(8,128)(2,1)S(1)}, bf16[384,128]{1,0:T(8,128)(2,1)S(1)}, u32[]{:S(2)}, u32[]{:S(2)}) collective-permute-start(bf16[384,128]{1,0:T(8,128)(2,1)S(1)} %get-tuple-element.38.refs_2_), channel_id=1, source_target_pairs={{0,1},{1,0},{2,3},{3,2},{4,5},{5,4},{6,7},{7,6},{8,9},{9,8},{10,11... | collective-permute-start | bytes 294920 | tf_op jit(solution)/shard_map/ppermute | solution.py:344

commit v12 on v11

--- a/solution.py
+++ b/solution.py
@@ -157,13 +157,27 @@
     send[...] = total.astype(BF16)
 
 
-def round_in_kernel(kept, got, label, *pays):
-    slab = kept.shape[0] // len(pays)
+def round_in_kernel(kept, got, label, own, next_, far):
+    slab = own.shape[0]
     d = lax.axis_index("dp")
-    for k, pay in enumerate(pays):
+
+    def part(k):
         rows = pl.ds(pl.multiple_of((d ^ k) * slab, 16), slab)
-        pay[:slab, :] = (kept[rows, :] + got[rows, :].astype(F32)).astype(BF16)
-        pay[slab:, :] = label[...]
+        return (kept[rows, :] + got[rows, :].astype(F32)).astype(BF16)
+
+    own[...] = part(0)
+    next_[...] = part(1)
+    far[:slab, :] = part(2)
+    far[slab : 2 * slab, :] = part(3)
+    far[2 * slab :, :] = label[...]
+
+
+def relay_kernel(next_, far, label, out):
+    slab = next_.shape[0]
+    out[:slab, :] = next_[...]
+    out[slab : 2 * slab, :] = far[slab : 2 * slab, :]
+    out[2 * slab : 2 * slab + LABEL_ROWS, :] = label[...]
+    out[2 * slab + LABEL_ROWS :, :] = far[2 * slab :, :]
 
 
 def pair_out_kernel(kept, got, keep, send):
@@ -176,36 +190,40 @@
 
 
 def round_kernel(kept, got, out):
-    outer = kept.shape[0]
-    out[:outer, :] = (kept[...] + got[...].astype(F32)).astype(BF16)
-    out[outer:, :] = jnp.zeros((out.shape[0] - outer, 128), BF16)
-
-
-def stack_kernel(*refs):
-    *pieces, first, second = refs
-    slab = pieces[0].shape[0] - LABEL_ROWS
-    for k, piece in enumerate(pieces):
-        out = (first, second)[k * 2 // len(pieces)]
-        at = k * slab % out.shape[0]
-        out[at : at + slab, :] = piece[:slab, :]
-
-
-def mask_kernel(counts, *refs):
-    mine, other, pieces = refs[:2], refs[2:4], refs[4:-2]
-    out, divisor = refs[-2:]
-    experts, dp = out.shape[0], len(pieces)
-    slab = 2 * mine[0].shape[0] // dp
+    out[...] = (kept[...] + got[...].astype(F32)).astype(BF16)
+
+
+def stack_kernel(near, far, first, second):
+    rows = first.shape[0]
+    slab = rows * 2 // 3
+    first[:slab, :] = near[:slab, :]
+    first[slab:, :] = far[: rows - slab, :]
+    second[: rows - slab, :] = far[rows - slab : slab, :]
+    second[rows - slab :, :] = near[slab : 2 * slab, :]
+
+
+def mask_kernel(counts, own, first, second, own_, first_, second_, label, near, far, out, divisor):
+    experts = out.shape[0]
+    dp = out.shape[2] // 128
+    slab = own.shape[0]
     half = slab // experts
     core = lax.rem(lax.axis_index("tensor"), 2)
+    at = 2 * slab
+    named = [
+        label[...],
+        near[at : at + LABEL_ROWS, :],
+        far[at : at + LABEL_ROWS, :],
+        near[at + LABEL_ROWS :, :],
+    ]
     for e in range(experts):
         divisor[e] = jnp.full(divisor.shape[1:], counts[e].astype(F32), F32)
         rows, labels = [], []
-        for which, parts in ((core, mine), (1 - core, other)):
-            for k, piece in enumerate(pieces):
-                at = k % (dp // 2) * slab + e * half
-                rows.append(parts[k // (dp // 2)][at : at + half, :])
-                label = piece[slab:, :].astype(F32)[2 * e : 2 * e + 2, :half]
-                labels.append(jnp.where(which == 0, label[0:1], label[1:2]))
+        for which, refs in ((core, (own, first, second)), (1 - core, (own_, first_, second_))):
+            every = jnp.concatenate([ref[...] for ref in refs], axis=0)
+            for k in range(dp):
+                rows.append(every[k * slab + e * half : k * slab + (e + 1) * half])
+                mine = named[k].astype(F32)[2 * e : 2 * e + 2, :half]
+                labels.append(jnp.where(which == 0, mine[0:1], mine[1:2]))
         rows = jnp.concatenate(rows, axis=0).astype(F32)
         labels = jnp.concatenate(labels, axis=1)
         labels = jnp.broadcast_to(labels, (128, labels.shape[1])).T
@@ -308,7 +326,6 @@
         split_in_kernel, "split_in", (rows(half, F32), rows(half, F32)), flops=8 * 10**9
     )(acc)
     got = lax.ppermute(send, "tensor", core)
-    slab = half // dp
     early = call(choose_kernel, "choose", jax.ShapeDtypeStruct((wide, EARLY), BF16))(early, pick)
     keep_in, send_in = call(
         pair_in_kernel, "pair_in", (rows(half, F32), rows(half, BF16)), after=[early]
@@ -334,13 +351,17 @@
     got = lax.ppermute(send, "tensor", across)
 
     slab = half // dp
-    pieces = call(round_in_kernel, "round_in", [rows(slab + LABEL_ROWS, BF16)] * dp)(
-        keep_in, got_in, label
-    )
-    pieces = [pieces[0]] + [swap(pieces[k], k) for k in DISTANCES]
-    out = call(round_kernel, "round_out", rows(wide + 16, BF16))(keep, got)
+    own, next_, far = call(
+        round_in_kernel,
+        "round_in",
+        (rows(slab, BF16), rows(slab, BF16), rows(2 * slab + LABEL_ROWS, BF16)),
+    )(keep_in, got_in, label)
+    far = swap(far, 2)
+    near = call(relay_kernel, "relay_in", rows(2 * (slab + LABEL_ROWS), BF16))(next_, far, label)
+    near = swap(near, 1)
+    out = call(round_kernel, "round_out", rows(wide, BF16))(keep, got)
     outs = [swap(out, k) for k in LATEST]
-    mine = call(stack_kernel, "stack_in", [rows(half // 2, BF16)] * 2)(*pieces)
+    mine = (own, *call(stack_kernel, "stack_in", [rows(3 * slab // 2, BF16)] * 2)(near, far))
     other = [lax.ppermute(x, "tensor", core) for x in mine]
     masked, divisor = call(
         mask_kernel,
@@ -349,8 +370,8 @@
             jax.ShapeDtypeStruct((experts, dp * cap, dp * 128), BF16),
             jax.ShapeDtypeStruct((experts, 8, 128), F32),
         ),
-        [smem] + [vmem] * (4 + dp),
-    )(expert_counts, *mine, *other, *pieces)
+        [smem] + [vmem] * 9,
+    )(expert_counts, *mine, *other, label, near, far)
     result = jax.ShapeDtypeStruct((experts, 128, 128), F32)
     return call(
         blocks_kernel,

time: 35 us -> 35.7 us (1.020)
  waiting for transfers between devices: 9.11 us -> 10.9 us
  starting transfers between devices: 14.6 us -> 13.4 us
    ppermute x6 -> x5, waiting for transfers between devices: 5.38 us -> 8.97 us  [swap(): return lax.ppermute(x, 'dp', [(d, d ^ k) for d in range(dp)])]
    ppermute x2, waiting for transfers between devices: 2.27 us -> 0.56 us  [fast(): got = lax.ppermute(send, 'tensor', core)]
    ppermute x6 -> x5, starting transfers between devices: 8.68 us -> 7.77 us  [swap(): return lax.ppermute(x, 'dp', [(d, d ^ k) for d in range(dp)])]
    pallas_call x12 -> x13, Pallas kernels: 11 us -> 11.1 us  [run(): pl.pallas_call(body, out_shape=out_shape, in_specs=(specs or [vmem] * len...]
    ppermute x2 -> x3, waiting for transfers between devices: 0.94 us -> 0.91 us  [fast(): other = [lax.ppermute(x, 'tensor', core) for x in mine]]
where the time goes in v12:
time: 35.7 us; the launch traced here: 35.6 us
  starting transfers between devices  13.4 us (38%)
  Pallas kernels  11.1 us (31%)
  waiting for transfers between devices  10.9 us (31%)
    pallas_call x13, Pallas kernels, run(): pl.pallas_call(body, out_shape=out_shape, in_specs=(specs or [vmem] * len...  11.1 us
    ppermute x5, waiting for transfers between devices, swap(): return lax.ppermute(x, 'dp', [(d, d ^ k) for d in range(dp)])  8.97 us
    ppermute x5, starting transfers between devices, swap(): return lax.ppermute(x, 'dp', [(d, d ^ k) for d in range(dp)])  7.77 us
    ppermute x1, starting transfers between devices, fast(): got_in = lax.ppermute(send_in, 'tensor', across)  2.92 us
    ppermute x1, starting transfers between devices, fast(): got = lax.ppermute(send, 'tensor', across)  1.55 us
    ppermute x3, waiting for transfers between devices, fast(): other = [lax.ppermute(x, 'tensor', core) for x in mine]  0.91 us
  transfers between devices with their start and end apart: 12, of which 7 were waited for; matrix products, arithmetic and copies ran while one was open for 0% of the time, Pallas kernels for 19%

profile of v12, /device:TPU:0, one launch (start us, length us, event | category | flops | bytes accessed | tf_op | source)
XLA Modules:
  0.0 35.6 jit_solution(6028330881407363409)
XLA Ops:
  0.0 3.1 %rotate_in.1 = (f32[2,192,512]{2,1,0:T(8,128)S(1)}, bf16[16,128]{1,0:T(8,128)(2,1)S(1)}, bf16[384,768]{1,0:T(8,128)(2,1)S(1)}, bf16[384,2,1024]{2,1,0:T(2,128)(2,1)S(1)}) custom-call(bf16[384,1536]{1,0:T(8,128)(2,1)} %refs_0_.3, s32[2,384]{1,0:T(2,128)} %bitcast.3, s32[384]{0:T(512)} %refs_2_.2, bf16[2,1536,512]{2,1,0:T(8,128)(2,1)} %refs_3_.1, ...), custom_call_target="tpu_custom_call" | custom-call | flops 1 | bytes 1 | tf_op jit(solution)/shard_map/rotate_in/pallas_call | solution.py:269
  3.1 0.0 slice-start
  3.1 0.0 slice-start.1
  3.1 0.1 split_in.1
  3.2 0.5 %collective-permute-start = (f32[768,128]{1,0:T(8,128)S(1)}, f32[768,128]{1,0:T(8,128)S(1)}, u32[]{:S(2)}, u32[]{:S(2)}) collective-permute-start(f32[768,128]{1,0:T(8,128)S(1)} %get-tuple-element.26), channel_id=1, source_target_pairs={{0,1},{1,0},{2,3},{3,2},{4,5},{5,4},{6,7},{7,6},{8,9},{9,8},{10,11... | collective-permute-start | bytes 1179656 | tf_op jit(solution)/shard_map/ppermute | solution.py:328
  3.7 0.8 %choose.1.refs_2_.refs_3_ = bf16[384,1024]{1,0:T(8,128)(2,1)S(1)} custom-call(bf16[384,2,1024]{2,1,0:T(2,128)(2,1)S(1)} %get-tuple-element.27.refs_0_, bf16[384,768]{1,0:T(8,128)(2,1)S(1)} %get-tuple-element.28.refs_1_), custom_call_target="tpu_custom_call" | custom-call | flops 1 | bytes 1 | tf_op jit(solution)/shard_map/choose/pallas_call | solution.py:269
  4.5 0.6 %collective-permute-done.refs_1_ = f32[768,128]{1,0:T(8,128)S(1)} collective-permute-done((f32[768,128]{1,0:T(8,128)S(1)}, f32[768,128]{1,0:T(8,128)S(1)}, u32[]{:S(2)}, u32[]{:S(2)}) %collective-permute-start) | collective-permute-done | bytes 393248 | tf_op jit(solution)/shard_map/ppermute | solution.py:328
  5.1 2.9 %collective-permute-start.1 = (bf16[768,128]{1,0:T(8,128)(2,1)S(1)}, bf16[768,128]{1,0:T(8,128)(2,1)S(1)}, u32[]{:S(2)}, u32[]{:S(2)}) collective-permute-start(bf16[768,128]{1,0:T(8,128)(2,1)S(1)} %get-tuple-element.30.refs_4_), channel_id=1, source_target_pairs={{0,2},{1,3},{2,0},{3,1},{4,6},{5,7},{6,4},{7,5},{8,10},{9,11},{10,... | collective-permute-start | bytes 589832 | tf_op jit(solution)/shard_map/ppermute | solution.py:333
  8.1 0.0 slice-done
  8.1 0.0 slice-done.1
  8.1 4.7 %rotate_out.1.refs_0_ = f32[2,192,512]{2,1,0:T(8,128)S(1)} custom-call(bf16[384,2,4096]{2,1,0:T(2,128)(2,1)} %refs_0_.5, bf16[384,768]{1,0:T(8,128)(2,1)S(1)} %get-tuple-element.28.refs_1_, bf16[2,4096,512]{2,1,0:T(8,128)(2,1)S(1)} %bitcast.2, bf16[384,1024]{1,0:T(8,128)(2,1)S(1)} %choose.1.refs_2_.refs_3_, bf16[768,128]{1,0:T(8,128)(2,1)S(1)} %get-tuple-element.30.refs_4_), custom_call_target="tpu_custom_call" | custom-call | flops 1 | bytes 1 | tf_op jit(solution)/shard_map/rotate_out/pallas_call | solution.py:269
  12.8 0.0 copy-start
  12.8 0.5 %collective-permute-done.1.refs_1_ = bf16[768,128]{1,0:T(8,128)(2,1)S(1)} collective-permute-done((bf16[768,128]{1,0:T(8,128)(2,1)S(1)}, bf16[768,128]{1,0:T(8,128)(2,1)S(1)}, u32[]{:S(2)}, u32[]{:S(2)}) %collective-permute-start.1) | collective-permute-done | bytes 196640 | tf_op jit(solution)/shard_map/ppermute | solution.py:333
  13.3 0.1 split_out.1
  13.4 0.1 collective-permute-start.7
  13.5 2.9 %collective-permute-start.2 = (bf16[400,128]{1,0:T(8,128)(2,1)S(1)}, bf16[400,128]{1,0:T(8,128)(2,1)S(1)}, u32[]{:S(2)}, u32[]{:S(2)}) collective-permute-start(bf16[400,128]{1,0:T(8,128)(2,1)S(1)} %get-tuple-element.34), channel_id=1, source_target_pairs={{0,8},{4,12},{8,0},{12,4},{1,9},{5,13},{9,1},{13,5},{2,10},{6,14},... | collective-permute-start | bytes 307208 | tf_op jit(solution)/shard_map/ppermute | solution.py:304
  16.4 0.0 collective-permute-done.7.refs_1_
  16.4 0.1 pair_out.1
  16.5 1.6 %collective-permute-start.8 = (bf16[384,128]{1,0:T(8,128)(2,1)S(1)}, bf16[384,128]{1,0:T(8,128)(2,1)S(1)}, u32[]{:S(2)}, u32[]{:S(2)}) collective-permute-start(bf16[384,128]{1,0:T(8,128)(2,1)S(1)} %get-tuple-element.42), channel_id=1, source_target_pairs={{0,2},{1,3},{2,0},{3,1},{4,6},{5,7},{6,4},{7,5},{8,10},{9,11},{10,... | collective-permute-start | bytes 294920 | tf_op jit(solution)/shard_map/ppermute | solution.py:351
  18.0 4.1 %collective-permute-done.2.refs_1_.refs_9_ = bf16[400,128]{1,0:T(8,128)(2,1)S(1)} collective-permute-done((bf16[400,128]{1,0:T(8,128)(2,1)S(1)}, bf16[400,128]{1,0:T(8,128)(2,1)S(1)}, u32[]{:S(2)}, u32[]{:S(2)}) %collective-permute-start.2) | collective-permute-done | bytes 102432 | tf_op jit(solution)/shard_map/ppermute | solution.py:304
  22.1 0.8 %collective-permute-start.3 = (bf16[416,128]{1,0:T(8,128)(2,1)S(1)}, bf16[416,128]{1,0:T(8,128)(2,1)S(1)}, u32[]{:S(2)}, u32[]{:S(2)}) collective-permute-start(bf16[416,128]{1,0:T(8,128)(2,1)S(1)} %relay_in.1), channel_id=1, source_target_pairs={{0,4},{4,0},{8,12},{12,8},{1,5},{5,1},{9,13},{13,9},{2,6},{6,2},{1... | collective-permute-start | bytes 319496 | tf_op jit(solution)/shard_map/ppermute | solution.py:304
  22.9 0.0 collective-permute-start.4
  22.9 0.0 collective-permute-done.8.refs_1_
  23.0 3.4 %collective-permute-start.11 = (bf16[384,128]{1,0:T(8,128)(2,1)S(1)}, bf16[384,128]{1,0:T(8,128)(2,1)S(1)}, u32[]{:S(2)}, u32[]{:S(2)}) collective-permute-start(bf16[384,128]{1,0:T(8,128)(2,1)S(1)} %round_out.1.refs_2_), channel_id=1, source_target_pairs={{0,8},{4,12},{8,0},{12,4},{1,9},{5,13},{9,1},{13,5},{2,10},{6,14},... | collective-permute-start | bytes 294920 | tf_op jit(solution)/shard_map/ppermute | solution.py:304
  26.4 0.3 collective-permute-start.10
  26.7 0.4 %collective-permute-start.9 = (bf16[384,128]{1,0:T(8,128)(2,1)S(1)}, bf16[384,128]{1,0:T(8,128)(2,1)S(1)}, u32[]{:S(2)}, u32[]{:S(2)}) collective-permute-start(bf16[384,128]{1,0:T(8,128)(2,1)S(1)} %round_out.1.refs_2_), channel_id=1, source_target_pairs={{0,4},{4,0},{8,12},{12,8},{1,5},{5,1},{9,13},{13,9},{2,6},{6,2},{1... | collective-permute-start | bytes 294920 | tf_op jit(solution)/shard_map/ppermute | solution.py:304
  27.0 0.0 collective-permute-done.3.refs_0_.refs_8_
  27.1 0.1 collective-permute-start.5
  27.1 0.0 collective-permute-done.4.refs_4_
  27.1 0.5 %collective-permute-start.6 = (bf16[288,128]{1,0:T(8,128)(2,1)S(1)}, bf16[288,128]{1,0:T(8,128)(2,1)S(1)}, u32[]{:S(2)}, u32[]{:S(2)}) collective-permute-start(bf16[288,128]{1,0:T(8,128)(2,1)S(1)} %get-tuple-element.36.refs_3_), channel_id=1, source_target_pairs={{0,1},{1,0},{2,3},{3,2},{4,5},{5,4},{6,7},{7,6},{8,9},{9,8},{10,11... | collective-permute-start | bytes 221192 | tf_op jit(solution)/shard_map/ppermute | solution.py:365
  27.6 0.8 %collective-permute-done.5.refs_5_ = bf16[288,128]{1,0:T(8,128)(2,1)S(1)} collective-permute-done((bf16[288,128]{1,0:T(8,128)(2,1)S(1)}, bf16[288,128]{1,0:T(8,128)(2,1)S(1)}, u32[]{:S(2)}, u32[]{:S(2)}) %collective-permute-start.5) | collective-permute-done | bytes 73760 | tf_op jit(solution)/shard_map/ppermute | solution.py:365
  28.4 0.2 collective-permute-done.6.refs_6_
  28.6 0.0 copy-done
  28.6 1.1 %mask_in.1 = (bf16[2,768,512]{2,1,0:T(8,128)(2,1)S(1)}, f32[2,8,128]{2,1,0:T(8,128)S(1)}) custom-call(s32[2]{0:T(128)S(1)} %copy-done, bf16[192,128]{1,0:T(8,128)(2,1)S(1)} %get-tuple-element.32.refs_1_, bf16[288,128]{1,0:T(8,128)(2,1)S(1)} %get-tuple-element.35.refs_2_, bf16[288,128]{1,0:T(8,128)(2,1)S(1)} %get-tuple-element.36.refs_3_, ...), custom_call_target="tpu_custom_call" | custom-call | flops 1 | bytes 1 | tf_op jit(solution)/shard_map/mask_in/pallas_call | solution.py:269
  29.6 4.7 %collective-permute-done.11.refs_5_ = bf16[384,128]{1,0:T(8,128)(2,1)S(1)} collective-permute-done((bf16[384,128]{1,0:T(8,128)(2,1)S(1)}, bf16[384,128]{1,0:T(8,128)(2,1)S(1)}, u32[]{:S(2)}, u32[]{:S(2)}) %collective-permute-start.11) | collective-permute-done | bytes 98336 | tf_op jit(solution)/shard_map/ppermute | solution.py:304
  34.3 0.0 collective-permute-done.10.refs_4_
  34.3 0.2 collective-permute-done.9.refs_3_
  34.5 1.1 %blocks.1 = f32[2,128,128]{2,1,0:T(8,128)} custom-call(f32[2,8,128]{2,1,0:T(8,128)S(1)} %get-tuple-element.37.refs_0_, bf16[2,768,512]{2,1,0:T(8,128)(2,1)S(1)} %get-tuple-element.38.refs_1_, bf16[384,128]{1,0:T(8,128)(2,1)S(1)} %round_out.1.refs_2_, bf16[384,128]{1,0:T(8,128)(2,1)S(1)} %collective-permute-done.9.refs_3_, ...), custom_call_target="tpu_custom_call" | custom-call | flops 1 | bytes 1 | tf_op jit(solution)/shard_map/blocks/pallas_call | solution.py:269
  (6 shorter events, 0.1 us)
Async XLA Ops:
  3.1 5.0 %slice-start = ((s8[8388608]{0:T(1024)(128)(4,1)}), s8[4194304]{0:T(1024)(128)(4,1)S(1)}, s32[]{:S(2)}) async-start(s8[8388608]{0:T(1024)(128)(4,1)} %bitcast.1), calls=%async_computation | async-start | bytes 8388608
  3.1 4.9 %slice-start.1 = ((s8[8388608]{0:T(1024)(128)(4,1)}), s8[4194304]{0:T(1024)(128)(4,1)S(1)}, s32[]{:S(2)}) async-start(s8[8388608]{0:T(1024)(128)(4,1)} %bitcast.1), calls=%async_computation.1 | async-start | bytes 8388608
  3.2 1.9 %collective-permute-start = (f32[768,128]{1,0:T(8,128)S(1)}, f32[768,128]{1,0:T(8,128)S(1)}, u32[]{:S(2)}, u32[]{:S(2)}) collective-permute-start(f32[768,128]{1,0:T(8,128)S(1)} %get-tuple-element.26), channel_id=1, source_target_pairs={{0,1},{1,0},{2,3},{3,2},{4,5},{5,4},{6,7},{7,6},{8,9},{9,8},{10,11... | collective-permute-start | bytes 1179656 | tf_op jit(solution)/shard_map/ppermute | solution.py:328
  5.1 8.1 %collective-permute-start.1 = (bf16[768,128]{1,0:T(8,128)(2,1)S(1)}, bf16[768,128]{1,0:T(8,128)(2,1)S(1)}, u32[]{:S(2)}, u32[]{:S(2)}) collective-permute-start(bf16[768,128]{1,0:T(8,128)(2,1)S(1)} %get-tuple-element.30.refs_4_), channel_id=1, source_target_pairs={{0,2},{1,3},{2,0},{3,1},{4,6},{5,7},{6,4},{7,5},{8,10},{9,11},{10,... | collective-permute-start | bytes 589832 | tf_op jit(solution)/shard_map/ppermute | solution.py:333
  12.8 15.8 %copy-start = (s32[2]{0:T(128)S(1)}, s32[2]{0:T(128)}, u32[]{:S(2)}) copy-start(s32[2]{0:T(128)} %refs_0_.4) | copy-start | bytes 28
  13.4 3.0 %collective-permute-start.7 = (f32[768,128]{1,0:T(8,128)S(1)}, f32[768,128]{1,0:T(8,128)S(1)}, u32[]{:S(2)}, u32[]{:S(2)}) collective-permute-start(f32[768,128]{1,0:T(8,128)S(1)} %get-tuple-element.40), channel_id=1, source_target_pairs={{0,1},{1,0},{2,3},{3,2},{4,5},{5,4},{6,7},{7,6},{8,9},{9,8},{10,11... | collective-permute-start | bytes 1179656 | tf_op jit(solution)/shard_map/ppermute | solution.py:349
  13.5 8.6 %collective-permute-start.2 = (bf16[400,128]{1,0:T(8,128)(2,1)S(1)}, bf16[400,128]{1,0:T(8,128)(2,1)S(1)}, u32[]{:S(2)}, u32[]{:S(2)}) collective-permute-start(bf16[400,128]{1,0:T(8,128)(2,1)S(1)} %get-tuple-element.34), channel_id=1, source_target_pairs={{0,8},{4,12},{8,0},{12,4},{1,9},{5,13},{9,1},{13,5},{2,10},{6,14},... | collective-permute-start | bytes 307208 | tf_op jit(solution)/shard_map/ppermute | solution.py:304
  16.5 6.5 %collective-permute-start.8 = (bf16[384,128]{1,0:T(8,128)(2,1)S(1)}, bf16[384,128]{1,0:T(8,128)(2,1)S(1)}, u32[]{:S(2)}, u32[]{:S(2)}) collective-permute-start(bf16[384,128]{1,0:T(8,128)(2,1)S(1)} %get-tuple-element.42), channel_id=1, source_target_pairs={{0,2},{1,3},{2,0},{3,1},{4,6},{5,7},{6,4},{7,5},{8,10},{9,11},{10,... | collective-permute-start | bytes 294920 | tf_op jit(solution)/shard_map/ppermute | solution.py:351
  22.1 4.9 %collective-permute-start.3 = (bf16[416,128]{1,0:T(8,128)(2,1)S(1)}, bf16[416,128]{1,0:T(8,128)(2,1)S(1)}, u32[]{:S(2)}, u32[]{:S(2)}) collective-permute-start(bf16[416,128]{1,0:T(8,128)(2,1)S(1)} %relay_in.1), channel_id=1, source_target_pairs={{0,4},{4,0},{8,12},{12,8},{1,5},{5,1},{9,13},{13,9},{2,6},{6,2},{1... | collective-permute-start | bytes 319496 | tf_op jit(solution)/shard_map/ppermute | solution.py:304
  22.9 4.2 %collective-permute-start.4 = (bf16[192,128]{1,0:T(8,128)(2,1)S(1)}, bf16[192,128]{1,0:T(8,128)(2,1)S(1)}, u32[]{:S(2)}, u32[]{:S(2)}) collective-permute-start(bf16[192,128]{1,0:T(8,128)(2,1)S(1)} %get-tuple-element.32.refs_1_), channel_id=1, source_target_pairs={{0,1},{1,0},{2,3},{3,2},{4,5},{5,4},{6,7},{7,6},{8,9},{9,8},{10,11... | collective-permute-start | bytes 147464 | tf_op jit(solution)/shard_map/ppermute | solution.py:365
  23.0 11.3 %collective-permute-start.11 = (bf16[384,128]{1,0:T(8,128)(2,1)S(1)}, bf16[384,128]{1,0:T(8,128)(2,1)S(1)}, u32[]{:S(2)}, u32[]{:S(2)}) collective-permute-start(bf16[384,128]{1,0:T(8,128)(2,1)S(1)} %round_out.1.refs_2_), channel_id=1, source_target_pairs={{0,8},{4,12},{8,0},{12,4},{1,9},{5,13},{9,1},{13,5},{2,10},{6,14},... | collective-permute-start | bytes 294920 | tf_op jit(solution)/shard_map/ppermute | solution.py:304
  26.4 7.9 %collective-permute-start.10 = (bf16[384,128]{1,0:T(8,128)(2,1)S(1)}, bf16[384,128]{1,0:T(8,128)(2,1)S(1)}, u32[]{:S(2)}, u32[]{:S(2)}) collective-permute-start(bf16[384,128]{1,0:T(8,128)(2,1)S(1)} %round_out.1.refs_2_), channel_id=1, source_target_pairs={{0,12},{4,8},{8,4},{12,0},{1,13},{5,9},{9,5},{13,1},{2,14},{6,10},... | collective-permute-start | bytes 294920 | tf_op jit(solution)/shard_map/ppermute | solution.py:304
  26.7 7.8 %collective-permute-start.9 = (bf16[384,128]{1,0:T(8,128)(2,1)S(1)}, bf16[384,128]{1,0:T(8,128)(2,1)S(1)}, u32[]{:S(2)}, u32[]{:S(2)}) collective-permute-start(bf16[384,128]{1,0:T(8,128)(2,1)S(1)} %round_out.1.refs_2_), channel_id=1, source_target_pairs={{0,4},{4,0},{8,12},{12,8},{1,5},{5,1},{9,13},{13,9},{2,6},{6,2},{1... | collective-permute-start | bytes 294920 | tf_op jit(solution)/shard_map/ppermute | solution.py:304
  27.1 1.3 %collective-permute-start.5 = (bf16[288,128]{1,0:T(8,128)(2,1)S(1)}, bf16[288,128]{1,0:T(8,128)(2,1)S(1)}, u32[]{:S(2)}, u32[]{:S(2)}) collective-permute-start(bf16[288,128]{1,0:T(8,128)(2,1)S(1)} %get-tuple-element.35.refs_2_), channel_id=1, source_target_pairs={{0,1},{1,0},{2,3},{3,2},{4,5},{5,4},{6,7},{7,6},{8,9},{9,8},{10,11... | collective-permute-start | bytes 221192 | tf_op jit(solution)/shard_map/ppermute | solution.py:365
  27.1 1.4 %collective-permute-start.6 = (bf16[288,128]{1,0:T(8,128)(2,1)S(1)}, bf16[288,128]{1,0:T(8,128)(2,1)S(1)}, u32[]{:S(2)}, u32[]{:S(2)}) collective-permute-start(bf16[288,128]{1,0:T(8,128)(2,1)S(1)} %get-tuple-element.36.refs_3_), channel_id=1, source_target_pairs={{0,1},{1,0},{2,3},{3,2},{4,5},{5,4},{6,7},{7,6},{8,9},{9,8},{10,11... | collective-permute-start | bytes 221192 | tf_op jit(solution)/shard_map/ppermute | solution.py:365

commit v13 on v11

--- a/solution.py
+++ b/solution.py
@@ -138,23 +138,23 @@
             acc[e] += dot(chosen[e * cap : (e + 1) * cap], basis_out[e, part, :])
 
 
-def split_out_kernel(acc, keep, send):
+def split_out_kernel(acc, *refs):
     experts, cap, width = acc.shape
     core = lax.rem(lax.axis_index("tensor"), 2)
-    at = 0
-    for x in range(width // 256):
-        for e in range(experts):
-            for ref, which in ((keep, core), (send, 1 - core)):
-                ref[at : at + cap, :] = acc[
+    for e in range(experts):
+        for ref, which in ((refs[e], core), (refs[experts + e], 1 - core)):
+            for x in range(width // 256):
+                ref[x * cap : (x + 1) * cap, :] = acc[
                     e, :, pl.ds(pl.multiple_of((2 * x + which) * 128, 128), 128)
                 ]
-            at += cap
 
 
 def pair_in_kernel(kept, got, keep, send):
     total = kept[...] + got[...]
+    outer = total.shape[0]
     keep[...] = total
-    send[...] = total.astype(BF16)
+    send[:outer, :] = total.astype(BF16)
+    send[outer:, :] = jnp.zeros((send.shape[0] - outer, 128), BF16)
 
 
 def round_in_kernel(kept, got, label, *pays):
@@ -166,50 +166,59 @@
         pay[slab:, :] = label[...]
 
 
-def pair_out_kernel(kept, got, keep, send):
-    outer = keep.shape[0]
+def pair_out_kernel(*refs):
+    *given, keep, send = refs
+    experts = len(given) // 2
+    cap = keep.shape[0] // experts
     x = lax.div(lax.axis_index("tensor"), 2)
-    mine = pl.ds(pl.multiple_of(x * outer, 16), outer)
-    keep[...] = kept[mine, :] + got[mine, :]
-    other = pl.ds(pl.multiple_of((1 - x) * outer, 16), outer)
-    send[...] = (kept[other, :] + got[other, :]).astype(BF16)
+    mine = pl.ds(pl.multiple_of(x * cap, 16), cap)
+    other = pl.ds(pl.multiple_of((1 - x) * cap, 16), cap)
+    for e in range(experts):
+        kept, got = given[e], given[experts + e]
+        at = pl.ds(e * cap, cap)
+        keep[at, :] = kept[mine, :] + got[mine, :]
+        send[at, :] = (kept[other, :] + got[other, :]).astype(BF16)
 
 
 def round_kernel(kept, got, out):
-    outer = kept.shape[0]
-    out[:outer, :] = (kept[...] + got[...].astype(F32)).astype(BF16)
-    out[outer:, :] = jnp.zeros((out.shape[0] - outer, 128), BF16)
+    out[...] = (kept[...] + got[...].astype(F32)).astype(BF16)
+
+
+def copy_kernel(x, out):
+    out[...] = x[: out.shape[0], :]
 
 
 def stack_kernel(*refs):
     *pieces, first, second = refs
+    rows = first.shape[0]
+    slab = 2 * rows // len(pieces)
+    for k, piece in enumerate(pieces):
+        for at in range(0, slab, slab // 2):
+            to = k * slab + at
+            out = (first, second)[to // rows]
+            out[to % rows : to % rows + slab // 2, :] = piece[at : at + slab // 2, :]
+
+
+def mask_kernel(counts, *refs):
+    other, pieces = refs[:3], refs[3:-2]
+    out, divisor = refs[-2:]
+    experts = out.shape[0]
     slab = pieces[0].shape[0] - LABEL_ROWS
-    for k, piece in enumerate(pieces):
-        out = (first, second)[k * 2 // len(pieces)]
-        at = k * slab % out.shape[0]
-        out[at : at + slab, :] = piece[:slab, :]
-
-
-def mask_kernel(counts, *refs):
-    mine, other, pieces = refs[:2], refs[2:4], refs[4:-2]
-    out, divisor = refs[-2:]
-    experts, dp = out.shape[0], len(pieces)
-    slab = 2 * mine[0].shape[0] // dp
     half = slab // experts
     core = lax.rem(lax.axis_index("tensor"), 2)
     for e in range(experts):
         divisor[e] = jnp.full(divisor.shape[1:], counts[e].astype(F32), F32)
         rows, labels = [], []
-        for which, parts in ((core, mine), (1 - core, other)):
+        for which, parts in ((core, [piece[:slab, :] for piece in pieces]), (1 - core, other)):
+            every = jnp.concatenate([part[...] for part in parts], axis=0)
             for k, piece in enumerate(pieces):
-                at = k % (dp // 2) * slab + e * half
-                rows.append(parts[k // (dp // 2)][at : at + half, :])
+                rows.append(every[k * slab + e * half : k * slab + (e + 1) * half])
                 label = piece[slab:, :].astype(F32)[2 * e : 2 * e + 2, :half]
                 labels.append(jnp.where(which == 0, label[0:1], label[1:2]))
         rows = jnp.concatenate(rows, axis=0).astype(F32)
         labels = jnp.concatenate(labels, axis=1)
         labels = jnp.broadcast_to(labels, (128, labels.shape[1])).T
-        for n in range(dp):
+        for n in range(len(pieces)):
             out[e, :, n * 128 : (n + 1) * 128] = jnp.where(
                 labels == float(n + 1), rows, 0.0
             ).astype(BF16)
@@ -308,10 +317,9 @@
         split_in_kernel, "split_in", (rows(half, F32), rows(half, F32)), flops=8 * 10**9
     )(acc)
     got = lax.ppermute(send, "tensor", core)
-    slab = half // dp
     early = call(choose_kernel, "choose", jax.ShapeDtypeStruct((wide, EARLY), BF16))(early, pick)
     keep_in, send_in = call(
-        pair_in_kernel, "pair_in", (rows(half, F32), rows(half, BF16)), after=[early]
+        pair_in_kernel, "pair_in", (rows(half, F32), rows(half + 16, BF16)), after=[early]
     )(keep, got)
     got_in = lax.ppermute(send_in, "tensor", across)
 
@@ -326,11 +334,11 @@
         ],
         after=[send_in],
     )(pin(grads), pick, basis_out, early)
+    split = call(split_out_kernel, "split_out", [rows(2 * cap, F32)] * (2 * experts))(acc)
+    got = [lax.ppermute(x, "tensor", core) for x in split[experts:]]
     keep, send = call(
-        split_out_kernel, "split_out", (rows(half, F32), rows(half, F32)), after=[got_in]
-    )(acc)
-    got = lax.ppermute(send, "tensor", core)
-    keep, send = call(pair_out_kernel, "pair_out", (rows(wide, F32), rows(wide, BF16)))(keep, got)
+        pair_out_kernel, "pair_out", (rows(wide, F32), rows(wide, BF16)), after=[got_in]
+    )(*split[:experts], *got)
     got = lax.ppermute(send, "tensor", across)
 
     slab = half // dp
@@ -338,10 +346,12 @@
         keep_in, got_in, label
     )
     pieces = [pieces[0]] + [swap(pieces[k], k) for k in DISTANCES]
-    out = call(round_kernel, "round_out", rows(wide + 16, BF16))(keep, got)
+    own = call(copy_kernel, "own_in", rows(slab, BF16))(pieces[0])
+    other = [lax.ppermute(own, "tensor", core)]
+    out = call(round_kernel, "round_out", rows(wide, BF16), after=other)(keep, got)
     outs = [swap(out, k) for k in LATEST]
-    mine = call(stack_kernel, "stack_in", [rows(half // 2, BF16)] * 2)(*pieces)
-    other = [lax.ppermute(x, "tensor", core) for x in mine]
+    mine = call(stack_kernel, "stack_in", [rows(3 * slab // 2, BF16)] * 2)(*pieces[1:])
+    other += [lax.ppermute(x, "tensor", core) for x in mine]
     masked, divisor = call(
         mask_kernel,
         "mask_in",
@@ -349,8 +359,8 @@
             jax.ShapeDtypeStruct((experts, dp * cap, dp * 128), BF16),
             jax.ShapeDtypeStruct((experts, 8, 128), F32),
         ),
-        [smem] + [vmem] * (4 + dp),
-    )(expert_counts, *mine, *other, *pieces)
+        [smem] + [vmem] * (3 + dp),
+    )(expert_counts, *other, *pieces)
     result = jax.ShapeDtypeStruct((experts, 128, 128), F32)
     return call(
         blocks_kernel,

time: 35 us -> 34.5 us (0.986)
  waiting for transfers between devices: 9.11 us -> 8.2 us
    ppermute x2 -> x1, waiting for transfers between devices: 2.27 us -> 0.56 us  [fast(): got = lax.ppermute(send, 'tensor', core)]
    ppermute x2 -> x5, waiting for transfers between devices: 0.94 us -> 2.13 us  [the longest x2 1.21 us: fast(): got = [lax.ppermute(x, 'tensor', core) for x in split[experts:]]]
    ppermute x2 -> x5, starting transfers between devices: 0.57 us -> 1.14 us  [the longest x2 0.57 us: fast(): other += [lax.ppermute(x, 'tensor', core) for x in mine]]
    ppermute x1, waiting for transfers between devices: 0.51 us -> 0.01 us  [fast(): got_in = lax.ppermute(send_in, 'tensor', across)]
    pallas_call x12 -> x13, Pallas kernels: 11 us -> 11.1 us  [run(): pl.pallas_call(body, out_shape=out_shape, in_specs=(specs or [vmem] * len...]
  transfers between devices with their start and end apart: 12 -> 14, of which waited for: 7 -> 8; matrix products, arithmetic and copies ran while one was open for 0% -> 0% of each run, Pallas kernels for 19% -> 20%
where the time goes in v13:
time: 34.5 us; the launch traced here: 34.3 us
  starting transfers between devices  14.8 us (43%)
  Pallas kernels  11.1 us (32%)
  waiting for transfers between devices  8.2 us (24%)
    pallas_call x13, Pallas kernels, run(): pl.pallas_call(body, out_shape=out_shape, in_specs=(specs or [vmem] * len...  11.1 us
    ppermute x6, starting transfers between devices, swap(): return lax.ppermute(x, 'dp', [(d, d ^ k) for d in range(dp)])  8.74 us
    ppermute x6, waiting for transfers between devices, swap(): return lax.ppermute(x, 'dp', [(d, d ^ k) for d in range(dp)])  5.5 us
    ppermute x1, starting transfers between devices, fast(): got_in = lax.ppermute(send_in, 'tensor', across)  2.92 us
    ppermute x1, starting transfers between devices, fast(): got = lax.ppermute(send, 'tensor', across)  1.51 us
    ppermute x2, waiting for transfers between devices, fast(): got = [lax.ppermute(x, 'tensor', core) for x in split[experts:]]  1.21 us
    ppermute x2, waiting for transfers between devices, fast(): other += [lax.ppermute(x, 'tensor', core) for x in mine]  0.91 us
  transfers between devices with their start and end apart: 14, of which 8 were waited for; matrix products, arithmetic and copies ran while one was open for 0% of the time, Pallas kernels for 20%

profile of v13, /device:TPU:0, one launch (start us, length us, event | category | flops | bytes accessed | tf_op | source)
XLA Modules:
  0.0 34.3 jit_solution(435945472484908522)
XLA Ops:
  0.0 3.1 %rotate_in.1 = (f32[2,192,512]{2,1,0:T(8,128)S(1)}, bf16[16,128]{1,0:T(8,128)(2,1)S(1)}, bf16[384,768]{1,0:T(8,128)(2,1)S(1)}, bf16[384,2,1024]{2,1,0:T(2,128)(2,1)S(1)}) custom-call(bf16[384,1536]{1,0:T(8,128)(2,1)} %refs_0_.3, s32[2,384]{1,0:T(2,128)} %bitcast.3, s32[384]{0:T(512)} %refs_2_.2, bf16[2,1536,512]{2,1,0:T(8,128)(2,1)} %refs_3_.1, ...), custom_call_target="tpu_custom_call" | custom-call | flops 1 | bytes 1 | tf_op jit(solution)/shard_map/rotate_in/pallas_call | solution.py:260
  3.1 0.0 slice-start
  3.1 0.0 slice-start.1
  3.1 0.1 split_in.1
  3.2 0.5 %collective-permute-start = (f32[768,128]{1,0:T(8,128)S(1)}, f32[768,128]{1,0:T(8,128)S(1)}, u32[]{:S(2)}, u32[]{:S(2)}) collective-permute-start(f32[768,128]{1,0:T(8,128)S(1)} %get-tuple-element.29), channel_id=1, source_target_pairs={{0,1},{1,0},{2,3},{3,2},{4,5},{5,4},{6,7},{7,6},{8,9},{9,8},{10,11... | collective-permute-start | bytes 1179656 | tf_op jit(solution)/shard_map/ppermute | solution.py:319
  3.7 0.8 %choose.1.refs_2_.refs_3_ = bf16[384,1024]{1,0:T(8,128)(2,1)S(1)} custom-call(bf16[384,2,1024]{2,1,0:T(2,128)(2,1)S(1)} %get-tuple-element.30.refs_0_, bf16[384,768]{1,0:T(8,128)(2,1)S(1)} %get-tuple-element.31.refs_1_), custom_call_target="tpu_custom_call" | custom-call | flops 1 | bytes 1 | tf_op jit(solution)/shard_map/choose/pallas_call | solution.py:260
  4.5 0.6 %collective-permute-done.refs_1_ = f32[768,128]{1,0:T(8,128)S(1)} collective-permute-done((f32[768,128]{1,0:T(8,128)S(1)}, f32[768,128]{1,0:T(8,128)S(1)}, u32[]{:S(2)}, u32[]{:S(2)}) %collective-permute-start) | collective-permute-done | bytes 393248 | tf_op jit(solution)/shard_map/ppermute | solution.py:319
  5.1 0.0 copy-start
  5.1 2.9 %collective-permute-start.1 = (bf16[784,128]{1,0:T(8,128)(2,1)S(1)}, bf16[784,128]{1,0:T(8,128)(2,1)S(1)}, u32[]{:S(2)}, u32[]{:S(2)}) collective-permute-start(bf16[784,128]{1,0:T(8,128)(2,1)S(1)} %get-tuple-element.33.refs_4_), channel_id=1, source_target_pairs={{0,2},{1,3},{2,0},{3,1},{4,6},{5,7},{6,4},{7,5},{8,10},{9,11},{10,... | collective-permute-start | bytes 602120 | tf_op jit(solution)/shard_map/ppermute | solution.py:324
  8.1 0.0 slice-done
  8.1 0.0 slice-done.1
  8.1 4.7 %rotate_out.1.refs_0_ = f32[2,192,512]{2,1,0:T(8,128)S(1)} custom-call(bf16[384,2,4096]{2,1,0:T(2,128)(2,1)} %refs_0_.5, bf16[384,768]{1,0:T(8,128)(2,1)S(1)} %get-tuple-element.31.refs_1_, bf16[2,4096,512]{2,1,0:T(8,128)(2,1)S(1)} %bitcast.2, bf16[384,1024]{1,0:T(8,128)(2,1)S(1)} %choose.1.refs_2_.refs_3_, bf16[784,128]{1,0:T(8,128)(2,1)S(1)} %get-tuple-element.33.refs_4_), custom_call_target="tpu_custom_call" | custom-call | flops 1 | bytes 1 | tf_op jit(solution)/shard_map/rotate_out/pallas_call | solution.py:260
  12.8 0.1 split_out.1
  12.9 0.1 collective-permute-start.8
  13.0 0.5 %collective-permute-start.9 = (f32[384,128]{1,0:T(8,128)S(1)}, f32[384,128]{1,0:T(8,128)S(1)}, u32[]{:S(2)}, u32[]{:S(2)}) collective-permute-start(f32[384,128]{1,0:T(8,128)S(1)} %get-tuple-element.46), channel_id=1, source_target_pairs={{0,1},{1,0},{2,3},{3,2},{4,5},{5,4},{6,7},{7,6},{8,9},{9,8},{10,11... | collective-permute-start | bytes 589832 | tf_op jit(solution)/shard_map/ppermute | solution.py:338
  13.5 0.9 %collective-permute-done.8.refs_2_ = f32[384,128]{1,0:T(8,128)S(1)} collective-permute-done((f32[384,128]{1,0:T(8,128)S(1)}, f32[384,128]{1,0:T(8,128)S(1)}, u32[]{:S(2)}, u32[]{:S(2)}) %collective-permute-start.8) | collective-permute-done | bytes 196640 | tf_op jit(solution)/shard_map/ppermute | solution.py:338
  14.5 0.3 collective-permute-done.9.refs_3_
  14.7 0.0 collective-permute-done.1.refs_1_.refs_4_
  14.8 1.5 %collective-permute-start.10 = (bf16[384,128]{1,0:T(8,128)(2,1)S(1)}, bf16[384,128]{1,0:T(8,128)(2,1)S(1)}, u32[]{:S(2)}, u32[]{:S(2)}) collective-permute-start(bf16[384,128]{1,0:T(8,128)(2,1)S(1)} %get-tuple-element.48), channel_id=1, source_target_pairs={{0,2},{1,3},{2,0},{3,1},{4,6},{5,7},{6,4},{7,5},{8,10},{9,11},{10,... | collective-permute-start | bytes 294920 | tf_op jit(solution)/shard_map/ppermute | solution.py:342
  16.3 1.6 %collective-permute-start.3 = (bf16[208,128]{1,0:T(8,128)(2,1)S(1)}, bf16[208,128]{1,0:T(8,128)(2,1)S(1)}, u32[]{:S(2)}, u32[]{:S(2)}) collective-permute-start(bf16[208,128]{1,0:T(8,128)(2,1)S(1)} %get-tuple-element.36), channel_id=1, source_target_pairs={{0,4},{4,0},{8,12},{12,8},{1,5},{5,1},{9,13},{13,9},{2,6},{6,2},{1... | collective-permute-start | bytes 159752 | tf_op jit(solution)/shard_map/ppermute | solution.py:295
  18.0 0.0 collective-permute-start.2
  18.0 2.7 %collective-permute-start.4 = (bf16[208,128]{1,0:T(8,128)(2,1)S(1)}, bf16[208,128]{1,0:T(8,128)(2,1)S(1)}, u32[]{:S(2)}, u32[]{:S(2)}) collective-permute-start(bf16[208,128]{1,0:T(8,128)(2,1)S(1)} %get-tuple-element.37), channel_id=1, source_target_pairs={{0,8},{4,12},{8,0},{12,4},{1,9},{5,13},{9,1},{13,5},{2,10},{6,14},... | collective-permute-start | bytes 159752 | tf_op jit(solution)/shard_map/ppermute | solution.py:295
  20.6 0.2 collective-permute-start.5
  20.9 0.0 collective-permute-done.2.refs_1_.refs_2_
  20.9 0.0 collective-permute-done.10.refs_1_
  20.9 1.8 %collective-permute-start.13 = (bf16[384,128]{1,0:T(8,128)(2,1)S(1)}, bf16[384,128]{1,0:T(8,128)(2,1)S(1)}, u32[]{:S(2)}, u32[]{:S(2)}) collective-permute-start(bf16[384,128]{1,0:T(8,128)(2,1)S(1)} %round_out.1.refs_2_), channel_id=1, source_target_pairs={{0,8},{4,12},{8,0},{12,4},{1,9},{5,13},{9,1},{13,5},{2,10},{6,14},... | collective-permute-start | bytes 294920 | tf_op jit(solution)/shard_map/ppermute | solution.py:295
  22.6 2.0 %collective-permute-start.12 = (bf16[384,128]{1,0:T(8,128)(2,1)S(1)}, bf16[384,128]{1,0:T(8,128)(2,1)S(1)}, u32[]{:S(2)}, u32[]{:S(2)}) collective-permute-start(bf16[384,128]{1,0:T(8,128)(2,1)S(1)} %round_out.1.refs_2_), channel_id=1, source_target_pairs={{0,12},{4,8},{8,4},{12,0},{1,13},{5,9},{9,5},{13,1},{2,14},{6,10},... | collective-permute-start | bytes 294920 | tf_op jit(solution)/shard_map/ppermute | solution.py:295
  24.6 0.0 collective-permute-done.3.refs_0_.refs_5_
  24.6 0.5 %collective-permute-start.11 = (bf16[384,128]{1,0:T(8,128)(2,1)S(1)}, bf16[384,128]{1,0:T(8,128)(2,1)S(1)}, u32[]{:S(2)}, u32[]{:S(2)}) collective-permute-start(bf16[384,128]{1,0:T(8,128)(2,1)S(1)} %round_out.1.refs_2_), channel_id=1, source_target_pairs={{0,4},{4,0},{8,12},{12,8},{1,5},{5,1},{9,13},{13,9},{2,6},{6,2},{1... | collective-permute-start | bytes 294920 | tf_op jit(solution)/shard_map/ppermute | solution.py:295
  25.1 0.0 collective-permute-done.4.refs_1_.refs_6_
  25.1 2.1 %collective-permute-done.5.refs_2_.refs_7_ = bf16[208,128]{1,0:T(8,128)(2,1)S(1)} collective-permute-done((bf16[208,128]{1,0:T(8,128)(2,1)S(1)}, bf16[208,128]{1,0:T(8,128)(2,1)S(1)}, u32[]{:S(2)}, u32[]{:S(2)}) %collective-permute-start.5) | collective-permute-done | bytes 53280 | tf_op jit(solution)/shard_map/ppermute | solution.py:295
  27.2 0.1 collective-permute-start.6
  27.3 0.5 %collective-permute-start.7 = (bf16[288,128]{1,0:T(8,128)(2,1)S(1)}, bf16[288,128]{1,0:T(8,128)(2,1)S(1)}, u32[]{:S(2)}, u32[]{:S(2)}) collective-permute-start(bf16[288,128]{1,0:T(8,128)(2,1)S(1)} %get-tuple-element.40), channel_id=1, source_target_pairs={{0,1},{1,0},{2,3},{3,2},{4,5},{5,4},{6,7},{7,6},{8,9},{9,8},{10,11... | collective-permute-start | bytes 221192 | tf_op jit(solution)/shard_map/ppermute | solution.py:354
  27.8 0.8 %collective-permute-done.6.refs_2_ = bf16[288,128]{1,0:T(8,128)(2,1)S(1)} collective-permute-done((bf16[288,128]{1,0:T(8,128)(2,1)S(1)}, bf16[288,128]{1,0:T(8,128)(2,1)S(1)}, u32[]{:S(2)}, u32[]{:S(2)}) %collective-permute-start.6) | collective-permute-done | bytes 73760 | tf_op jit(solution)/shard_map/ppermute | solution.py:354
  28.6 0.2 collective-permute-done.7.refs_3_
  28.7 0.0 copy-done
  28.7 1.1 %mask_in.1 = (bf16[2,768,512]{2,1,0:T(8,128)(2,1)S(1)}, f32[2,8,128]{2,1,0:T(8,128)S(1)}) custom-call(s32[2]{0:T(128)S(1)} %copy-done, bf16[192,128]{1,0:T(8,128)(2,1)S(1)} %collective-permute-done.2.refs_1_.refs_2_, bf16[288,128]{1,0:T(8,128)(2,1)S(1)} %collective-permute-done.6.refs_2_, bf16[288,128]{1,0:T(8,128)(2,1)S(1)} %collective-permute-done.7.refs_3_, ...), custom_call_target="tpu_custom_call" | custom-call | flops 1 | bytes 1 | tf_op jit(solution)/shard_map/mask_in/pallas_call | solution.py:260
  29.8 3.2 %collective-permute-done.13.refs_5_ = bf16[384,128]{1,0:T(8,128)(2,1)S(1)} collective-permute-done((bf16[384,128]{1,0:T(8,128)(2,1)S(1)}, bf16[384,128]{1,0:T(8,128)(2,1)S(1)}, u32[]{:S(2)}, u32[]{:S(2)}) %collective-permute-start.13) | collective-permute-done | bytes 98336 | tf_op jit(solution)/shard_map/ppermute | solution.py:295
  33.0 0.0 collective-permute-done.12.refs_4_
  33.0 0.2 collective-permute-done.11.refs_3_
  33.2 1.1 %blocks.1 = f32[2,128,128]{2,1,0:T(8,128)} custom-call(f32[2,8,128]{2,1,0:T(8,128)S(1)} %get-tuple-element.41.refs_0_, bf16[2,768,512]{2,1,0:T(8,128)(2,1)S(1)} %get-tuple-element.42.refs_1_, bf16[384,128]{1,0:T(8,128)(2,1)S(1)} %round_out.1.refs_2_, bf16[384,128]{1,0:T(8,128)(2,1)S(1)} %collective-permute-done.11.refs_3_, ...), custom_call_target="tpu_custom_call" | custom-call | flops 1 | bytes 1 | tf_op jit(solution)/shard_map/blocks/pallas_call | solution.py:260
  (7 shorter events, 0.2 us)
Async XLA Ops:
  3.1 5.0 %slice-start = ((s8[8388608]{0:T(1024)(128)(4,1)}), s8[4194304]{0:T(1024)(128)(4,1)S(1)}, s32[]{:S(2)}) async-start(s8[8388608]{0:T(1024)(128)(4,1)} %bitcast.1), calls=%async_computation | async-start | bytes 8388608
  3.1 5.0 %slice-start.1 = ((s8[8388608]{0:T(1024)(128)(4,1)}), s8[4194304]{0:T(1024)(128)(4,1)S(1)}, s32[]{:S(2)}) async-start(s8[8388608]{0:T(1024)(128)(4,1)} %bitcast.1), calls=%async_computation.1 | async-start | bytes 8388608
  3.2 1.9 %collective-permute-start = (f32[768,128]{1,0:T(8,128)S(1)}, f32[768,128]{1,0:T(8,128)S(1)}, u32[]{:S(2)}, u32[]{:S(2)}) collective-permute-start(f32[768,128]{1,0:T(8,128)S(1)} %get-tuple-element.29), channel_id=1, source_target_pairs={{0,1},{1,0},{2,3},{3,2},{4,5},{5,4},{6,7},{7,6},{8,9},{9,8},{10,11... | collective-permute-start | bytes 1179656 | tf_op jit(solution)/shard_map/ppermute | solution.py:319
  5.1 23.6 %copy-start = (s32[2]{0:T(128)S(1)}, s32[2]{0:T(128)}, u32[]{:S(2)}) copy-start(s32[2]{0:T(128)} %refs_0_.4) | copy-start | bytes 28
  5.1 9.6 %collective-permute-start.1 = (bf16[784,128]{1,0:T(8,128)(2,1)S(1)}, bf16[784,128]{1,0:T(8,128)(2,1)S(1)}, u32[]{:S(2)}, u32[]{:S(2)}) collective-permute-start(bf16[784,128]{1,0:T(8,128)(2,1)S(1)} %get-tuple-element.33.refs_4_), channel_id=1, source_target_pairs={{0,2},{1,3},{2,0},{3,1},{4,6},{5,7},{6,4},{7,5},{8,10},{9,11},{10,... | collective-permute-start | bytes 602120 | tf_op jit(solution)/shard_map/ppermute | solution.py:324
  12.9 1.5 %collective-permute-start.8 = (f32[384,128]{1,0:T(8,128)S(1)}, f32[384,128]{1,0:T(8,128)S(1)}, u32[]{:S(2)}, u32[]{:S(2)}) collective-permute-start(f32[384,128]{1,0:T(8,128)S(1)} %get-tuple-element.45), channel_id=1, source_target_pairs={{0,1},{1,0},{2,3},{3,2},{4,5},{5,4},{6,7},{7,6},{8,9},{9,8},{10,11... | collective-permute-start | bytes 589832 | tf_op jit(solution)/shard_map/ppermute | solution.py:338
  13.0 1.7 %collective-permute-start.9 = (f32[384,128]{1,0:T(8,128)S(1)}, f32[384,128]{1,0:T(8,128)S(1)}, u32[]{:S(2)}, u32[]{:S(2)}) collective-permute-start(f32[384,128]{1,0:T(8,128)S(1)} %get-tuple-element.46), channel_id=1, source_target_pairs={{0,1},{1,0},{2,3},{3,2},{4,5},{5,4},{6,7},{7,6},{8,9},{9,8},{10,11... | collective-permute-start | bytes 589832 | tf_op jit(solution)/shard_map/ppermute | solution.py:338
  14.8 6.1 %collective-permute-start.10 = (bf16[384,128]{1,0:T(8,128)(2,1)S(1)}, bf16[384,128]{1,0:T(8,128)(2,1)S(1)}, u32[]{:S(2)}, u32[]{:S(2)}) collective-permute-start(bf16[384,128]{1,0:T(8,128)(2,1)S(1)} %get-tuple-element.48), channel_id=1, source_target_pairs={{0,2},{1,3},{2,0},{3,1},{4,6},{5,7},{6,4},{7,5},{8,10},{9,11},{10,... | collective-permute-start | bytes 294920 | tf_op jit(solution)/shard_map/ppermute | solution.py:342
  16.3 8.3 %collective-permute-start.3 = (bf16[208,128]{1,0:T(8,128)(2,1)S(1)}, bf16[208,128]{1,0:T(8,128)(2,1)S(1)}, u32[]{:S(2)}, u32[]{:S(2)}) collective-permute-start(bf16[208,128]{1,0:T(8,128)(2,1)S(1)} %get-tuple-element.36), channel_id=1, source_target_pairs={{0,4},{4,0},{8,12},{12,8},{1,5},{5,1},{9,13},{13,9},{2,6},{6,2},{1... | collective-permute-start | bytes 159752 | tf_op jit(solution)/shard_map/ppermute | solution.py:295
  18.0 2.9 %collective-permute-start.2 = (bf16[192,128]{1,0:T(8,128)(2,1)S(1)}, bf16[192,128]{1,0:T(8,128)(2,1)S(1)}, u32[]{:S(2)}, u32[]{:S(2)}) collective-permute-start(bf16[192,128]{1,0:T(8,128)(2,1)S(1)} %own_in.1), channel_id=1, source_target_pairs={{0,1},{1,0},{2,3},{3,2},{4,5},{5,4},{6,7},{7,6},{8,9},{9,8},{10,11... | collective-permute-start | bytes 147464 | tf_op jit(solution)/shard_map/ppermute | solution.py:350
  18.0 7.1 %collective-permute-start.4 = (bf16[208,128]{1,0:T(8,128)(2,1)S(1)}, bf16[208,128]{1,0:T(8,128)(2,1)S(1)}, u32[]{:S(2)}, u32[]{:S(2)}) collective-permute-start(bf16[208,128]{1,0:T(8,128)(2,1)S(1)} %get-tuple-element.37), channel_id=1, source_target_pairs={{0,8},{4,12},{8,0},{12,4},{1,9},{5,13},{9,1},{13,5},{2,10},{6,14},... | collective-permute-start | bytes 159752 | tf_op jit(solution)/shard_map/ppermute | solution.py:295
  20.6 6.6 %collective-permute-start.5 = (bf16[208,128]{1,0:T(8,128)(2,1)S(1)}, bf16[208,128]{1,0:T(8,128)(2,1)S(1)}, u32[]{:S(2)}, u32[]{:S(2)}) collective-permute-start(bf16[208,128]{1,0:T(8,128)(2,1)S(1)} %get-tuple-element.38), channel_id=1, source_target_pairs={{0,12},{4,8},{8,4},{12,0},{1,13},{5,9},{9,5},{13,1},{2,14},{6,10},... | collective-permute-start | bytes 159752 | tf_op jit(solution)/shard_map/ppermute | solution.py:295
  20.9 12.1 %collective-permute-start.13 = (bf16[384,128]{1,0:T(8,128)(2,1)S(1)}, bf16[384,128]{1,0:T(8,128)(2,1)S(1)}, u32[]{:S(2)}, u32[]{:S(2)}) collective-permute-start(bf16[384,128]{1,0:T(8,128)(2,1)S(1)} %round_out.1.refs_2_), channel_id=1, source_target_pairs={{0,8},{4,12},{8,0},{12,4},{1,9},{5,13},{9,1},{13,5},{2,10},{6,14},... | collective-permute-start | bytes 294920 | tf_op jit(solution)/shard_map/ppermute | solution.py:295
  22.6 10.4 %collective-permute-start.12 = (bf16[384,128]{1,0:T(8,128)(2,1)S(1)}, bf16[384,128]{1,0:T(8,128)(2,1)S(1)}, u32[]{:S(2)}, u32[]{:S(2)}) collective-permute-start(bf16[384,128]{1,0:T(8,128)(2,1)S(1)} %round_out.1.refs_2_), channel_id=1, source_target_pairs={{0,12},{4,8},{8,4},{12,0},{1,13},{5,9},{9,5},{13,1},{2,14},{6,10},... | collective-permute-start | bytes 294920 | tf_op jit(solution)/shard_map/ppermute | solution.py:295
  24.6 8.6 %collective-permute-start.11 = (bf16[384,128]{1,0:T(8,128)(2,1)S(1)}, bf16[384,128]{1,0:T(8,128)(2,1)S(1)}, u32[]{:S(2)}, u32[]{:S(2)}) collective-permute-start(bf16[384,128]{1,0:T(8,128)(2,1)S(1)} %round_out.1.refs_2_), channel_id=1, source_target_pairs={{0,4},{4,0},{8,12},{12,8},{1,5},{5,1},{9,13},{13,9},{2,6},{6,2},{1... | collective-permute-start | bytes 294920 | tf_op jit(solution)/shard_map/ppermute | solution.py:295
  27.2 1.3 %collective-permute-start.6 = (bf16[288,128]{1,0:T(8,128)(2,1)S(1)}, bf16[288,128]{1,0:T(8,128)(2,1)S(1)}, u32[]{:S(2)}, u32[]{:S(2)}) collective-permute-start(bf16[288,128]{1,0:T(8,128)(2,1)S(1)} %get-tuple-element.39), channel_id=1, source_target_pairs={{0,1},{1,0},{2,3},{3,2},{4,5},{5,4},{6,7},{7,6},{8,9},{9,8},{10,11... | collective-permute-start | bytes 221192 | tf_op jit(solution)/shard_map/ppermute | solution.py:354
  27.3 1.4 %collective-permute-start.7 = (bf16[288,128]{1,0:T(8,128)(2,1)S(1)}, bf16[288,128]{1,0:T(8,128)(2,1)S(1)}, u32[]{:S(2)}, u32[]{:S(2)}) collective-permute-start(bf16[288,128]{1,0:T(8,128)(2,1)S(1)} %get-tuple-element.40), channel_id=1, source_target_pairs={{0,1},{1,0},{2,3},{3,2},{4,5},{5,4},{6,7},{7,6},{8,9},{9,8},{10,11... | collective-permute-start | bytes 221192 | tf_op jit(solution)/shard_map/ppermute | solution.py:354

commit v14 on v13

--- a/solution.py
+++ b/solution.py
@@ -151,10 +151,8 @@
 
 def pair_in_kernel(kept, got, keep, send):
     total = kept[...] + got[...]
-    outer = total.shape[0]
     keep[...] = total
-    send[:outer, :] = total.astype(BF16)
-    send[outer:, :] = jnp.zeros((send.shape[0] - outer, 128), BF16)
+    send[...] = total.astype(BF16)
 
 
 def round_in_kernel(kept, got, label, *pays):
@@ -199,23 +197,18 @@
             out[to % rows : to % rows + slab // 2, :] = piece[at : at + slab // 2, :]
 
 
-def mask_kernel(counts, *refs):
-    other, pieces = refs[:3], refs[3:-2]
-    out, divisor = refs[-2:]
-    experts = out.shape[0]
-    slab = pieces[0].shape[0] - LABEL_ROWS
-    half = slab // experts
-    core = lax.rem(lax.axis_index("tensor"), 2)
-    for e in range(experts):
-        divisor[e] = jnp.full(divisor.shape[1:], counts[e].astype(F32), F32)
+def mask(which, parts, pieces, out):
+    experts, slots, _ = out.shape
+    half = slots // len(pieces)
+    slab = experts * half
+    every = jnp.concatenate(parts, axis=0).astype(F32)
+    for e in range(experts):
         rows, labels = [], []
-        for which, parts in ((core, [piece[:slab, :] for piece in pieces]), (1 - core, other)):
-            every = jnp.concatenate([part[...] for part in parts], axis=0)
-            for k, piece in enumerate(pieces):
-                rows.append(every[k * slab + e * half : k * slab + (e + 1) * half])
-                label = piece[slab:, :].astype(F32)[2 * e : 2 * e + 2, :half]
-                labels.append(jnp.where(which == 0, label[0:1], label[1:2]))
-        rows = jnp.concatenate(rows, axis=0).astype(F32)
+        for k, piece in enumerate(pieces):
+            rows.append(every[k * slab + e * half : k * slab + (e + 1) * half])
+            label = piece[slab : slab + LABEL_ROWS, :].astype(F32)[2 * e : 2 * e + 2, :half]
+            labels.append(jnp.where(which == 0, label[0:1], label[1:2]))
+        rows = jnp.concatenate(rows, axis=0)
         labels = jnp.concatenate(labels, axis=1)
         labels = jnp.broadcast_to(labels, (128, labels.shape[1])).T
         for n in range(len(pieces)):
@@ -224,11 +217,26 @@
             ).astype(BF16)
 
 
-def blocks_kernel(divisor, masked, own, *refs):
+def mask_own_kernel(counts, *refs):
+    *pieces, out, divisor = refs
+    slab = out.shape[0] * out.shape[1] // len(pieces)
+    core = lax.rem(lax.axis_index("tensor"), 2)
+    mask(core, [piece[:slab, :] for piece in pieces], pieces, out)
+    for e in range(out.shape[0]):
+        divisor[e] = jnp.full(divisor.shape[1:], counts[e].astype(F32), F32)
+
+
+def mask_other_kernel(first, second, third, *refs):
+    *pieces, out = refs
+    core = lax.rem(lax.axis_index("tensor"), 2)
+    mask(1 - core, [first[...], second[...], third[...]], pieces, out)
+
+
+def blocks_kernel(divisor, masked_own, masked_other, own, *refs):
     *far, result, final, sems = refs
     outs = [own] + [far[LATEST.index(k)] for k in DISTANCES]
-    experts, slots, _ = masked.shape
-    half = slots // (2 * len(outs))
+    experts, slots, _ = masked_own.shape
+    half = slots // len(outs)
     core = lax.rem(lax.axis_index("tensor"), 2)
     copies = []
     for e in range(experts):
@@ -237,7 +245,8 @@
             for which in (core, 1 - core)
             for ref in outs
         ]
-        blocks = dot(jnp.concatenate(rows, axis=0).T, masked[e])
+        rows = jnp.concatenate(rows, axis=0).T
+        blocks = dot(rows[:, :slots], masked_own[e]) + dot(rows[:, slots:], masked_other[e])
         squares = blocks * blocks
         summed = squares[:, :128]
         for at in range(128, squares.shape[1], 128):
@@ -319,7 +328,7 @@
     got = lax.ppermute(send, "tensor", core)
     early = call(choose_kernel, "choose", jax.ShapeDtypeStruct((wide, EARLY), BF16))(early, pick)
     keep_in, send_in = call(
-        pair_in_kernel, "pair_in", (rows(half, F32), rows(half + 16, BF16)), after=[early]
+        pair_in_kernel, "pair_in", (rows(half, F32), rows(half, BF16)), after=[early]
     )(keep, got)
     got_in = lax.ppermute(send_in, "tensor", across)
 
@@ -336,31 +345,29 @@
     )(pin(grads), pick, basis_out, early)
     split = call(split_out_kernel, "split_out", [rows(2 * cap, F32)] * (2 * experts))(acc)
     got = [lax.ppermute(x, "tensor", core) for x in split[experts:]]
-    keep, send = call(
-        pair_out_kernel, "pair_out", (rows(wide, F32), rows(wide, BF16)), after=[got_in]
-    )(*split[:experts], *got)
-    got = lax.ppermute(send, "tensor", across)
-
     slab = half // dp
     pieces = call(round_in_kernel, "round_in", [rows(slab + LABEL_ROWS, BF16)] * dp)(
         keep_in, got_in, label
     )
-    pieces = [pieces[0]] + [swap(pieces[k], k) for k in DISTANCES]
     own = call(copy_kernel, "own_in", rows(slab, BF16))(pieces[0])
     other = [lax.ppermute(own, "tensor", core)]
-    out = call(round_kernel, "round_out", rows(wide, BF16), after=other)(keep, got)
+    keep, send = call(
+        pair_out_kernel, "pair_out", (rows(wide, F32), rows(wide, BF16)), after=other
+    )(*split[:experts], *got)
+    got = lax.ppermute(send, "tensor", across)
+    pieces = [pieces[0]] + [swap(pieces[k], k) for k in DISTANCES]
+    out = call(round_kernel, "round_out", rows(wide, BF16))(keep, got)
     outs = [swap(out, k) for k in LATEST]
     mine = call(stack_kernel, "stack_in", [rows(3 * slab // 2, BF16)] * 2)(*pieces[1:])
     other += [lax.ppermute(x, "tensor", core) for x in mine]
-    masked, divisor = call(
-        mask_kernel,
-        "mask_in",
-        (
-            jax.ShapeDtypeStruct((experts, dp * cap, dp * 128), BF16),
-            jax.ShapeDtypeStruct((experts, 8, 128), F32),
-        ),
-        [smem] + [vmem] * (3 + dp),
-    )(expert_counts, *other, *pieces)
+    masked = jax.ShapeDtypeStruct((experts, dp * cap // 2, dp * 128), BF16)
+    masked_own, divisor = call(
+        mask_own_kernel,
+        "mask_own",
+        (masked, jax.ShapeDtypeStruct((experts, 8, 128), F32)),
+        [smem] + [vmem] * dp,
+    )(expert_counts, *pieces)
+    masked_other = call(mask_other_kernel, "mask_other", masked, after=[divisor])(*other, *pieces)
     result = jax.ShapeDtypeStruct((experts, 128, 128), F32)
     return call(
         blocks_kernel,
@@ -368,7 +375,7 @@
         result,
         scratch=[pltpu.VMEM(result.shape, F32), pltpu.SemaphoreType.DMA((experts,))],
         out_specs=hbm,
-    )(divisor, masked, out, *outs)
+    )(divisor, masked_own, masked_other, out, *outs)
 
 
 EX_DEV = 1

time: 34.5 us -> 34.2 us (level)
  waiting for transfers between devices: 8.2 us -> 7.61 us
    ppermute x2, waiting for transfers between devices: 0.91 us -> 0.01 us  [fast(): other += [lax.ppermute(x, 'tensor', core) for x in mine]]
    ppermute x6, waiting for transfers between devices: 5.5 us -> 5.88 us  [swap(): return lax.ppermute(x, 'dp', [(d, d ^ k) for d in range(dp)])]
    pallas_call x13 -> x14, Pallas kernels: 11.1 us -> 11.3 us  [run(): pl.pallas_call(body, out_shape=out_shape, in_specs=(specs or [vmem] * len...]
  transfers between devices with their start and end apart: 14 -> 14, of which waited for: 8 -> 6; matrix products, arithmetic and copies ran while one was open for 0% -> 0% of each run, Pallas kernels for 20% -> 20%
where the time goes in v14:
time: 34.2 us; the launch traced here: 34 us
  starting transfers between devices  15 us (44%)
  Pallas kernels  11.3 us (33%)
  waiting for transfers between devices  7.61 us (22%)
    pallas_call x14, Pallas kernels, run(): pl.pallas_call(body, out_shape=out_shape, in_specs=(specs or [vmem] * len...  11.3 us
    ppermute x6, starting transfers between devices, swap(): return lax.ppermute(x, 'dp', [(d, d ^ k) for d in range(dp)])  8.62 us
    ppermute x6, waiting for transfers between devices, swap(): return lax.ppermute(x, 'dp', [(d, d ^ k) for d in range(dp)])  5.88 us
    ppermute x1, starting transfers between devices, fast(): got_in = lax.ppermute(send_in, 'tensor', across)  2.92 us
    ppermute x1, starting transfers between devices, fast(): got = lax.ppermute(send, 'tensor', across)  1.61 us
    ppermute x2, waiting for transfers between devices, fast(): got = [lax.ppermute(x, 'tensor', core) for x in split[experts:]]  0.99 us
  transfers between devices with their start and end apart: 14, of which 6 were waited for; matrix products, arithmetic and copies ran while one was open for 0% of the time, Pallas kernels for 20%

profile of v14, /device:TPU:0, one launch (start us, length us, event | category | flops | bytes accessed | tf_op | source)
XLA Modules:
  0.0 34.0 jit_solution(17034948920377889741)
XLA Ops:
  0.0 3.1 %rotate_in.1 = (f32[2,192,512]{2,1,0:T(8,128)S(1)}, bf16[16,128]{1,0:T(8,128)(2,1)S(1)}, bf16[384,768]{1,0:T(8,128)(2,1)S(1)}, bf16[384,2,1024]{2,1,0:T(2,128)(2,1)S(1)}) custom-call(bf16[384,1536]{1,0:T(8,128)(2,1)} %refs_0_.3, s32[2,384]{1,0:T(2,128)} %bitcast.3, s32[384]{0:T(512)} %refs_2_.2, bf16[2,1536,512]{2,1,0:T(8,128)(2,1)} %refs_3_.1, ...), custom_call_target="tpu_custom_call" | custom-call | flops 1 | bytes 1 | tf_op jit(solution)/shard_map/rotate_in/pallas_call | solution.py:269
  3.1 0.0 slice-start
  3.1 0.0 slice-start.1
  3.1 0.1 split_in.1
  3.2 0.5 %collective-permute-start = (f32[768,128]{1,0:T(8,128)S(1)}, f32[768,128]{1,0:T(8,128)S(1)}, u32[]{:S(2)}, u32[]{:S(2)}) collective-permute-start(f32[768,128]{1,0:T(8,128)S(1)} %get-tuple-element.29), channel_id=1, source_target_pairs={{0,1},{1,0},{2,3},{3,2},{4,5},{5,4},{6,7},{7,6},{8,9},{9,8},{10,11... | collective-permute-start | bytes 1179656 | tf_op jit(solution)/shard_map/ppermute | solution.py:328
  3.7 0.8 %choose.1.refs_2_.refs_3_ = bf16[384,1024]{1,0:T(8,128)(2,1)S(1)} custom-call(bf16[384,2,1024]{2,1,0:T(2,128)(2,1)S(1)} %get-tuple-element.30.refs_0_, bf16[384,768]{1,0:T(8,128)(2,1)S(1)} %get-tuple-element.31.refs_1_), custom_call_target="tpu_custom_call" | custom-call | flops 1 | bytes 1 | tf_op jit(solution)/shard_map/choose/pallas_call | solution.py:269
  4.5 0.6 %collective-permute-done.refs_1_ = f32[768,128]{1,0:T(8,128)S(1)} collective-permute-done((f32[768,128]{1,0:T(8,128)S(1)}, f32[768,128]{1,0:T(8,128)S(1)}, u32[]{:S(2)}, u32[]{:S(2)}) %collective-permute-start) | collective-permute-done | bytes 393248 | tf_op jit(solution)/shard_map/ppermute | solution.py:328
  5.1 0.0 copy-start
  5.1 2.9 %collective-permute-start.1 = (bf16[768,128]{1,0:T(8,128)(2,1)S(1)}, bf16[768,128]{1,0:T(8,128)(2,1)S(1)}, u32[]{:S(2)}, u32[]{:S(2)}) collective-permute-start(bf16[768,128]{1,0:T(8,128)(2,1)S(1)} %get-tuple-element.33.refs_4_), channel_id=1, source_target_pairs={{0,2},{1,3},{2,0},{3,1},{4,6},{5,7},{6,4},{7,5},{8,10},{9,11},{10,... | collective-permute-start | bytes 589832 | tf_op jit(solution)/shard_map/ppermute | solution.py:333
  8.1 0.0 slice-done
  8.1 0.0 slice-done.1
  8.1 4.7 %rotate_out.1.refs_0_ = f32[2,192,512]{2,1,0:T(8,128)S(1)} custom-call(bf16[384,2,4096]{2,1,0:T(2,128)(2,1)} %refs_0_.5, bf16[384,768]{1,0:T(8,128)(2,1)S(1)} %get-tuple-element.31.refs_1_, bf16[2,4096,512]{2,1,0:T(8,128)(2,1)S(1)} %bitcast.2, bf16[384,1024]{1,0:T(8,128)(2,1)S(1)} %choose.1.refs_2_.refs_3_, bf16[768,128]{1,0:T(8,128)(2,1)S(1)} %get-tuple-element.33.refs_4_), custom_call_target="tpu_custom_call" | custom-call | flops 1 | bytes 1 | tf_op jit(solution)/shard_map/rotate_out/pallas_call | solution.py:269
  12.8 0.1 split_out.1
  12.9 0.1 collective-permute-start.8
  13.0 0.5 %collective-permute-start.9 = (f32[384,128]{1,0:T(8,128)S(1)}, f32[384,128]{1,0:T(8,128)S(1)}, u32[]{:S(2)}, u32[]{:S(2)}) collective-permute-start(f32[384,128]{1,0:T(8,128)S(1)} %get-tuple-element.46), channel_id=1, source_target_pairs={{0,1},{1,0},{2,3},{3,2},{4,5},{5,4},{6,7},{7,6},{8,9},{9,8},{10,11... | collective-permute-start | bytes 589832 | tf_op jit(solution)/shard_map/ppermute | solution.py:347
  13.5 0.0 collective-permute-done.1.refs_1_
  13.5 0.1 round_in.1
  13.5 0.1 collective-permute-start.5
  13.7 0.7 %collective-permute-done.8.refs_2_ = f32[384,128]{1,0:T(8,128)S(1)} collective-permute-done((f32[384,128]{1,0:T(8,128)S(1)}, f32[384,128]{1,0:T(8,128)S(1)}, u32[]{:S(2)}, u32[]{:S(2)}) %collective-permute-start.8) | collective-permute-done | bytes 196640 | tf_op jit(solution)/shard_map/ppermute | solution.py:347
  14.4 0.3 collective-permute-done.9.refs_3_
  14.7 0.2 collective-permute-done.5.refs_0_.refs_4_
  14.9 1.6 %collective-permute-start.10 = (bf16[384,128]{1,0:T(8,128)(2,1)S(1)}, bf16[384,128]{1,0:T(8,128)(2,1)S(1)}, u32[]{:S(2)}, u32[]{:S(2)}) collective-permute-start(bf16[384,128]{1,0:T(8,128)(2,1)S(1)} %get-tuple-element.48), channel_id=1, source_target_pairs={{0,2},{1,3},{2,0},{3,1},{4,6},{5,7},{6,4},{7,5},{8,10},{9,11},{10,... | collective-permute-start | bytes 294920 | tf_op jit(solution)/shard_map/ppermute | solution.py:357
  16.5 1.6 %collective-permute-start.2 = (bf16[208,128]{1,0:T(8,128)(2,1)S(1)}, bf16[208,128]{1,0:T(8,128)(2,1)S(1)}, u32[]{:S(2)}, u32[]{:S(2)}) collective-permute-start(bf16[208,128]{1,0:T(8,128)(2,1)S(1)} %get-tuple-element.36), channel_id=1, source_target_pairs={{0,4},{4,0},{8,12},{12,8},{1,5},{5,1},{9,13},{13,9},{2,6},{6,2},{1... | collective-permute-start | bytes 159752 | tf_op jit(solution)/shard_map/ppermute | solution.py:304
  18.1 2.6 %collective-permute-start.3 = (bf16[208,128]{1,0:T(8,128)(2,1)S(1)}, bf16[208,128]{1,0:T(8,128)(2,1)S(1)}, u32[]{:S(2)}, u32[]{:S(2)}) collective-permute-start(bf16[208,128]{1,0:T(8,128)(2,1)S(1)} %get-tuple-element.37), channel_id=1, source_target_pairs={{0,8},{4,12},{8,0},{12,4},{1,9},{5,13},{9,1},{13,5},{2,10},{6,14},... | collective-permute-start | bytes 159752 | tf_op jit(solution)/shard_map/ppermute | solution.py:304
  20.6 0.2 collective-permute-start.4
  20.9 0.0 collective-permute-done.10.refs_1_
  20.9 1.7 %collective-permute-start.13 = (bf16[384,128]{1,0:T(8,128)(2,1)S(1)}, bf16[384,128]{1,0:T(8,128)(2,1)S(1)}, u32[]{:S(2)}, u32[]{:S(2)}) collective-permute-start(bf16[384,128]{1,0:T(8,128)(2,1)S(1)} %round_out.1.refs_3_), channel_id=1, source_target_pairs={{0,8},{4,12},{8,0},{12,4},{1,9},{5,13},{9,1},{13,5},{2,10},{6,14},... | collective-permute-start | bytes 294920 | tf_op jit(solution)/shard_map/ppermute | solution.py:304
  22.6 2.0 %collective-permute-start.12 = (bf16[384,128]{1,0:T(8,128)(2,1)S(1)}, bf16[384,128]{1,0:T(8,128)(2,1)S(1)}, u32[]{:S(2)}, u32[]{:S(2)}) collective-permute-start(bf16[384,128]{1,0:T(8,128)(2,1)S(1)} %round_out.1.refs_3_), channel_id=1, source_target_pairs={{0,12},{4,8},{8,4},{12,0},{1,13},{5,9},{9,5},{13,1},{2,14},{6,10},... | collective-permute-start | bytes 294920 | tf_op jit(solution)/shard_map/ppermute | solution.py:304
  24.6 0.0 collective-permute-done.2.refs_2_.refs_0_.refs_4_
  24.6 0.5 %collective-permute-start.11 = (bf16[384,128]{1,0:T(8,128)(2,1)S(1)}, bf16[384,128]{1,0:T(8,128)(2,1)S(1)}, u32[]{:S(2)}, u32[]{:S(2)}) collective-permute-start(bf16[384,128]{1,0:T(8,128)(2,1)S(1)} %round_out.1.refs_3_), channel_id=1, source_target_pairs={{0,4},{4,0},{8,12},{12,8},{1,5},{5,1},{9,13},{13,9},{2,6},{6,2},{1... | collective-permute-start | bytes 294920 | tf_op jit(solution)/shard_map/ppermute | solution.py:304
  25.1 0.0 collective-permute-done.3.refs_3_.refs_1_.refs_5_
  25.1 2.2 %collective-permute-done.4.refs_4_.refs_2_.refs_6_ = bf16[208,128]{1,0:T(8,128)(2,1)S(1)} collective-permute-done((bf16[208,128]{1,0:T(8,128)(2,1)S(1)}, bf16[208,128]{1,0:T(8,128)(2,1)S(1)}, u32[]{:S(2)}, u32[]{:S(2)}) %collective-permute-start.4) | collective-permute-done | bytes 53280 | tf_op jit(solution)/shard_map/ppermute | solution.py:304
  27.4 0.1 collective-permute-start.6
  27.5 0.5 %collective-permute-start.7 = (bf16[288,128]{1,0:T(8,128)(2,1)S(1)}, bf16[288,128]{1,0:T(8,128)(2,1)S(1)}, u32[]{:S(2)}, u32[]{:S(2)}) collective-permute-start(bf16[288,128]{1,0:T(8,128)(2,1)S(1)} %get-tuple-element.42), channel_id=1, source_target_pairs={{0,1},{1,0},{2,3},{3,2},{4,5},{5,4},{6,7},{7,6},{8,9},{9,8},{10,11... | collective-permute-start | bytes 221192 | tf_op jit(solution)/shard_map/ppermute | solution.py:362
  28.0 0.0 copy-done
  28.0 0.9 %mask_own.1 = (bf16[2,384,512]{2,1,0:T(8,128)(2,1)S(1)}, f32[2,8,128]{2,1,0:T(8,128)S(1)}) custom-call(s32[2]{0:T(128)S(1)} %copy-done, bf16[208,128]{1,0:T(8,128)(2,1)S(1)} %get-tuple-element.35.refs_1_.refs_0_.refs_3_, bf16[208,128]{1,0:T(8,128)(2,1)S(1)} %collective-permute-done.2.refs_2_.refs_0_.refs_4_, ...), custom_call_target="tpu_custom_call" | custom-call | flops 1 | bytes 1 | tf_op jit(solution)/shard_map/mask_own/pallas_call | solution.py:269
  28.9 0.0 collective-permute-done.6.refs_1_
  28.9 0.0 collective-permute-done.7.refs_2_
  28.9 0.3 %mask_other.1.refs_2_ = bf16[2,384,512]{2,1,0:T(8,128)(2,1)S(1)} custom-call(bf16[192,128]{1,0:T(8,128)(2,1)S(1)} %collective-permute-done.5.refs_0_.refs_4_, bf16[288,128]{1,0:T(8,128)(2,1)S(1)} %collective-permute-done.6.refs_1_, bf16[288,128]{1,0:T(8,128)(2,1)S(1)} %collective-permute-done.7.refs_2_, ...), custom_call_target="tpu_custom_call" | custom-call | flops 1 | bytes 1 | tf_op jit(solution)/shard_map/mask_other/pallas_call | solution.py:269
  29.2 3.6 %collective-permute-done.13.refs_6_ = bf16[384,128]{1,0:T(8,128)(2,1)S(1)} collective-permute-done((bf16[384,128]{1,0:T(8,128)(2,1)S(1)}, bf16[384,128]{1,0:T(8,128)(2,1)S(1)}, u32[]{:S(2)}, u32[]{:S(2)}) %collective-permute-start.13) | collective-permute-done | bytes 98336 | tf_op jit(solution)/shard_map/ppermute | solution.py:304
  32.9 0.0 collective-permute-done.12.refs_5_
  32.9 0.0 collective-permute-done.11.refs_4_
  32.9 1.1 %blocks.1 = f32[2,128,128]{2,1,0:T(8,128)} custom-call(f32[2,8,128]{2,1,0:T(8,128)S(1)} %get-tuple-element.39.refs_7_.refs_0_, bf16[2,384,512]{2,1,0:T(8,128)(2,1)S(1)} %get-tuple-element.40.refs_1_, bf16[2,384,512]{2,1,0:T(8,128)(2,1)S(1)} %mask_other.1.refs_2_, bf16[384,128]{1,0:T(8,128)(2,1)S(1)} %round_out.1.refs_3_, ...), custom_call_target="tpu_custom_call" | custom-call | flops 1 | bytes 1 | tf_op jit(solution)/shard_map/blocks/pallas_call | solution.py:269
  (6 shorter events, 0.1 us)
Async XLA Ops:
  3.1 5.0 %slice-start = ((s8[8388608]{0:T(1024)(128)(4,1)}), s8[4194304]{0:T(1024)(128)(4,1)S(1)}, s32[]{:S(2)}) async-start(s8[8388608]{0:T(1024)(128)(4,1)} %bitcast.1), calls=%async_computation | async-start | bytes 8388608
  3.1 5.0 %slice-start.1 = ((s8[8388608]{0:T(1024)(128)(4,1)}), s8[4194304]{0:T(1024)(128)(4,1)S(1)}, s32[]{:S(2)}) async-start(s8[8388608]{0:T(1024)(128)(4,1)} %bitcast.1), calls=%async_computation.1 | async-start | bytes 8388608
  3.2 1.9 %collective-permute-start = (f32[768,128]{1,0:T(8,128)S(1)}, f32[768,128]{1,0:T(8,128)S(1)}, u32[]{:S(2)}, u32[]{:S(2)}) collective-permute-start(f32[768,128]{1,0:T(8,128)S(1)} %get-tuple-element.29), channel_id=1, source_target_pairs={{0,1},{1,0},{2,3},{3,2},{4,5},{5,4},{6,7},{7,6},{8,9},{9,8},{10,11... | collective-permute-start | bytes 1179656 | tf_op jit(solution)/shard_map/ppermute | solution.py:328
  5.1 22.8 %copy-start = (s32[2]{0:T(128)S(1)}, s32[2]{0:T(128)}, u32[]{:S(2)}) copy-start(s32[2]{0:T(128)} %refs_0_.4) | copy-start | bytes 28
  5.1 8.3 %collective-permute-start.1 = (bf16[768,128]{1,0:T(8,128)(2,1)S(1)}, bf16[768,128]{1,0:T(8,128)(2,1)S(1)}, u32[]{:S(2)}, u32[]{:S(2)}) collective-permute-start(bf16[768,128]{1,0:T(8,128)(2,1)S(1)} %get-tuple-element.33.refs_4_), channel_id=1, source_target_pairs={{0,2},{1,3},{2,0},{3,1},{4,6},{5,7},{6,4},{7,5},{8,10},{9,11},{10,... | collective-permute-start | bytes 589832 | tf_op jit(solution)/shard_map/ppermute | solution.py:333
  12.9 1.5 %collective-permute-start.8 = (f32[384,128]{1,0:T(8,128)S(1)}, f32[384,128]{1,0:T(8,128)S(1)}, u32[]{:S(2)}, u32[]{:S(2)}) collective-permute-start(f32[384,128]{1,0:T(8,128)S(1)} %get-tuple-element.45), channel_id=1, source_target_pairs={{0,1},{1,0},{2,3},{3,2},{4,5},{5,4},{6,7},{7,6},{8,9},{9,8},{10,11... | collective-permute-start | bytes 589832 | tf_op jit(solution)/shard_map/ppermute | solution.py:347
  13.0 1.7 %collective-permute-start.9 = (f32[384,128]{1,0:T(8,128)S(1)}, f32[384,128]{1,0:T(8,128)S(1)}, u32[]{:S(2)}, u32[]{:S(2)}) collective-permute-start(f32[384,128]{1,0:T(8,128)S(1)} %get-tuple-element.46), channel_id=1, source_target_pairs={{0,1},{1,0},{2,3},{3,2},{4,5},{5,4},{6,7},{7,6},{8,9},{9,8},{10,11... | collective-permute-start | bytes 589832 | tf_op jit(solution)/shard_map/ppermute | solution.py:347
  13.5 1.3 %collective-permute-start.5 = (bf16[192,128]{1,0:T(8,128)(2,1)S(1)}, bf16[192,128]{1,0:T(8,128)(2,1)S(1)}, u32[]{:S(2)}, u32[]{:S(2)}) collective-permute-start(bf16[192,128]{1,0:T(8,128)(2,1)S(1)} %own_in.1), channel_id=1, source_target_pairs={{0,1},{1,0},{2,3},{3,2},{4,5},{5,4},{6,7},{7,6},{8,9},{9,8},{10,11... | collective-permute-start | bytes 147464 | tf_op jit(solution)/shard_map/ppermute | solution.py:353
  14.9 6.0 %collective-permute-start.10 = (bf16[384,128]{1,0:T(8,128)(2,1)S(1)}, bf16[384,128]{1,0:T(8,128)(2,1)S(1)}, u32[]{:S(2)}, u32[]{:S(2)}) collective-permute-start(bf16[384,128]{1,0:T(8,128)(2,1)S(1)} %get-tuple-element.48), channel_id=1, source_target_pairs={{0,2},{1,3},{2,0},{3,1},{4,6},{5,7},{6,4},{7,5},{8,10},{9,11},{10,... | collective-permute-start | bytes 294920 | tf_op jit(solution)/shard_map/ppermute | solution.py:357
  16.5 8.2 %collective-permute-start.2 = (bf16[208,128]{1,0:T(8,128)(2,1)S(1)}, bf16[208,128]{1,0:T(8,128)(2,1)S(1)}, u32[]{:S(2)}, u32[]{:S(2)}) collective-permute-start(bf16[208,128]{1,0:T(8,128)(2,1)S(1)} %get-tuple-element.36), channel_id=1, source_target_pairs={{0,4},{4,0},{8,12},{12,8},{1,5},{5,1},{9,13},{13,9},{2,6},{6,2},{1... | collective-permute-start | bytes 159752 | tf_op jit(solution)/shard_map/ppermute | solution.py:304
  18.1 7.1 %collective-permute-start.3 = (bf16[208,128]{1,0:T(8,128)(2,1)S(1)}, bf16[208,128]{1,0:T(8,128)(2,1)S(1)}, u32[]{:S(2)}, u32[]{:S(2)}) collective-permute-start(bf16[208,128]{1,0:T(8,128)(2,1)S(1)} %get-tuple-element.37), channel_id=1, source_target_pairs={{0,8},{4,12},{8,0},{12,4},{1,9},{5,13},{9,1},{13,5},{2,10},{6,14},... | collective-permute-start | bytes 159752 | tf_op jit(solution)/shard_map/ppermute | solution.py:304
  20.6 6.7 %collective-permute-start.4 = (bf16[208,128]{1,0:T(8,128)(2,1)S(1)}, bf16[208,128]{1,0:T(8,128)(2,1)S(1)}, u32[]{:S(2)}, u32[]{:S(2)}) collective-permute-start(bf16[208,128]{1,0:T(8,128)(2,1)S(1)} %get-tuple-element.38), channel_id=1, source_target_pairs={{0,12},{4,8},{8,4},{12,0},{1,13},{5,9},{9,5},{13,1},{2,14},{6,10},... | collective-permute-start | bytes 159752 | tf_op jit(solution)/shard_map/ppermute | solution.py:304
  20.9 12.0 %collective-permute-start.13 = (bf16[384,128]{1,0:T(8,128)(2,1)S(1)}, bf16[384,128]{1,0:T(8,128)(2,1)S(1)}, u32[]{:S(2)}, u32[]{:S(2)}) collective-permute-start(bf16[384,128]{1,0:T(8,128)(2,1)S(1)} %round_out.1.refs_3_), channel_id=1, source_target_pairs={{0,8},{4,12},{8,0},{12,4},{1,9},{5,13},{9,1},{13,5},{2,10},{6,14},... | collective-permute-start | bytes 294920 | tf_op jit(solution)/shard_map/ppermute | solution.py:304
  22.6 10.2 %collective-permute-start.12 = (bf16[384,128]{1,0:T(8,128)(2,1)S(1)}, bf16[384,128]{1,0:T(8,128)(2,1)S(1)}, u32[]{:S(2)}, u32[]{:S(2)}) collective-permute-start(bf16[384,128]{1,0:T(8,128)(2,1)S(1)} %round_out.1.refs_3_), channel_id=1, source_target_pairs={{0,12},{4,8},{8,4},{12,0},{1,13},{5,9},{9,5},{13,1},{2,14},{6,10},... | collective-permute-start | bytes 294920 | tf_op jit(solution)/shard_map/ppermute | solution.py:304
  24.6 8.2 %collective-permute-start.11 = (bf16[384,128]{1,0:T(8,128)(2,1)S(1)}, bf16[384,128]{1,0:T(8,128)(2,1)S(1)}, u32[]{:S(2)}, u32[]{:S(2)}) collective-permute-start(bf16[384,128]{1,0:T(8,128)(2,1)S(1)} %round_out.1.refs_3_), channel_id=1, source_target_pairs={{0,4},{4,0},{8,12},{12,8},{1,5},{5,1},{9,13},{13,9},{2,6},{6,2},{1... | collective-permute-start | bytes 294920 | tf_op jit(solution)/shard_map/ppermute | solution.py:304
  27.4 1.5 %collective-permute-start.6 = (bf16[288,128]{1,0:T(8,128)(2,1)S(1)}, bf16[288,128]{1,0:T(8,128)(2,1)S(1)}, u32[]{:S(2)}, u32[]{:S(2)}) collective-permute-start(bf16[288,128]{1,0:T(8,128)(2,1)S(1)} %get-tuple-element.41), channel_id=1, source_target_pairs={{0,1},{1,0},{2,3},{3,2},{4,5},{5,4},{6,7},{7,6},{8,9},{9,8},{10,11... | collective-permute-start | bytes 221192 | tf_op jit(solution)/shard_map/ppermute | solution.py:362
  27.5 1.4 %collective-permute-start.7 = (bf16[288,128]{1,0:T(8,128)(2,1)S(1)}, bf16[288,128]{1,0:T(8,128)(2,1)S(1)}, u32[]{:S(2)}, u32[]{:S(2)}) collective-permute-start(bf16[288,128]{1,0:T(8,128)(2,1)S(1)} %get-tuple-element.42), channel_id=1, source_target_pairs={{0,1},{1,0},{2,3},{3,2},{4,5},{5,4},{6,7},{7,6},{8,9},{9,8},{10,11... | collective-permute-start | bytes 221192 | tf_op jit(solution)/shard_map/ppermute | solution.py:362

commit v15 on v14

--- a/solution.py
+++ b/solution.py
@@ -11,7 +11,7 @@
 BF16 = jnp.bfloat16
 CHUNK = 1024
 VMEM = 20 * 2**20
-EARLY = 1024
+EARLY = 1536
 DISTANCES = (1, 2, 3)
 LATEST = (1, 3, 2)
 LABEL_ROWS = 16
@@ -123,7 +123,7 @@
     experts, cap, _ = acc.shape
     fetch = fetcher(sems)
     done = early.shape[1]
-    cuts = sorted({done, done + CHUNK // 2, *range(done + CHUNK, hidden + 1, CHUNK)})
+    cuts = sorted({done, done + CHUNK // 2, *range(done + CHUNK, hidden, CHUNK), hidden})
     parts = [(at, pl.ds(at, end - at)) for at, end in zip(cuts, cuts[1:])]
     copies = [
         fetch(grads.at[:, :, part], grads_v.at[:, :, pl.ds(at - done, part.size)])
@@ -151,8 +151,10 @@
 
 def pair_in_kernel(kept, got, keep, send):
     total = kept[...] + got[...]
+    outer = total.shape[0]
     keep[...] = total
-    send[...] = total.astype(BF16)
+    send[:outer, :] = total.astype(BF16)
+    send[outer:, :] = jnp.zeros((send.shape[0] - outer, 128), BF16)
 
 
 def round_in_kernel(kept, got, label, *pays):
@@ -328,7 +330,7 @@
     got = lax.ppermute(send, "tensor", core)
     early = call(choose_kernel, "choose", jax.ShapeDtypeStruct((wide, EARLY), BF16))(early, pick)
     keep_in, send_in = call(
-        pair_in_kernel, "pair_in", (rows(half, F32), rows(half, BF16)), after=[early]
+        pair_in_kernel, "pair_in", (rows(half, F32), rows(half + 16, BF16)), after=[early]
     )(keep, got)
     got_in = lax.ppermute(send_in, "tensor", across)
 
@@ -339,24 +341,25 @@
         [hbm, vmem, vmem, vmem],
         [
             pltpu.VMEM((tokens, 2, grads.shape[2] - EARLY), BF16),
-            pltpu.SemaphoreType.DMA((grads.shape[2] // CHUNK,)),
+            pltpu.SemaphoreType.DMA((grads.shape[2] // CHUNK + 1,)),
         ],
         after=[send_in],
     )(pin(grads), pick, basis_out, early)
     split = call(split_out_kernel, "split_out", [rows(2 * cap, F32)] * (2 * experts))(acc)
     got = [lax.ppermute(x, "tensor", core) for x in split[experts:]]
+    keep, send = call(
+        pair_out_kernel, "pair_out", (rows(wide, F32), rows(wide, BF16)), after=[got_in]
+    )(*split[:experts], *got)
+    got = lax.ppermute(send, "tensor", across)
+
     slab = half // dp
     pieces = call(round_in_kernel, "round_in", [rows(slab + LABEL_ROWS, BF16)] * dp)(
         keep_in, got_in, label
     )
     own = call(copy_kernel, "own_in", rows(slab, BF16))(pieces[0])
     other = [lax.ppermute(own, "tensor", core)]
-    keep, send = call(
-        pair_out_kernel, "pair_out", (rows(wide, F32), rows(wide, BF16)), after=other
-    )(*split[:experts], *got)
-    got = lax.ppermute(send, "tensor", across)
     pieces = [pieces[0]] + [swap(pieces[k], k) for k in DISTANCES]
-    out = call(round_kernel, "round_out", rows(wide, BF16))(keep, got)
+    out = call(round_kernel, "round_out", rows(wide, BF16), after=other)(keep, got)
     outs = [swap(out, k) for k in LATEST]
     mine = call(stack_kernel, "stack_in", [rows(3 * slab // 2, BF16)] * 2)(*pieces[1:])
     other += [lax.ppermute(x, "tensor", core) for x in mine]

time: 34.2 us -> 34.1 us (level)
    ppermute x6, waiting for transfers between devices: 5.88 us -> 6.23 us  [swap(): return lax.ppermute(x, 'dp', [(d, d ^ k) for d in range(dp)])]
where the time goes in v15:
time: 34.1 us; the launch traced here: 33.9 us
  starting transfers between devices  14.8 us (43%)
  Pallas kernels  11.2 us (33%)
  waiting for transfers between devices  7.71 us (23%)
    pallas_call x14, Pallas kernels, run(): pl.pallas_call(body, out_shape=out_shape, in_specs=(specs or [vmem] * len...  11.2 us
    ppermute x6, starting transfers between devices, swap(): return lax.ppermute(x, 'dp', [(d, d ^ k) for d in range(dp)])  8.74 us
    ppermute x6, waiting for transfers between devices, swap(): return lax.ppermute(x, 'dp', [(d, d ^ k) for d in range(dp)])  6.23 us
    ppermute x1, starting transfers between devices, fast(): got_in = lax.ppermute(send_in, 'tensor', across)  2.92 us
    ppermute x1, starting transfers between devices, fast(): got = lax.ppermute(send, 'tensor', across)  1.52 us
    ppermute x2, waiting for transfers between devices, fast(): got = [lax.ppermute(x, 'tensor', core) for x in split[experts:]]  1.21 us
  transfers between devices with their start and end apart: 14, of which 6 were waited for; matrix products, arithmetic and copies ran while one was open for 0% of the time, Pallas kernels for 20%

profile of v15, /device:TPU:0, one launch (start us, length us, event | category | flops | bytes accessed | tf_op | source)
XLA Modules:
  0.0 33.9 jit_solution(13788372997462639640)
XLA Ops:
  0.0 3.1 %rotate_in.1 = (f32[2,192,512]{2,1,0:T(8,128)S(1)}, bf16[16,128]{1,0:T(8,128)(2,1)S(1)}, bf16[384,768]{1,0:T(8,128)(2,1)S(1)}, bf16[384,2,1536]{2,1,0:T(2,128)(2,1)S(1)}) custom-call(bf16[384,1536]{1,0:T(8,128)(2,1)} %refs_0_.3, s32[2,384]{1,0:T(2,128)} %bitcast.3, s32[384]{0:T(512)} %refs_2_.2, bf16[2,1536,512]{2,1,0:T(8,128)(2,1)} %refs_3_.1, ...), custom_call_target="tpu_custom_call" | custom-call | flops 1 | bytes 1 | tf_op jit(solution)/shard_map/rotate_in/pallas_call | solution.py:271
  3.1 0.0 slice-start
  3.1 0.0 slice-start.1
  3.1 0.1 split_in.1
  3.2 0.5 %collective-permute-start = (f32[768,128]{1,0:T(8,128)S(1)}, f32[768,128]{1,0:T(8,128)S(1)}, u32[]{:S(2)}, u32[]{:S(2)}) collective-permute-start(f32[768,128]{1,0:T(8,128)S(1)} %get-tuple-element.29), channel_id=1, source_target_pairs={{0,1},{1,0},{2,3},{3,2},{4,5},{5,4},{6,7},{7,6},{8,9},{9,8},{10,11... | collective-permute-start | bytes 1179656 | tf_op jit(solution)/shard_map/ppermute | solution.py:330
  3.7 1.1 %choose.1.refs_2_.refs_3_ = bf16[384,1536]{1,0:T(8,128)(2,1)S(1)} custom-call(bf16[384,2,1536]{2,1,0:T(2,128)(2,1)S(1)} %get-tuple-element.30.refs_0_, bf16[384,768]{1,0:T(8,128)(2,1)S(1)} %get-tuple-element.31.refs_1_), custom_call_target="tpu_custom_call" | custom-call | flops 1 | bytes 1 | tf_op jit(solution)/shard_map/choose/pallas_call | solution.py:271
  4.8 0.3 collective-permute-done.refs_1_
  5.1 0.0 copy-start
  5.1 2.9 %collective-permute-start.1 = (bf16[784,128]{1,0:T(8,128)(2,1)S(1)}, bf16[784,128]{1,0:T(8,128)(2,1)S(1)}, u32[]{:S(2)}, u32[]{:S(2)}) collective-permute-start(bf16[784,128]{1,0:T(8,128)(2,1)S(1)} %get-tuple-element.33.refs_4_), channel_id=1, source_target_pairs={{0,2},{1,3},{2,0},{3,1},{4,6},{5,7},{6,4},{7,5},{8,10},{9,11},{10,... | collective-permute-start | bytes 602120 | tf_op jit(solution)/shard_map/ppermute | solution.py:335
  8.1 0.0 slice-done
  8.1 0.0 slice-done.1
  8.1 4.3 %rotate_out.1.refs_0_ = f32[2,192,512]{2,1,0:T(8,128)S(1)} custom-call(bf16[384,2,4096]{2,1,0:T(2,128)(2,1)} %refs_0_.5, bf16[384,768]{1,0:T(8,128)(2,1)S(1)} %get-tuple-element.31.refs_1_, bf16[2,4096,512]{2,1,0:T(8,128)(2,1)S(1)} %bitcast.2, bf16[384,1536]{1,0:T(8,128)(2,1)S(1)} %choose.1.refs_2_.refs_3_, bf16[784,128]{1,0:T(8,128)(2,1)S(1)} %get-tuple-element.33.refs_4_), custom_call_target="tpu_custom_call" | custom-call | flops 1 | bytes 1 | tf_op jit(solution)/shard_map/rotate_out/pallas_call | solution.py:271
  12.4 0.1 split_out.1
  12.5 0.1 collective-permute-start.8
  12.6 0.5 %collective-permute-start.9 = (f32[384,128]{1,0:T(8,128)S(1)}, f32[384,128]{1,0:T(8,128)S(1)}, u32[]{:S(2)}, u32[]{:S(2)}) collective-permute-start(f32[384,128]{1,0:T(8,128)S(1)} %get-tuple-element.46), channel_id=1, source_target_pairs={{0,1},{1,0},{2,3},{3,2},{4,5},{5,4},{6,7},{7,6},{8,9},{9,8},{10,11... | collective-permute-start | bytes 589832 | tf_op jit(solution)/shard_map/ppermute | solution.py:349
  13.1 0.9 %collective-permute-done.8.refs_2_ = f32[384,128]{1,0:T(8,128)S(1)} collective-permute-done((f32[384,128]{1,0:T(8,128)S(1)}, f32[384,128]{1,0:T(8,128)S(1)}, u32[]{:S(2)}, u32[]{:S(2)}) %collective-permute-start.8) | collective-permute-done | bytes 196640 | tf_op jit(solution)/shard_map/ppermute | solution.py:349
  14.0 0.3 collective-permute-done.9.refs_3_
  14.3 0.0 collective-permute-done.1.refs_1_.refs_4_
  14.3 1.5 %collective-permute-start.10 = (bf16[384,128]{1,0:T(8,128)(2,1)S(1)}, bf16[384,128]{1,0:T(8,128)(2,1)S(1)}, u32[]{:S(2)}, u32[]{:S(2)}) collective-permute-start(bf16[384,128]{1,0:T(8,128)(2,1)S(1)} %get-tuple-element.48), channel_id=1, source_target_pairs={{0,2},{1,3},{2,0},{3,1},{4,6},{5,7},{6,4},{7,5},{8,10},{9,11},{10,... | collective-permute-start | bytes 294920 | tf_op jit(solution)/shard_map/ppermute | solution.py:353
  15.8 0.1 round_in.1
  15.9 1.6 %collective-permute-start.2 = (bf16[208,128]{1,0:T(8,128)(2,1)S(1)}, bf16[208,128]{1,0:T(8,128)(2,1)S(1)}, u32[]{:S(2)}, u32[]{:S(2)}) collective-permute-start(bf16[208,128]{1,0:T(8,128)(2,1)S(1)} %get-tuple-element.36), channel_id=1, source_target_pairs={{0,4},{4,0},{8,12},{12,8},{1,5},{5,1},{9,13},{13,9},{2,6},{6,2},{1... | collective-permute-start | bytes 159752 | tf_op jit(solution)/shard_map/ppermute | solution.py:306
  17.5 0.0 collective-permute-start.5
  17.5 2.7 %collective-permute-start.3 = (bf16[208,128]{1,0:T(8,128)(2,1)S(1)}, bf16[208,128]{1,0:T(8,128)(2,1)S(1)}, u32[]{:S(2)}, u32[]{:S(2)}) collective-permute-start(bf16[208,128]{1,0:T(8,128)(2,1)S(1)} %get-tuple-element.37), channel_id=1, source_target_pairs={{0,8},{4,12},{8,0},{12,4},{1,9},{5,13},{9,1},{13,5},{2,10},{6,14},... | collective-permute-start | bytes 159752 | tf_op jit(solution)/shard_map/ppermute | solution.py:306
  20.2 0.2 collective-permute-start.4
  20.4 0.0 collective-permute-done.5.refs_0_.refs_2_
  20.4 0.0 collective-permute-done.10.refs_1_
  20.4 1.7 %collective-permute-start.13 = (bf16[384,128]{1,0:T(8,128)(2,1)S(1)}, bf16[384,128]{1,0:T(8,128)(2,1)S(1)}, u32[]{:S(2)}, u32[]{:S(2)}) collective-permute-start(bf16[384,128]{1,0:T(8,128)(2,1)S(1)} %round_out.1.refs_3_), channel_id=1, source_target_pairs={{0,8},{4,12},{8,0},{12,4},{1,9},{5,13},{9,1},{13,5},{2,10},{6,14},... | collective-permute-start | bytes 294920 | tf_op jit(solution)/shard_map/ppermute | solution.py:306
  22.2 2.0 %collective-permute-start.12 = (bf16[384,128]{1,0:T(8,128)(2,1)S(1)}, bf16[384,128]{1,0:T(8,128)(2,1)S(1)}, u32[]{:S(2)}, u32[]{:S(2)}) collective-permute-start(bf16[384,128]{1,0:T(8,128)(2,1)S(1)} %round_out.1.refs_3_), channel_id=1, source_target_pairs={{0,12},{4,8},{8,4},{12,0},{1,13},{5,9},{9,5},{13,1},{2,14},{6,10},... | collective-permute-start | bytes 294920 | tf_op jit(solution)/shard_map/ppermute | solution.py:306
  24.2 0.0 collective-permute-done.2.refs_2_.refs_0_.refs_4_
  24.2 0.5 %collective-permute-start.11 = (bf16[384,128]{1,0:T(8,128)(2,1)S(1)}, bf16[384,128]{1,0:T(8,128)(2,1)S(1)}, u32[]{:S(2)}, u32[]{:S(2)}) collective-permute-start(bf16[384,128]{1,0:T(8,128)(2,1)S(1)} %round_out.1.refs_3_), channel_id=1, source_target_pairs={{0,4},{4,0},{8,12},{12,8},{1,5},{5,1},{9,13},{13,9},{2,6},{6,2},{1... | collective-permute-start | bytes 294920 | tf_op jit(solution)/shard_map/ppermute | solution.py:306
  24.7 0.0 collective-permute-done.3.refs_3_.refs_1_.refs_5_
  24.7 2.1 %collective-permute-done.4.refs_4_.refs_2_.refs_6_ = bf16[208,128]{1,0:T(8,128)(2,1)S(1)} collective-permute-done((bf16[208,128]{1,0:T(8,128)(2,1)S(1)}, bf16[208,128]{1,0:T(8,128)(2,1)S(1)}, u32[]{:S(2)}, u32[]{:S(2)}) %collective-permute-start.4) | collective-permute-done | bytes 53280 | tf_op jit(solution)/shard_map/ppermute | solution.py:306
  26.8 0.1 collective-permute-start.6
  26.9 0.5 %collective-permute-start.7 = (bf16[288,128]{1,0:T(8,128)(2,1)S(1)}, bf16[288,128]{1,0:T(8,128)(2,1)S(1)}, u32[]{:S(2)}, u32[]{:S(2)}) collective-permute-start(bf16[288,128]{1,0:T(8,128)(2,1)S(1)} %get-tuple-element.42), channel_id=1, source_target_pairs={{0,1},{1,0},{2,3},{3,2},{4,5},{5,4},{6,7},{7,6},{8,9},{9,8},{10,11... | collective-permute-start | bytes 221192 | tf_op jit(solution)/shard_map/ppermute | solution.py:365
  27.4 0.0 copy-done
  27.4 0.9 %mask_own.1 = (bf16[2,384,512]{2,1,0:T(8,128)(2,1)S(1)}, f32[2,8,128]{2,1,0:T(8,128)S(1)}) custom-call(s32[2]{0:T(128)S(1)} %copy-done, bf16[208,128]{1,0:T(8,128)(2,1)S(1)} %get-tuple-element.35.refs_1_.refs_0_.refs_3_, bf16[208,128]{1,0:T(8,128)(2,1)S(1)} %collective-permute-done.2.refs_2_.refs_0_.refs_4_, ...), custom_call_target="tpu_custom_call" | custom-call | flops 1 | bytes 1 | tf_op jit(solution)/shard_map/mask_own/pallas_call | solution.py:271
  28.2 0.0 collective-permute-done.6.refs_1_
  28.3 0.0 collective-permute-done.7.refs_2_
  28.3 0.3 %mask_other.1.refs_2_ = bf16[2,384,512]{2,1,0:T(8,128)(2,1)S(1)} custom-call(bf16[192,128]{1,0:T(8,128)(2,1)S(1)} %collective-permute-done.5.refs_0_.refs_2_, bf16[288,128]{1,0:T(8,128)(2,1)S(1)} %collective-permute-done.6.refs_1_, bf16[288,128]{1,0:T(8,128)(2,1)S(1)} %collective-permute-done.7.refs_2_, ...), custom_call_target="tpu_custom_call" | custom-call | flops 1 | bytes 1 | tf_op jit(solution)/shard_map/mask_other/pallas_call | solution.py:271
  28.6 3.9 %collective-permute-done.13.refs_6_ = bf16[384,128]{1,0:T(8,128)(2,1)S(1)} collective-permute-done((bf16[384,128]{1,0:T(8,128)(2,1)S(1)}, bf16[384,128]{1,0:T(8,128)(2,1)S(1)}, u32[]{:S(2)}, u32[]{:S(2)}) %collective-permute-start.13) | collective-permute-done | bytes 98336 | tf_op jit(solution)/shard_map/ppermute | solution.py:306
  32.6 0.0 collective-permute-done.12.refs_5_
  32.6 0.2 collective-permute-done.11.refs_4_
  32.8 1.1 %blocks.1 = f32[2,128,128]{2,1,0:T(8,128)} custom-call(f32[2,8,128]{2,1,0:T(8,128)S(1)} %get-tuple-element.39.refs_7_.refs_0_, bf16[2,384,512]{2,1,0:T(8,128)(2,1)S(1)} %get-tuple-element.40.refs_1_, bf16[2,384,512]{2,1,0:T(8,128)(2,1)S(1)} %mask_other.1.refs_2_, bf16[384,128]{1,0:T(8,128)(2,1)S(1)} %round_out.1.refs_3_, ...), custom_call_target="tpu_custom_call" | custom-call | flops 1 | bytes 1 | tf_op jit(solution)/shard_map/blocks/pallas_call | solution.py:271
  (6 shorter events, 0.1 us)
Async XLA Ops:
  3.1 5.0 %slice-start = ((s8[8388608]{0:T(1024)(128)(4,1)}), s8[4194304]{0:T(1024)(128)(4,1)S(1)}, s32[]{:S(2)}) async-start(s8[8388608]{0:T(1024)(128)(4,1)} %bitcast.1), calls=%async_computation | async-start | bytes 8388608
  3.1 5.0 %slice-start.1 = ((s8[8388608]{0:T(1024)(128)(4,1)}), s8[4194304]{0:T(1024)(128)(4,1)S(1)}, s32[]{:S(2)}) async-start(s8[8388608]{0:T(1024)(128)(4,1)} %bitcast.1), calls=%async_computation.1 | async-start | bytes 8388608
  3.2 1.9 %collective-permute-start = (f32[768,128]{1,0:T(8,128)S(1)}, f32[768,128]{1,0:T(8,128)S(1)}, u32[]{:S(2)}, u32[]{:S(2)}) collective-permute-start(f32[768,128]{1,0:T(8,128)S(1)} %get-tuple-element.29), channel_id=1, source_target_pairs={{0,1},{1,0},{2,3},{3,2},{4,5},{5,4},{6,7},{7,6},{8,9},{9,8},{10,11... | collective-permute-start | bytes 1179656 | tf_op jit(solution)/shard_map/ppermute | solution.py:330
  5.1 22.2 %copy-start = (s32[2]{0:T(128)S(1)}, s32[2]{0:T(128)}, u32[]{:S(2)}) copy-start(s32[2]{0:T(128)} %refs_0_.4) | copy-start | bytes 28
  5.1 9.1 %collective-permute-start.1 = (bf16[784,128]{1,0:T(8,128)(2,1)S(1)}, bf16[784,128]{1,0:T(8,128)(2,1)S(1)}, u32[]{:S(2)}, u32[]{:S(2)}) collective-permute-start(bf16[784,128]{1,0:T(8,128)(2,1)S(1)} %get-tuple-element.33.refs_4_), channel_id=1, source_target_pairs={{0,2},{1,3},{2,0},{3,1},{4,6},{5,7},{6,4},{7,5},{8,10},{9,11},{10,... | collective-permute-start | bytes 602120 | tf_op jit(solution)/shard_map/ppermute | solution.py:335
  12.5 1.5 %collective-permute-start.8 = (f32[384,128]{1,0:T(8,128)S(1)}, f32[384,128]{1,0:T(8,128)S(1)}, u32[]{:S(2)}, u32[]{:S(2)}) collective-permute-start(f32[384,128]{1,0:T(8,128)S(1)} %get-tuple-element.45), channel_id=1, source_target_pairs={{0,1},{1,0},{2,3},{3,2},{4,5},{5,4},{6,7},{7,6},{8,9},{9,8},{10,11... | collective-permute-start | bytes 589832 | tf_op jit(solution)/shard_map/ppermute | solution.py:349
  12.6 1.7 %collective-permute-start.9 = (f32[384,128]{1,0:T(8,128)S(1)}, f32[384,128]{1,0:T(8,128)S(1)}, u32[]{:S(2)}, u32[]{:S(2)}) collective-permute-start(f32[384,128]{1,0:T(8,128)S(1)} %get-tuple-element.46), channel_id=1, source_target_pairs={{0,1},{1,0},{2,3},{3,2},{4,5},{5,4},{6,7},{7,6},{8,9},{9,8},{10,11... | collective-permute-start | bytes 589832 | tf_op jit(solution)/shard_map/ppermute | solution.py:349
  14.3 6.1 %collective-permute-start.10 = (bf16[384,128]{1,0:T(8,128)(2,1)S(1)}, bf16[384,128]{1,0:T(8,128)(2,1)S(1)}, u32[]{:S(2)}, u32[]{:S(2)}) collective-permute-start(bf16[384,128]{1,0:T(8,128)(2,1)S(1)} %get-tuple-element.48), channel_id=1, source_target_pairs={{0,2},{1,3},{2,0},{3,1},{4,6},{5,7},{6,4},{7,5},{8,10},{9,11},{10,... | collective-permute-start | bytes 294920 | tf_op jit(solution)/shard_map/ppermute | solution.py:353
  15.9 8.3 %collective-permute-start.2 = (bf16[208,128]{1,0:T(8,128)(2,1)S(1)}, bf16[208,128]{1,0:T(8,128)(2,1)S(1)}, u32[]{:S(2)}, u32[]{:S(2)}) collective-permute-start(bf16[208,128]{1,0:T(8,128)(2,1)S(1)} %get-tuple-element.36), channel_id=1, source_target_pairs={{0,4},{4,0},{8,12},{12,8},{1,5},{5,1},{9,13},{13,9},{2,6},{6,2},{1... | collective-permute-start | bytes 159752 | tf_op jit(solution)/shard_map/ppermute | solution.py:306
  17.5 2.9 %collective-permute-start.5 = (bf16[192,128]{1,0:T(8,128)(2,1)S(1)}, bf16[192,128]{1,0:T(8,128)(2,1)S(1)}, u32[]{:S(2)}, u32[]{:S(2)}) collective-permute-start(bf16[192,128]{1,0:T(8,128)(2,1)S(1)} %own_in.1), channel_id=1, source_target_pairs={{0,1},{1,0},{2,3},{3,2},{4,5},{5,4},{6,7},{7,6},{8,9},{9,8},{10,11... | collective-permute-start | bytes 147464 | tf_op jit(solution)/shard_map/ppermute | solution.py:360
  17.5 7.2 %collective-permute-start.3 = (bf16[208,128]{1,0:T(8,128)(2,1)S(1)}, bf16[208,128]{1,0:T(8,128)(2,1)S(1)}, u32[]{:S(2)}, u32[]{:S(2)}) collective-permute-start(bf16[208,128]{1,0:T(8,128)(2,1)S(1)} %get-tuple-element.37), channel_id=1, source_target_pairs={{0,8},{4,12},{8,0},{12,4},{1,9},{5,13},{9,1},{13,5},{2,10},{6,14},... | collective-permute-start | bytes 159752 | tf_op jit(solution)/shard_map/ppermute | solution.py:306
  20.2 6.6 %collective-permute-start.4 = (bf16[208,128]{1,0:T(8,128)(2,1)S(1)}, bf16[208,128]{1,0:T(8,128)(2,1)S(1)}, u32[]{:S(2)}, u32[]{:S(2)}) collective-permute-start(bf16[208,128]{1,0:T(8,128)(2,1)S(1)} %get-tuple-element.38), channel_id=1, source_target_pairs={{0,12},{4,8},{8,4},{12,0},{1,13},{5,9},{9,5},{13,1},{2,14},{6,10},... | collective-permute-start | bytes 159752 | tf_op jit(solution)/shard_map/ppermute | solution.py:306
  20.4 12.1 %collective-permute-start.13 = (bf16[384,128]{1,0:T(8,128)(2,1)S(1)}, bf16[384,128]{1,0:T(8,128)(2,1)S(1)}, u32[]{:S(2)}, u32[]{:S(2)}) collective-permute-start(bf16[384,128]{1,0:T(8,128)(2,1)S(1)} %round_out.1.refs_3_), channel_id=1, source_target_pairs={{0,8},{4,12},{8,0},{12,4},{1,9},{5,13},{9,1},{13,5},{2,10},{6,14},... | collective-permute-start | bytes 294920 | tf_op jit(solution)/shard_map/ppermute | solution.py:306
  22.2 10.4 %collective-permute-start.12 = (bf16[384,128]{1,0:T(8,128)(2,1)S(1)}, bf16[384,128]{1,0:T(8,128)(2,1)S(1)}, u32[]{:S(2)}, u32[]{:S(2)}) collective-permute-start(bf16[384,128]{1,0:T(8,128)(2,1)S(1)} %round_out.1.refs_3_), channel_id=1, source_target_pairs={{0,12},{4,8},{8,4},{12,0},{1,13},{5,9},{9,5},{13,1},{2,14},{6,10},... | collective-permute-start | bytes 294920 | tf_op jit(solution)/shard_map/ppermute | solution.py:306
  24.2 8.6 %collective-permute-start.11 = (bf16[384,128]{1,0:T(8,128)(2,1)S(1)}, bf16[384,128]{1,0:T(8,128)(2,1)S(1)}, u32[]{:S(2)}, u32[]{:S(2)}) collective-permute-start(bf16[384,128]{1,0:T(8,128)(2,1)S(1)} %round_out.1.refs_3_), channel_id=1, source_target_pairs={{0,4},{4,0},{8,12},{12,8},{1,5},{5,1},{9,13},{13,9},{2,6},{6,2},{1... | collective-permute-start | bytes 294920 | tf_op jit(solution)/shard_map/ppermute | solution.py:306
  26.8 1.5 %collective-permute-start.6 = (bf16[288,128]{1,0:T(8,128)(2,1)S(1)}, bf16[288,128]{1,0:T(8,128)(2,1)S(1)}, u32[]{:S(2)}, u32[]{:S(2)}) collective-permute-start(bf16[288,128]{1,0:T(8,128)(2,1)S(1)} %get-tuple-element.41), channel_id=1, source_target_pairs={{0,1},{1,0},{2,3},{3,2},{4,5},{5,4},{6,7},{7,6},{8,9},{9,8},{10,11... | collective-permute-start | bytes 221192 | tf_op jit(solution)/shard_map/ppermute | solution.py:365
  26.9 1.4 %collective-permute-start.7 = (bf16[288,128]{1,0:T(8,128)(2,1)S(1)}, bf16[288,128]{1,0:T(8,128)(2,1)S(1)}, u32[]{:S(2)}, u32[]{:S(2)}) collective-permute-start(bf16[288,128]{1,0:T(8,128)(2,1)S(1)} %get-tuple-element.42), channel_id=1, source_target_pairs={{0,1},{1,0},{2,3},{3,2},{4,5},{5,4},{6,7},{7,6},{8,9},{9,8},{10,11... | collective-permute-start | bytes 221192 | tf_op jit(solution)/shard_map/ppermute | solution.py:365

commit v16 on v15

--- a/solution.py
+++ b/solution.py
@@ -13,7 +13,6 @@
 VMEM = 20 * 2**20
 EARLY = 1536
 DISTANCES = (1, 2, 3)
-LATEST = (1, 3, 2)
 LABEL_ROWS = 16
 
 
@@ -189,14 +188,10 @@
 
 
 def stack_kernel(*refs):
-    *pieces, first, second = refs
-    rows = first.shape[0]
-    slab = 2 * rows // len(pieces)
+    *pieces, out = refs
+    slab = out.shape[0] // len(pieces)
     for k, piece in enumerate(pieces):
-        for at in range(0, slab, slab // 2):
-            to = k * slab + at
-            out = (first, second)[to // rows]
-            out[to % rows : to % rows + slab // 2, :] = piece[at : at + slab // 2, :]
+        out[k * slab : (k + 1) * slab, :] = piece[:slab, :]
 
 
 def mask(which, parts, pieces, out):
@@ -228,15 +223,15 @@
         divisor[e] = jnp.full(divisor.shape[1:], counts[e].astype(F32), F32)
 
 
-def mask_other_kernel(first, second, third, *refs):
+def mask_other_kernel(own, others, *refs):
     *pieces, out = refs
     core = lax.rem(lax.axis_index("tensor"), 2)
-    mask(1 - core, [first[...], second[...], third[...]], pieces, out)
+    mask(1 - core, [own[...], others[...]], pieces, out)
 
 
 def blocks_kernel(divisor, masked_own, masked_other, own, *refs):
     *far, result, final, sems = refs
-    outs = [own] + [far[LATEST.index(k)] for k in DISTANCES]
+    outs = [own, *far]
     experts, slots, _ = masked_own.shape
     half = slots // len(outs)
     core = lax.rem(lax.axis_index("tensor"), 2)
@@ -360,9 +355,11 @@
     other = [lax.ppermute(own, "tensor", core)]
     pieces = [pieces[0]] + [swap(pieces[k], k) for k in DISTANCES]
     out = call(round_kernel, "round_out", rows(wide, BF16), after=other)(keep, got)
-    outs = [swap(out, k) for k in LATEST]
-    mine = call(stack_kernel, "stack_in", [rows(3 * slab // 2, BF16)] * 2)(*pieces[1:])
-    other += [lax.ppermute(x, "tensor", core) for x in mine]
+    near, far = swap(out, 1), swap(out, 2)
+    relayed = call(copy_kernel, "relay_out", rows(wide, BF16), after=[near])(far)
+    outs = [near, far, swap(relayed, 1)]
+    mine = call(stack_kernel, "stack_in", rows(3 * slab, BF16))(*pieces[1:])
+    other.append(lax.ppermute(mine, "tensor", core))
     masked = jax.ShapeDtypeStruct((experts, dp * cap // 2, dp * 128), BF16)
     masked_own, divisor = call(
         mask_own_kernel,

time: 34.1 us -> 36.2 us (1.062)
  waiting for transfers between devices: 7.71 us -> 10.2 us
  starting transfers between devices: 14.8 us -> 14.4 us
    ppermute x6, waiting for transfers between devices: 6.23 us -> 8.69 us  [swap(): return lax.ppermute(x, 'dp', [(d, d ^ k) for d in range(dp)])]
    ppermute x2 -> x1, starting transfers between devices: 0.57 us -> 0.07 us  [fast(): other.append(lax.ppermute(mine, 'tensor', core))]
    pallas_call x14 -> x15, Pallas kernels: 11.2 us -> 11.2 us  [run(): pl.pallas_call(body, out_shape=out_shape, in_specs=(specs or [vmem] * len...]
  transfers between devices with their start and end apart: 14 -> 13, of which waited for: 6 -> 6; matrix products, arithmetic and copies ran while one was open for 0% -> 0% of each run, Pallas kernels for 20% -> 19%
where the time goes in v16:
time: 36.2 us; the launch traced here: 36 us
  starting transfers between devices  14.4 us (40%)
  Pallas kernels  11.2 us (31%)
  waiting for transfers between devices  10.2 us (28%)
    pallas_call x15, Pallas kernels, run(): pl.pallas_call(body, out_shape=out_shape, in_specs=(specs or [vmem] * len...  11.2 us
    ppermute x6, starting transfers between devices, swap(): return lax.ppermute(x, 'dp', [(d, d ^ k) for d in range(dp)])  8.75 us
    ppermute x6, waiting for transfers between devices, swap(): return lax.ppermute(x, 'dp', [(d, d ^ k) for d in range(dp)])  8.69 us
    ppermute x1, starting transfers between devices, fast(): got_in = lax.ppermute(send_in, 'tensor', across)  2.92 us
    ppermute x1, starting transfers between devices, fast(): got = lax.ppermute(send, 'tensor', across)  1.53 us
    ppermute x2, waiting for transfers between devices, fast(): got = [lax.ppermute(x, 'tensor', core) for x in split[experts:]]  1.21 us
  transfers between devices with their start and end apart: 13, of which 6 were waited for; matrix products, arithmetic and copies ran while one was open for 0% of the time, Pallas kernels for 19%

profile of v16, /device:TPU:0, one launch (start us, length us, event | category | flops | bytes accessed | tf_op | source)
XLA Modules:
  0.0 36.0 jit_solution(11368629068148058912)
XLA Ops:
  0.0 3.1 %rotate_in.1 = (f32[2,192,512]{2,1,0:T(8,128)S(1)}, bf16[16,128]{1,0:T(8,128)(2,1)S(1)}, bf16[384,768]{1,0:T(8,128)(2,1)S(1)}, bf16[384,2,1536]{2,1,0:T(2,128)(2,1)S(1)}) custom-call(bf16[384,1536]{1,0:T(8,128)(2,1)} %refs_0_.3, s32[2,384]{1,0:T(2,128)} %bitcast.3, s32[384]{0:T(512)} %refs_2_.2, bf16[2,1536,512]{2,1,0:T(8,128)(2,1)} %refs_3_.1, ...), custom_call_target="tpu_custom_call" | custom-call | flops 1 | bytes 1 | tf_op jit(solution)/shard_map/rotate_in/pallas_call | solution.py:266
  3.1 0.0 slice-start
  3.1 0.0 slice-start.1
  3.1 0.1 split_in.1
  3.2 0.5 %collective-permute-start = (f32[768,128]{1,0:T(8,128)S(1)}, f32[768,128]{1,0:T(8,128)S(1)}, u32[]{:S(2)}, u32[]{:S(2)}) collective-permute-start(f32[768,128]{1,0:T(8,128)S(1)} %get-tuple-element.27), channel_id=1, source_target_pairs={{0,1},{1,0},{2,3},{3,2},{4,5},{5,4},{6,7},{7,6},{8,9},{9,8},{10,11... | collective-permute-start | bytes 1179656 | tf_op jit(solution)/shard_map/ppermute | solution.py:325
  3.7 1.1 %choose.1.refs_2_.refs_3_ = bf16[384,1536]{1,0:T(8,128)(2,1)S(1)} custom-call(bf16[384,2,1536]{2,1,0:T(2,128)(2,1)S(1)} %get-tuple-element.28.refs_0_, bf16[384,768]{1,0:T(8,128)(2,1)S(1)} %get-tuple-element.29.refs_1_), custom_call_target="tpu_custom_call" | custom-call | flops 1 | bytes 1 | tf_op jit(solution)/shard_map/choose/pallas_call | solution.py:266
  4.8 0.3 collective-permute-done.refs_1_
  5.1 2.9 %collective-permute-start.1 = (bf16[784,128]{1,0:T(8,128)(2,1)S(1)}, bf16[784,128]{1,0:T(8,128)(2,1)S(1)}, u32[]{:S(2)}, u32[]{:S(2)}) collective-permute-start(bf16[784,128]{1,0:T(8,128)(2,1)S(1)} %get-tuple-element.31.refs_4_), channel_id=1, source_target_pairs={{0,2},{1,3},{2,0},{3,1},{4,6},{5,7},{6,4},{7,5},{8,10},{9,11},{10,... | collective-permute-start | bytes 602120 | tf_op jit(solution)/shard_map/ppermute | solution.py:330
  8.1 0.0 slice-done
  8.1 0.0 slice-done.1
  8.1 4.3 %rotate_out.1.refs_0_ = f32[2,192,512]{2,1,0:T(8,128)S(1)} custom-call(bf16[384,2,4096]{2,1,0:T(2,128)(2,1)} %refs_0_.5, bf16[384,768]{1,0:T(8,128)(2,1)S(1)} %get-tuple-element.29.refs_1_, bf16[2,4096,512]{2,1,0:T(8,128)(2,1)S(1)} %bitcast.2, bf16[384,1536]{1,0:T(8,128)(2,1)S(1)} %choose.1.refs_2_.refs_3_, bf16[784,128]{1,0:T(8,128)(2,1)S(1)} %get-tuple-element.31.refs_4_), custom_call_target="tpu_custom_call" | custom-call | flops 1 | bytes 1 | tf_op jit(solution)/shard_map/rotate_out/pallas_call | solution.py:266
  12.3 0.0 copy-start
  12.4 0.1 split_out.1
  12.5 0.1 collective-permute-start.7
  12.6 0.5 %collective-permute-start.8 = (f32[384,128]{1,0:T(8,128)S(1)}, f32[384,128]{1,0:T(8,128)S(1)}, u32[]{:S(2)}, u32[]{:S(2)}) collective-permute-start(f32[384,128]{1,0:T(8,128)S(1)} %get-tuple-element.42), channel_id=1, source_target_pairs={{0,1},{1,0},{2,3},{3,2},{4,5},{5,4},{6,7},{7,6},{8,9},{9,8},{10,11... | collective-permute-start | bytes 589832 | tf_op jit(solution)/shard_map/ppermute | solution.py:344
  13.1 0.9 %collective-permute-done.7.refs_2_ = f32[384,128]{1,0:T(8,128)S(1)} collective-permute-done((f32[384,128]{1,0:T(8,128)S(1)}, f32[384,128]{1,0:T(8,128)S(1)}, u32[]{:S(2)}, u32[]{:S(2)}) %collective-permute-start.7) | collective-permute-done | bytes 196640 | tf_op jit(solution)/shard_map/ppermute | solution.py:344
  14.0 0.3 collective-permute-done.8.refs_3_
  14.3 0.0 collective-permute-done.1.refs_1_.refs_4_
  14.3 1.5 %collective-permute-start.9 = (bf16[384,128]{1,0:T(8,128)(2,1)S(1)}, bf16[384,128]{1,0:T(8,128)(2,1)S(1)}, u32[]{:S(2)}, u32[]{:S(2)}) collective-permute-start(bf16[384,128]{1,0:T(8,128)(2,1)S(1)} %get-tuple-element.44), channel_id=1, source_target_pairs={{0,2},{1,3},{2,0},{3,1},{4,6},{5,7},{6,4},{7,5},{8,10},{9,11},{10,... | collective-permute-start | bytes 294920 | tf_op jit(solution)/shard_map/ppermute | solution.py:348
  15.8 0.1 round_in.1
  15.9 0.1 collective-permute-start.5
  16.0 1.6 %collective-permute-start.2 = (bf16[208,128]{1,0:T(8,128)(2,1)S(1)}, bf16[208,128]{1,0:T(8,128)(2,1)S(1)}, u32[]{:S(2)}, u32[]{:S(2)}) collective-permute-start(bf16[208,128]{1,0:T(8,128)(2,1)S(1)} %get-tuple-element.34), channel_id=1, source_target_pairs={{0,4},{4,0},{8,12},{12,8},{1,5},{5,1},{9,13},{13,9},{2,6},{6,2},{1... | collective-permute-start | bytes 159752 | tf_op jit(solution)/shard_map/ppermute | solution.py:301
  17.6 2.6 %collective-permute-start.3 = (bf16[208,128]{1,0:T(8,128)(2,1)S(1)}, bf16[208,128]{1,0:T(8,128)(2,1)S(1)}, u32[]{:S(2)}, u32[]{:S(2)}) collective-permute-start(bf16[208,128]{1,0:T(8,128)(2,1)S(1)} %get-tuple-element.35), channel_id=1, source_target_pairs={{0,8},{4,12},{8,0},{12,4},{1,9},{5,13},{9,1},{13,5},{2,10},{6,14},... | collective-permute-start | bytes 159752 | tf_op jit(solution)/shard_map/ppermute | solution.py:301
  20.2 0.2 collective-permute-start.4
  20.4 0.0 collective-permute-done.5.refs_0_.refs_2_
  20.5 0.0 collective-permute-done.9.refs_1_
  20.5 1.7 %collective-permute-start.11 = (bf16[384,128]{1,0:T(8,128)(2,1)S(1)}, bf16[384,128]{1,0:T(8,128)(2,1)S(1)}, u32[]{:S(2)}, u32[]{:S(2)}) collective-permute-start(bf16[384,128]{1,0:T(8,128)(2,1)S(1)} %round_out.1.refs_3_), channel_id=1, source_target_pairs={{0,8},{4,12},{8,0},{12,4},{1,9},{5,13},{9,1},{13,5},{2,10},{6,14},... | collective-permute-start | bytes 294920 | tf_op jit(solution)/shard_map/ppermute | solution.py:301
  22.2 2.5 %collective-permute-start.10 = (bf16[384,128]{1,0:T(8,128)(2,1)S(1)}, bf16[384,128]{1,0:T(8,128)(2,1)S(1)}, u32[]{:S(2)}, u32[]{:S(2)}) collective-permute-start(bf16[384,128]{1,0:T(8,128)(2,1)S(1)} %round_out.1.refs_3_), channel_id=1, source_target_pairs={{0,4},{4,0},{8,12},{12,8},{1,5},{5,1},{9,13},{13,9},{2,6},{6,2},{1... | collective-permute-start | bytes 294920 | tf_op jit(solution)/shard_map/ppermute | solution.py:301
  24.7 0.0 collective-permute-done.2.refs_2_.refs_0_.refs_3_
  24.7 0.0 collective-permute-done.3.refs_3_.refs_1_.refs_4_
  24.7 2.1 %collective-permute-done.4.refs_4_.refs_2_.refs_5_ = bf16[208,128]{1,0:T(8,128)(2,1)S(1)} collective-permute-done((bf16[208,128]{1,0:T(8,128)(2,1)S(1)}, bf16[208,128]{1,0:T(8,128)(2,1)S(1)}, u32[]{:S(2)}, u32[]{:S(2)}) %collective-permute-start.4) | collective-permute-done | bytes 53280 | tf_op jit(solution)/shard_map/ppermute | solution.py:301
  26.8 0.1 collective-permute-start.6
  26.9 3.3 %collective-permute-done.11.refs_0_.refs_5_ = bf16[384,128]{1,0:T(8,128)(2,1)S(1)} collective-permute-done((bf16[384,128]{1,0:T(8,128)(2,1)S(1)}, bf16[384,128]{1,0:T(8,128)(2,1)S(1)}, u32[]{:S(2)}, u32[]{:S(2)}) %collective-permute-start.11) | collective-permute-done | bytes 98336 | tf_op jit(solution)/shard_map/ppermute | solution.py:301
  30.2 0.0 collective-permute-done.10.refs_1_.refs_4_
  30.2 0.1 collective-permute-start.12
  30.3 0.0 copy-done
  30.3 0.9 %mask_own.1 = (bf16[2,384,512]{2,1,0:T(8,128)(2,1)S(1)}, f32[2,8,128]{2,1,0:T(8,128)S(1)}) custom-call(s32[2]{0:T(128)S(1)} %copy-done, bf16[208,128]{1,0:T(8,128)(2,1)S(1)} %get-tuple-element.33.refs_1_.refs_0_.refs_2_, bf16[208,128]{1,0:T(8,128)(2,1)S(1)} %collective-permute-done.2.refs_2_.refs_0_.refs_3_, ...), custom_call_target="tpu_custom_call" | custom-call | flops 1 | bytes 1 | tf_op jit(solution)/shard_map/mask_own/pallas_call | solution.py:266
  31.2 0.0 collective-permute-done.6.refs_1_
  31.2 0.3 mask_other.1.refs_2_
  31.5 3.3 %collective-permute-done.12.refs_6_ = bf16[384,128]{1,0:T(8,128)(2,1)S(1)} collective-permute-done((bf16[384,128]{1,0:T(8,128)(2,1)S(1)}, bf16[384,128]{1,0:T(8,128)(2,1)S(1)}, u32[]{:S(2)}, u32[]{:S(2)}) %collective-permute-start.12) | collective-permute-done | bytes 98336 | tf_op jit(solution)/shard_map/ppermute | solution.py:301
  34.9 1.1 %blocks.1 = f32[2,128,128]{2,1,0:T(8,128)} custom-call(f32[2,8,128]{2,1,0:T(8,128)S(1)} %get-tuple-element.37.refs_6_.refs_0_, bf16[2,384,512]{2,1,0:T(8,128)(2,1)S(1)} %get-tuple-element.38.refs_1_, bf16[2,384,512]{2,1,0:T(8,128)(2,1)S(1)} %mask_other.1.refs_2_, bf16[384,128]{1,0:T(8,128)(2,1)S(1)} %round_out.1.refs_3_, ...), custom_call_target="tpu_custom_call" | custom-call | flops 1 | bytes 1 | tf_op jit(solution)/shard_map/blocks/pallas_call | solution.py:266
  (7 shorter events, 0.1 us)
Async XLA Ops:
  3.1 5.0 %slice-start = ((s8[8388608]{0:T(1024)(128)(4,1)}), s8[4194304]{0:T(1024)(128)(4,1)S(1)}, s32[]{:S(2)}) async-start(s8[8388608]{0:T(1024)(128)(4,1)} %bitcast.1), calls=%async_computation | async-start | bytes 8388608
  3.1 4.9 %slice-start.1 = ((s8[8388608]{0:T(1024)(128)(4,1)}), s8[4194304]{0:T(1024)(128)(4,1)S(1)}, s32[]{:S(2)}) async-start(s8[8388608]{0:T(1024)(128)(4,1)} %bitcast.1), calls=%async_computation.1 | async-start | bytes 8388608
  3.2 1.9 %collective-permute-start = (f32[768,128]{1,0:T(8,128)S(1)}, f32[768,128]{1,0:T(8,128)S(1)}, u32[]{:S(2)}, u32[]{:S(2)}) collective-permute-start(f32[768,128]{1,0:T(8,128)S(1)} %get-tuple-element.27), channel_id=1, source_target_pairs={{0,1},{1,0},{2,3},{3,2},{4,5},{5,4},{6,7},{7,6},{8,9},{9,8},{10,11... | collective-permute-start | bytes 1179656 | tf_op jit(solution)/shard_map/ppermute | solution.py:325
  5.1 9.1 %collective-permute-start.1 = (bf16[784,128]{1,0:T(8,128)(2,1)S(1)}, bf16[784,128]{1,0:T(8,128)(2,1)S(1)}, u32[]{:S(2)}, u32[]{:S(2)}) collective-permute-start(bf16[784,128]{1,0:T(8,128)(2,1)S(1)} %get-tuple-element.31.refs_4_), channel_id=1, source_target_pairs={{0,2},{1,3},{2,0},{3,1},{4,6},{5,7},{6,4},{7,5},{8,10},{9,11},{10,... | collective-permute-start | bytes 602120 | tf_op jit(solution)/shard_map/ppermute | solution.py:330
  12.3 17.9 %copy-start = (s32[2]{0:T(128)S(1)}, s32[2]{0:T(128)}, u32[]{:S(2)}) copy-start(s32[2]{0:T(128)} %refs_0_.4) | copy-start | bytes 28
  12.5 1.5 %collective-permute-start.7 = (f32[384,128]{1,0:T(8,128)S(1)}, f32[384,128]{1,0:T(8,128)S(1)}, u32[]{:S(2)}, u32[]{:S(2)}) collective-permute-start(f32[384,128]{1,0:T(8,128)S(1)} %get-tuple-element.41), channel_id=1, source_target_pairs={{0,1},{1,0},{2,3},{3,2},{4,5},{5,4},{6,7},{7,6},{8,9},{9,8},{10,11... | collective-permute-start | bytes 589832 | tf_op jit(solution)/shard_map/ppermute | solution.py:344
  12.6 1.7 %collective-permute-start.8 = (f32[384,128]{1,0:T(8,128)S(1)}, f32[384,128]{1,0:T(8,128)S(1)}, u32[]{:S(2)}, u32[]{:S(2)}) collective-permute-start(f32[384,128]{1,0:T(8,128)S(1)} %get-tuple-element.42), channel_id=1, source_target_pairs={{0,1},{1,0},{2,3},{3,2},{4,5},{5,4},{6,7},{7,6},{8,9},{9,8},{10,11... | collective-permute-start | bytes 589832 | tf_op jit(solution)/shard_map/ppermute | solution.py:344
  14.3 6.1 %collective-permute-start.9 = (bf16[384,128]{1,0:T(8,128)(2,1)S(1)}, bf16[384,128]{1,0:T(8,128)(2,1)S(1)}, u32[]{:S(2)}, u32[]{:S(2)}) collective-permute-start(bf16[384,128]{1,0:T(8,128)(2,1)S(1)} %get-tuple-element.44), channel_id=1, source_target_pairs={{0,2},{1,3},{2,0},{3,1},{4,6},{5,7},{6,4},{7,5},{8,10},{9,11},{10,... | collective-permute-start | bytes 294920 | tf_op jit(solution)/shard_map/ppermute | solution.py:348
  15.9 4.5 %collective-permute-start.5 = (bf16[192,128]{1,0:T(8,128)(2,1)S(1)}, bf16[192,128]{1,0:T(8,128)(2,1)S(1)}, u32[]{:S(2)}, u32[]{:S(2)}) collective-permute-start(bf16[192,128]{1,0:T(8,128)(2,1)S(1)} %own_in.1), channel_id=1, source_target_pairs={{0,1},{1,0},{2,3},{3,2},{4,5},{5,4},{6,7},{7,6},{8,9},{9,8},{10,11... | collective-permute-start | bytes 147464 | tf_op jit(solution)/shard_map/ppermute | solution.py:355
  16.0 8.7 %collective-permute-start.2 = (bf16[208,128]{1,0:T(8,128)(2,1)S(1)}, bf16[208,128]{1,0:T(8,128)(2,1)S(1)}, u32[]{:S(2)}, u32[]{:S(2)}) collective-permute-start(bf16[208,128]{1,0:T(8,128)(2,1)S(1)} %get-tuple-element.34), channel_id=1, source_target_pairs={{0,4},{4,0},{8,12},{12,8},{1,5},{5,1},{9,13},{13,9},{2,6},{6,2},{1... | collective-permute-start | bytes 159752 | tf_op jit(solution)/shard_map/ppermute | solution.py:301
  17.6 7.1 %collective-permute-start.3 = (bf16[208,128]{1,0:T(8,128)(2,1)S(1)}, bf16[208,128]{1,0:T(8,128)(2,1)S(1)}, u32[]{:S(2)}, u32[]{:S(2)}) collective-permute-start(bf16[208,128]{1,0:T(8,128)(2,1)S(1)} %get-tuple-element.35), channel_id=1, source_target_pairs={{0,8},{4,12},{8,0},{12,4},{1,9},{5,13},{9,1},{13,5},{2,10},{6,14},... | collective-permute-start | bytes 159752 | tf_op jit(solution)/shard_map/ppermute | solution.py:301
  20.2 6.6 %collective-permute-start.4 = (bf16[208,128]{1,0:T(8,128)(2,1)S(1)}, bf16[208,128]{1,0:T(8,128)(2,1)S(1)}, u32[]{:S(2)}, u32[]{:S(2)}) collective-permute-start(bf16[208,128]{1,0:T(8,128)(2,1)S(1)} %get-tuple-element.36), channel_id=1, source_target_pairs={{0,12},{4,8},{8,4},{12,0},{1,13},{5,9},{9,5},{13,1},{2,14},{6,10},... | collective-permute-start | bytes 159752 | tf_op jit(solution)/shard_map/ppermute | solution.py:301
  20.5 9.7 %collective-permute-start.11 = (bf16[384,128]{1,0:T(8,128)(2,1)S(1)}, bf16[384,128]{1,0:T(8,128)(2,1)S(1)}, u32[]{:S(2)}, u32[]{:S(2)}) collective-permute-start(bf16[384,128]{1,0:T(8,128)(2,1)S(1)} %round_out.1.refs_3_), channel_id=1, source_target_pairs={{0,8},{4,12},{8,0},{12,4},{1,9},{5,13},{9,1},{13,5},{2,10},{6,14},... | collective-permute-start | bytes 294920 | tf_op jit(solution)/shard_map/ppermute | solution.py:301
  22.2 7.9 %collective-permute-start.10 = (bf16[384,128]{1,0:T(8,128)(2,1)S(1)}, bf16[384,128]{1,0:T(8,128)(2,1)S(1)}, u32[]{:S(2)}, u32[]{:S(2)}) collective-permute-start(bf16[384,128]{1,0:T(8,128)(2,1)S(1)} %round_out.1.refs_3_), channel_id=1, source_target_pairs={{0,4},{4,0},{8,12},{12,8},{1,5},{5,1},{9,13},{13,9},{2,6},{6,2},{1... | collective-permute-start | bytes 294920 | tf_op jit(solution)/shard_map/ppermute | solution.py:301
  26.8 4.4 %collective-permute-start.6 = (bf16[576,128]{1,0:T(8,128)(2,1)S(1)}, bf16[576,128]{1,0:T(8,128)(2,1)S(1)}, u32[]{:S(2)}, u32[]{:S(2)}) collective-permute-start(bf16[576,128]{1,0:T(8,128)(2,1)S(1)} %stack_in.1), channel_id=1, source_target_pairs={{0,1},{1,0},{2,3},{3,2},{4,5},{5,4},{6,7},{7,6},{8,9},{9,8},{10,11... | collective-permute-start | bytes 442376 | tf_op jit(solution)/shard_map/ppermute | solution.py:362
  30.2 4.7 %collective-permute-start.12 = (bf16[384,128]{1,0:T(8,128)(2,1)S(1)}, bf16[384,128]{1,0:T(8,128)(2,1)S(1)}, u32[]{:S(2)}, u32[]{:S(2)}) collective-permute-start(bf16[384,128]{1,0:T(8,128)(2,1)S(1)} %relay_out.1), channel_id=1, source_target_pairs={{0,4},{4,0},{8,12},{12,8},{1,5},{5,1},{9,13},{13,9},{2,6},{6,2},{1... | collective-permute-start | bytes 294920 | tf_op jit(solution)/shard_map/ppermute | solution.py:301

commit v17 on v15

--- a/solution.py
+++ b/solution.py
@@ -12,7 +12,7 @@
 CHUNK = 1024
 VMEM = 20 * 2**20
 EARLY = 1536
-DISTANCES = (1, 2, 3)
+DISTANCES = (1, 3, 2)
 LATEST = (1, 3, 2)
 LABEL_ROWS = 16
 

time: 34.1 us -> 34.8 us (1.021)
  waiting for transfers between devices: 7.71 us -> 8.68 us
    ppermute x6, waiting for transfers between devices: 6.23 us -> 7.19 us  [swap(): return lax.ppermute(x, 'dp', [(d, d ^ k) for d in range(dp)])]
where the time goes in v17:
time: 34.8 us; the launch traced here: 34.6 us
  starting transfers between devices  14.6 us (42%)
  Pallas kernels  11.2 us (32%)
  waiting for transfers between devices  8.68 us (25%)
    pallas_call x14, Pallas kernels, run(): pl.pallas_call(body, out_shape=out_shape, in_specs=(specs or [vmem] * len...  11.2 us
    ppermute x6, starting transfers between devices, swap(): return lax.ppermute(x, 'dp', [(d, d ^ k) for d in range(dp)])  8.51 us
    ppermute x6, waiting for transfers between devices, swap(): return lax.ppermute(x, 'dp', [(d, d ^ k) for d in range(dp)])  7.19 us
    ppermute x1, starting transfers between devices, fast(): got_in = lax.ppermute(send_in, 'tensor', across)  2.92 us
    ppermute x1, starting transfers between devices, fast(): got = lax.ppermute(send, 'tensor', across)  1.52 us
    ppermute x2, waiting for transfers between devices, fast(): got = [lax.ppermute(x, 'tensor', core) for x in split[experts:]]  1.21 us
  transfers between devices with their start and end apart: 14, of which 6 were waited for; matrix products, arithmetic and copies ran while one was open for 0% of the time, Pallas kernels for 20%

profile of v17, /device:TPU:0, one launch (start us, length us, event | category | flops | bytes accessed | tf_op | source)
XLA Modules:
  0.0 34.6 jit_solution(14822714340873303658)
XLA Ops:
  0.0 3.1 %rotate_in.1 = (f32[2,192,512]{2,1,0:T(8,128)S(1)}, bf16[16,128]{1,0:T(8,128)(2,1)S(1)}, bf16[384,768]{1,0:T(8,128)(2,1)S(1)}, bf16[384,2,1536]{2,1,0:T(2,128)(2,1)S(1)}) custom-call(bf16[384,1536]{1,0:T(8,128)(2,1)} %refs_0_.3, s32[2,384]{1,0:T(2,128)} %bitcast.3, s32[384]{0:T(512)} %refs_2_.2, bf16[2,1536,512]{2,1,0:T(8,128)(2,1)} %refs_3_.1, ...), custom_call_target="tpu_custom_call" | custom-call | flops 1 | bytes 1 | tf_op jit(solution)/shard_map/rotate_in/pallas_call | solution.py:271
  3.1 0.0 slice-start
  3.1 0.0 slice-start.1
  3.1 0.1 split_in.1
  3.2 0.5 %collective-permute-start = (f32[768,128]{1,0:T(8,128)S(1)}, f32[768,128]{1,0:T(8,128)S(1)}, u32[]{:S(2)}, u32[]{:S(2)}) collective-permute-start(f32[768,128]{1,0:T(8,128)S(1)} %get-tuple-element.29), channel_id=1, source_target_pairs={{0,1},{1,0},{2,3},{3,2},{4,5},{5,4},{6,7},{7,6},{8,9},{9,8},{10,11... | collective-permute-start | bytes 1179656 | tf_op jit(solution)/shard_map/ppermute | solution.py:330
  3.7 1.1 %choose.1.refs_2_.refs_3_ = bf16[384,1536]{1,0:T(8,128)(2,1)S(1)} custom-call(bf16[384,2,1536]{2,1,0:T(2,128)(2,1)S(1)} %get-tuple-element.30.refs_0_, bf16[384,768]{1,0:T(8,128)(2,1)S(1)} %get-tuple-element.31.refs_1_), custom_call_target="tpu_custom_call" | custom-call | flops 1 | bytes 1 | tf_op jit(solution)/shard_map/choose/pallas_call | solution.py:271
  4.8 0.3 collective-permute-done.refs_1_
  5.1 0.0 copy-start
  5.1 2.9 %collective-permute-start.1 = (bf16[784,128]{1,0:T(8,128)(2,1)S(1)}, bf16[784,128]{1,0:T(8,128)(2,1)S(1)}, u32[]{:S(2)}, u32[]{:S(2)}) collective-permute-start(bf16[784,128]{1,0:T(8,128)(2,1)S(1)} %get-tuple-element.33.refs_4_), channel_id=1, source_target_pairs={{0,2},{1,3},{2,0},{3,1},{4,6},{5,7},{6,4},{7,5},{8,10},{9,11},{10,... | collective-permute-start | bytes 602120 | tf_op jit(solution)/shard_map/ppermute | solution.py:335
  8.1 0.0 slice-done
  8.1 0.0 slice-done.1
  8.1 4.3 %rotate_out.1.refs_0_ = f32[2,192,512]{2,1,0:T(8,128)S(1)} custom-call(bf16[384,2,4096]{2,1,0:T(2,128)(2,1)} %refs_0_.5, bf16[384,768]{1,0:T(8,128)(2,1)S(1)} %get-tuple-element.31.refs_1_, bf16[2,4096,512]{2,1,0:T(8,128)(2,1)S(1)} %bitcast.2, bf16[384,1536]{1,0:T(8,128)(2,1)S(1)} %choose.1.refs_2_.refs_3_, bf16[784,128]{1,0:T(8,128)(2,1)S(1)} %get-tuple-element.33.refs_4_), custom_call_target="tpu_custom_call" | custom-call | flops 1 | bytes 1 | tf_op jit(solution)/shard_map/rotate_out/pallas_call | solution.py:271
  12.4 0.1 split_out.1
  12.5 0.1 collective-permute-start.8
  12.6 0.5 %collective-permute-start.9 = (f32[384,128]{1,0:T(8,128)S(1)}, f32[384,128]{1,0:T(8,128)S(1)}, u32[]{:S(2)}, u32[]{:S(2)}) collective-permute-start(f32[384,128]{1,0:T(8,128)S(1)} %get-tuple-element.46), channel_id=1, source_target_pairs={{0,1},{1,0},{2,3},{3,2},{4,5},{5,4},{6,7},{7,6},{8,9},{9,8},{10,11... | collective-permute-start | bytes 589832 | tf_op jit(solution)/shard_map/ppermute | solution.py:349
  13.1 0.9 %collective-permute-done.8.refs_2_ = f32[384,128]{1,0:T(8,128)S(1)} collective-permute-done((f32[384,128]{1,0:T(8,128)S(1)}, f32[384,128]{1,0:T(8,128)S(1)}, u32[]{:S(2)}, u32[]{:S(2)}) %collective-permute-start.8) | collective-permute-done | bytes 196640 | tf_op jit(solution)/shard_map/ppermute | solution.py:349
  14.0 0.3 collective-permute-done.9.refs_3_
  14.3 0.0 collective-permute-done.1.refs_1_.refs_4_
  14.3 1.5 %collective-permute-start.10 = (bf16[384,128]{1,0:T(8,128)(2,1)S(1)}, bf16[384,128]{1,0:T(8,128)(2,1)S(1)}, u32[]{:S(2)}, u32[]{:S(2)}) collective-permute-start(bf16[384,128]{1,0:T(8,128)(2,1)S(1)} %get-tuple-element.48), channel_id=1, source_target_pairs={{0,2},{1,3},{2,0},{3,1},{4,6},{5,7},{6,4},{7,5},{8,10},{9,11},{10,... | collective-permute-start | bytes 294920 | tf_op jit(solution)/shard_map/ppermute | solution.py:353
  15.8 0.1 round_in.1
  15.9 1.6 %collective-permute-start.2 = (bf16[208,128]{1,0:T(8,128)(2,1)S(1)}, bf16[208,128]{1,0:T(8,128)(2,1)S(1)}, u32[]{:S(2)}, u32[]{:S(2)}) collective-permute-start(bf16[208,128]{1,0:T(8,128)(2,1)S(1)} %get-tuple-element.36), channel_id=1, source_target_pairs={{0,4},{4,0},{8,12},{12,8},{1,5},{5,1},{9,13},{13,9},{2,6},{6,2},{1... | collective-permute-start | bytes 159752 | tf_op jit(solution)/shard_map/ppermute | solution.py:306
  17.5 0.0 collective-permute-start.5
  17.5 2.5 %collective-permute-start.3 = (bf16[208,128]{1,0:T(8,128)(2,1)S(1)}, bf16[208,128]{1,0:T(8,128)(2,1)S(1)}, u32[]{:S(2)}, u32[]{:S(2)}) collective-permute-start(bf16[208,128]{1,0:T(8,128)(2,1)S(1)} %get-tuple-element.37), channel_id=1, source_target_pairs={{0,12},{4,8},{8,4},{12,0},{1,13},{5,9},{9,5},{13,1},{2,14},{6,10},... | collective-permute-start | bytes 159752 | tf_op jit(solution)/shard_map/ppermute | solution.py:306
  20.1 0.2 collective-permute-start.4
  20.3 0.0 collective-permute-done.5.refs_0_.refs_2_
  20.3 0.0 collective-permute-done.10.refs_1_
  20.3 2.8 %collective-permute-start.13 = (bf16[384,128]{1,0:T(8,128)(2,1)S(1)}, bf16[384,128]{1,0:T(8,128)(2,1)S(1)}, u32[]{:S(2)}, u32[]{:S(2)}) collective-permute-start(bf16[384,128]{1,0:T(8,128)(2,1)S(1)} %round_out.1.refs_3_), channel_id=1, source_target_pairs={{0,8},{4,12},{8,0},{12,4},{1,9},{5,13},{9,1},{13,5},{2,10},{6,14},... | collective-permute-start | bytes 294920 | tf_op jit(solution)/shard_map/ppermute | solution.py:306
  23.1 1.3 %collective-permute-start.12 = (bf16[384,128]{1,0:T(8,128)(2,1)S(1)}, bf16[384,128]{1,0:T(8,128)(2,1)S(1)}, u32[]{:S(2)}, u32[]{:S(2)}) collective-permute-start(bf16[384,128]{1,0:T(8,128)(2,1)S(1)} %round_out.1.refs_3_), channel_id=1, source_target_pairs={{0,12},{4,8},{8,4},{12,0},{1,13},{5,9},{9,5},{13,1},{2,14},{6,10},... | collective-permute-start | bytes 294920 | tf_op jit(solution)/shard_map/ppermute | solution.py:306
  24.4 0.0 collective-permute-done.2.refs_2_.refs_0_.refs_4_
  24.4 0.0 collective-permute-start.11
  24.5 0.0 collective-permute-done.3.refs_3_.refs_1_.refs_5_
  24.5 6.1 %collective-permute-done.4.refs_4_.refs_2_.refs_6_ = bf16[208,128]{1,0:T(8,128)(2,1)S(1)} collective-permute-done((bf16[208,128]{1,0:T(8,128)(2,1)S(1)}, bf16[208,128]{1,0:T(8,128)(2,1)S(1)}, u32[]{:S(2)}, u32[]{:S(2)}) %collective-permute-start.4) | collective-permute-done | bytes 53280 | tf_op jit(solution)/shard_map/ppermute | solution.py:306
  30.6 0.1 collective-permute-start.6
  30.7 0.5 %collective-permute-start.7 = (bf16[288,128]{1,0:T(8,128)(2,1)S(1)}, bf16[288,128]{1,0:T(8,128)(2,1)S(1)}, u32[]{:S(2)}, u32[]{:S(2)}) collective-permute-start(bf16[288,128]{1,0:T(8,128)(2,1)S(1)} %get-tuple-element.42), channel_id=1, source_target_pairs={{0,1},{1,0},{2,3},{3,2},{4,5},{5,4},{6,7},{7,6},{8,9},{9,8},{10,11... | collective-permute-start | bytes 221192 | tf_op jit(solution)/shard_map/ppermute | solution.py:365
  31.2 0.0 copy-done
  31.2 0.9 %mask_own.1 = (bf16[2,384,512]{2,1,0:T(8,128)(2,1)S(1)}, f32[2,8,128]{2,1,0:T(8,128)S(1)}) custom-call(s32[2]{0:T(128)S(1)} %copy-done, bf16[208,128]{1,0:T(8,128)(2,1)S(1)} %get-tuple-element.35.refs_1_.refs_0_.refs_3_, bf16[208,128]{1,0:T(8,128)(2,1)S(1)} %collective-permute-done.2.refs_2_.refs_0_.refs_4_, ...), custom_call_target="tpu_custom_call" | custom-call | flops 1 | bytes 1 | tf_op jit(solution)/shard_map/mask_own/pallas_call | solution.py:271
  32.1 0.0 collective-permute-done.6.refs_1_
  32.1 0.0 collective-permute-done.7.refs_2_
  32.1 0.3 %mask_other.1.refs_2_ = bf16[2,384,512]{2,1,0:T(8,128)(2,1)S(1)} custom-call(bf16[192,128]{1,0:T(8,128)(2,1)S(1)} %collective-permute-done.5.refs_0_.refs_2_, bf16[288,128]{1,0:T(8,128)(2,1)S(1)} %collective-permute-done.6.refs_1_, bf16[288,128]{1,0:T(8,128)(2,1)S(1)} %collective-permute-done.7.refs_2_, ...), custom_call_target="tpu_custom_call" | custom-call | flops 1 | bytes 1 | tf_op jit(solution)/shard_map/mask_other/pallas_call | solution.py:271
  32.4 0.2 collective-permute-done.13.refs_6_
  32.6 0.0 collective-permute-done.12.refs_5_
  32.6 0.9 %collective-permute-done.11.refs_4_ = bf16[384,128]{1,0:T(8,128)(2,1)S(1)} collective-permute-done((bf16[384,128]{1,0:T(8,128)(2,1)S(1)}, bf16[384,128]{1,0:T(8,128)(2,1)S(1)}, u32[]{:S(2)}, u32[]{:S(2)}) %collective-permute-start.11) | collective-permute-done | bytes 98336 | tf_op jit(solution)/shard_map/ppermute | solution.py:306
  33.5 1.1 %blocks.1 = f32[2,128,128]{2,1,0:T(8,128)} custom-call(f32[2,8,128]{2,1,0:T(8,128)S(1)} %get-tuple-element.39.refs_7_.refs_0_, bf16[2,384,512]{2,1,0:T(8,128)(2,1)S(1)} %get-tuple-element.40.refs_1_, bf16[2,384,512]{2,1,0:T(8,128)(2,1)S(1)} %mask_other.1.refs_2_, bf16[384,128]{1,0:T(8,128)(2,1)S(1)} %round_out.1.refs_3_, ...), custom_call_target="tpu_custom_call" | custom-call | flops 1 | bytes 1 | tf_op jit(solution)/shard_map/blocks/pallas_call | solution.py:271
  (6 shorter events, 0.1 us)
Async XLA Ops:
  3.1 5.0 %slice-start = ((s8[8388608]{0:T(1024)(128)(4,1)}), s8[4194304]{0:T(1024)(128)(4,1)S(1)}, s32[]{:S(2)}) async-start(s8[8388608]{0:T(1024)(128)(4,1)} %bitcast.1), calls=%async_computation | async-start | bytes 8388608
  3.1 5.0 %slice-start.1 = ((s8[8388608]{0:T(1024)(128)(4,1)}), s8[4194304]{0:T(1024)(128)(4,1)S(1)}, s32[]{:S(2)}) async-start(s8[8388608]{0:T(1024)(128)(4,1)} %bitcast.1), calls=%async_computation.1 | async-start | bytes 8388608
  3.2 1.9 %collective-permute-start = (f32[768,128]{1,0:T(8,128)S(1)}, f32[768,128]{1,0:T(8,128)S(1)}, u32[]{:S(2)}, u32[]{:S(2)}) collective-permute-start(f32[768,128]{1,0:T(8,128)S(1)} %get-tuple-element.29), channel_id=1, source_target_pairs={{0,1},{1,0},{2,3},{3,2},{4,5},{5,4},{6,7},{7,6},{8,9},{9,8},{10,11... | collective-permute-start | bytes 1179656 | tf_op jit(solution)/shard_map/ppermute | solution.py:330
  5.1 26.0 %copy-start = (s32[2]{0:T(128)S(1)}, s32[2]{0:T(128)}, u32[]{:S(2)}) copy-start(s32[2]{0:T(128)} %refs_0_.4) | copy-start | bytes 28
  5.1 9.1 %collective-permute-start.1 = (bf16[784,128]{1,0:T(8,128)(2,1)S(1)}, bf16[784,128]{1,0:T(8,128)(2,1)S(1)}, u32[]{:S(2)}, u32[]{:S(2)}) collective-permute-start(bf16[784,128]{1,0:T(8,128)(2,1)S(1)} %get-tuple-element.33.refs_4_), channel_id=1, source_target_pairs={{0,2},{1,3},{2,0},{3,1},{4,6},{5,7},{6,4},{7,5},{8,10},{9,11},{10,... | collective-permute-start | bytes 602120 | tf_op jit(solution)/shard_map/ppermute | solution.py:335
  12.5 1.5 %collective-permute-start.8 = (f32[384,128]{1,0:T(8,128)S(1)}, f32[384,128]{1,0:T(8,128)S(1)}, u32[]{:S(2)}, u32[]{:S(2)}) collective-permute-start(f32[384,128]{1,0:T(8,128)S(1)} %get-tuple-element.45), channel_id=1, source_target_pairs={{0,1},{1,0},{2,3},{3,2},{4,5},{5,4},{6,7},{7,6},{8,9},{9,8},{10,11... | collective-permute-start | bytes 589832 | tf_op jit(solution)/shard_map/ppermute | solution.py:349
  12.6 1.7 %collective-permute-start.9 = (f32[384,128]{1,0:T(8,128)S(1)}, f32[384,128]{1,0:T(8,128)S(1)}, u32[]{:S(2)}, u32[]{:S(2)}) collective-permute-start(f32[384,128]{1,0:T(8,128)S(1)} %get-tuple-element.46), channel_id=1, source_target_pairs={{0,1},{1,0},{2,3},{3,2},{4,5},{5,4},{6,7},{7,6},{8,9},{9,8},{10,11... | collective-permute-start | bytes 589832 | tf_op jit(solution)/shard_map/ppermute | solution.py:349
  14.3 6.0 %collective-permute-start.10 = (bf16[384,128]{1,0:T(8,128)(2,1)S(1)}, bf16[384,128]{1,0:T(8,128)(2,1)S(1)}, u32[]{:S(2)}, u32[]{:S(2)}) collective-permute-start(bf16[384,128]{1,0:T(8,128)(2,1)S(1)} %get-tuple-element.48), channel_id=1, source_target_pairs={{0,2},{1,3},{2,0},{3,1},{4,6},{5,7},{6,4},{7,5},{8,10},{9,11},{10,... | collective-permute-start | bytes 294920 | tf_op jit(solution)/shard_map/ppermute | solution.py:353
  15.9 8.6 %collective-permute-start.2 = (bf16[208,128]{1,0:T(8,128)(2,1)S(1)}, bf16[208,128]{1,0:T(8,128)(2,1)S(1)}, u32[]{:S(2)}, u32[]{:S(2)}) collective-permute-start(bf16[208,128]{1,0:T(8,128)(2,1)S(1)} %get-tuple-element.36), channel_id=1, source_target_pairs={{0,4},{4,0},{8,12},{12,8},{1,5},{5,1},{9,13},{13,9},{2,6},{6,2},{1... | collective-permute-start | bytes 159752 | tf_op jit(solution)/shard_map/ppermute | solution.py:306
  17.5 2.8 %collective-permute-start.5 = (bf16[192,128]{1,0:T(8,128)(2,1)S(1)}, bf16[192,128]{1,0:T(8,128)(2,1)S(1)}, u32[]{:S(2)}, u32[]{:S(2)}) collective-permute-start(bf16[192,128]{1,0:T(8,128)(2,1)S(1)} %own_in.1), channel_id=1, source_target_pairs={{0,1},{1,0},{2,3},{3,2},{4,5},{5,4},{6,7},{7,6},{8,9},{9,8},{10,11... | collective-permute-start | bytes 147464 | tf_op jit(solution)/shard_map/ppermute | solution.py:360
  17.5 6.9 %collective-permute-start.3 = (bf16[208,128]{1,0:T(8,128)(2,1)S(1)}, bf16[208,128]{1,0:T(8,128)(2,1)S(1)}, u32[]{:S(2)}, u32[]{:S(2)}) collective-permute-start(bf16[208,128]{1,0:T(8,128)(2,1)S(1)} %get-tuple-element.37), channel_id=1, source_target_pairs={{0,12},{4,8},{8,4},{12,0},{1,13},{5,9},{9,5},{13,1},{2,14},{6,10},... | collective-permute-start | bytes 159752 | tf_op jit(solution)/shard_map/ppermute | solution.py:306
  20.1 10.5 %collective-permute-start.4 = (bf16[208,128]{1,0:T(8,128)(2,1)S(1)}, bf16[208,128]{1,0:T(8,128)(2,1)S(1)}, u32[]{:S(2)}, u32[]{:S(2)}) collective-permute-start(bf16[208,128]{1,0:T(8,128)(2,1)S(1)} %get-tuple-element.38), channel_id=1, source_target_pairs={{0,8},{4,12},{8,0},{12,4},{1,9},{5,13},{9,1},{13,5},{2,10},{6,14},... | collective-permute-start | bytes 159752 | tf_op jit(solution)/shard_map/ppermute | solution.py:306
  20.3 12.3 %collective-permute-start.13 = (bf16[384,128]{1,0:T(8,128)(2,1)S(1)}, bf16[384,128]{1,0:T(8,128)(2,1)S(1)}, u32[]{:S(2)}, u32[]{:S(2)}) collective-permute-start(bf16[384,128]{1,0:T(8,128)(2,1)S(1)} %round_out.1.refs_3_), channel_id=1, source_target_pairs={{0,8},{4,12},{8,0},{12,4},{1,9},{5,13},{9,1},{13,5},{2,10},{6,14},... | collective-permute-start | bytes 294920 | tf_op jit(solution)/shard_map/ppermute | solution.py:306
  23.1 9.5 %collective-permute-start.12 = (bf16[384,128]{1,0:T(8,128)(2,1)S(1)}, bf16[384,128]{1,0:T(8,128)(2,1)S(1)}, u32[]{:S(2)}, u32[]{:S(2)}) collective-permute-start(bf16[384,128]{1,0:T(8,128)(2,1)S(1)} %round_out.1.refs_3_), channel_id=1, source_target_pairs={{0,12},{4,8},{8,4},{12,0},{1,13},{5,9},{9,5},{13,1},{2,14},{6,10},... | collective-permute-start | bytes 294920 | tf_op jit(solution)/shard_map/ppermute | solution.py:306
  24.4 9.1 %collective-permute-start.11 = (bf16[384,128]{1,0:T(8,128)(2,1)S(1)}, bf16[384,128]{1,0:T(8,128)(2,1)S(1)}, u32[]{:S(2)}, u32[]{:S(2)}) collective-permute-start(bf16[384,128]{1,0:T(8,128)(2,1)S(1)} %round_out.1.refs_3_), channel_id=1, source_target_pairs={{0,4},{4,0},{8,12},{12,8},{1,5},{5,1},{9,13},{13,9},{2,6},{6,2},{1... | collective-permute-start | bytes 294920 | tf_op jit(solution)/shard_map/ppermute | solution.py:306
  30.6 1.5 %collective-permute-start.6 = (bf16[288,128]{1,0:T(8,128)(2,1)S(1)}, bf16[288,128]{1,0:T(8,128)(2,1)S(1)}, u32[]{:S(2)}, u32[]{:S(2)}) collective-permute-start(bf16[288,128]{1,0:T(8,128)(2,1)S(1)} %get-tuple-element.41), channel_id=1, source_target_pairs={{0,1},{1,0},{2,3},{3,2},{4,5},{5,4},{6,7},{7,6},{8,9},{9,8},{10,11... | collective-permute-start | bytes 221192 | tf_op jit(solution)/shard_map/ppermute | solution.py:365
  30.7 1.4 %collective-permute-start.7 = (bf16[288,128]{1,0:T(8,128)(2,1)S(1)}, bf16[288,128]{1,0:T(8,128)(2,1)S(1)}, u32[]{:S(2)}, u32[]{:S(2)}) collective-permute-start(bf16[288,128]{1,0:T(8,128)(2,1)S(1)} %get-tuple-element.42), channel_id=1, source_target_pairs={{0,1},{1,0},{2,3},{3,2},{4,5},{5,4},{6,7},{7,6},{8,9},{9,8},{10,11... | collective-permute-start | bytes 221192 | tf_op jit(solution)/shard_map/ppermute | solution.py:365

commit v18 on v17

--- a/solution.py
+++ b/solution.py
@@ -11,8 +11,8 @@
 BF16 = jnp.bfloat16
 CHUNK = 1024
 VMEM = 20 * 2**20
-EARLY = 1536
-DISTANCES = (1, 3, 2)
+EARLY = 2048
+DISTANCES = (3, 2, 1)
 LATEST = (1, 3, 2)
 LABEL_ROWS = 16
 

time: 34.8 us -> 32.8 us (0.943)
  waiting for transfers between devices: 8.68 us -> 6.9 us
    ppermute x6, waiting for transfers between devices: 7.19 us -> 5.29 us  [swap(): return lax.ppermute(x, 'dp', [(d, d ^ k) for d in range(dp)])]
    ppermute x1, waiting for transfers between devices: 0.01 us -> 0.38 us  [fast(): other = [lax.ppermute(own, 'tensor', core)]]
  transfers between devices with their start and end apart: 14 -> 14, of which waited for: 6 -> 7; matrix products, arithmetic and copies ran while one was open for 0% -> 0% of each run, Pallas kernels for 20% -> 20%
where the time goes in v18:
time: 32.8 us; the launch traced here: 32.6 us
  starting transfers between devices  14.5 us (44%)
  Pallas kernels  11.1 us (34%)
  waiting for transfers between devices  6.9 us (21%)
    pallas_call x14, Pallas kernels, run(): pl.pallas_call(body, out_shape=out_shape, in_specs=(specs or [vmem] * len...  11.1 us
    ppermute x6, starting transfers between devices, swap(): return lax.ppermute(x, 'dp', [(d, d ^ k) for d in range(dp)])  8.36 us
    ppermute x6, waiting for transfers between devices, swap(): return lax.ppermute(x, 'dp', [(d, d ^ k) for d in range(dp)])  5.29 us
    ppermute x1, starting transfers between devices, fast(): got_in = lax.ppermute(send_in, 'tensor', across)  2.86 us
    ppermute x1, starting transfers between devices, fast(): got = lax.ppermute(send, 'tensor', across)  1.58 us
    ppermute x2, waiting for transfers between devices, fast(): got = [lax.ppermute(x, 'tensor', core) for x in split[experts:]]  1.21 us
  transfers between devices with their start and end apart: 14, of which 7 were waited for; matrix products, arithmetic and copies ran while one was open for 0% of the time, Pallas kernels for 20%

profile of v18, /device:TPU:0, one launch (start us, length us, event | category | flops | bytes accessed | tf_op | source)
XLA Modules:
  0.0 32.6 jit_solution(10322554272786374622)
XLA Ops:
  0.0 3.3 %rotate_in.1 = (f32[2,192,512]{2,1,0:T(8,128)S(1)}, bf16[16,128]{1,0:T(8,128)(2,1)S(1)}, bf16[384,768]{1,0:T(8,128)(2,1)S(1)}, bf16[384,2,2048]{2,1,0:T(2,128)(2,1)S(1)}) custom-call(bf16[384,1536]{1,0:T(8,128)(2,1)} %refs_0_.3, s32[2,384]{1,0:T(2,128)} %bitcast.3, s32[384]{0:T(512)} %refs_2_.2, bf16[2,1536,512]{2,1,0:T(8,128)(2,1)} %refs_3_.1, ...), custom_call_target="tpu_custom_call" | custom-call | flops 1 | bytes 1 | tf_op jit(solution)/shard_map/rotate_in/pallas_call | solution.py:271
  3.3 0.0 slice-start
  3.3 0.0 slice-start.1
  3.3 0.1 split_in.1
  3.4 0.5 %collective-permute-start = (f32[768,128]{1,0:T(8,128)S(1)}, f32[768,128]{1,0:T(8,128)S(1)}, u32[]{:S(2)}, u32[]{:S(2)}) collective-permute-start(f32[768,128]{1,0:T(8,128)S(1)} %get-tuple-element.29), channel_id=1, source_target_pairs={{0,1},{1,0},{2,3},{3,2},{4,5},{5,4},{6,7},{7,6},{8,9},{9,8},{10,11... | collective-permute-start | bytes 1179656 | tf_op jit(solution)/shard_map/ppermute | solution.py:330
  3.9 1.4 %choose.1.refs_2_.refs_3_ = bf16[384,2048]{1,0:T(8,128)(2,1)S(1)} custom-call(bf16[384,2,2048]{2,1,0:T(2,128)(2,1)S(1)} %get-tuple-element.30.refs_0_, bf16[384,768]{1,0:T(8,128)(2,1)S(1)} %get-tuple-element.31.refs_1_), custom_call_target="tpu_custom_call" | custom-call | flops 1 | bytes 1 | tf_op jit(solution)/shard_map/choose/pallas_call | solution.py:271
  5.3 0.0 collective-permute-done.refs_1_
  5.4 0.0 copy-start
  5.4 2.9 %collective-permute-start.1 = (bf16[784,128]{1,0:T(8,128)(2,1)S(1)}, bf16[784,128]{1,0:T(8,128)(2,1)S(1)}, u32[]{:S(2)}, u32[]{:S(2)}) collective-permute-start(bf16[784,128]{1,0:T(8,128)(2,1)S(1)} %get-tuple-element.33.refs_4_), channel_id=1, source_target_pairs={{0,2},{1,3},{2,0},{3,1},{4,6},{5,7},{6,4},{7,5},{8,10},{9,11},{10,... | collective-permute-start | bytes 602120 | tf_op jit(solution)/shard_map/ppermute | solution.py:335
  8.2 0.0 slice-done
  8.2 0.0 slice-done.1
  8.3 3.6 %rotate_out.1.refs_0_ = f32[2,192,512]{2,1,0:T(8,128)S(1)} custom-call(bf16[384,2,4096]{2,1,0:T(2,128)(2,1)} %refs_0_.5, bf16[384,768]{1,0:T(8,128)(2,1)S(1)} %get-tuple-element.31.refs_1_, bf16[2,4096,512]{2,1,0:T(8,128)(2,1)S(1)} %bitcast.2, bf16[384,2048]{1,0:T(8,128)(2,1)S(1)} %choose.1.refs_2_.refs_3_, bf16[784,128]{1,0:T(8,128)(2,1)S(1)} %get-tuple-element.33.refs_4_), custom_call_target="tpu_custom_call" | custom-call | flops 1 | bytes 1 | tf_op jit(solution)/shard_map/rotate_out/pallas_call | solution.py:271
  11.9 0.1 split_out.1
  12.0 0.1 collective-permute-start.8
  12.1 0.5 %collective-permute-start.9 = (f32[384,128]{1,0:T(8,128)S(1)}, f32[384,128]{1,0:T(8,128)S(1)}, u32[]{:S(2)}, u32[]{:S(2)}) collective-permute-start(f32[384,128]{1,0:T(8,128)S(1)} %get-tuple-element.46), channel_id=1, source_target_pairs={{0,1},{1,0},{2,3},{3,2},{4,5},{5,4},{6,7},{7,6},{8,9},{9,8},{10,11... | collective-permute-start | bytes 589832 | tf_op jit(solution)/shard_map/ppermute | solution.py:349
  12.6 0.9 %collective-permute-done.8.refs_2_ = f32[384,128]{1,0:T(8,128)S(1)} collective-permute-done((f32[384,128]{1,0:T(8,128)S(1)}, f32[384,128]{1,0:T(8,128)S(1)}, u32[]{:S(2)}, u32[]{:S(2)}) %collective-permute-start.8) | collective-permute-done | bytes 196640 | tf_op jit(solution)/shard_map/ppermute | solution.py:349
  13.5 0.3 collective-permute-done.9.refs_3_
  13.8 0.0 collective-permute-done.1.refs_1_.refs_4_
  13.9 1.6 %collective-permute-start.10 = (bf16[384,128]{1,0:T(8,128)(2,1)S(1)}, bf16[384,128]{1,0:T(8,128)(2,1)S(1)}, u32[]{:S(2)}, u32[]{:S(2)}) collective-permute-start(bf16[384,128]{1,0:T(8,128)(2,1)S(1)} %get-tuple-element.48), channel_id=1, source_target_pairs={{0,2},{1,3},{2,0},{3,1},{4,6},{5,7},{6,4},{7,5},{8,10},{9,11},{10,... | collective-permute-start | bytes 294920 | tf_op jit(solution)/shard_map/ppermute | solution.py:353
  15.5 0.1 round_in.1
  15.5 3.7 %collective-permute-start.2 = (bf16[208,128]{1,0:T(8,128)(2,1)S(1)}, bf16[208,128]{1,0:T(8,128)(2,1)S(1)}, u32[]{:S(2)}, u32[]{:S(2)}) collective-permute-start(bf16[208,128]{1,0:T(8,128)(2,1)S(1)} %get-tuple-element.36), channel_id=1, source_target_pairs={{0,12},{4,8},{8,4},{12,0},{1,13},{5,9},{9,5},{13,1},{2,14},{6,10},... | collective-permute-start | bytes 159752 | tf_op jit(solution)/shard_map/ppermute | solution.py:306
  19.2 0.0 collective-permute-start.5
  19.2 0.1 collective-permute-start.3
  19.3 0.8 %collective-permute-start.4 = (bf16[208,128]{1,0:T(8,128)(2,1)S(1)}, bf16[208,128]{1,0:T(8,128)(2,1)S(1)}, u32[]{:S(2)}, u32[]{:S(2)}) collective-permute-start(bf16[208,128]{1,0:T(8,128)(2,1)S(1)} %get-tuple-element.38), channel_id=1, source_target_pairs={{0,4},{4,0},{8,12},{12,8},{1,5},{5,1},{9,13},{13,9},{2,6},{6,2},{1... | collective-permute-start | bytes 159752 | tf_op jit(solution)/shard_map/ppermute | solution.py:306
  20.0 0.4 %collective-permute-done.5.refs_0_.refs_2_ = bf16[192,128]{1,0:T(8,128)(2,1)S(1)} collective-permute-done((bf16[192,128]{1,0:T(8,128)(2,1)S(1)}, bf16[192,128]{1,0:T(8,128)(2,1)S(1)}, u32[]{:S(2)}, u32[]{:S(2)}) %collective-permute-start.5) | collective-permute-done | bytes 49184 | tf_op jit(solution)/shard_map/ppermute | solution.py:360
  20.4 0.0 collective-permute-done.10.refs_1_
  20.4 1.8 %collective-permute-start.13 = (bf16[384,128]{1,0:T(8,128)(2,1)S(1)}, bf16[384,128]{1,0:T(8,128)(2,1)S(1)}, u32[]{:S(2)}, u32[]{:S(2)}) collective-permute-start(bf16[384,128]{1,0:T(8,128)(2,1)S(1)} %round_out.1.refs_3_), channel_id=1, source_target_pairs={{0,8},{4,12},{8,0},{12,4},{1,9},{5,13},{9,1},{13,5},{2,10},{6,14},... | collective-permute-start | bytes 294920 | tf_op jit(solution)/shard_map/ppermute | solution.py:306
  22.3 1.5 %collective-permute-start.12 = (bf16[384,128]{1,0:T(8,128)(2,1)S(1)}, bf16[384,128]{1,0:T(8,128)(2,1)S(1)}, u32[]{:S(2)}, u32[]{:S(2)}) collective-permute-start(bf16[384,128]{1,0:T(8,128)(2,1)S(1)} %round_out.1.refs_3_), channel_id=1, source_target_pairs={{0,12},{4,8},{8,4},{12,0},{1,13},{5,9},{9,5},{13,1},{2,14},{6,10},... | collective-permute-start | bytes 294920 | tf_op jit(solution)/shard_map/ppermute | solution.py:306
  23.8 0.0 collective-permute-done.2.refs_2_.refs_0_.refs_4_
  23.8 0.5 %collective-permute-start.11 = (bf16[384,128]{1,0:T(8,128)(2,1)S(1)}, bf16[384,128]{1,0:T(8,128)(2,1)S(1)}, u32[]{:S(2)}, u32[]{:S(2)}) collective-permute-start(bf16[384,128]{1,0:T(8,128)(2,1)S(1)} %round_out.1.refs_3_), channel_id=1, source_target_pairs={{0,4},{4,0},{8,12},{12,8},{1,5},{5,1},{9,13},{13,9},{2,6},{6,2},{1... | collective-permute-start | bytes 294920 | tf_op jit(solution)/shard_map/ppermute | solution.py:306
  24.3 0.5 %collective-permute-done.3.refs_3_.refs_1_.refs_5_ = bf16[208,128]{1,0:T(8,128)(2,1)S(1)} collective-permute-done((bf16[208,128]{1,0:T(8,128)(2,1)S(1)}, bf16[208,128]{1,0:T(8,128)(2,1)S(1)}, u32[]{:S(2)}, u32[]{:S(2)}) %collective-permute-start.3) | collective-permute-done | bytes 53280 | tf_op jit(solution)/shard_map/ppermute | solution.py:306
  24.8 0.3 collective-permute-done.4.refs_4_.refs_2_.refs_6_
  25.2 0.1 collective-permute-start.6
  25.2 0.5 %collective-permute-start.7 = (bf16[288,128]{1,0:T(8,128)(2,1)S(1)}, bf16[288,128]{1,0:T(8,128)(2,1)S(1)}, u32[]{:S(2)}, u32[]{:S(2)}) collective-permute-start(bf16[288,128]{1,0:T(8,128)(2,1)S(1)} %get-tuple-element.42), channel_id=1, source_target_pairs={{0,1},{1,0},{2,3},{3,2},{4,5},{5,4},{6,7},{7,6},{8,9},{9,8},{10,11... | collective-permute-start | bytes 221192 | tf_op jit(solution)/shard_map/ppermute | solution.py:365
  25.7 0.0 copy-done
  25.8 0.9 %mask_own.1 = (bf16[2,384,512]{2,1,0:T(8,128)(2,1)S(1)}, f32[2,8,128]{2,1,0:T(8,128)S(1)}) custom-call(s32[2]{0:T(128)S(1)} %copy-done, bf16[208,128]{1,0:T(8,128)(2,1)S(1)} %get-tuple-element.35.refs_1_.refs_0_.refs_3_, bf16[208,128]{1,0:T(8,128)(2,1)S(1)} %collective-permute-done.2.refs_2_.refs_0_.refs_4_, ...), custom_call_target="tpu_custom_call" | custom-call | flops 1 | bytes 1 | tf_op jit(solution)/shard_map/mask_own/pallas_call | solution.py:271
  26.6 0.0 collective-permute-done.6.refs_1_
  26.7 0.0 collective-permute-done.7.refs_2_
  26.7 0.3 %mask_other.1.refs_2_ = bf16[2,384,512]{2,1,0:T(8,128)(2,1)S(1)} custom-call(bf16[192,128]{1,0:T(8,128)(2,1)S(1)} %collective-permute-done.5.refs_0_.refs_2_, bf16[288,128]{1,0:T(8,128)(2,1)S(1)} %collective-permute-done.6.refs_1_, bf16[288,128]{1,0:T(8,128)(2,1)S(1)} %collective-permute-done.7.refs_2_, ...), custom_call_target="tpu_custom_call" | custom-call | flops 1 | bytes 1 | tf_op jit(solution)/shard_map/mask_other/pallas_call | solution.py:271
  27.0 4.3 %collective-permute-done.13.refs_6_ = bf16[384,128]{1,0:T(8,128)(2,1)S(1)} collective-permute-done((bf16[384,128]{1,0:T(8,128)(2,1)S(1)}, bf16[384,128]{1,0:T(8,128)(2,1)S(1)}, u32[]{:S(2)}, u32[]{:S(2)}) %collective-permute-start.13) | collective-permute-done | bytes 98336 | tf_op jit(solution)/shard_map/ppermute | solution.py:306
  31.3 0.0 collective-permute-done.12.refs_5_
  31.3 0.2 collective-permute-done.11.refs_4_
  31.5 1.1 %blocks.1 = f32[2,128,128]{2,1,0:T(8,128)} custom-call(f32[2,8,128]{2,1,0:T(8,128)S(1)} %get-tuple-element.39.refs_7_.refs_0_, bf16[2,384,512]{2,1,0:T(8,128)(2,1)S(1)} %get-tuple-element.40.refs_1_, bf16[2,384,512]{2,1,0:T(8,128)(2,1)S(1)} %mask_other.1.refs_2_, bf16[384,128]{1,0:T(8,128)(2,1)S(1)} %round_out.1.refs_3_, ...), custom_call_target="tpu_custom_call" | custom-call | flops 1 | bytes 1 | tf_op jit(solution)/shard_map/blocks/pallas_call | solution.py:271
  (6 shorter events, 0.1 us)
Async XLA Ops:
  3.3 5.0 %slice-start = ((s8[8388608]{0:T(1024)(128)(4,1)}), s8[4194304]{0:T(1024)(128)(4,1)S(1)}, s32[]{:S(2)}) async-start(s8[8388608]{0:T(1024)(128)(4,1)} %bitcast.1), calls=%async_computation | async-start | bytes 8388608
  3.3 4.9 %slice-start.1 = ((s8[8388608]{0:T(1024)(128)(4,1)}), s8[4194304]{0:T(1024)(128)(4,1)S(1)}, s32[]{:S(2)}) async-start(s8[8388608]{0:T(1024)(128)(4,1)} %bitcast.1), calls=%async_computation.1 | async-start | bytes 8388608
  3.4 1.9 %collective-permute-start = (f32[768,128]{1,0:T(8,128)S(1)}, f32[768,128]{1,0:T(8,128)S(1)}, u32[]{:S(2)}, u32[]{:S(2)}) collective-permute-start(f32[768,128]{1,0:T(8,128)S(1)} %get-tuple-element.29), channel_id=1, source_target_pairs={{0,1},{1,0},{2,3},{3,2},{4,5},{5,4},{6,7},{7,6},{8,9},{9,8},{10,11... | collective-permute-start | bytes 1179656 | tf_op jit(solution)/shard_map/ppermute | solution.py:330
  5.4 20.4 %copy-start = (s32[2]{0:T(128)S(1)}, s32[2]{0:T(128)}, u32[]{:S(2)}) copy-start(s32[2]{0:T(128)} %refs_0_.4) | copy-start | bytes 28
  5.4 8.4 %collective-permute-start.1 = (bf16[784,128]{1,0:T(8,128)(2,1)S(1)}, bf16[784,128]{1,0:T(8,128)(2,1)S(1)}, u32[]{:S(2)}, u32[]{:S(2)}) collective-permute-start(bf16[784,128]{1,0:T(8,128)(2,1)S(1)} %get-tuple-element.33.refs_4_), channel_id=1, source_target_pairs={{0,2},{1,3},{2,0},{3,1},{4,6},{5,7},{6,4},{7,5},{8,10},{9,11},{10,... | collective-permute-start | bytes 602120 | tf_op jit(solution)/shard_map/ppermute | solution.py:335
  12.0 1.5 %collective-permute-start.8 = (f32[384,128]{1,0:T(8,128)S(1)}, f32[384,128]{1,0:T(8,128)S(1)}, u32[]{:S(2)}, u32[]{:S(2)}) collective-permute-start(f32[384,128]{1,0:T(8,128)S(1)} %get-tuple-element.45), channel_id=1, source_target_pairs={{0,1},{1,0},{2,3},{3,2},{4,5},{5,4},{6,7},{7,6},{8,9},{9,8},{10,11... | collective-permute-start | bytes 589832 | tf_op jit(solution)/shard_map/ppermute | solution.py:349
  12.1 1.7 %collective-permute-start.9 = (f32[384,128]{1,0:T(8,128)S(1)}, f32[384,128]{1,0:T(8,128)S(1)}, u32[]{:S(2)}, u32[]{:S(2)}) collective-permute-start(f32[384,128]{1,0:T(8,128)S(1)} %get-tuple-element.46), channel_id=1, source_target_pairs={{0,1},{1,0},{2,3},{3,2},{4,5},{5,4},{6,7},{7,6},{8,9},{9,8},{10,11... | collective-permute-start | bytes 589832 | tf_op jit(solution)/shard_map/ppermute | solution.py:349
  13.9 6.5 %collective-permute-start.10 = (bf16[384,128]{1,0:T(8,128)(2,1)S(1)}, bf16[384,128]{1,0:T(8,128)(2,1)S(1)}, u32[]{:S(2)}, u32[]{:S(2)}) collective-permute-start(bf16[384,128]{1,0:T(8,128)(2,1)S(1)} %get-tuple-element.48), channel_id=1, source_target_pairs={{0,2},{1,3},{2,0},{3,1},{4,6},{5,7},{6,4},{7,5},{8,10},{9,11},{10,... | collective-permute-start | bytes 294920 | tf_op jit(solution)/shard_map/ppermute | solution.py:353
  15.5 8.3 %collective-permute-start.2 = (bf16[208,128]{1,0:T(8,128)(2,1)S(1)}, bf16[208,128]{1,0:T(8,128)(2,1)S(1)}, u32[]{:S(2)}, u32[]{:S(2)}) collective-permute-start(bf16[208,128]{1,0:T(8,128)(2,1)S(1)} %get-tuple-element.36), channel_id=1, source_target_pairs={{0,12},{4,8},{8,4},{12,0},{1,13},{5,9},{9,5},{13,1},{2,14},{6,10},... | collective-permute-start | bytes 159752 | tf_op jit(solution)/shard_map/ppermute | solution.py:306
  19.2 1.2 %collective-permute-start.5 = (bf16[192,128]{1,0:T(8,128)(2,1)S(1)}, bf16[192,128]{1,0:T(8,128)(2,1)S(1)}, u32[]{:S(2)}, u32[]{:S(2)}) collective-permute-start(bf16[192,128]{1,0:T(8,128)(2,1)S(1)} %own_in.1), channel_id=1, source_target_pairs={{0,1},{1,0},{2,3},{3,2},{4,5},{5,4},{6,7},{7,6},{8,9},{9,8},{10,11... | collective-permute-start | bytes 147464 | tf_op jit(solution)/shard_map/ppermute | solution.py:360
  19.2 5.7 %collective-permute-start.3 = (bf16[208,128]{1,0:T(8,128)(2,1)S(1)}, bf16[208,128]{1,0:T(8,128)(2,1)S(1)}, u32[]{:S(2)}, u32[]{:S(2)}) collective-permute-start(bf16[208,128]{1,0:T(8,128)(2,1)S(1)} %get-tuple-element.37), channel_id=1, source_target_pairs={{0,8},{4,12},{8,0},{12,4},{1,9},{5,13},{9,1},{13,5},{2,10},{6,14},... | collective-permute-start | bytes 159752 | tf_op jit(solution)/shard_map/ppermute | solution.py:306
  19.3 5.9 %collective-permute-start.4 = (bf16[208,128]{1,0:T(8,128)(2,1)S(1)}, bf16[208,128]{1,0:T(8,128)(2,1)S(1)}, u32[]{:S(2)}, u32[]{:S(2)}) collective-permute-start(bf16[208,128]{1,0:T(8,128)(2,1)S(1)} %get-tuple-element.38), channel_id=1, source_target_pairs={{0,4},{4,0},{8,12},{12,8},{1,5},{5,1},{9,13},{13,9},{2,6},{6,2},{1... | collective-permute-start | bytes 159752 | tf_op jit(solution)/shard_map/ppermute | solution.py:306
  20.4 10.9 %collective-permute-start.13 = (bf16[384,128]{1,0:T(8,128)(2,1)S(1)}, bf16[384,128]{1,0:T(8,128)(2,1)S(1)}, u32[]{:S(2)}, u32[]{:S(2)}) collective-permute-start(bf16[384,128]{1,0:T(8,128)(2,1)S(1)} %round_out.1.refs_3_), channel_id=1, source_target_pairs={{0,8},{4,12},{8,0},{12,4},{1,9},{5,13},{9,1},{13,5},{2,10},{6,14},... | collective-permute-start | bytes 294920 | tf_op jit(solution)/shard_map/ppermute | solution.py:306
  22.3 9.0 %collective-permute-start.12 = (bf16[384,128]{1,0:T(8,128)(2,1)S(1)}, bf16[384,128]{1,0:T(8,128)(2,1)S(1)}, u32[]{:S(2)}, u32[]{:S(2)}) collective-permute-start(bf16[384,128]{1,0:T(8,128)(2,1)S(1)} %round_out.1.refs_3_), channel_id=1, source_target_pairs={{0,12},{4,8},{8,4},{12,0},{1,13},{5,9},{9,5},{13,1},{2,14},{6,10},... | collective-permute-start | bytes 294920 | tf_op jit(solution)/shard_map/ppermute | solution.py:306
  23.8 7.6 %collective-permute-start.11 = (bf16[384,128]{1,0:T(8,128)(2,1)S(1)}, bf16[384,128]{1,0:T(8,128)(2,1)S(1)}, u32[]{:S(2)}, u32[]{:S(2)}) collective-permute-start(bf16[384,128]{1,0:T(8,128)(2,1)S(1)} %round_out.1.refs_3_), channel_id=1, source_target_pairs={{0,4},{4,0},{8,12},{12,8},{1,5},{5,1},{9,13},{13,9},{2,6},{6,2},{1... | collective-permute-start | bytes 294920 | tf_op jit(solution)/shard_map/ppermute | solution.py:306
  25.2 1.5 %collective-permute-start.6 = (bf16[288,128]{1,0:T(8,128)(2,1)S(1)}, bf16[288,128]{1,0:T(8,128)(2,1)S(1)}, u32[]{:S(2)}, u32[]{:S(2)}) collective-permute-start(bf16[288,128]{1,0:T(8,128)(2,1)S(1)} %get-tuple-element.41), channel_id=1, source_target_pairs={{0,1},{1,0},{2,3},{3,2},{4,5},{5,4},{6,7},{7,6},{8,9},{9,8},{10,11... | collective-permute-start | bytes 221192 | tf_op jit(solution)/shard_map/ppermute | solution.py:365
  25.2 1.4 %collective-permute-start.7 = (bf16[288,128]{1,0:T(8,128)(2,1)S(1)}, bf16[288,128]{1,0:T(8,128)(2,1)S(1)}, u32[]{:S(2)}, u32[]{:S(2)}) collective-permute-start(bf16[288,128]{1,0:T(8,128)(2,1)S(1)} %get-tuple-element.42), channel_id=1, source_target_pairs={{0,1},{1,0},{2,3},{3,2},{4,5},{5,4},{6,7},{7,6},{8,9},{9,8},{10,11... | collective-permute-start | bytes 221192 | tf_op jit(solution)/shard_map/ppermute | solution.py:365

commit v19 on v18

--- a/solution.py
+++ b/solution.py
@@ -118,7 +118,8 @@
     out[...] = choose(pick, grads[...])
 
 
-def rotate_out_kernel(grads, pick, basis_out, early, acc, grads_v, sems):
+def rotate_out_kernel(grads, pick, basis_out, early, *refs):
+    *split, acc, grads_v, sems = refs
     hidden = grads.shape[2]
     experts, cap, _ = acc.shape
     fetch = fetcher(sems)
@@ -136,9 +137,10 @@
         chosen = choose(pick, grads_v[:, :, pl.ds(at - done, part.size)])
         for e in range(experts):
             acc[e] += dot(chosen[e * cap : (e + 1) * cap], basis_out[e, part, :])
-
-
-def split_out_kernel(acc, *refs):
+    split_out(acc, *split)
+
+
+def split_out(acc, *refs):
     experts, cap, width = acc.shape
     core = lax.rem(lax.axis_index("tensor"), 2)
     for e in range(experts):
@@ -158,8 +160,13 @@
 
 
 def round_in_kernel(kept, got, label, *pays):
+    *pays, own = pays
     slab = kept.shape[0] // len(pays)
     d = lax.axis_index("dp")
+    own[...] = (
+        kept[pl.ds(pl.multiple_of(d * slab, 16), slab), :]
+        + got[pl.ds(pl.multiple_of(d * slab, 16), slab), :].astype(F32)
+    ).astype(BF16)
     for k, pay in enumerate(pays):
         rows = pl.ds(pl.multiple_of((d ^ k) * slab, 16), slab)
         pay[:slab, :] = (kept[rows, :] + got[rows, :].astype(F32)).astype(BF16)
@@ -182,10 +189,6 @@
 
 def round_kernel(kept, got, out):
     out[...] = (kept[...] + got[...].astype(F32)).astype(BF16)
-
-
-def copy_kernel(x, out):
-    out[...] = x[: out.shape[0], :]
 
 
 def stack_kernel(*refs):
@@ -334,18 +337,18 @@
     )(keep, got)
     got_in = lax.ppermute(send_in, "tensor", across)
 
-    acc = call(
+    split = call(
         rotate_out_kernel,
         "rotate_out",
-        partial,
+        [rows(2 * cap, F32)] * (2 * experts),
         [hbm, vmem, vmem, vmem],
         [
+            pltpu.VMEM(partial.shape, F32),
             pltpu.VMEM((tokens, 2, grads.shape[2] - EARLY), BF16),
             pltpu.SemaphoreType.DMA((grads.shape[2] // CHUNK + 1,)),
         ],
         after=[send_in],
     )(pin(grads), pick, basis_out, early)
-    split = call(split_out_kernel, "split_out", [rows(2 * cap, F32)] * (2 * experts))(acc)
     got = [lax.ppermute(x, "tensor", core) for x in split[experts:]]
     keep, send = call(
         pair_out_kernel, "pair_out", (rows(wide, F32), rows(wide, BF16)), after=[got_in]
@@ -353,10 +356,9 @@
     got = lax.ppermute(send, "tensor", across)
 
     slab = half // dp
-    pieces = call(round_in_kernel, "round_in", [rows(slab + LABEL_ROWS, BF16)] * dp)(
-        keep_in, got_in, label
-    )
-    own = call(copy_kernel, "own_in", rows(slab, BF16))(pieces[0])
+    *pieces, own = call(
+        round_in_kernel, "round_in", [rows(slab + LABEL_ROWS, BF16)] * dp + [rows(slab, BF16)]
+    )(keep_in, got_in, label)
     other = [lax.ppermute(own, "tensor", core)]
     pieces = [pieces[0]] + [swap(pieces[k], k) for k in DISTANCES]
     out = call(round_kernel, "round_out", rows(wide, BF16), after=other)(keep, got)

time: 32.8 us -> 32.7 us (level)
    pallas_call x14 -> x12, Pallas kernels: 11.1 us -> 11.1 us  [run(): pl.pallas_call(body, out_shape=out_shape, in_specs=(specs or [vmem] * len...]
where the time goes in v19:
time: 32.7 us; the launch traced here: 32.6 us
  starting transfers between devices  14.3 us (44%)
  Pallas kernels  11.1 us (34%)
  waiting for transfers between devices  6.99 us (21%)
    pallas_call x12, Pallas kernels, run(): pl.pallas_call(body, out_shape=out_shape, in_specs=(specs or [vmem] * len...  11.1 us
    ppermute x6, starting transfers between devices, swap(): return lax.ppermute(x, 'dp', [(d, d ^ k) for d in range(dp)])  8.25 us
    ppermute x6, waiting for transfers between devices, swap(): return lax.ppermute(x, 'dp', [(d, d ^ k) for d in range(dp)])  5.32 us
    ppermute x1, starting transfers between devices, fast(): got_in = lax.ppermute(send_in, 'tensor', across)  2.86 us
    ppermute x1, starting transfers between devices, fast(): got = lax.ppermute(send, 'tensor', across)  1.58 us
    ppermute x2, waiting for transfers between devices, fast(): got = [lax.ppermute(x, 'tensor', core) for x in split[experts:]]  1.21 us
  transfers between devices with their start and end apart: 14, of which 7 were waited for; matrix products, arithmetic and copies ran while one was open for 0% of the time, Pallas kernels for 20%

profile of v19, /device:TPU:0, one launch (start us, length us, event | category | flops | bytes accessed | tf_op | source)
XLA Modules:
  0.0 32.6 jit_solution(12297710804167611565)
XLA Ops:
  0.0 3.3 %rotate_in.1 = (f32[2,192,512]{2,1,0:T(8,128)S(1)}, bf16[16,128]{1,0:T(8,128)(2,1)S(1)}, bf16[384,768]{1,0:T(8,128)(2,1)S(1)}, bf16[384,2,2048]{2,1,0:T(2,128)(2,1)S(1)}) custom-call(bf16[384,1536]{1,0:T(8,128)(2,1)} %refs_0_.3, s32[2,384]{1,0:T(2,128)} %bitcast.3, s32[384]{0:T(512)} %refs_2_.2, bf16[2,1536,512]{2,1,0:T(8,128)(2,1)} %refs_3_.1, ...), custom_call_target="tpu_custom_call" | custom-call | flops 1 | bytes 1 | tf_op jit(solution)/shard_map/rotate_in/pallas_call | solution.py:274
  3.3 0.0 slice-start
  3.3 0.0 slice-start.1
  3.3 0.1 split_in.1
  3.4 0.5 %collective-permute-start = (f32[768,128]{1,0:T(8,128)S(1)}, f32[768,128]{1,0:T(8,128)S(1)}, u32[]{:S(2)}, u32[]{:S(2)}) collective-permute-start(f32[768,128]{1,0:T(8,128)S(1)} %get-tuple-element.30), channel_id=1, source_target_pairs={{0,1},{1,0},{2,3},{3,2},{4,5},{5,4},{6,7},{7,6},{8,9},{9,8},{10,11... | collective-permute-start | bytes 1179656 | tf_op jit(solution)/shard_map/ppermute | solution.py:333
  3.9 1.4 %choose.1.refs_2_.refs_3_ = bf16[384,2048]{1,0:T(8,128)(2,1)S(1)} custom-call(bf16[384,2,2048]{2,1,0:T(2,128)(2,1)S(1)} %get-tuple-element.31.refs_0_, bf16[384,768]{1,0:T(8,128)(2,1)S(1)} %get-tuple-element.32.refs_1_), custom_call_target="tpu_custom_call" | custom-call | flops 1 | bytes 1 | tf_op jit(solution)/shard_map/choose/pallas_call | solution.py:274
  5.3 0.0 collective-permute-done.refs_1_
  5.4 0.0 copy-start
  5.4 2.9 %collective-permute-start.1 = (bf16[784,128]{1,0:T(8,128)(2,1)S(1)}, bf16[784,128]{1,0:T(8,128)(2,1)S(1)}, u32[]{:S(2)}, u32[]{:S(2)}) collective-permute-start(bf16[784,128]{1,0:T(8,128)(2,1)S(1)} %get-tuple-element.34.refs_4_), channel_id=1, source_target_pairs={{0,2},{1,3},{2,0},{3,1},{4,6},{5,7},{6,4},{7,5},{8,10},{9,11},{10,... | collective-permute-start | bytes 602120 | tf_op jit(solution)/shard_map/ppermute | solution.py:338
  8.2 0.0 slice-done
  8.2 0.0 slice-done.1
  8.3 3.8 %rotate_out.1 = (f32[384,128]{1,0:T(8,128)S(1)}, f32[384,128]{1,0:T(8,128)S(1)}, f32[384,128]{1,0:T(8,128)S(1)}, f32[384,128]{1,0:T(8,128)S(1)}) custom-call(bf16[384,2,4096]{2,1,0:T(2,128)(2,1)} %refs_0_.5, bf16[384,768]{1,0:T(8,128)(2,1)S(1)} %get-tuple-element.32.refs_1_, bf16[2,4096,512]{2,1,0:T(8,128)(2,1)S(1)} %bitcast.2, ...), custom_call_target="tpu_custom_call" | custom-call | flops 1 | bytes 1 | tf_op jit(solution)/shard_map/rotate_out/pallas_call | solution.py:274
  12.0 0.1 collective-permute-start.8
  12.1 0.5 %collective-permute-start.9 = (f32[384,128]{1,0:T(8,128)S(1)}, f32[384,128]{1,0:T(8,128)S(1)}, u32[]{:S(2)}, u32[]{:S(2)}) collective-permute-start(f32[384,128]{1,0:T(8,128)S(1)} %get-tuple-element.48), channel_id=1, source_target_pairs={{0,1},{1,0},{2,3},{3,2},{4,5},{5,4},{6,7},{7,6},{8,9},{9,8},{10,11... | collective-permute-start | bytes 589832 | tf_op jit(solution)/shard_map/ppermute | solution.py:352
  12.6 0.9 %collective-permute-done.8.refs_2_ = f32[384,128]{1,0:T(8,128)S(1)} collective-permute-done((f32[384,128]{1,0:T(8,128)S(1)}, f32[384,128]{1,0:T(8,128)S(1)}, u32[]{:S(2)}, u32[]{:S(2)}) %collective-permute-start.8) | collective-permute-done | bytes 196640 | tf_op jit(solution)/shard_map/ppermute | solution.py:352
  13.5 0.3 collective-permute-done.9.refs_3_
  13.8 0.0 collective-permute-done.1.refs_1_.refs_4_
  13.9 1.6 %collective-permute-start.10 = (bf16[384,128]{1,0:T(8,128)(2,1)S(1)}, bf16[384,128]{1,0:T(8,128)(2,1)S(1)}, u32[]{:S(2)}, u32[]{:S(2)}) collective-permute-start(bf16[384,128]{1,0:T(8,128)(2,1)S(1)} %get-tuple-element.50), channel_id=1, source_target_pairs={{0,2},{1,3},{2,0},{3,1},{4,6},{5,7},{6,4},{7,5},{8,10},{9,11},{10,... | collective-permute-start | bytes 294920 | tf_op jit(solution)/shard_map/ppermute | solution.py:356
  15.5 0.1 round_in.1
  15.5 3.7 %collective-permute-start.2 = (bf16[208,128]{1,0:T(8,128)(2,1)S(1)}, bf16[208,128]{1,0:T(8,128)(2,1)S(1)}, u32[]{:S(2)}, u32[]{:S(2)}) collective-permute-start(bf16[208,128]{1,0:T(8,128)(2,1)S(1)} %get-tuple-element.37), channel_id=1, source_target_pairs={{0,12},{4,8},{8,4},{12,0},{1,13},{5,9},{9,5},{13,1},{2,14},{6,10},... | collective-permute-start | bytes 159752 | tf_op jit(solution)/shard_map/ppermute | solution.py:309
  19.2 0.0 collective-permute-start.5
  19.2 0.0 collective-permute-start.3
  19.2 0.8 %collective-permute-start.4 = (bf16[208,128]{1,0:T(8,128)(2,1)S(1)}, bf16[208,128]{1,0:T(8,128)(2,1)S(1)}, u32[]{:S(2)}, u32[]{:S(2)}) collective-permute-start(bf16[208,128]{1,0:T(8,128)(2,1)S(1)} %get-tuple-element.39), channel_id=1, source_target_pairs={{0,4},{4,0},{8,12},{12,8},{1,5},{5,1},{9,13},{13,9},{2,6},{6,2},{1... | collective-permute-start | bytes 159752 | tf_op jit(solution)/shard_map/ppermute | solution.py:309
  20.0 0.4 %collective-permute-done.5.refs_0_.refs_2_ = bf16[192,128]{1,0:T(8,128)(2,1)S(1)} collective-permute-done((bf16[192,128]{1,0:T(8,128)(2,1)S(1)}, bf16[192,128]{1,0:T(8,128)(2,1)S(1)}, u32[]{:S(2)}, u32[]{:S(2)}) %collective-permute-start.5) | collective-permute-done | bytes 49184 | tf_op jit(solution)/shard_map/ppermute | solution.py:362
  20.4 0.0 collective-permute-done.10.refs_1_
  20.4 1.8 %collective-permute-start.13 = (bf16[384,128]{1,0:T(8,128)(2,1)S(1)}, bf16[384,128]{1,0:T(8,128)(2,1)S(1)}, u32[]{:S(2)}, u32[]{:S(2)}) collective-permute-start(bf16[384,128]{1,0:T(8,128)(2,1)S(1)} %round_out.1.refs_3_), channel_id=1, source_target_pairs={{0,8},{4,12},{8,0},{12,4},{1,9},{5,13},{9,1},{13,5},{2,10},{6,14},... | collective-permute-start | bytes 294920 | tf_op jit(solution)/shard_map/ppermute | solution.py:309
  22.2 1.5 %collective-permute-start.12 = (bf16[384,128]{1,0:T(8,128)(2,1)S(1)}, bf16[384,128]{1,0:T(8,128)(2,1)S(1)}, u32[]{:S(2)}, u32[]{:S(2)}) collective-permute-start(bf16[384,128]{1,0:T(8,128)(2,1)S(1)} %round_out.1.refs_3_), channel_id=1, source_target_pairs={{0,12},{4,8},{8,4},{12,0},{1,13},{5,9},{9,5},{13,1},{2,14},{6,10},... | collective-permute-start | bytes 294920 | tf_op jit(solution)/shard_map/ppermute | solution.py:309
  23.7 0.0 collective-permute-done.2.refs_2_.refs_0_.refs_4_
  23.8 0.5 %collective-permute-start.11 = (bf16[384,128]{1,0:T(8,128)(2,1)S(1)}, bf16[384,128]{1,0:T(8,128)(2,1)S(1)}, u32[]{:S(2)}, u32[]{:S(2)}) collective-permute-start(bf16[384,128]{1,0:T(8,128)(2,1)S(1)} %round_out.1.refs_3_), channel_id=1, source_target_pairs={{0,4},{4,0},{8,12},{12,8},{1,5},{5,1},{9,13},{13,9},{2,6},{6,2},{1... | collective-permute-start | bytes 294920 | tf_op jit(solution)/shard_map/ppermute | solution.py:309
  24.2 0.6 %collective-permute-done.3.refs_3_.refs_1_.refs_5_ = bf16[208,128]{1,0:T(8,128)(2,1)S(1)} collective-permute-done((bf16[208,128]{1,0:T(8,128)(2,1)S(1)}, bf16[208,128]{1,0:T(8,128)(2,1)S(1)}, u32[]{:S(2)}, u32[]{:S(2)}) %collective-permute-start.3) | collective-permute-done | bytes 53280 | tf_op jit(solution)/shard_map/ppermute | solution.py:309
  24.8 0.3 collective-permute-done.4.refs_4_.refs_2_.refs_6_
  25.1 0.1 collective-permute-start.6
  25.2 0.5 %collective-permute-start.7 = (bf16[288,128]{1,0:T(8,128)(2,1)S(1)}, bf16[288,128]{1,0:T(8,128)(2,1)S(1)}, u32[]{:S(2)}, u32[]{:S(2)}) collective-permute-start(bf16[288,128]{1,0:T(8,128)(2,1)S(1)} %get-tuple-element.44), channel_id=1, source_target_pairs={{0,1},{1,0},{2,3},{3,2},{4,5},{5,4},{6,7},{7,6},{8,9},{9,8},{10,11... | collective-permute-start | bytes 221192 | tf_op jit(solution)/shard_map/ppermute | solution.py:367
  25.7 0.0 copy-done
  25.7 0.9 %mask_own.1 = (bf16[2,384,512]{2,1,0:T(8,128)(2,1)S(1)}, f32[2,8,128]{2,1,0:T(8,128)S(1)}) custom-call(s32[2]{0:T(128)S(1)} %copy-done, bf16[208,128]{1,0:T(8,128)(2,1)S(1)} %get-tuple-element.36.refs_1_.refs_3_, bf16[208,128]{1,0:T(8,128)(2,1)S(1)} %collective-permute-done.2.refs_2_.refs_0_.refs_4_, ...), custom_call_target="tpu_custom_call" | custom-call | flops 1 | bytes 1 | tf_op jit(solution)/shard_map/mask_own/pallas_call | solution.py:274
  26.6 0.0 collective-permute-done.6.refs_1_
  26.6 0.0 collective-permute-done.7.refs_2_
  26.6 0.3 %mask_other.1.refs_2_ = bf16[2,384,512]{2,1,0:T(8,128)(2,1)S(1)} custom-call(bf16[192,128]{1,0:T(8,128)(2,1)S(1)} %collective-permute-done.5.refs_0_.refs_2_, bf16[288,128]{1,0:T(8,128)(2,1)S(1)} %collective-permute-done.6.refs_1_, bf16[288,128]{1,0:T(8,128)(2,1)S(1)} %collective-permute-done.7.refs_2_, ...), custom_call_target="tpu_custom_call" | custom-call | flops 1 | bytes 1 | tf_op jit(solution)/shard_map/mask_other/pallas_call | solution.py:274
  27.0 4.3 %collective-permute-done.13.refs_6_ = bf16[384,128]{1,0:T(8,128)(2,1)S(1)} collective-permute-done((bf16[384,128]{1,0:T(8,128)(2,1)S(1)}, bf16[384,128]{1,0:T(8,128)(2,1)S(1)}, u32[]{:S(2)}, u32[]{:S(2)}) %collective-permute-start.13) | collective-permute-done | bytes 98336 | tf_op jit(solution)/shard_map/ppermute | solution.py:309
  31.3 0.0 collective-permute-done.12.refs_5_
  31.3 0.1 collective-permute-done.11.refs_4_
  31.4 1.1 %blocks.1 = f32[2,128,128]{2,1,0:T(8,128)} custom-call(f32[2,8,128]{2,1,0:T(8,128)S(1)} %get-tuple-element.40.refs_7_.refs_0_, bf16[2,384,512]{2,1,0:T(8,128)(2,1)S(1)} %get-tuple-element.41.refs_1_, bf16[2,384,512]{2,1,0:T(8,128)(2,1)S(1)} %mask_other.1.refs_2_, bf16[384,128]{1,0:T(8,128)(2,1)S(1)} %round_out.1.refs_3_, ...), custom_call_target="tpu_custom_call" | custom-call | flops 1 | bytes 1 | tf_op jit(solution)/shard_map/blocks/pallas_call | solution.py:274
  (5 shorter events, 0.1 us)
Async XLA Ops:
  3.3 5.0 %slice-start = ((s8[8388608]{0:T(1024)(128)(4,1)}), s8[4194304]{0:T(1024)(128)(4,1)S(1)}, s32[]{:S(2)}) async-start(s8[8388608]{0:T(1024)(128)(4,1)} %bitcast.1), calls=%async_computation | async-start | bytes 8388608
  3.3 4.9 %slice-start.1 = ((s8[8388608]{0:T(1024)(128)(4,1)}), s8[4194304]{0:T(1024)(128)(4,1)S(1)}, s32[]{:S(2)}) async-start(s8[8388608]{0:T(1024)(128)(4,1)} %bitcast.1), calls=%async_computation.1 | async-start | bytes 8388608
  3.4 1.9 %collective-permute-start = (f32[768,128]{1,0:T(8,128)S(1)}, f32[768,128]{1,0:T(8,128)S(1)}, u32[]{:S(2)}, u32[]{:S(2)}) collective-permute-start(f32[768,128]{1,0:T(8,128)S(1)} %get-tuple-element.30), channel_id=1, source_target_pairs={{0,1},{1,0},{2,3},{3,2},{4,5},{5,4},{6,7},{7,6},{8,9},{9,8},{10,11... | collective-permute-start | bytes 1179656 | tf_op jit(solution)/shard_map/ppermute | solution.py:333
  5.4 20.3 %copy-start = (s32[2]{0:T(128)S(1)}, s32[2]{0:T(128)}, u32[]{:S(2)}) copy-start(s32[2]{0:T(128)} %refs_0_.4) | copy-start | bytes 28
  5.4 8.4 %collective-permute-start.1 = (bf16[784,128]{1,0:T(8,128)(2,1)S(1)}, bf16[784,128]{1,0:T(8,128)(2,1)S(1)}, u32[]{:S(2)}, u32[]{:S(2)}) collective-permute-start(bf16[784,128]{1,0:T(8,128)(2,1)S(1)} %get-tuple-element.34.refs_4_), channel_id=1, source_target_pairs={{0,2},{1,3},{2,0},{3,1},{4,6},{5,7},{6,4},{7,5},{8,10},{9,11},{10,... | collective-permute-start | bytes 602120 | tf_op jit(solution)/shard_map/ppermute | solution.py:338
  12.0 1.5 %collective-permute-start.8 = (f32[384,128]{1,0:T(8,128)S(1)}, f32[384,128]{1,0:T(8,128)S(1)}, u32[]{:S(2)}, u32[]{:S(2)}) collective-permute-start(f32[384,128]{1,0:T(8,128)S(1)} %get-tuple-element.47), channel_id=1, source_target_pairs={{0,1},{1,0},{2,3},{3,2},{4,5},{5,4},{6,7},{7,6},{8,9},{9,8},{10,11... | collective-permute-start | bytes 589832 | tf_op jit(solution)/shard_map/ppermute | solution.py:352
  12.1 1.7 %collective-permute-start.9 = (f32[384,128]{1,0:T(8,128)S(1)}, f32[384,128]{1,0:T(8,128)S(1)}, u32[]{:S(2)}, u32[]{:S(2)}) collective-permute-start(f32[384,128]{1,0:T(8,128)S(1)} %get-tuple-element.48), channel_id=1, source_target_pairs={{0,1},{1,0},{2,3},{3,2},{4,5},{5,4},{6,7},{7,6},{8,9},{9,8},{10,11... | collective-permute-start | bytes 589832 | tf_op jit(solution)/shard_map/ppermute | solution.py:352
  13.9 6.5 %collective-permute-start.10 = (bf16[384,128]{1,0:T(8,128)(2,1)S(1)}, bf16[384,128]{1,0:T(8,128)(2,1)S(1)}, u32[]{:S(2)}, u32[]{:S(2)}) collective-permute-start(bf16[384,128]{1,0:T(8,128)(2,1)S(1)} %get-tuple-element.50), channel_id=1, source_target_pairs={{0,2},{1,3},{2,0},{3,1},{4,6},{5,7},{6,4},{7,5},{8,10},{9,11},{10,... | collective-permute-start | bytes 294920 | tf_op jit(solution)/shard_map/ppermute | solution.py:356
  15.5 8.2 %collective-permute-start.2 = (bf16[208,128]{1,0:T(8,128)(2,1)S(1)}, bf16[208,128]{1,0:T(8,128)(2,1)S(1)}, u32[]{:S(2)}, u32[]{:S(2)}) collective-permute-start(bf16[208,128]{1,0:T(8,128)(2,1)S(1)} %get-tuple-element.37), channel_id=1, source_target_pairs={{0,12},{4,8},{8,4},{12,0},{1,13},{5,9},{9,5},{13,1},{2,14},{6,10},... | collective-permute-start | bytes 159752 | tf_op jit(solution)/shard_map/ppermute | solution.py:309
  19.2 1.2 %collective-permute-start.5 = (bf16[192,128]{1,0:T(8,128)(2,1)S(1)}, bf16[192,128]{1,0:T(8,128)(2,1)S(1)}, u32[]{:S(2)}, u32[]{:S(2)}) collective-permute-start(bf16[192,128]{1,0:T(8,128)(2,1)S(1)} %get-tuple-element.42), channel_id=1, source_target_pairs={{0,1},{1,0},{2,3},{3,2},{4,5},{5,4},{6,7},{7,6},{8,9},{9,8},{10,11... | collective-permute-start | bytes 147464 | tf_op jit(solution)/shard_map/ppermute | solution.py:362
  19.2 5.7 %collective-permute-start.3 = (bf16[208,128]{1,0:T(8,128)(2,1)S(1)}, bf16[208,128]{1,0:T(8,128)(2,1)S(1)}, u32[]{:S(2)}, u32[]{:S(2)}) collective-permute-start(bf16[208,128]{1,0:T(8,128)(2,1)S(1)} %get-tuple-element.38), channel_id=1, source_target_pairs={{0,8},{4,12},{8,0},{12,4},{1,9},{5,13},{9,1},{13,5},{2,10},{6,14},... | collective-permute-start | bytes 159752 | tf_op jit(solution)/shard_map/ppermute | solution.py:309
  19.2 5.9 %collective-permute-start.4 = (bf16[208,128]{1,0:T(8,128)(2,1)S(1)}, bf16[208,128]{1,0:T(8,128)(2,1)S(1)}, u32[]{:S(2)}, u32[]{:S(2)}) collective-permute-start(bf16[208,128]{1,0:T(8,128)(2,1)S(1)} %get-tuple-element.39), channel_id=1, source_target_pairs={{0,4},{4,0},{8,12},{12,8},{1,5},{5,1},{9,13},{13,9},{2,6},{6,2},{1... | collective-permute-start | bytes 159752 | tf_op jit(solution)/shard_map/ppermute | solution.py:309
  20.4 10.9 %collective-permute-start.13 = (bf16[384,128]{1,0:T(8,128)(2,1)S(1)}, bf16[384,128]{1,0:T(8,128)(2,1)S(1)}, u32[]{:S(2)}, u32[]{:S(2)}) collective-permute-start(bf16[384,128]{1,0:T(8,128)(2,1)S(1)} %round_out.1.refs_3_), channel_id=1, source_target_pairs={{0,8},{4,12},{8,0},{12,4},{1,9},{5,13},{9,1},{13,5},{2,10},{6,14},... | collective-permute-start | bytes 294920 | tf_op jit(solution)/shard_map/ppermute | solution.py:309
  22.2 9.1 %collective-permute-start.12 = (bf16[384,128]{1,0:T(8,128)(2,1)S(1)}, bf16[384,128]{1,0:T(8,128)(2,1)S(1)}, u32[]{:S(2)}, u32[]{:S(2)}) collective-permute-start(bf16[384,128]{1,0:T(8,128)(2,1)S(1)} %round_out.1.refs_3_), channel_id=1, source_target_pairs={{0,12},{4,8},{8,4},{12,0},{1,13},{5,9},{9,5},{13,1},{2,14},{6,10},... | collective-permute-start | bytes 294920 | tf_op jit(solution)/shard_map/ppermute | solution.py:309
  23.8 7.7 %collective-permute-start.11 = (bf16[384,128]{1,0:T(8,128)(2,1)S(1)}, bf16[384,128]{1,0:T(8,128)(2,1)S(1)}, u32[]{:S(2)}, u32[]{:S(2)}) collective-permute-start(bf16[384,128]{1,0:T(8,128)(2,1)S(1)} %round_out.1.refs_3_), channel_id=1, source_target_pairs={{0,4},{4,0},{8,12},{12,8},{1,5},{5,1},{9,13},{13,9},{2,6},{6,2},{1... | collective-permute-start | bytes 294920 | tf_op jit(solution)/shard_map/ppermute | solution.py:309
  25.1 1.5 %collective-permute-start.6 = (bf16[288,128]{1,0:T(8,128)(2,1)S(1)}, bf16[288,128]{1,0:T(8,128)(2,1)S(1)}, u32[]{:S(2)}, u32[]{:S(2)}) collective-permute-start(bf16[288,128]{1,0:T(8,128)(2,1)S(1)} %get-tuple-element.43), channel_id=1, source_target_pairs={{0,1},{1,0},{2,3},{3,2},{4,5},{5,4},{6,7},{7,6},{8,9},{9,8},{10,11... | collective-permute-start | bytes 221192 | tf_op jit(solution)/shard_map/ppermute | solution.py:367
  25.2 1.4 %collective-permute-start.7 = (bf16[288,128]{1,0:T(8,128)(2,1)S(1)}, bf16[288,128]{1,0:T(8,128)(2,1)S(1)}, u32[]{:S(2)}, u32[]{:S(2)}) collective-permute-start(bf16[288,128]{1,0:T(8,128)(2,1)S(1)} %get-tuple-element.44), channel_id=1, source_target_pairs={{0,1},{1,0},{2,3},{3,2},{4,5},{5,4},{6,7},{7,6},{8,9},{9,8},{10,11... | collective-permute-start | bytes 221192 | tf_op jit(solution)/shard_map/ppermute | solution.py:367

commit v20 on v18

--- a/solution.py
+++ b/solution.py
@@ -111,7 +111,19 @@
 
 
 def choose(pick, rows):
-    return dot(pick[...], rows.reshape(2 * rows.shape[0], rows.shape[2])).astype(BF16)
+    rows = rows.reshape(2 * rows.shape[0], rows.shape[2])
+    cap, first = rows.shape[0] // 4, 128
+    starts = range(0, pick.shape[0], cap)
+    low = dot(
+        jnp.concatenate([pick[at : at + first, : 2 * first] for at in starts], axis=0),
+        rows[: 2 * first],
+    )
+    high = dot(pick[:, 2 * first :], rows[2 * first :])
+    parts = []
+    for e, at in enumerate(starts):
+        parts.append(high[at : at + first] + low[e * first : (e + 1) * first])
+        parts.append(high[at + first : at + cap])
+    return jnp.concatenate(parts, axis=0).astype(BF16)
 
 
 def choose_kernel(grads, pick, out):

time: 32.8 us -> 32.7 us (level)
  transfers between devices with their start and end apart: 14 -> 14, of which waited for: 7 -> 8; matrix products, arithmetic and copies ran while one was open for 0% -> 0% of each run, Pallas kernels for 20% -> 19%
where the time goes in v20:
time: 32.7 us; the launch traced here: 32.5 us
  starting transfers between devices  14.6 us (45%)
  Pallas kernels  10.8 us (33%)
  waiting for transfers between devices  6.96 us (21%)
    pallas_call x14, Pallas kernels, run(): pl.pallas_call(body, out_shape=out_shape, in_specs=(specs or [vmem] * len...  10.8 us
    ppermute x6, starting transfers between devices, swap(): return lax.ppermute(x, 'dp', [(d, d ^ k) for d in range(dp)])  8.36 us
    ppermute x6, waiting for transfers between devices, swap(): return lax.ppermute(x, 'dp', [(d, d ^ k) for d in range(dp)])  5.29 us
    ppermute x1, starting transfers between devices, fast(): got_in = lax.ppermute(send_in, 'tensor', across)  2.92 us
    ppermute x1, starting transfers between devices, fast(): got = lax.ppermute(send, 'tensor', across)  1.65 us
    ppermute x2, waiting for transfers between devices, fast(): got = [lax.ppermute(x, 'tensor', core) for x in split[experts:]]  1.21 us
  transfers between devices with their start and end apart: 14, of which 8 were waited for; matrix products, arithmetic and copies ran while one was open for 0% of the time, Pallas kernels for 19%

profile of v20, /device:TPU:0, one launch (start us, length us, event | category | flops | bytes accessed | tf_op | source)
XLA Modules:
  0.0 32.5 jit_solution(4811624049146084276)
XLA Ops:
  0.0 3.3 %rotate_in.1 = (f32[2,192,512]{2,1,0:T(8,128)S(1)}, bf16[16,128]{1,0:T(8,128)(2,1)S(1)}, bf16[384,768]{1,0:T(8,128)(2,1)S(1)}, bf16[384,2,2048]{2,1,0:T(2,128)(2,1)S(1)}) custom-call(bf16[384,1536]{1,0:T(8,128)(2,1)} %refs_0_.3, s32[2,384]{1,0:T(2,128)} %bitcast.3, s32[384]{0:T(512)} %refs_2_.2, bf16[2,1536,512]{2,1,0:T(8,128)(2,1)} %refs_3_.1, ...), custom_call_target="tpu_custom_call" | custom-call | flops 1 | bytes 1 | tf_op jit(solution)/shard_map/rotate_in/pallas_call | solution.py:283
  3.3 0.0 slice-start
  3.3 0.0 slice-start.1
  3.3 0.1 split_in.1
  3.4 0.5 %collective-permute-start = (f32[768,128]{1,0:T(8,128)S(1)}, f32[768,128]{1,0:T(8,128)S(1)}, u32[]{:S(2)}, u32[]{:S(2)}) collective-permute-start(f32[768,128]{1,0:T(8,128)S(1)} %get-tuple-element.29), channel_id=1, source_target_pairs={{0,1},{1,0},{2,3},{3,2},{4,5},{5,4},{6,7},{7,6},{8,9},{9,8},{10,11... | collective-permute-start | bytes 1179656 | tf_op jit(solution)/shard_map/ppermute | solution.py:342
  3.9 1.3 %choose.1.refs_2_.refs_3_ = bf16[384,2048]{1,0:T(8,128)(2,1)S(1)} custom-call(bf16[384,2,2048]{2,1,0:T(2,128)(2,1)S(1)} %get-tuple-element.30.refs_0_, bf16[384,768]{1,0:T(8,128)(2,1)S(1)} %get-tuple-element.31.refs_1_), custom_call_target="tpu_custom_call" | custom-call | flops 1 | bytes 1 | tf_op jit(solution)/shard_map/choose/pallas_call | solution.py:283
  5.2 0.1 collective-permute-done.refs_1_
  5.3 0.0 copy-start
  5.3 2.9 %collective-permute-start.1 = (bf16[784,128]{1,0:T(8,128)(2,1)S(1)}, bf16[784,128]{1,0:T(8,128)(2,1)S(1)}, u32[]{:S(2)}, u32[]{:S(2)}) collective-permute-start(bf16[784,128]{1,0:T(8,128)(2,1)S(1)} %get-tuple-element.33.refs_4_), channel_id=1, source_target_pairs={{0,2},{1,3},{2,0},{3,1},{4,6},{5,7},{6,4},{7,5},{8,10},{9,11},{10,... | collective-permute-start | bytes 602120 | tf_op jit(solution)/shard_map/ppermute | solution.py:347
  8.2 0.0 slice-done
  8.2 0.0 slice-done.1
  8.3 3.5 %rotate_out.1.refs_0_ = f32[2,192,512]{2,1,0:T(8,128)S(1)} custom-call(bf16[384,2,4096]{2,1,0:T(2,128)(2,1)} %refs_0_.5, bf16[384,768]{1,0:T(8,128)(2,1)S(1)} %get-tuple-element.31.refs_1_, bf16[2,4096,512]{2,1,0:T(8,128)(2,1)S(1)} %bitcast.2, bf16[384,2048]{1,0:T(8,128)(2,1)S(1)} %choose.1.refs_2_.refs_3_, bf16[784,128]{1,0:T(8,128)(2,1)S(1)} %get-tuple-element.33.refs_4_), custom_call_target="tpu_custom_call" | custom-call | flops 1 | bytes 1 | tf_op jit(solution)/shard_map/rotate_out/pallas_call | solution.py:283
  11.8 0.1 split_out.1
  11.9 0.1 collective-permute-start.8
  12.0 0.5 %collective-permute-start.9 = (f32[384,128]{1,0:T(8,128)S(1)}, f32[384,128]{1,0:T(8,128)S(1)}, u32[]{:S(2)}, u32[]{:S(2)}) collective-permute-start(f32[384,128]{1,0:T(8,128)S(1)} %get-tuple-element.46), channel_id=1, source_target_pairs={{0,1},{1,0},{2,3},{3,2},{4,5},{5,4},{6,7},{7,6},{8,9},{9,8},{10,11... | collective-permute-start | bytes 589832 | tf_op jit(solution)/shard_map/ppermute | solution.py:361
  12.5 0.9 %collective-permute-done.8.refs_2_ = f32[384,128]{1,0:T(8,128)S(1)} collective-permute-done((f32[384,128]{1,0:T(8,128)S(1)}, f32[384,128]{1,0:T(8,128)S(1)}, u32[]{:S(2)}, u32[]{:S(2)}) %collective-permute-start.8) | collective-permute-done | bytes 196640 | tf_op jit(solution)/shard_map/ppermute | solution.py:361
  13.4 0.3 collective-permute-done.9.refs_3_
  13.7 0.0 collective-permute-done.1.refs_1_.refs_4_
  13.7 1.7 %collective-permute-start.10 = (bf16[384,128]{1,0:T(8,128)(2,1)S(1)}, bf16[384,128]{1,0:T(8,128)(2,1)S(1)}, u32[]{:S(2)}, u32[]{:S(2)}) collective-permute-start(bf16[384,128]{1,0:T(8,128)(2,1)S(1)} %get-tuple-element.48), channel_id=1, source_target_pairs={{0,2},{1,3},{2,0},{3,1},{4,6},{5,7},{6,4},{7,5},{8,10},{9,11},{10,... | collective-permute-start | bytes 294920 | tf_op jit(solution)/shard_map/ppermute | solution.py:365
  15.4 0.1 round_in.1
  15.4 3.7 %collective-permute-start.2 = (bf16[208,128]{1,0:T(8,128)(2,1)S(1)}, bf16[208,128]{1,0:T(8,128)(2,1)S(1)}, u32[]{:S(2)}, u32[]{:S(2)}) collective-permute-start(bf16[208,128]{1,0:T(8,128)(2,1)S(1)} %get-tuple-element.36), channel_id=1, source_target_pairs={{0,12},{4,8},{8,4},{12,0},{1,13},{5,9},{9,5},{13,1},{2,14},{6,10},... | collective-permute-start | bytes 159752 | tf_op jit(solution)/shard_map/ppermute | solution.py:318
  19.1 0.0 collective-permute-start.5
  19.1 0.1 collective-permute-start.3
  19.2 0.8 %collective-permute-start.4 = (bf16[208,128]{1,0:T(8,128)(2,1)S(1)}, bf16[208,128]{1,0:T(8,128)(2,1)S(1)}, u32[]{:S(2)}, u32[]{:S(2)}) collective-permute-start(bf16[208,128]{1,0:T(8,128)(2,1)S(1)} %get-tuple-element.38), channel_id=1, source_target_pairs={{0,4},{4,0},{8,12},{12,8},{1,5},{5,1},{9,13},{13,9},{2,6},{6,2},{1... | collective-permute-start | bytes 159752 | tf_op jit(solution)/shard_map/ppermute | solution.py:318
  20.0 0.4 %collective-permute-done.5.refs_0_.refs_2_ = bf16[192,128]{1,0:T(8,128)(2,1)S(1)} collective-permute-done((bf16[192,128]{1,0:T(8,128)(2,1)S(1)}, bf16[192,128]{1,0:T(8,128)(2,1)S(1)}, u32[]{:S(2)}, u32[]{:S(2)}) %collective-permute-start.5) | collective-permute-done | bytes 49184 | tf_op jit(solution)/shard_map/ppermute | solution.py:372
  20.3 0.0 collective-permute-done.10.refs_1_
  20.4 1.8 %collective-permute-start.13 = (bf16[384,128]{1,0:T(8,128)(2,1)S(1)}, bf16[384,128]{1,0:T(8,128)(2,1)S(1)}, u32[]{:S(2)}, u32[]{:S(2)}) collective-permute-start(bf16[384,128]{1,0:T(8,128)(2,1)S(1)} %round_out.1.refs_3_), channel_id=1, source_target_pairs={{0,8},{4,12},{8,0},{12,4},{1,9},{5,13},{9,1},{13,5},{2,10},{6,14},... | collective-permute-start | bytes 294920 | tf_op jit(solution)/shard_map/ppermute | solution.py:318
  22.2 1.5 %collective-permute-start.12 = (bf16[384,128]{1,0:T(8,128)(2,1)S(1)}, bf16[384,128]{1,0:T(8,128)(2,1)S(1)}, u32[]{:S(2)}, u32[]{:S(2)}) collective-permute-start(bf16[384,128]{1,0:T(8,128)(2,1)S(1)} %round_out.1.refs_3_), channel_id=1, source_target_pairs={{0,12},{4,8},{8,4},{12,0},{1,13},{5,9},{9,5},{13,1},{2,14},{6,10},... | collective-permute-start | bytes 294920 | tf_op jit(solution)/shard_map/ppermute | solution.py:318
  23.8 0.0 collective-permute-done.2.refs_2_.refs_0_.refs_4_
  23.8 0.5 %collective-permute-start.11 = (bf16[384,128]{1,0:T(8,128)(2,1)S(1)}, bf16[384,128]{1,0:T(8,128)(2,1)S(1)}, u32[]{:S(2)}, u32[]{:S(2)}) collective-permute-start(bf16[384,128]{1,0:T(8,128)(2,1)S(1)} %round_out.1.refs_3_), channel_id=1, source_target_pairs={{0,4},{4,0},{8,12},{12,8},{1,5},{5,1},{9,13},{13,9},{2,6},{6,2},{1... | collective-permute-start | bytes 294920 | tf_op jit(solution)/shard_map/ppermute | solution.py:318
  24.2 0.5 %collective-permute-done.3.refs_3_.refs_1_.refs_5_ = bf16[208,128]{1,0:T(8,128)(2,1)S(1)} collective-permute-done((bf16[208,128]{1,0:T(8,128)(2,1)S(1)}, bf16[208,128]{1,0:T(8,128)(2,1)S(1)}, u32[]{:S(2)}, u32[]{:S(2)}) %collective-permute-start.3) | collective-permute-done | bytes 53280 | tf_op jit(solution)/shard_map/ppermute | solution.py:318
  24.8 0.3 collective-permute-done.4.refs_4_.refs_2_.refs_6_
  25.1 0.1 collective-permute-start.6
  25.2 0.5 %collective-permute-start.7 = (bf16[288,128]{1,0:T(8,128)(2,1)S(1)}, bf16[288,128]{1,0:T(8,128)(2,1)S(1)}, u32[]{:S(2)}, u32[]{:S(2)}) collective-permute-start(bf16[288,128]{1,0:T(8,128)(2,1)S(1)} %get-tuple-element.42), channel_id=1, source_target_pairs={{0,1},{1,0},{2,3},{3,2},{4,5},{5,4},{6,7},{7,6},{8,9},{9,8},{10,11... | collective-permute-start | bytes 221192 | tf_op jit(solution)/shard_map/ppermute | solution.py:377
  25.7 0.0 copy-done
  25.7 0.9 %mask_own.1 = (bf16[2,384,512]{2,1,0:T(8,128)(2,1)S(1)}, f32[2,8,128]{2,1,0:T(8,128)S(1)}) custom-call(s32[2]{0:T(128)S(1)} %copy-done, bf16[208,128]{1,0:T(8,128)(2,1)S(1)} %get-tuple-element.35.refs_1_.refs_0_.refs_3_, bf16[208,128]{1,0:T(8,128)(2,1)S(1)} %collective-permute-done.2.refs_2_.refs_0_.refs_4_, ...), custom_call_target="tpu_custom_call" | custom-call | flops 1 | bytes 1 | tf_op jit(solution)/shard_map/mask_own/pallas_call | solution.py:283
  26.6 0.0 collective-permute-done.6.refs_1_
  26.6 0.0 collective-permute-done.7.refs_2_
  26.6 0.3 %mask_other.1.refs_2_ = bf16[2,384,512]{2,1,0:T(8,128)(2,1)S(1)} custom-call(bf16[192,128]{1,0:T(8,128)(2,1)S(1)} %collective-permute-done.5.refs_0_.refs_2_, bf16[288,128]{1,0:T(8,128)(2,1)S(1)} %collective-permute-done.6.refs_1_, bf16[288,128]{1,0:T(8,128)(2,1)S(1)} %collective-permute-done.7.refs_2_, ...), custom_call_target="tpu_custom_call" | custom-call | flops 1 | bytes 1 | tf_op jit(solution)/shard_map/mask_other/pallas_call | solution.py:283
  27.0 4.3 %collective-permute-done.13.refs_6_ = bf16[384,128]{1,0:T(8,128)(2,1)S(1)} collective-permute-done((bf16[384,128]{1,0:T(8,128)(2,1)S(1)}, bf16[384,128]{1,0:T(8,128)(2,1)S(1)}, u32[]{:S(2)}, u32[]{:S(2)}) %collective-permute-start.13) | collective-permute-done | bytes 98336 | tf_op jit(solution)/shard_map/ppermute | solution.py:318
  31.2 0.0 collective-permute-done.12.refs_5_
  31.2 0.2 collective-permute-done.11.refs_4_
  31.4 1.1 %blocks.1 = f32[2,128,128]{2,1,0:T(8,128)} custom-call(f32[2,8,128]{2,1,0:T(8,128)S(1)} %get-tuple-element.39.refs_7_.refs_0_, bf16[2,384,512]{2,1,0:T(8,128)(2,1)S(1)} %get-tuple-element.40.refs_1_, bf16[2,384,512]{2,1,0:T(8,128)(2,1)S(1)} %mask_other.1.refs_2_, bf16[384,128]{1,0:T(8,128)(2,1)S(1)} %round_out.1.refs_3_, ...), custom_call_target="tpu_custom_call" | custom-call | flops 1 | bytes 1 | tf_op jit(solution)/shard_map/blocks/pallas_call | solution.py:283
  (6 shorter events, 0.1 us)
Async XLA Ops:
  3.3 5.0 %slice-start = ((s8[8388608]{0:T(1024)(128)(4,1)}), s8[4194304]{0:T(1024)(128)(4,1)S(1)}, s32[]{:S(2)}) async-start(s8[8388608]{0:T(1024)(128)(4,1)} %bitcast.1), calls=%async_computation | async-start | bytes 8388608
  3.3 4.9 %slice-start.1 = ((s8[8388608]{0:T(1024)(128)(4,1)}), s8[4194304]{0:T(1024)(128)(4,1)S(1)}, s32[]{:S(2)}) async-start(s8[8388608]{0:T(1024)(128)(4,1)} %bitcast.1), calls=%async_computation.1 | async-start | bytes 8388608
  3.4 1.9 %collective-permute-start = (f32[768,128]{1,0:T(8,128)S(1)}, f32[768,128]{1,0:T(8,128)S(1)}, u32[]{:S(2)}, u32[]{:S(2)}) collective-permute-start(f32[768,128]{1,0:T(8,128)S(1)} %get-tuple-element.29), channel_id=1, source_target_pairs={{0,1},{1,0},{2,3},{3,2},{4,5},{5,4},{6,7},{7,6},{8,9},{9,8},{10,11... | collective-permute-start | bytes 1179656 | tf_op jit(solution)/shard_map/ppermute | solution.py:342
  5.3 20.4 %copy-start = (s32[2]{0:T(128)S(1)}, s32[2]{0:T(128)}, u32[]{:S(2)}) copy-start(s32[2]{0:T(128)} %refs_0_.4) | copy-start | bytes 28
  5.3 8.4 %collective-permute-start.1 = (bf16[784,128]{1,0:T(8,128)(2,1)S(1)}, bf16[784,128]{1,0:T(8,128)(2,1)S(1)}, u32[]{:S(2)}, u32[]{:S(2)}) collective-permute-start(bf16[784,128]{1,0:T(8,128)(2,1)S(1)} %get-tuple-element.33.refs_4_), channel_id=1, source_target_pairs={{0,2},{1,3},{2,0},{3,1},{4,6},{5,7},{6,4},{7,5},{8,10},{9,11},{10,... | collective-permute-start | bytes 602120 | tf_op jit(solution)/shard_map/ppermute | solution.py:347
  11.9 1.5 %collective-permute-start.8 = (f32[384,128]{1,0:T(8,128)S(1)}, f32[384,128]{1,0:T(8,128)S(1)}, u32[]{:S(2)}, u32[]{:S(2)}) collective-permute-start(f32[384,128]{1,0:T(8,128)S(1)} %get-tuple-element.45), channel_id=1, source_target_pairs={{0,1},{1,0},{2,3},{3,2},{4,5},{5,4},{6,7},{7,6},{8,9},{9,8},{10,11... | collective-permute-start | bytes 589832 | tf_op jit(solution)/shard_map/ppermute | solution.py:361
  12.0 1.7 %collective-permute-start.9 = (f32[384,128]{1,0:T(8,128)S(1)}, f32[384,128]{1,0:T(8,128)S(1)}, u32[]{:S(2)}, u32[]{:S(2)}) collective-permute-start(f32[384,128]{1,0:T(8,128)S(1)} %get-tuple-element.46), channel_id=1, source_target_pairs={{0,1},{1,0},{2,3},{3,2},{4,5},{5,4},{6,7},{7,6},{8,9},{9,8},{10,11... | collective-permute-start | bytes 589832 | tf_op jit(solution)/shard_map/ppermute | solution.py:361
  13.7 6.6 %collective-permute-start.10 = (bf16[384,128]{1,0:T(8,128)(2,1)S(1)}, bf16[384,128]{1,0:T(8,128)(2,1)S(1)}, u32[]{:S(2)}, u32[]{:S(2)}) collective-permute-start(bf16[384,128]{1,0:T(8,128)(2,1)S(1)} %get-tuple-element.48), channel_id=1, source_target_pairs={{0,2},{1,3},{2,0},{3,1},{4,6},{5,7},{6,4},{7,5},{8,10},{9,11},{10,... | collective-permute-start | bytes 294920 | tf_op jit(solution)/shard_map/ppermute | solution.py:365
  15.4 8.3 %collective-permute-start.2 = (bf16[208,128]{1,0:T(8,128)(2,1)S(1)}, bf16[208,128]{1,0:T(8,128)(2,1)S(1)}, u32[]{:S(2)}, u32[]{:S(2)}) collective-permute-start(bf16[208,128]{1,0:T(8,128)(2,1)S(1)} %get-tuple-element.36), channel_id=1, source_target_pairs={{0,12},{4,8},{8,4},{12,0},{1,13},{5,9},{9,5},{13,1},{2,14},{6,10},... | collective-permute-start | bytes 159752 | tf_op jit(solution)/shard_map/ppermute | solution.py:318
  19.1 1.2 %collective-permute-start.5 = (bf16[192,128]{1,0:T(8,128)(2,1)S(1)}, bf16[192,128]{1,0:T(8,128)(2,1)S(1)}, u32[]{:S(2)}, u32[]{:S(2)}) collective-permute-start(bf16[192,128]{1,0:T(8,128)(2,1)S(1)} %own_in.1), channel_id=1, source_target_pairs={{0,1},{1,0},{2,3},{3,2},{4,5},{5,4},{6,7},{7,6},{8,9},{9,8},{10,11... | collective-permute-start | bytes 147464 | tf_op jit(solution)/shard_map/ppermute | solution.py:372
  19.1 5.7 %collective-permute-start.3 = (bf16[208,128]{1,0:T(8,128)(2,1)S(1)}, bf16[208,128]{1,0:T(8,128)(2,1)S(1)}, u32[]{:S(2)}, u32[]{:S(2)}) collective-permute-start(bf16[208,128]{1,0:T(8,128)(2,1)S(1)} %get-tuple-element.37), channel_id=1, source_target_pairs={{0,8},{4,12},{8,0},{12,4},{1,9},{5,13},{9,1},{13,5},{2,10},{6,14},... | collective-permute-start | bytes 159752 | tf_op jit(solution)/shard_map/ppermute | solution.py:318
  19.2 5.9 %collective-permute-start.4 = (bf16[208,128]{1,0:T(8,128)(2,1)S(1)}, bf16[208,128]{1,0:T(8,128)(2,1)S(1)}, u32[]{:S(2)}, u32[]{:S(2)}) collective-permute-start(bf16[208,128]{1,0:T(8,128)(2,1)S(1)} %get-tuple-element.38), channel_id=1, source_target_pairs={{0,4},{4,0},{8,12},{12,8},{1,5},{5,1},{9,13},{13,9},{2,6},{6,2},{1... | collective-permute-start | bytes 159752 | tf_op jit(solution)/shard_map/ppermute | solution.py:318
  20.4 10.9 %collective-permute-start.13 = (bf16[384,128]{1,0:T(8,128)(2,1)S(1)}, bf16[384,128]{1,0:T(8,128)(2,1)S(1)}, u32[]{:S(2)}, u32[]{:S(2)}) collective-permute-start(bf16[384,128]{1,0:T(8,128)(2,1)S(1)} %round_out.1.refs_3_), channel_id=1, source_target_pairs={{0,8},{4,12},{8,0},{12,4},{1,9},{5,13},{9,1},{13,5},{2,10},{6,14},... | collective-permute-start | bytes 294920 | tf_op jit(solution)/shard_map/ppermute | solution.py:318
  22.2 9.0 %collective-permute-start.12 = (bf16[384,128]{1,0:T(8,128)(2,1)S(1)}, bf16[384,128]{1,0:T(8,128)(2,1)S(1)}, u32[]{:S(2)}, u32[]{:S(2)}) collective-permute-start(bf16[384,128]{1,0:T(8,128)(2,1)S(1)} %round_out.1.refs_3_), channel_id=1, source_target_pairs={{0,12},{4,8},{8,4},{12,0},{1,13},{5,9},{9,5},{13,1},{2,14},{6,10},... | collective-permute-start | bytes 294920 | tf_op jit(solution)/shard_map/ppermute | solution.py:318
  23.8 7.6 %collective-permute-start.11 = (bf16[384,128]{1,0:T(8,128)(2,1)S(1)}, bf16[384,128]{1,0:T(8,128)(2,1)S(1)}, u32[]{:S(2)}, u32[]{:S(2)}) collective-permute-start(bf16[384,128]{1,0:T(8,128)(2,1)S(1)} %round_out.1.refs_3_), channel_id=1, source_target_pairs={{0,4},{4,0},{8,12},{12,8},{1,5},{5,1},{9,13},{13,9},{2,6},{6,2},{1... | collective-permute-start | bytes 294920 | tf_op jit(solution)/shard_map/ppermute | solution.py:318
  25.1 1.5 %collective-permute-start.6 = (bf16[288,128]{1,0:T(8,128)(2,1)S(1)}, bf16[288,128]{1,0:T(8,128)(2,1)S(1)}, u32[]{:S(2)}, u32[]{:S(2)}) collective-permute-start(bf16[288,128]{1,0:T(8,128)(2,1)S(1)} %get-tuple-element.41), channel_id=1, source_target_pairs={{0,1},{1,0},{2,3},{3,2},{4,5},{5,4},{6,7},{7,6},{8,9},{9,8},{10,11... | collective-permute-start | bytes 221192 | tf_op jit(solution)/shard_map/ppermute | solution.py:377
  25.2 1.4 %collective-permute-start.7 = (bf16[288,128]{1,0:T(8,128)(2,1)S(1)}, bf16[288,128]{1,0:T(8,128)(2,1)S(1)}, u32[]{:S(2)}, u32[]{:S(2)}) collective-permute-start(bf16[288,128]{1,0:T(8,128)(2,1)S(1)} %get-tuple-element.42), channel_id=1, source_target_pairs={{0,1},{1,0},{2,3},{3,2},{4,5},{5,4},{6,7},{7,6},{8,9},{9,8},{10,11... | collective-permute-start | bytes 221192 | tf_op jit(solution)/shard_map/ppermute | solution.py:377
